TPU v7x, 32 devices: a whole 2x2x4 slice. The times are simulated.
32 devices in a mesh: ctx: 16 (over z, y, x), head: 2 (over core).
Axes of the slice: x: 2, y: 2, z: 4, core: 2. Of those that a mesh axis runs over, the one named last changes fastest.
Arguments:
- queries: bfloat16 [4096, 2048], P('ctx', 'head'), may hold values from -8 to 8
- keys: bfloat16 [4096, 2048], P('ctx', 'head'), may hold values from -8 to 8
- values: bfloat16 [4096, 2048], P('ctx', 'head'), may hold values from -6 to 6
- out_weight: bfloat16 [2048, 2048], replicated, may hold values from -0.125 to 0.125
- cotangent: bfloat16 [4096, 2048], P('ctx', 'head'), may hold values from -6 to 6
- bounds: int32 [4], replicated, may hold values from 0 to 3968, as said below
Outputs:
- output: bfloat16 [4096, 2048], P('ctx', 'head')
- grad_queries: bfloat16 [4096, 2048], P('ctx', 'head')
- grad_keys: bfloat16 [4096, 2048], P('ctx', 'head')
- grad_values: bfloat16 [4096, 2048], P('ctx', 'head')
Inputs may be any that keep to these rules, and one draw needn't show every extreme that they name: bounds starts at 0 and rises strictly; the last document begins 256 // 2 positions before the end of the sequence.
All inputs are finite; a program needn't handle non-finite values.
Results may differ from a plain program's by a relative error of at most 0.0079.
Values may be sent and summed in bfloat16 or wider, within the bound.
No kernel may reach another device: no remote copies, remote signals or barrier semaphores. Data moves between devices by JAX's collectives and lax.ppermute only.
A program may use at most 128 MiB of HBM per device.

v0:
```python
import math

import jax
import jax.numpy as jnp
from jax import lax
from jax.sharding import PartitionSpec as P

DH = 128
DILATION_STEP = 4


def from_behind(block, axis, distance):
    devices = range(lax.axis_size(axis))
    route = [(i - distance, i) for i in devices if i - distance in devices]
    return lax.ppermute(block, axis, route)


def doc_index(positions, bounds):
    return jnp.sum((bounds[None, :] <= positions[:, None]).astype(jnp.int32), axis=1)


def settle(nearby_block, extra, picked_rows, block_width):
    block_list = nearby_block.reshape(picked_rows, DILATION_STEP, block_width)
    block_list = jnp.concatenate([block_list[:, :1] + extra[:, None], block_list[:, 1:]], 1)
    return block_list.reshape(picked_rows * DILATION_STEP, block_width).astype(jnp.bfloat16)


def per_device(queries, keys, values, out_weight, cotangent, bounds):
    token_count, block_width = queries.shape
    heads_here = block_width // DH
    picked_rows = token_count // DILATION_STEP
    levels = lax.axis_size("ctx").bit_length() - 1
    device_piece = lax.axis_index("ctx")
    group = lax.axis_index("head")
    scale = 1.0 / math.sqrt(DH)
    w_rows = lax.dynamic_slice_in_dim(out_weight, group * block_width, block_width, 0)
    sparse_keys = keys.reshape(picked_rows, DILATION_STEP, block_width)[:, 0]
    sparse_values = values.reshape(picked_rows, DILATION_STEP, block_width)[:, 0]
    own_pos = device_piece * token_count + jnp.arange(token_count, dtype=jnp.int32)
    key_parts = [keys]
    value_parts = [values]
    key_positions = [own_pos]
    for level_number in range(levels):
        distant_keys, distant_values = from_behind(
            (sparse_keys, sparse_values), "ctx", 2**level_number
        )
        key_parts.append(distant_keys)
        value_parts.append(distant_values)
        key_positions.append(
            (device_piece - 2**level_number) * token_count
            + jnp.arange(picked_rows, dtype=jnp.int32) * DILATION_STEP
        )
    all_k = jnp.concatenate(key_parts, 0)
    all_v = jnp.concatenate(value_parts, 0)
    all_pos = jnp.concatenate(key_positions, 0)
    key_count = all_k.shape[0]
    allowed = doc_index(own_pos, bounds)[:, None] == doc_index(all_pos, bounds)[None, :]
    allowed = allowed & (all_pos[None, :] <= own_pos[:, None]) & (all_pos[None, :] >= 0)
    q3 = queries.reshape(token_count, heads_here, DH)
    k3 = all_k.reshape(key_count, heads_here, DH)
    v3 = all_v.reshape(key_count, heads_here, DH)
    scores = jnp.einsum("qhd,khd->hqk", q3, k3, preferred_element_type=jnp.float32) * scale
    scores = jnp.where(allowed[None], scores, -jnp.inf)
    top = jnp.max(scores, axis=2, keepdims=True)
    lse = top + jnp.log(jnp.sum(jnp.exp(scores - top), axis=2, keepdims=True))
    prob = jnp.exp(scores - lse)
    weights = prob.astype(jnp.bfloat16)
    attn = jnp.einsum("hqk,khd->qhd", weights, v3, preferred_element_type=jnp.float32)
    attn = attn.astype(jnp.bfloat16).reshape(token_count, block_width)
    term = jnp.dot(attn, w_rows, preferred_element_type=jnp.float32)
    output = lax.psum_scatter(term, "head", scatter_dimension=1, tiled=True).astype(jnp.bfloat16)
    full_cot = lax.all_gather(cotangent, "head", axis=1, tiled=True)
    grad_attn = lax.dot_general(
        full_cot, w_rows, (((1,), (1,)), ((), ())), preferred_element_type=jnp.float32
    )
    ga3 = grad_attn.astype(jnp.bfloat16).reshape(token_count, heads_here, DH)
    grad_prob = jnp.einsum("qhd,khd->hqk", ga3, v3, preferred_element_type=jnp.float32)
    delta = jnp.sum(prob * grad_prob, axis=2, keepdims=True)
    grad_scores = (prob * (grad_prob - delta) * scale).astype(jnp.bfloat16)
    grad_q = jnp.einsum("hqk,khd->qhd", grad_scores, k3, preferred_element_type=jnp.float32)
    grad_q = grad_q.astype(jnp.bfloat16).reshape(token_count, block_width)
    grad_k_all = jnp.einsum(
        "hqk,qhd->khd", grad_scores, q3, preferred_element_type=jnp.float32
    ).reshape(key_count, block_width)
    grad_v_all = jnp.einsum(
        "hqk,qhd->khd", weights, ga3, preferred_element_type=jnp.float32
    ).reshape(key_count, block_width)
    far_gk = [
        grad_k_all[
            token_count
            + level_number * picked_rows : token_count
            + (level_number + 1) * picked_rows
        ]
        for level_number in range(levels)
    ]
    far_gv = [
        grad_v_all[
            token_count
            + level_number * picked_rows : token_count
            + (level_number + 1) * picked_rows
        ]
        for level_number in range(levels)
    ]
    extra_k = jnp.zeros((picked_rows, block_width), jnp.float32)
    extra_v = jnp.zeros((picked_rows, block_width), jnp.float32)
    for level_number in range(levels):
        back_k, back_v = from_behind(
            (far_gk[level_number], far_gv[level_number]), "ctx", -(2**level_number)
        )
        extra_k = extra_k + back_k
        extra_v = extra_v + back_v
    grad_k = settle(grad_k_all[:token_count], extra_k, picked_rows, block_width)
    grad_v = settle(grad_v_all[:token_count], extra_v, picked_rows, block_width)
    return (output, grad_q, grad_k, grad_v)


def solution(mesh):
    placed = (P("ctx", "head"), P("ctx", "head"), P("ctx", "head"), P(), P("ctx", "head"), P())
    return jax.shard_map(
        per_device,
        mesh=mesh,
        in_specs=placed,
        out_specs=(P("ctx", "head"), P("ctx", "head"), P("ctx", "head"), P("ctx", "head")),
        check_vma=False,
    )
```

profile of v0, /device:TPU:13, one launch (start us, length us, event | category | flops | bytes accessed | tf_op | source)
XLA Modules:
  0.0 165.7 jit_solution(229297050523951856)
XLA Ops:
  8.8 3.1 %collective-permute-start.4 = (bf16[64,1024]{1,0:T(8,128)(2,1)S(1)}, bf16[64,1024]{1,0:T(8,128)(2,1)S(1)}, u32[]{:S(2)}, u32[]{:S(2)}) collective-permute-start(bf16[64,1024]{1,0:T(8,128)(2,1)S(1)} %bitcast.112), channel_id=1, source_target_pairs={{0,2},{2,4},{4,6},{6,8},{8,10},{10,12},{12,14},{14,16},{16,18},{18... | collective-permute-start | bytes 393224 | tf_op jit(solution)/shard_map/ppermute | solution.py:15
  12.0 3.1 %collective-permute-start.5 = (bf16[64,1024]{1,0:T(8,128)(2,1)S(1)}, bf16[64,1024]{1,0:T(8,128)(2,1)S(1)}, u32[]{:S(2)}, u32[]{:S(2)}) collective-permute-start(bf16[64,1024]{1,0:T(8,128)(2,1)S(1)} %bitcast.113), channel_id=1, source_target_pairs={{0,4},{2,6},{4,8},{6,10},{8,12},{10,14},{12,16},{14,18},{16,20},{1... | collective-permute-start | bytes 393224 | tf_op jit(solution)/shard_map/ppermute | solution.py:15
  15.1 3.2 %collective-permute-start.6 = (bf16[64,1024]{1,0:T(8,128)(2,1)S(1)}, bf16[64,1024]{1,0:T(8,128)(2,1)S(1)}, u32[]{:S(2)}, u32[]{:S(2)}) collective-permute-start(bf16[64,1024]{1,0:T(8,128)(2,1)S(1)} %bitcast.114), channel_id=1, source_target_pairs={{0,8},{2,10},{4,12},{6,14},{8,16},{10,18},{12,20},{14,22},{16,24},... | collective-permute-start | bytes 393224 | tf_op jit(solution)/shard_map/ppermute | solution.py:15
  21.1 3.1 %collective-permute-start = (bf16[64,1024]{1,0:T(8,128)(2,1)S(1)}, bf16[64,1024]{1,0:T(8,128)(2,1)}, u32[]{:S(2)}, u32[]{:S(2)}) collective-permute-start(bf16[64,1024]{1,0:T(8,128)(2,1)S(1)} %bitcast.108), channel_id=1, source_target_pairs={{0,2},{2,4},{4,6},{6,8},{8,10},{10,12},{12,14},{14,16},{16,18},{18... | collective-permute-start | bytes 393224 | tf_op jit(solution)/shard_map/ppermute | solution.py:15
  30.3 1.9 %collective-permute-start.3 = (bf16[64,1024]{1,0:T(8,128)(2,1)S(1)}, bf16[64,1024]{1,0:T(8,128)(2,1)}, u32[]{:S(2)}, u32[]{:S(2)}) collective-permute-start(bf16[64,1024]{1,0:T(8,128)(2,1)S(1)} %bitcast.111), channel_id=1, source_target_pairs={{0,16},{2,18},{4,20},{6,22},{8,24},{10,26},{12,28},{14,30},{1,17},... | collective-permute-start | bytes 393224 | tf_op jit(solution)/shard_map/ppermute | solution.py:15
  32.6 2.3 %concatenate.23 = bf16[512,1024]{0,1:T(8,128)(2,1)S(1)} concatenate(bf16[256,1024]{0,1:T(8,128)(2,1)S(1)} %copy.80, bf16[64,1024]{0,1:T(8,128)(2,1)S(1)} %copy.81, bf16[64,1024]{0,1:T(8,128)(2,1)S(1)} %copy.82, bf16[64,1024]{0,1:T(8,128)(2,1)S(1)} %copy.83, bf16[64,1024]{0,1:T(8,128)(2,1)S(1)} %copy.84), dimensions={0} | concatenate | bytes 2097152 | tf_op jit(solution)/shard_map/concatenate | solution.py:53
  35.8 2.0 %copy-done.1 = f32[8,512,256]{2,1,0:T(8,128)} copy-done((f32[8,512,256]{2,1,0:T(8,128)}, f32[8,512,256]{2,1,0:T(8,128)S(1)}, u32[]{:S(2)}) %copy-start.1) | copy-done | bytes 4194328
  46.4 3.4 %convolution_convert_fusion = bf16[8,128,256]{2,1,0:T(8,128)(2,1)S(1)} fusion(bf16[512,8,128]{0,2,1:T(8,128)(2,1)S(1)} %bitcast.99, f32[8,512,256]{2,1,0:T(8,128)} %copy-done.1, f32[8,256]{1,0:T(8,128)S(1)} %log_add_fusion, pred[256,512]{0,1:T(8,128)(4,1)S(1)} %and_and_fusion), kind=kOutput, calls=%fused_computation.18 | convolution fusion | flops 272891904 | bytes 5906432 | tf_op jit(solution)/shard_map/hqk,khd->qhd/dot_general | solution.py:68
  49.8 4.8 %fusion.4 = f32[256,2048]{1,0:T(8,128)} fusion(bf16[256,1024]{0,1:T(8,128)(2,1)S(1)} %bitcast.116, bf16[2048,2048]{1,0:T(8,128)(2,1)} %param.9, s32[]{:T(128)S(6)} %select_n.8), kind=kOutput, calls=%fused_computation.9 | convolution fusion | flops 1073741824 | bytes 6815748 | tf_op jit(solution)/shard_map/dot_general | solution.py:70
  54.7 3.8 %fusion.23 = bf16[1024,256]{1,0:T(8,128)(2,1)S(1)} fusion(bf16[256,2048]{1,0:T(8,128)(2,1)} %all-gather.2.cloned.1.call-done, bf16[2048,2048]{1,0:T(8,128)(2,1)} %param.9, s32[]{:T(128)S(6)} %select_n.8), kind=kOutput, calls=%fused_computation.20 | convolution fusion | flops 1074003968 | bytes 5767172 | tf_op jit(solution)/shard_map/dot_general | solution.py:73
  59.3 2.7 %fusion.46 = f32[8,256,512]{1,2,0:T(8,128)} fusion(bf16[256,8,128]{0,2,1:T(8,128)(2,1)S(1)} %bitcast.105, bf16[512,8,128]{0,2,1:T(8,128)(2,1)S(1)} %bitcast.100), kind=kOutput, calls=%fused_computation.71 | convolution fusion | flops 268435456 | bytes 5767168 | tf_op jit(solution)/shard_map/qhd,khd->hqk/dot_general | solution.py:77
  62.0 9.5 %fusion.20 = bf16[8,128,256]{2,1,0:T(8,128)(2,1)S(1)} fusion(bf16[512,8,128]{0,2,1:T(8,128)(2,1)S(1)} %bitcast.98, f32[8,256,512]{1,2,0:T(8,128)} %fusion.46, f32[8,512,256]{2,1,0:T(8,128)} %copy-done.1, f32[8,256]{1,0:T(8,128)S(1)} %log_add_fusion, pred[256,512]{0,1:T(8,128)(4,1)S(1)} %and_and_fusion), kind=kOutput, calls=%fused_computation.19 | convolution fusion | flops 280234496 | bytes 10100736 | tf_op jit(solution)/shard_map/hqk,khd->qhd/dot_general | solution.py:80
  72.6 8.5 %fusion.17 = f32[512,8,128]{2,0,1:T(8,128)S(1)} fusion(f32[8,256,512]{1,2,0:T(8,128)} %fusion.46, f32[8,512,256]{2,1,0:T(8,128)} %copy-done.1, f32[8,256]{1,0:T(8,128)S(1)} %log_add_fusion, pred[256,512]{0,1:T(8,128)(4,1)S(1)} %and_and_fusion, bf16[256,1024]{1,0:T(8,128)(2,1)S(1)} %copy-done), kind=kOutput, calls=%fused_computation.16 | convolution fusion | flops 279972352 | bytes 11149312 | tf_op jit(solution)/shard_map/hqk,qhd->khd/dot_general | solution.py:82
  88.4 3.4 %collective-permute-start.10 = (f32[64,1024]{1,0:T(8,128)}, f32[64,1024]{1,0:T(8,128)}, u32[]{:S(2)}, u32[]{:S(2)}) collective-permute-start(f32[64,1024]{1,0:T(8,128)} %bitcast.92), channel_id=1, source_target_pairs={{8,0},{10,2},{12,4},{14,6},{16,8},{18,10},{20,12},{22,14},{24,16},... | collective-permute-start | bytes 786440 | tf_op jit(solution)/shard_map/ppermute | solution.py:15
  92.6 4.1 %collective-permute-start.8 = (f32[64,1024]{1,0:T(8,128)}, f32[64,1024]{1,0:T(8,128)}, u32[]{:S(2)}, u32[]{:S(2)}) collective-permute-start(f32[64,1024]{1,0:T(8,128)} %bitcast.94), channel_id=1, source_target_pairs={{2,0},{4,2},{6,4},{8,6},{10,8},{12,10},{14,12},{16,14},{18,16},{20... | collective-permute-start | bytes 786440 | tf_op jit(solution)/shard_map/ppermute | solution.py:15
  101.7 2.6 %copy.100 = f32[256,8,128]{2,1,0:T(8,128)} copy(f32[256,8,128]{0,2,1:T(8,128)} %slice.109) | data formatting | bytes 2097152 | tf_op jit(solution)/shard_map/slice | solution.py:113
  104.3 2.6 %reshape.184 = f32[64,4,1024]{2,1,0:T(4,128)} reshape(f32[256,8,128]{2,1,0:T(8,128)} %copy.100) | data formatting | bytes 2097152 | tf_op jit(solution)/shard_map/reshape | solution.py:23
  106.9 2.3 %slice.128 = bf16[64,3,1024]{2,1,0:T(4,128)(2,1)} slice(f32[64,4,1024]{2,1,0:T(4,128)} %reshape.184), slice={[0:64], [1:4], [0:1024]} | slice | bytes 786432 | tf_op jit(solution)/shard_map/slice | solution.py:24
  115.3 2.0 %copy.101 = f32[64,1024]{1,0:T(8,128)} copy(f32[64,1024]{0,1:T(8,128)} %bitcast.102) | data formatting | bytes 524288 | tf_op jit(solution)/shard_map/slice | solution.py:97
  120.5 2.4 %collective-permute-start.12 = (f32[64,1024]{1,0:T(8,128)}, f32[64,1024]{1,0:T(8,128)}, u32[]{:S(2)}, u32[]{:S(2)}) collective-permute-start(f32[64,1024]{1,0:T(8,128)} %copy.101), channel_id=1, source_target_pairs={{2,0},{4,2},{6,4},{8,6},{10,8},{12,10},{14,12},{16,14},{18,16},{20... | collective-permute-start | bytes 786440 | tf_op jit(solution)/shard_map/ppermute | solution.py:15
  122.9 2.0 %collective-permute-start.13 = (f32[64,1024]{1,0:T(8,128)S(1)}, f32[64,1024]{1,0:T(8,128)}, u32[]{:S(2)}, u32[]{:S(2)}) collective-permute-start(f32[64,1024]{1,0:T(8,128)S(1)} %copy.102), channel_id=1, source_target_pairs={{4,0},{6,2},{8,4},{10,6},{12,8},{14,10},{16,12},{18,14},{20,16},{2... | collective-permute-start | bytes 786440 | tf_op jit(solution)/shard_map/ppermute | solution.py:15
  124.9 4.4 %collective-permute-done.9 = f32[64,1024]{1,0:T(8,128)} collective-permute-done((f32[64,1024]{1,0:T(8,128)}, f32[64,1024]{1,0:T(8,128)}, u32[]{:S(2)}, u32[]{:S(2)}) %collective-permute-start.9) | collective-permute-done | bytes 262176 | tf_op jit(solution)/shard_map/ppermute | solution.py:15
  133.4 19.2 %collective-permute-done.13 = f32[64,1024]{1,0:T(8,128)} collective-permute-done((f32[64,1024]{1,0:T(8,128)S(1)}, f32[64,1024]{1,0:T(8,128)}, u32[]{:S(2)}, u32[]{:S(2)}) %collective-permute-start.13) | collective-permute-done | bytes 262176 | tf_op jit(solution)/shard_map/ppermute | solution.py:15
  156.8 2.1 %convert_element_type.46 = bf16[256,1024]{1,0:T(8,128)(2,1)} convert(f32[256,1024]{1,0:T(8,128)} %reduce-scatter.2.cloned.1.call-done) | non-fusion elementwise | flops 262144 | bytes 1572864 | tf_op jit(solution)/shard_map/convert_element_type | solution.py:71
  (100 shorter events, 52.6 us)
Async XLA Ops:
  7.2 27.7 %copy-start = (bf16[256,1024]{1,0:T(8,128)(2,1)S(1)}, bf16[256,1024]{1,0:T(8,128)(2,1)}, u32[]{:S(2)}) copy-start(bf16[256,1024]{1,0:T(8,128)(2,1)} %param.6) | copy-start | bytes 1572868
  7.2 17.7 %copy-start.5 = (bf16[256,1024]{1,0:T(8,128)(2,1)S(1)}, bf16[256,1024]{1,0:T(8,128)(2,1)}, u32[]{:S(2)}) copy-start(bf16[256,1024]{1,0:T(8,128)(2,1)} %param.7) | copy-start | bytes 1572868
  7.2 18.0 %copy-start.6 = (bf16[256,1024]{1,0:T(8,128)(2,1)S(1)}, bf16[256,1024]{1,0:T(8,128)(2,1)}, u32[]{:S(2)}) copy-start(bf16[256,1024]{1,0:T(8,128)(2,1)} %param.8) | copy-start | bytes 1572868
  7.2 17.2 %copy-start.10 = (s32[4]{0:T(128)S(1)}, s32[4]{0:T(128)}, u32[]{:S(2)}) copy-start(s32[4]{0:T(128)} %param.11) | copy-start | bytes 52
  7.2 47.5 %all-gather.2.cloned.1.call-start = ((), (), s32[]{:S(2)}) async-start(), calls=%async_computation.2 | async-start | bytes 1572864 | tf_op jit(solution)/shard_map/all_gather | solution.py:72
  8.8 17.2 %collective-permute-start.4 = (bf16[64,1024]{1,0:T(8,128)(2,1)S(1)}, bf16[64,1024]{1,0:T(8,128)(2,1)S(1)}, u32[]{:S(2)}, u32[]{:S(2)}) collective-permute-start(bf16[64,1024]{1,0:T(8,128)(2,1)S(1)} %bitcast.112), channel_id=1, source_target_pairs={{0,2},{2,4},{4,6},{6,8},{8,10},{10,12},{12,14},{14,16},{16,18},{18... | collective-permute-start | bytes 393224 | tf_op jit(solution)/shard_map/ppermute | solution.py:15
  12.0 16.2 %collective-permute-start.5 = (bf16[64,1024]{1,0:T(8,128)(2,1)S(1)}, bf16[64,1024]{1,0:T(8,128)(2,1)S(1)}, u32[]{:S(2)}, u32[]{:S(2)}) collective-permute-start(bf16[64,1024]{1,0:T(8,128)(2,1)S(1)} %bitcast.113), channel_id=1, source_target_pairs={{0,4},{2,6},{4,8},{6,10},{8,12},{10,14},{12,16},{14,18},{16,20},{1... | collective-permute-start | bytes 393224 | tf_op jit(solution)/shard_map/ppermute | solution.py:15
  15.1 15.1 %collective-permute-start.6 = (bf16[64,1024]{1,0:T(8,128)(2,1)S(1)}, bf16[64,1024]{1,0:T(8,128)(2,1)S(1)}, u32[]{:S(2)}, u32[]{:S(2)}) collective-permute-start(bf16[64,1024]{1,0:T(8,128)(2,1)S(1)} %bitcast.114), channel_id=1, source_target_pairs={{0,8},{2,10},{4,12},{6,14},{8,16},{10,18},{12,20},{14,22},{16,24},... | collective-permute-start | bytes 393224 | tf_op jit(solution)/shard_map/ppermute | solution.py:15
  18.3 14.0 %collective-permute-start.7 = (bf16[64,1024]{1,0:T(8,128)(2,1)S(1)}, bf16[64,1024]{1,0:T(8,128)(2,1)S(1)}, u32[]{:S(2)}, u32[]{:S(2)}) collective-permute-start(bf16[64,1024]{1,0:T(8,128)(2,1)S(1)} %bitcast.115), channel_id=1, source_target_pairs={{0,16},{2,18},{4,20},{6,22},{8,24},{10,26},{12,28},{14,30},{1,17},... | collective-permute-start | bytes 393224 | tf_op jit(solution)/shard_map/ppermute | solution.py:15
  21.1 17.5 %collective-permute-start = (bf16[64,1024]{1,0:T(8,128)(2,1)S(1)}, bf16[64,1024]{1,0:T(8,128)(2,1)}, u32[]{:S(2)}, u32[]{:S(2)}) collective-permute-start(bf16[64,1024]{1,0:T(8,128)(2,1)S(1)} %bitcast.108), channel_id=1, source_target_pairs={{0,2},{2,4},{4,6},{6,8},{8,10},{10,12},{12,14},{14,16},{16,18},{18... | collective-permute-start | bytes 393224 | tf_op jit(solution)/shard_map/ppermute | solution.py:15
  24.3 132.5 %reduce-scatter.2.cloned.1.call-start = ((), (), s32[]{:S(2)}) async-start(), calls=%async_computation.1 | async-start | bytes 3145728 | tf_op jit(solution)/shard_map/reduce_scatter | solution.py:71
  26.0 14.2 %collective-permute-start.1 = (bf16[64,1024]{1,0:T(8,128)(2,1)S(1)}, bf16[64,1024]{1,0:T(8,128)(2,1)}, u32[]{:S(2)}, u32[]{:S(2)}) collective-permute-start(bf16[64,1024]{1,0:T(8,128)(2,1)S(1)} %bitcast.109), channel_id=1, source_target_pairs={{0,4},{2,6},{4,8},{6,10},{8,12},{10,14},{12,16},{14,18},{16,20},{1... | collective-permute-start | bytes 393224 | tf_op jit(solution)/shard_map/ppermute | solution.py:15
  28.1 13.6 %collective-permute-start.2 = (bf16[64,1024]{1,0:T(8,128)(2,1)S(1)}, bf16[64,1024]{1,0:T(8,128)(2,1)}, u32[]{:S(2)}, u32[]{:S(2)}) collective-permute-start(bf16[64,1024]{1,0:T(8,128)(2,1)S(1)} %bitcast.110), channel_id=1, source_target_pairs={{0,8},{2,10},{4,12},{6,14},{8,16},{10,18},{12,20},{14,22},{16,24},... | collective-permute-start | bytes 393224 | tf_op jit(solution)/shard_map/ppermute | solution.py:15
  30.3 13.1 %collective-permute-start.3 = (bf16[64,1024]{1,0:T(8,128)(2,1)S(1)}, bf16[64,1024]{1,0:T(8,128)(2,1)}, u32[]{:S(2)}, u32[]{:S(2)}) collective-permute-start(bf16[64,1024]{1,0:T(8,128)(2,1)S(1)} %bitcast.111), channel_id=1, source_target_pairs={{0,16},{2,18},{4,20},{6,22},{8,24},{10,26},{12,28},{14,30},{1,17},... | collective-permute-start | bytes 393224 | tf_op jit(solution)/shard_map/ppermute | solution.py:15
  83.5 15.8 %copy-start.2 = (f32[8,512,256]{2,1,0:T(8,128)S(1)}, f32[8,512,256]{2,1,0:T(8,128)}, u32[]{:S(2)}) copy-start(f32[8,512,256]{2,1,0:T(8,128)} %copy-done.1) | copy-start | bytes 12582916
  86.4 32.2 %collective-permute-start.11 = (f32[64,1024]{1,0:T(8,128)}, f32[64,1024]{1,0:T(8,128)S(1)}, u32[]{:S(2)}, u32[]{:S(2)}) collective-permute-start(f32[64,1024]{1,0:T(8,128)} %bitcast.91), channel_id=1, source_target_pairs={{16,0},{18,2},{20,4},{22,6},{24,8},{26,10},{28,12},{30,14},{17,1},... | collective-permute-start | bytes 786440 | tf_op jit(solution)/shard_map/ppermute | solution.py:15
  88.4 32.1 %collective-permute-start.10 = (f32[64,1024]{1,0:T(8,128)}, f32[64,1024]{1,0:T(8,128)}, u32[]{:S(2)}, u32[]{:S(2)}) collective-permute-start(f32[64,1024]{1,0:T(8,128)} %bitcast.92), channel_id=1, source_target_pairs={{8,0},{10,2},{12,4},{14,6},{16,8},{18,10},{20,12},{22,14},{24,16},... | collective-permute-start | bytes 786440 | tf_op jit(solution)/shard_map/ppermute | solution.py:15
  92.6 30.3 %collective-permute-start.8 = (f32[64,1024]{1,0:T(8,128)}, f32[64,1024]{1,0:T(8,128)}, u32[]{:S(2)}, u32[]{:S(2)}) collective-permute-start(f32[64,1024]{1,0:T(8,128)} %bitcast.94), channel_id=1, source_target_pairs={{2,0},{4,2},{6,4},{8,6},{10,8},{12,10},{14,12},{16,14},{18,16},{20... | collective-permute-start | bytes 786440 | tf_op jit(solution)/shard_map/ppermute | solution.py:15
  97.4 31.9 %collective-permute-start.9 = (f32[64,1024]{1,0:T(8,128)}, f32[64,1024]{1,0:T(8,128)}, u32[]{:S(2)}, u32[]{:S(2)}) collective-permute-start(f32[64,1024]{1,0:T(8,128)} %bitcast.93), channel_id=1, source_target_pairs={{4,0},{6,2},{8,4},{10,6},{12,8},{14,10},{16,12},{18,14},{20,16},{2... | collective-permute-start | bytes 786440 | tf_op jit(solution)/shard_map/ppermute | solution.py:15
  112.1 21.4 %collective-permute-start.15 = (f32[64,1024]{1,0:T(8,128)S(1)}, f32[64,1024]{1,0:T(8,128)S(1)}, u32[]{:S(2)}, u32[]{:S(2)}) collective-permute-start(f32[64,1024]{1,0:T(8,128)S(1)} %copy.104), channel_id=1, source_target_pairs={{16,0},{18,2},{20,4},{22,6},{24,8},{26,10},{28,12},{30,14},{17,1},... | collective-permute-start | bytes 786440 | tf_op jit(solution)/shard_map/ppermute | solution.py:15
  115.3 40.0 %copy-start.7 = (bf16[64,3,1024]{2,1,0:T(4,128)(2,1)S(1)}, bf16[64,3,1024]{2,1,0:T(4,128)(2,1)}, u32[]{:S(2)}) copy-start(bf16[64,3,1024]{2,1,0:T(4,128)(2,1)} %slice.128) | copy-start | bytes 1179652
  118.5 14.9 %collective-permute-start.14 = (f32[64,1024]{1,0:T(8,128)}, f32[64,1024]{1,0:T(8,128)}, u32[]{:S(2)}, u32[]{:S(2)}) collective-permute-start(f32[64,1024]{1,0:T(8,128)} %copy.103), channel_id=1, source_target_pairs={{8,0},{10,2},{12,4},{14,6},{16,8},{18,10},{20,12},{22,14},{24,16},... | collective-permute-start | bytes 786440 | tf_op jit(solution)/shard_map/ppermute | solution.py:15
  120.5 13.0 %collective-permute-start.12 = (f32[64,1024]{1,0:T(8,128)}, f32[64,1024]{1,0:T(8,128)}, u32[]{:S(2)}, u32[]{:S(2)}) collective-permute-start(f32[64,1024]{1,0:T(8,128)} %copy.101), channel_id=1, source_target_pairs={{2,0},{4,2},{6,4},{8,6},{10,8},{12,10},{14,12},{16,14},{18,16},{20... | collective-permute-start | bytes 786440 | tf_op jit(solution)/shard_map/ppermute | solution.py:15
  122.9 29.7 %collective-permute-start.13 = (f32[64,1024]{1,0:T(8,128)S(1)}, f32[64,1024]{1,0:T(8,128)}, u32[]{:S(2)}, u32[]{:S(2)}) collective-permute-start(f32[64,1024]{1,0:T(8,128)S(1)} %copy.102), channel_id=1, source_target_pairs={{4,0},{6,2},{8,4},{10,6},{12,8},{14,10},{16,12},{18,14},{20,16},{2... | collective-permute-start | bytes 786440 | tf_op jit(solution)/shard_map/ppermute | solution.py:15
  (5 other events, 33.8 us)
Sparse Core Ops, SparseCore 0:
  24.4 9.9 all-gather.1
  54.8 12.2 reduce-scatter.1
where the time goes:
time: 167 us; the launch traced here: 166 us
  local copies, waits for them, and re-layouts  44.6 us (27%)
  starting transfers between devices  38.1 us (23%)
  matrix products  34.9 us (21%)
  waiting for transfers between devices  23.6 us (14%)
  between operations  14.6 us (9%)
  other arithmetic  9.9 us (6%)
    ppermute x16, starting transfers between devices, from_behind(): return lax.ppermute(block, axis, route)  38 us
    ppermute x16, waiting for transfers between devices, from_behind(): return lax.ppermute(block, axis, route)  23.6 us
    unnamed x31, local copies, waits for them, and re-layouts  12.8 us
    dot_general x1, matrix products, per_device(): jnp.einsum('hqk,khd->qhd', grad_scores, k3, preferred_element_type=jnp.fl...  9.53 us
    dot_general x1, matrix products, per_device(): jnp.einsum('hqk,qhd->khd', grad_scores, q3, preferred_element_type=jnp.fl...  8.5 us
    slice x5, local copies, waits for them, and re-layouts, per_device(): grad_v_all[token_count + level_number * picked_rows:token_count + (level_...  8.03 us
    dot_general x1, matrix products, per_device(): term = jnp.dot(attn, w_rows, preferred_element_type=jnp.float32)  4.84 us
    dot_general x1, matrix products, per_device(): lax.dot_general(full_cot, w_rows, (((1,), (1,)), ((), ())), preferred_ele...  3.78 us
  transfers between devices with their start and end apart: 18, of which 2 were waited for; matrix products, arithmetic and copies ran while one was open for 49% of the time, Pallas kernels for 0%

commit v1 on v0

v1 whole, which is shorter than its diff:
```python
import functools
import math

import jax
import jax.numpy as jnp
from jax import lax
from jax.experimental import pallas as pl
from jax.experimental.pallas import tpu as pltpu
from jax.sharding import PartitionSpec as P

DH = 128
STEP = 4
VMEM_LIMIT = 40 * 1024 * 1024
BF16 = jnp.bfloat16
F32 = jnp.float32


def shift(block, axis, distance):
    devices = range(lax.axis_size(axis))
    route = [(i, i + distance) for i in devices if i + distance in devices]
    return lax.ppermute(block, axis, route)


def swap(block):
    return lax.ppermute(block, "head", [(0, 1), (1, 0)])


def nt(a, b):
    return lax.dot_general(a, b, (((1,), (1,)), ((), ())), preferred_element_type=F32)


def tn(a, b):
    return lax.dot_general(a, b, (((0,), (0,)), ((), ())), preferred_element_type=F32)


def nn(a, b):
    return jnp.dot(a, b, preferred_element_type=F32)


def params():
    return pltpu.CompilerParams(vmem_limit_bytes=VMEM_LIMIT)


def pick_kernel(k_ref, v_ref, out_ref):
    tokens = k_ref.shape[0]
    rows = tokens // STEP
    at = lax.broadcasted_iota(jnp.int32, (rows, tokens), 0) * STEP
    choose = (at == lax.broadcasted_iota(jnp.int32, (rows, tokens), 1)).astype(BF16)
    out_ref[:rows] = nn(choose, k_ref[...]).astype(BF16)
    out_ref[rows:] = nn(choose, v_ref[...]).astype(BF16)


def pick(keys, values):
    tokens, width = keys.shape
    return pl.pallas_call(
        pick_kernel,
        out_shape=jax.ShapeDtypeStruct((2 * tokens // STEP, width), BF16),
        compiler_params=params(),
        name="pick",
    )(keys, values)


def grad_attn_kernel(g_ref, own_ref, other_ref, w_own_ref, w_other_ref, out_ref):
    total = nt(own_ref[...], w_own_ref[...]) + nt(other_ref[...], w_other_ref[...])
    out_ref[...] = total.astype(BF16)


def grad_attn(group, own, other, weight):
    tokens, width = own.shape
    tile = 256
    tiles = width // tile
    whole = pl.BlockSpec((tokens, width), lambda i, g: (0, 0))
    return pl.pallas_call(
        grad_attn_kernel,
        grid_spec=pltpu.PrefetchScalarGridSpec(
            num_scalar_prefetch=1,
            grid=(tiles,),
            in_specs=[
                whole,
                whole,
                pl.BlockSpec((tile, width), lambda i, g: (g[0] * tiles + i, g[0])),
                pl.BlockSpec((tile, width), lambda i, g: (g[0] * tiles + i, 1 - g[0])),
            ],
            out_specs=pl.BlockSpec((tokens, tile), lambda i, g: (0, i)),
        ),
        out_shape=jax.ShapeDtypeStruct((tokens, width), BF16),
        compiler_params=params(),
        cost_estimate=pl.CostEstimate(
            flops=4 * tokens * width * width, bytes_accessed=6 * width * width, transcendentals=0
        ),
        name="grad_attn",
    )(group, own, other, weight, weight)


def project_kernel(g_ref, own_ref, other_ref, w_own_ref, w_other_ref, out_ref):
    total = nn(own_ref[...], w_own_ref[...]) + nn(other_ref[...], w_other_ref[...])
    out_ref[...] = total.astype(BF16)


def project(group, own, other, weight):
    tokens, width = own.shape
    tile = 256
    tiles = width // tile
    whole = pl.BlockSpec((tokens, width), lambda i, g: (0, 0))
    return pl.pallas_call(
        project_kernel,
        grid_spec=pltpu.PrefetchScalarGridSpec(
            num_scalar_prefetch=1,
            grid=(tiles,),
            in_specs=[
                whole,
                whole,
                pl.BlockSpec((width, tile), lambda i, g: (g[0], g[0] * tiles + i)),
                pl.BlockSpec((width, tile), lambda i, g: (1 - g[0], g[0] * tiles + i)),
            ],
            out_specs=pl.BlockSpec((tokens, tile), lambda i, g: (0, i)),
        ),
        out_shape=jax.ShapeDtypeStruct((tokens, width), BF16),
        compiler_params=params(),
        cost_estimate=pl.CostEstimate(
            flops=4 * tokens * width * width, bytes_accessed=6 * width * width, transcendentals=0
        ),
        name="project",
    )(group, own, other, weight, weight)


def documents(positions, bounds_ref):
    count = jnp.zeros(positions.shape, jnp.int32)
    for i in range(bounds_ref.shape[0]):
        count = count + (bounds_ref[i] <= positions).astype(jnp.int32)
    return count


def mask_bias(me, bounds_ref, tokens, levels):
    rows = tokens // STEP
    own = lax.broadcasted_iota(jnp.int32, (tokens, 1), 0) + me * tokens
    parts = [lax.broadcasted_iota(jnp.int32, (1, tokens), 1) + me * tokens]
    far = lax.broadcasted_iota(jnp.int32, (1, levels * rows), 1)
    level = far // rows
    source = me - (jnp.ones_like(level) << level)
    parts.append(source * tokens + (far - level * rows) * STEP)
    own_doc = documents(own, bounds_ref)
    out = []
    for part in parts:
        part_doc = jnp.where(part >= 0, documents(part, bounds_ref), -1)
        ok = (own_doc == part_doc) & (part <= own)
        out.append(jnp.where(ok, 0.0, -jnp.inf).astype(F32))
    return jnp.concatenate(out, 1)


def attention_kernel(levels, *refs):
    me_ref, bounds_ref, q_ref, k_ref, v_ref, ga_ref = refs[:6]
    far_refs = refs[6 : 6 + levels]
    attn_ref, gq_ref, gk_ref, gv_ref = refs[6 + levels : 10 + levels]
    gfar_refs = refs[10 + levels : 10 + 2 * levels]
    bias_ref = refs[10 + 2 * levels]
    tokens = q_ref.shape[0]
    rows = tokens // STEP
    scale = 1.0 / math.sqrt(DH)

    @pl.when(pl.program_id(0) == 0)
    def _():
        bias_ref[...] = mask_bias(me_ref[0], bounds_ref, tokens, levels)

    for h in range(q_ref.shape[1] // DH):
        cols = slice(h * DH, (h + 1) * DH)
        q, ga = q_ref[:, cols], ga_ref[:, cols]
        k = jnp.concatenate([k_ref[:, cols]] + [r[:rows, cols] for r in far_refs], 0)
        v = jnp.concatenate([v_ref[:, cols]] + [r[rows:, cols] for r in far_refs], 0)
        scores = nt(q, k) * scale + bias_ref[...]
        top = jnp.max(scores, axis=1, keepdims=True)
        grown = jnp.exp(scores - top)
        prob = grown * (1.0 / jnp.sum(grown, axis=1, keepdims=True))
        weights = prob.astype(BF16)
        grad_prob = nt(ga, v)
        delta = jnp.sum(prob * grad_prob, axis=1, keepdims=True)
        grad_scores = (prob * (grad_prob - delta) * scale).astype(BF16)
        gk = tn(grad_scores, q)
        gv = tn(weights, ga)
        for i in range(levels):
            at = tokens + i * rows
            gfar_refs[i][:rows, cols] = gk[at : at + rows].astype(BF16)
            gfar_refs[i][rows:, cols] = gv[at : at + rows].astype(BF16)
        gk_ref[:, cols] = gk[:tokens]
        gv_ref[:, cols] = gv[:tokens]
        attn_ref[:, cols] = nn(weights, v).astype(BF16)
        gq_ref[:, cols] = nn(grad_scores, k).astype(BF16)


def attention(me, bounds, q, k, v, ga, far):
    tokens, width = q.shape
    levels = len(far)
    rows = tokens // STEP
    cols = 2 * DH
    block = pl.BlockSpec((tokens, cols), lambda i: (0, i))
    far_block = pl.BlockSpec((2 * rows, cols), lambda i: (0, i))
    smem = pl.BlockSpec(memory_space=pltpu.SMEM)
    bf = jax.ShapeDtypeStruct((tokens, width), BF16)
    f32 = jax.ShapeDtypeStruct((tokens, width), F32)
    return pl.pallas_call(
        functools.partial(attention_kernel, levels),
        grid=(width // cols,),
        in_specs=[smem, smem] + [block] * 4 + [far_block] * levels,
        out_specs=[block] * 4 + [far_block] * levels,
        out_shape=[bf, bf, f32, f32] + [jax.ShapeDtypeStruct((2 * rows, width), BF16)] * levels,
        scratch_shapes=[pltpu.VMEM((tokens, tokens + levels * rows), F32)],
        compiler_params=params(),
        cost_estimate=pl.CostEstimate(
            flops=12 * tokens * (tokens + levels * rows) * width,
            bytes_accessed=16 * tokens * width,
            transcendentals=0,
        ),
        name="attention",
    )(me, bounds, q, k, v, ga, *far)


def settle_kernel(count, *refs):
    gk_ref, gv_ref = refs[:2]
    back_refs = refs[2 : 2 + count]
    out_k_ref, out_v_ref = refs[2 + count :]
    tokens = gk_ref.shape[0]
    rows = tokens // STEP
    at = lax.broadcasted_iota(jnp.int32, (tokens, rows), 0)
    place = (at == lax.broadcasted_iota(jnp.int32, (tokens, rows), 1) * STEP).astype(BF16)
    place = jnp.concatenate([place] * count, 1)
    extra_k = nn(place, jnp.concatenate([r[:rows] for r in back_refs], 0))
    extra_v = nn(place, jnp.concatenate([r[rows:] for r in back_refs], 0))
    out_k_ref[...] = (gk_ref[...] + extra_k).astype(BF16)
    out_v_ref[...] = (gv_ref[...] + extra_v).astype(BF16)


def settle(gk, gv, back):
    tokens, width = gk.shape
    out = jax.ShapeDtypeStruct((tokens, width), BF16)
    cols = 512
    block = pl.BlockSpec((tokens, cols), lambda i: (0, i))
    back_block = pl.BlockSpec((back[0].shape[0], cols), lambda i: (0, i))
    return pl.pallas_call(
        functools.partial(settle_kernel, len(back)),
        grid=(width // cols,),
        in_specs=[block] * 2 + [back_block] * len(back),
        out_specs=[block] * 2,
        out_shape=[out, out],
        compiler_params=params(),
        name="settle",
    )(gk, gv, *back)


def per_device(queries, keys, values, out_weight, cotangent, bounds):
    levels = lax.axis_size("ctx").bit_length() - 1
    me = lax.axis_index("ctx").astype(jnp.int32).reshape(1)
    group = lax.axis_index("head").astype(jnp.int32).reshape(1)
    other_cot = swap(cotangent)
    picked = pick(keys, values)
    far = [shift(picked, "ctx", 2**i) for i in range(levels)]
    ga = grad_attn(group, cotangent, other_cot, out_weight)
    attn, gq, gk, gv, *gfar = attention(me, bounds, queries, keys, values, ga, far)
    back = [shift(gfar[i], "ctx", -(2**i)) for i in range(levels)]
    other_attn = swap(attn)
    output = project(group, attn, other_attn, out_weight)
    gk, gv = settle(gk, gv, back)
    return output, gq, gk, gv


def solution(mesh):
    shared = P("ctx", "head")
    return jax.shard_map(
        per_device,
        mesh=mesh,
        in_specs=(shared, shared, shared, P(), shared, P()),
        out_specs=(shared,) * 4,
        check_vma=False,
    )
```

time: 167 us -> 90.2 us (0.54)
  the two profiles are of different devices: /device:TPU:13 before, /device:TPU:0 now
where the time goes in v1:
time: 90.2 us; the launch traced here: 89.8 us
  waiting for transfers between devices  44 us (49%)
  starting transfers between devices  21.5 us (24%)
  Pallas kernels  17 us (19%)
  local copies, waits for them, and re-layouts  6.52 us (7%)
    ppermute x8, waiting for transfers between devices, shift(): return lax.ppermute(block, axis, route)  44 us
    ppermute x8, starting transfers between devices, shift(): return lax.ppermute(block, axis, route)  21 us
    pallas_call x1, Pallas kernels, attention(): pl.pallas_call(functools.partial(attention_kernel, levels), grid=(width /...  9.42 us
    unnamed x18, local copies, waits for them, and re-layouts  6.52 us
    pallas_call x1, Pallas kernels, project(): pl.pallas_call(project_kernel, grid_spec=pltpu.PrefetchScalarGridSpec(num...  3.21 us
    pallas_call x1, Pallas kernels, grad_attn(): pl.pallas_call(grad_attn_kernel, grid_spec=pltpu.PrefetchScalarGridSpec(n...  2.38 us
  transfers between devices with their start and end apart: 10, of which 5 were waited for; matrix products, arithmetic and copies ran while one was open for 0% of the time, Pallas kernels for 5%

profile of v1, /device:TPU:0, one launch (start us, length us, event | category | flops | bytes accessed | tf_op | source)
XLA Modules:
  0.0 89.8 jit_solution(9475266198076798553)
XLA Ops:
  0.6 0.5 collective-permute-start
  1.1 1.0 %copy-done.2 = bf16[256,1024]{1,0:T(8,128)(2,1)S(1)} copy-done((bf16[256,1024]{1,0:T(8,128)(2,1)S(1)}, bf16[256,1024]{1,0:T(8,128)(2,1)}, u32[]{:S(2)}) %copy-start.2) | copy-done | bytes 524312
  2.2 1.0 %copy-done.4 = bf16[256,1024]{1,0:T(8,128)(2,1)S(1)} copy-done((bf16[256,1024]{1,0:T(8,128)(2,1)S(1)}, bf16[256,1024]{1,0:T(8,128)(2,1)}, u32[]{:S(2)}) %copy-start.4) | copy-done | bytes 524312
  3.2 0.3 pick.1
  3.5 5.5 %collective-permute-start.4 = (bf16[128,1024]{1,0:T(8,128)(2,1)S(1)}, bf16[128,1024]{1,0:T(8,128)(2,1)S(1)}, u32[]{:S(2)}, u32[]{:S(2)}) collective-permute-start(bf16[128,1024]{1,0:T(8,128)(2,1)S(1)} %pick.1), channel_id=1, source_target_pairs={{0,16},{2,18},{4,20},{6,22},{8,24},{10,26},{12,28},{14,30},{1,17},... | collective-permute-start | bytes 786440 | tf_op jit(solution)/shard_map/ppermute | solution.py:21
  9.1 3.5 %collective-permute-start.3 = (bf16[128,1024]{1,0:T(8,128)(2,1)S(1)}, bf16[128,1024]{1,0:T(8,128)(2,1)S(1)}, u32[]{:S(2)}, u32[]{:S(2)}) collective-permute-start(bf16[128,1024]{1,0:T(8,128)(2,1)S(1)} %pick.1), channel_id=1, source_target_pairs={{0,8},{2,10},{4,12},{6,14},{8,16},{10,18},{12,20},{14,22},{16,24},... | collective-permute-start | bytes 786440 | tf_op jit(solution)/shard_map/ppermute | solution.py:21
  12.6 3.4 %collective-permute-start.2 = (bf16[128,1024]{1,0:T(8,128)(2,1)S(1)}, bf16[128,1024]{1,0:T(8,128)(2,1)S(1)}, u32[]{:S(2)}, u32[]{:S(2)}) collective-permute-start(bf16[128,1024]{1,0:T(8,128)(2,1)S(1)} %pick.1), channel_id=1, source_target_pairs={{0,4},{2,6},{4,8},{6,10},{8,12},{10,14},{12,16},{14,18},{16,20},{1... | collective-permute-start | bytes 786440 | tf_op jit(solution)/shard_map/ppermute | solution.py:21
  16.0 3.4 %collective-permute-start.1 = (bf16[128,1024]{1,0:T(8,128)(2,1)S(1)}, bf16[128,1024]{1,0:T(8,128)(2,1)S(1)}, u32[]{:S(2)}, u32[]{:S(2)}) collective-permute-start(bf16[128,1024]{1,0:T(8,128)(2,1)S(1)} %pick.1), channel_id=1, source_target_pairs={{0,2},{2,4},{4,6},{6,8},{8,10},{10,12},{12,14},{14,16},{16,18},{18... | collective-permute-start | bytes 786440 | tf_op jit(solution)/shard_map/ppermute | solution.py:21
  19.5 3.4 %copy-done = bf16[2048,2048]{1,0:T(8,128)(2,1)S(1)} copy-done((bf16[2048,2048]{1,0:T(8,128)(2,1)S(1)}, bf16[2048,2048]{1,0:T(8,128)(2,1)}, u32[]{:S(2)}) %copy-start) | copy-done | bytes 8388632
  22.8 1.0 %copy-done.6 = bf16[256,1024]{1,0:T(8,128)(2,1)S(1)} copy-done((bf16[256,1024]{1,0:T(8,128)(2,1)S(1)}, bf16[256,1024]{1,0:T(8,128)(2,1)}, u32[]{:S(2)}) %copy-start.6) | copy-done | bytes 524312
  23.9 2.4 %grad_attn.1.refs_5_ = bf16[256,1024]{1,0:T(8,128)(2,1)S(1)} custom-call(s32[1]{0:T(128)} %bitcast.g_ref, bf16[256,1024]{1,0:T(8,128)(2,1)S(1)} %copy-done.6, bf16[256,1024]{1,0:T(8,128)(2,1)S(1)} %collective-permute-done.other_ref, bf16[2048,2048]{1,0:T(8,128)(2,1)S(1)} %copy-done, bf16[2048,2048]{1,0:T(8,128)(2,1)S(1)} %copy-done), custom_call_target="tpu_custom_call" | custom-call | flops 1073741824 | bytes 6291456 | tf_op jit(solution)/shard_map/grad_attn/pallas_call | solution.py:73
  26.3 0.0 copy-start.1
  26.3 1.0 %collective-permute-done.2.refs_7_ = bf16[128,1024]{1,0:T(8,128)(2,1)S(1)} collective-permute-done((bf16[128,1024]{1,0:T(8,128)(2,1)S(1)}, bf16[128,1024]{1,0:T(8,128)(2,1)S(1)}, u32[]{:S(2)}, u32[]{:S(2)}) %collective-permute-start.2) | collective-permute-done | bytes 262176 | tf_op jit(solution)/shard_map/ppermute | solution.py:21
  27.3 9.4 %attention.1 = (bf16[256,1024]{1,0:T(8,128)(2,1)S(1)}, bf16[256,1024]{1,0:T(8,128)(2,1)}, f32[256,1024]{1,0:T(8,128)S(1)}, f32[256,1024]{1,0:T(8,128)S(1)}, bf16...) custom-call(s32[1]{0:T(128)} %bitcast.1.refs_0_, ...), custom_call_target="tpu_custom_call" | custom-call | flops 1610612736 | bytes 4194304 | tf_op jit(solution)/shard_map/attention/pallas_call | solution.py:200
  36.7 1.3 %collective-permute-start.6 = (bf16[128,1024]{1,0:T(8,128)(2,1)S(1)}, bf16[128,1024]{1,0:T(8,128)(2,1)S(1)}, u32[]{:S(2)}, u32[]{:S(2)}) collective-permute-start(bf16[128,1024]{1,0:T(8,128)(2,1)S(1)} %get-tuple-element.18), channel_id=1, source_target_pairs={{2,0},{4,2},{6,4},{8,6},{10,8},{12,10},{14,12},{16,14},{18,16},{20... | collective-permute-start | bytes 786440 | tf_op jit(solution)/shard_map/ppermute | solution.py:21
  38.0 1.3 %collective-permute-start.7 = (bf16[128,1024]{1,0:T(8,128)(2,1)S(1)}, bf16[128,1024]{1,0:T(8,128)(2,1)S(1)}, u32[]{:S(2)}, u32[]{:S(2)}) collective-permute-start(bf16[128,1024]{1,0:T(8,128)(2,1)S(1)} %get-tuple-element.19), channel_id=1, source_target_pairs={{4,0},{6,2},{8,4},{10,6},{12,8},{14,10},{16,12},{18,14},{20,16},{2... | collective-permute-start | bytes 786440 | tf_op jit(solution)/shard_map/ppermute | solution.py:21
  39.3 1.3 %collective-permute-start.8 = (bf16[128,1024]{1,0:T(8,128)(2,1)S(1)}, bf16[128,1024]{1,0:T(8,128)(2,1)S(1)}, u32[]{:S(2)}, u32[]{:S(2)}) collective-permute-start(bf16[128,1024]{1,0:T(8,128)(2,1)S(1)} %get-tuple-element.20), channel_id=1, source_target_pairs={{8,0},{10,2},{12,4},{14,6},{16,8},{18,10},{20,12},{22,14},{24,16},... | collective-permute-start | bytes 786440 | tf_op jit(solution)/shard_map/ppermute | solution.py:21
  40.6 1.3 %collective-permute-start.9 = (bf16[128,1024]{1,0:T(8,128)(2,1)S(1)}, bf16[128,1024]{1,0:T(8,128)(2,1)S(1)}, u32[]{:S(2)}, u32[]{:S(2)}) collective-permute-start(bf16[128,1024]{1,0:T(8,128)(2,1)S(1)} %get-tuple-element.21), channel_id=1, source_target_pairs={{16,0},{18,2},{20,4},{22,6},{24,8},{26,10},{28,12},{30,14},{17,1},... | collective-permute-start | bytes 786440 | tf_op jit(solution)/shard_map/ppermute | solution.py:21
  41.9 5.4 %collective-permute-done.6.refs_2_ = bf16[128,1024]{1,0:T(8,128)(2,1)S(1)} collective-permute-done((bf16[128,1024]{1,0:T(8,128)(2,1)S(1)}, bf16[128,1024]{1,0:T(8,128)(2,1)S(1)}, u32[]{:S(2)}, u32[]{:S(2)}) %collective-permute-start.6) | collective-permute-done | bytes 262176 | tf_op jit(solution)/shard_map/ppermute | solution.py:21
  47.3 2.7 %collective-permute-done.7.refs_3_ = bf16[128,1024]{1,0:T(8,128)(2,1)S(1)} collective-permute-done((bf16[128,1024]{1,0:T(8,128)(2,1)S(1)}, bf16[128,1024]{1,0:T(8,128)(2,1)S(1)}, u32[]{:S(2)}, u32[]{:S(2)}) %collective-permute-start.7) | collective-permute-done | bytes 262176 | tf_op jit(solution)/shard_map/ppermute | solution.py:21
  50.0 17.2 %collective-permute-done.8.refs_4_ = bf16[128,1024]{1,0:T(8,128)(2,1)S(1)} collective-permute-done((bf16[128,1024]{1,0:T(8,128)(2,1)S(1)}, bf16[128,1024]{1,0:T(8,128)(2,1)S(1)}, u32[]{:S(2)}, u32[]{:S(2)}) %collective-permute-start.8) | collective-permute-done | bytes 262176 | tf_op jit(solution)/shard_map/ppermute | solution.py:21
  67.2 17.7 %collective-permute-done.9.refs_5_ = bf16[128,1024]{1,0:T(8,128)(2,1)S(1)} collective-permute-done((bf16[128,1024]{1,0:T(8,128)(2,1)S(1)}, bf16[128,1024]{1,0:T(8,128)(2,1)S(1)}, u32[]{:S(2)}, u32[]{:S(2)}) %collective-permute-start.9) | collective-permute-done | bytes 262176 | tf_op jit(solution)/shard_map/ppermute | solution.py:21
  84.9 1.7 %settle.1 = (bf16[256,1024]{1,0:T(8,128)(2,1)}, bf16[256,1024]{1,0:T(8,128)(2,1)}) custom-call(f32[256,1024]{1,0:T(8,128)S(1)} %get-tuple-element.16.refs_0_, f32[256,1024]{1,0:T(8,128)S(1)} %get-tuple-element.17.refs_1_, bf16[128,1024]{1,0:T(8,128)(2,1)S(1)} %collective-permute-done.6.refs_2_, bf16[128,1024]{1,0:T(8,128)(2,1)S(1)} %collective-permute-done.7.refs_3_, ...), custom_call_target="tpu_custom_call" | custom-call | tf_op jit(solution)/shard_map/settle/pallas_call | solution.py:238
  86.6 3.2 %project.1 = bf16[256,1024]{1,0:T(8,128)(2,1)} custom-call(s32[1]{0:T(128)} %bitcast.g_ref, bf16[256,1024]{1,0:T(8,128)(2,1)S(1)} %get-tuple-element.14.own_ref, bf16[256,1024]{1,0:T(8,128)(2,1)S(1)} %collective-permute-done.5.other_ref, bf16[2048,2048]{1,0:T(8,128)(2,1)S(1)} %copy-done.1, bf16[2048,2048]{1,0:T(8,128)(2,1)S(1)} %copy-done.1), custom_call_target="tpu_custom_call" | custom-call | flops 1073741824 | bytes 6291456 | tf_op jit(solution)/shard_map/project/pallas_call | solution.py:105
  (19 shorter events, 0.0 us)
Async XLA Ops:
  0.6 18.8 %collective-permute-start = (bf16[256,1024]{1,0:T(8,128)(2,1)}, bf16[256,1024]{1,0:T(8,128)(2,1)S(1)}, u32[]{:S(2)}, u32[]{:S(2)}) collective-permute-start(bf16[256,1024]{1,0:T(8,128)(2,1)} %own_ref.1), channel_id=1, source_target_pairs={{0,1},{1,0},{2,3},{3,2},{4,5},{5,4},{6,7},{7,6},{8,9},{9,8},{10,11... | collective-permute-start | bytes 1572872 | tf_op jit(solution)/shard_map/ppermute | solution.py:25
  1.1 1.0 %copy-start.2 = (bf16[256,1024]{1,0:T(8,128)(2,1)S(1)}, bf16[256,1024]{1,0:T(8,128)(2,1)}, u32[]{:S(2)}) copy-start(bf16[256,1024]{1,0:T(8,128)(2,1)} %refs_3_.1) | copy-start | bytes 1572868
  2.2 1.0 %copy-start.4 = (bf16[256,1024]{1,0:T(8,128)(2,1)S(1)}, bf16[256,1024]{1,0:T(8,128)(2,1)}, u32[]{:S(2)}) copy-start(bf16[256,1024]{1,0:T(8,128)(2,1)} %refs_4_.1) | copy-start | bytes 1572868
  3.5 22.8 %collective-permute-start.4 = (bf16[128,1024]{1,0:T(8,128)(2,1)S(1)}, bf16[128,1024]{1,0:T(8,128)(2,1)S(1)}, u32[]{:S(2)}, u32[]{:S(2)}) collective-permute-start(bf16[128,1024]{1,0:T(8,128)(2,1)S(1)} %pick.1), channel_id=1, source_target_pairs={{0,16},{2,18},{4,20},{6,22},{8,24},{10,26},{12,28},{14,30},{1,17},... | collective-permute-start | bytes 786440 | tf_op jit(solution)/shard_map/ppermute | solution.py:21
  9.1 17.2 %collective-permute-start.3 = (bf16[128,1024]{1,0:T(8,128)(2,1)S(1)}, bf16[128,1024]{1,0:T(8,128)(2,1)S(1)}, u32[]{:S(2)}, u32[]{:S(2)}) collective-permute-start(bf16[128,1024]{1,0:T(8,128)(2,1)S(1)} %pick.1), channel_id=1, source_target_pairs={{0,8},{2,10},{4,12},{6,14},{8,16},{10,18},{12,20},{14,22},{16,24},... | collective-permute-start | bytes 786440 | tf_op jit(solution)/shard_map/ppermute | solution.py:21
  12.6 14.7 %collective-permute-start.2 = (bf16[128,1024]{1,0:T(8,128)(2,1)S(1)}, bf16[128,1024]{1,0:T(8,128)(2,1)S(1)}, u32[]{:S(2)}, u32[]{:S(2)}) collective-permute-start(bf16[128,1024]{1,0:T(8,128)(2,1)S(1)} %pick.1), channel_id=1, source_target_pairs={{0,4},{2,6},{4,8},{6,10},{8,12},{10,14},{12,16},{14,18},{16,20},{1... | collective-permute-start | bytes 786440 | tf_op jit(solution)/shard_map/ppermute | solution.py:21
  16.0 11.2 %collective-permute-start.1 = (bf16[128,1024]{1,0:T(8,128)(2,1)S(1)}, bf16[128,1024]{1,0:T(8,128)(2,1)S(1)}, u32[]{:S(2)}, u32[]{:S(2)}) collective-permute-start(bf16[128,1024]{1,0:T(8,128)(2,1)S(1)} %pick.1), channel_id=1, source_target_pairs={{0,2},{2,4},{4,6},{6,8},{8,10},{10,12},{12,14},{14,16},{16,18},{18... | collective-permute-start | bytes 786440 | tf_op jit(solution)/shard_map/ppermute | solution.py:21
  19.4 3.4 %copy-start = (bf16[2048,2048]{1,0:T(8,128)(2,1)S(1)}, bf16[2048,2048]{1,0:T(8,128)(2,1)}, u32[]{:S(2)}) copy-start(bf16[2048,2048]{1,0:T(8,128)(2,1)} %w_other_ref.3) | copy-start | bytes 25165828
  22.8 1.0 %copy-start.6 = (bf16[256,1024]{1,0:T(8,128)(2,1)S(1)}, bf16[256,1024]{1,0:T(8,128)(2,1)}, u32[]{:S(2)}) copy-start(bf16[256,1024]{1,0:T(8,128)(2,1)} %own_ref.1) | copy-start | bytes 1572868
  23.9 3.4 %copy-start.3 = (bf16[256,1024]{1,0:T(8,128)(2,1)S(1)}, bf16[256,1024]{1,0:T(8,128)(2,1)}, u32[]{:S(2)}) copy-start(bf16[256,1024]{1,0:T(8,128)(2,1)} %refs_3_.1) | copy-start | bytes 1572868
  23.9 3.4 %copy-start.5 = (bf16[256,1024]{1,0:T(8,128)(2,1)S(1)}, bf16[256,1024]{1,0:T(8,128)(2,1)}, u32[]{:S(2)}) copy-start(bf16[256,1024]{1,0:T(8,128)(2,1)} %refs_4_.1) | copy-start | bytes 1572868
  23.9 3.4 %copy-start.7 = (bf16[256,1024]{1,0:T(8,128)(2,1)S(1)}, bf16[256,1024]{1,0:T(8,128)(2,1)}, u32[]{:S(2)}) copy-start(bf16[256,1024]{1,0:T(8,128)(2,1)} %refs_2_.1) | copy-start | bytes 1572868
  23.9 3.4 %copy-start.8 = (s32[4]{0:T(128)S(1)}, s32[4]{0:T(128)}, u32[]{:S(2)}) copy-start(s32[4]{0:T(128)} %refs_1_.1) | copy-start | bytes 52
  26.3 60.3 %copy-start.1 = (bf16[2048,2048]{1,0:T(8,128)(2,1)S(1)}, bf16[2048,2048]{1,0:T(8,128)(2,1)}, u32[]{:S(2)}) copy-start(bf16[2048,2048]{1,0:T(8,128)(2,1)} %w_other_ref.3) | copy-start | bytes 25165828
  36.7 49.9 %collective-permute-start.5 = (bf16[256,1024]{1,0:T(8,128)(2,1)S(1)}, bf16[256,1024]{1,0:T(8,128)(2,1)S(1)}, u32[]{:S(2)}, u32[]{:S(2)}) collective-permute-start(bf16[256,1024]{1,0:T(8,128)(2,1)S(1)} %get-tuple-element.14.own_ref), channel_id=1, source_target_pairs={{0,1},{1,0},{2,3},{3,2},{4,5},{5,4},{6,7},{7,6},{8,9},{9,8},{10,11... | collective-permute-start | bytes 1572872 | tf_op jit(solution)/shard_map/ppermute | solution.py:25
  36.7 10.6 %collective-permute-start.6 = (bf16[128,1024]{1,0:T(8,128)(2,1)S(1)}, bf16[128,1024]{1,0:T(8,128)(2,1)S(1)}, u32[]{:S(2)}, u32[]{:S(2)}) collective-permute-start(bf16[128,1024]{1,0:T(8,128)(2,1)S(1)} %get-tuple-element.18), channel_id=1, source_target_pairs={{2,0},{4,2},{6,4},{8,6},{10,8},{12,10},{14,12},{16,14},{18,16},{20... | collective-permute-start | bytes 786440 | tf_op jit(solution)/shard_map/ppermute | solution.py:21
  38.0 12.0 %collective-permute-start.7 = (bf16[128,1024]{1,0:T(8,128)(2,1)S(1)}, bf16[128,1024]{1,0:T(8,128)(2,1)S(1)}, u32[]{:S(2)}, u32[]{:S(2)}) collective-permute-start(bf16[128,1024]{1,0:T(8,128)(2,1)S(1)} %get-tuple-element.19), channel_id=1, source_target_pairs={{4,0},{6,2},{8,4},{10,6},{12,8},{14,10},{16,12},{18,14},{20,16},{2... | collective-permute-start | bytes 786440 | tf_op jit(solution)/shard_map/ppermute | solution.py:21
  39.3 27.9 %collective-permute-start.8 = (bf16[128,1024]{1,0:T(8,128)(2,1)S(1)}, bf16[128,1024]{1,0:T(8,128)(2,1)S(1)}, u32[]{:S(2)}, u32[]{:S(2)}) collective-permute-start(bf16[128,1024]{1,0:T(8,128)(2,1)S(1)} %get-tuple-element.20), channel_id=1, source_target_pairs={{8,0},{10,2},{12,4},{14,6},{16,8},{18,10},{20,12},{22,14},{24,16},... | collective-permute-start | bytes 786440 | tf_op jit(solution)/shard_map/ppermute | solution.py:21
  40.6 44.3 %collective-permute-start.9 = (bf16[128,1024]{1,0:T(8,128)(2,1)S(1)}, bf16[128,1024]{1,0:T(8,128)(2,1)S(1)}, u32[]{:S(2)}, u32[]{:S(2)}) collective-permute-start(bf16[128,1024]{1,0:T(8,128)(2,1)S(1)} %get-tuple-element.21), channel_id=1, source_target_pairs={{16,0},{18,2},{20,4},{22,6},{24,8},{26,10},{28,12},{30,14},{17,1},... | collective-permute-start | bytes 786440 | tf_op jit(solution)/shard_map/ppermute | solution.py:21

commit v2 on v1

--- a/solution.py
+++ b/solution.py
@@ -11,14 +11,23 @@
 DH = 128
 STEP = 4
 VMEM_LIMIT = 40 * 1024 * 1024
+VMEM_MOST = 58 * 1024 * 1024
 BF16 = jnp.bfloat16
 F32 = jnp.float32
 
 
-def shift(block, axis, distance):
-    devices = range(lax.axis_size(axis))
-    route = [(i, i + distance) for i in devices if i + distance in devices]
-    return lax.ppermute(block, axis, route)
+def hop(distance, n):
+    return [(i, i + distance) for i in range(n) if 0 <= i + distance < n]
+
+
+def pairs(n):
+    return [(i, i ^ 2) for i in range(n)]
+
+
+def mixed(block, route_of_core):
+    cores = len(route_of_core)
+    route = [(a * cores + c, b * cores + c) for c, r in enumerate(route_of_core) for a, b in r]
+    return lax.ppermute(block, ("ctx", "head"), route)
 
 
 def swap(block):
@@ -37,8 +46,8 @@
     return jnp.dot(a, b, preferred_element_type=F32)
 
 
-def params():
-    return pltpu.CompilerParams(vmem_limit_bytes=VMEM_LIMIT)
+def params(limit=VMEM_LIMIT):
+    return pltpu.CompilerParams(vmem_limit_bytes=limit)
 
 
 def pick_kernel(k_ref, v_ref, out_ref):
@@ -55,7 +64,7 @@
     return pl.pallas_call(
         pick_kernel,
         out_shape=jax.ShapeDtypeStruct((2 * tokens // STEP, width), BF16),
-        compiler_params=params(),
+        compiler_params=params(VMEM_MOST),
         name="pick",
     )(keys, values)
 
@@ -84,7 +93,7 @@
             out_specs=pl.BlockSpec((tokens, tile), lambda i, g: (0, i)),
         ),
         out_shape=jax.ShapeDtypeStruct((tokens, width), BF16),
-        compiler_params=params(),
+        compiler_params=params(VMEM_MOST),
         cost_estimate=pl.CostEstimate(
             flops=4 * tokens * width * width, bytes_accessed=6 * width * width, transcendentals=0
         ),
@@ -116,7 +125,7 @@
             out_specs=pl.BlockSpec((tokens, tile), lambda i, g: (0, i)),
         ),
         out_shape=jax.ShapeDtypeStruct((tokens, width), BF16),
-        compiler_params=params(),
+        compiler_params=params(VMEM_MOST),
         cost_estimate=pl.CostEstimate(
             flops=4 * tokens * width * width, bytes_accessed=6 * width * width, transcendentals=0
         ),
@@ -149,24 +158,28 @@
 
 
 def attention_kernel(levels, *refs):
-    me_ref, bounds_ref, q_ref, k_ref, v_ref, ga_ref = refs[:6]
-    far_refs = refs[6 : 6 + levels]
+    place_ref, bounds_ref, q_ref, k_ref, v_ref, ga_ref = refs[:6]
+    arrived_refs = refs[6 : 6 + levels]
     attn_ref, gq_ref, gk_ref, gv_ref = refs[6 + levels : 10 + levels]
     gfar_refs = refs[10 + levels : 10 + 2 * levels]
     bias_ref = refs[10 + 2 * levels]
     tokens = q_ref.shape[0]
     rows = tokens // STEP
     scale = 1.0 / math.sqrt(DH)
+    first = place_ref[1] == 0
 
     @pl.when(pl.program_id(0) == 0)
     def _():
-        bias_ref[...] = mask_bias(me_ref[0], bounds_ref, tokens, levels)
+        bias_ref[...] = mask_bias(place_ref[0], bounds_ref, tokens, levels)
 
     for h in range(q_ref.shape[1] // DH):
         cols = slice(h * DH, (h + 1) * DH)
         q, ga = q_ref[:, cols], ga_ref[:, cols]
-        k = jnp.concatenate([k_ref[:, cols]] + [r[:rows, cols] for r in far_refs], 0)
-        v = jnp.concatenate([v_ref[:, cols]] + [r[rows:, cols] for r in far_refs], 0)
+        one, two, three, four, *more = [r[:, cols] for r in arrived_refs]
+        far = [jnp.where(first, a, b) for a, b in ((two, one), (four, three), (one, two), (three, four))]
+        far += more
+        k = jnp.concatenate([k_ref[:, cols]] + [f[:rows] for f in far], 0)
+        v = jnp.concatenate([v_ref[:, cols]] + [f[rows:] for f in far], 0)
         scores = nt(q, k) * scale + bias_ref[...]
         top = jnp.max(scores, axis=1, keepdims=True)
         grown = jnp.exp(scores - top)
@@ -187,9 +200,9 @@
         gq_ref[:, cols] = nn(grad_scores, k).astype(BF16)
 
 
-def attention(me, bounds, q, k, v, ga, far):
+def attention(place, bounds, q, k, v, ga, arrived):
     tokens, width = q.shape
-    levels = len(far)
+    levels = len(arrived)
     rows = tokens // STEP
     cols = 2 * DH
     block = pl.BlockSpec((tokens, cols), lambda i: (0, i))
@@ -211,13 +224,13 @@
             transcendentals=0,
         ),
         name="attention",
-    )(me, bounds, q, k, v, ga, *far)
+    )(place, bounds, q, k, v, ga, *arrived)
 
 
 def settle_kernel(count, *refs):
     gk_ref, gv_ref = refs[:2]
     back_refs = refs[2 : 2 + count]
-    out_k_ref, out_v_ref = refs[2 + count :]
+    out_k_ref, out_v_ref = refs[3 + count :]
     tokens = gk_ref.shape[0]
     rows = tokens // STEP
     at = lax.broadcasted_iota(jnp.int32, (tokens, rows), 0)
@@ -229,7 +242,7 @@
     out_v_ref[...] = (gv_ref[...] + extra_v).astype(BF16)
 
 
-def settle(gk, gv, back):
+def settle(gk, gv, back, after):
     tokens, width = gk.shape
     out = jax.ShapeDtypeStruct((tokens, width), BF16)
     cols = 512
@@ -238,27 +251,60 @@
     return pl.pallas_call(
         functools.partial(settle_kernel, len(back)),
         grid=(width // cols,),
-        in_specs=[block] * 2 + [back_block] * len(back),
+        in_specs=[block] * 2 + [back_block] * len(back) + [pl.BlockSpec(memory_space=pl.ANY)],
         out_specs=[block] * 2,
         out_shape=[out, out],
         compiler_params=params(),
         name="settle",
-    )(gk, gv, *back)
+    )(gk, gv, *back, after)
+
+
+def add(*blocks):
+    total = blocks[0].astype(F32)
+    for block in blocks[1:]:
+        total = total + block.astype(F32)
+    return total.astype(BF16)
 
 
 def per_device(queries, keys, values, out_weight, cotangent, bounds):
-    levels = lax.axis_size("ctx").bit_length() - 1
-    me = lax.axis_index("ctx").astype(jnp.int32).reshape(1)
-    group = lax.axis_index("head").astype(jnp.int32).reshape(1)
+    n = lax.axis_size("ctx")
+    levels = n.bit_length() - 1
+    index, core = lax.axis_index("ctx"), lax.axis_index("head")
+    place = jnp.stack([index, core]).astype(jnp.int32)
+    group = core.astype(jnp.int32).reshape(1)
+    first = core == 0
+    low = (index & 2) == 0
+
     other_cot = swap(cotangent)
     picked = pick(keys, values)
-    far = [shift(picked, "ctx", 2**i) for i in range(levels)]
+    one = mixed(picked, (hop(4, n), hop(1, n)))
+    two = mixed(picked, (hop(1, n), hop(4, n)))
+    far4 = jnp.where(first, one, two)
+    lent = jnp.where(low, picked, far4)
+    three = mixed(jnp.where(first, far4, lent), (hop(4, n), pairs(n)))
+    four = mixed(jnp.where(first, lent, far4), (pairs(n), hop(4, n)))
+    arrived = [one, two, three, four]
+    farther = jnp.where(first, three, four) if levels > 4 else None
+    for i in range(4, levels):
+        farther = lax.ppermute(farther, "ctx", hop(2 ** (i - 1), n))
+        arrived.append(farther)
+
     ga = grad_attn(group, cotangent, other_cot, out_weight)
-    attn, gq, gk, gv, *gfar = attention(me, bounds, queries, keys, values, ga, far)
-    back = [shift(gfar[i], "ctx", -(2**i)) for i in range(levels)]
+    attn, gq, gk, gv, *gfar = attention(place, bounds, queries, keys, values, ga, arrived)
+
+    for i in reversed(range(4, levels)):
+        gfar[i - 1] = add(gfar[i - 1], lax.ppermute(gfar[i], "ctx", hop(-(2 ** (i - 1)), n)))
+    g1, g2, g4, g8 = gfar[:4]
+    one = mixed(jnp.where(first, g8, g2), (hop(-4, n), pairs(n)))
+    two = mixed(jnp.where(first, g2, g8), (pairs(n), hop(-4, n)))
+    back8, back2 = jnp.where(first, one, two), jnp.where(first, two, one)
+    zero = jnp.zeros_like(back2)
+    g4 = add(g4, back8, jnp.where(low, zero, back2))
+    three = mixed(jnp.where(first, g4, g1), (hop(-4, n), hop(-1, n)))
+    four = mixed(jnp.where(first, g1, g4), (hop(-1, n), hop(-4, n)))
     other_attn = swap(attn)
     output = project(group, attn, other_attn, out_weight)
-    gk, gv = settle(gk, gv, back)
+    gk, gv = settle(gk, gv, [jnp.where(low, back2, zero), three, four], output)
     return output, gq, gk, gv
 
 

time: 90.2 us -> 72.9 us (0.81)
  waiting for transfers between devices: 44 us -> 17.5 us
  Pallas kernels: 17 us -> 23.3 us
  starting transfers between devices: 21.5 us -> 25.8 us
  local copies, waits for them, and re-layouts: 6.52 us -> 3.67 us
  other arithmetic: 0 us -> 1.27 us
    ppermute x8, waiting for transfers between devices: 44 us -> 17.5 us  [mixed(): return lax.ppermute(block, ('ctx', 'head'), route)]
    unnamed x18, local copies, waits for them, and re-layouts: 6.52 us -> 3.67 us
    pallas_call x1, Pallas kernels: 2.38 us -> 5.05 us  [grad_attn(): pl.pallas_call(grad_attn_kernel, grid_spec=pltpu.PrefetchScalarGridSpec(n...]
    ppermute x8, starting transfers between devices: 21 us -> 23.2 us  [mixed(): return lax.ppermute(block, ('ctx', 'head'), route)]
    ppermute x2, starting transfers between devices: 0.52 us -> 2.63 us  [swap(): return lax.ppermute(block, 'head', [(0, 1), (1, 0)])]
    pallas_call x1, Pallas kernels: 0.29 us -> 2.2 us  [pick(): pl.pallas_call(pick_kernel, out_shape=jax.ShapeDtypeStruct((2 * tokens //...]
    pallas_call x1, Pallas kernels: 3.21 us -> 5.01 us  [project(): pl.pallas_call(project_kernel, grid_spec=pltpu.PrefetchScalarGridSpec(num...]
    select_n x0 -> x3, other arithmetic: none -> 1.19 us  [the longest x1 1 us: per_device(): four = mixed(jnp.where(first, lent, far4), (pairs(n), hop(4, n)))]
  transfers between devices with their start and end apart: 10 -> 10, of which waited for: 5 -> 7; matrix products, arithmetic and copies ran while one was open for 0% -> 2% of each run, Pallas kernels for 5% -> 14%
where the time goes in v2:
time: 72.9 us; the launch traced here: 72.3 us
  starting transfers between devices  25.8 us (35%)
  Pallas kernels  23.3 us (32%)
  waiting for transfers between devices  17.5 us (24%)
  local copies, waits for them, and re-layouts  3.67 us (5%)
  other arithmetic  1.27 us (2%)
  between operations  0.79 us (1%)
    ppermute x8, starting transfers between devices, mixed(): return lax.ppermute(block, ('ctx', 'head'), route)  23.2 us
    ppermute x8, waiting for transfers between devices, mixed(): return lax.ppermute(block, ('ctx', 'head'), route)  17.5 us
    pallas_call x1, Pallas kernels, attention(): pl.pallas_call(functools.partial(attention_kernel, levels), grid=(width /...  9.37 us
    pallas_call x1, Pallas kernels, grad_attn(): pl.pallas_call(grad_attn_kernel, grid_spec=pltpu.PrefetchScalarGridSpec(n...  5.05 us
    pallas_call x1, Pallas kernels, project(): pl.pallas_call(project_kernel, grid_spec=pltpu.PrefetchScalarGridSpec(num...  5.01 us
    unnamed x18, local copies, waits for them, and re-layouts  3.67 us
    ppermute x2, starting transfers between devices, swap(): return lax.ppermute(block, 'head', [(0, 1), (1, 0)])  2.63 us
    pallas_call x1, Pallas kernels, pick(): pl.pallas_call(pick_kernel, out_shape=jax.ShapeDtypeStruct((2 * tokens //...  2.2 us
  transfers between devices with their start and end apart: 10, of which 7 were waited for; matrix products, arithmetic and copies ran while one was open for 2% of the time, Pallas kernels for 14%

profile of v2, /device:TPU:0, one launch (start us, length us, event | category | flops | bytes accessed | tf_op | source)
XLA Modules:
  0.0 72.3 jit_solution(3872033997337078800)
XLA Ops:
  0.6 2.2 %pick.1 = bf16[128,1024]{1,0:T(8,128)(2,1)} custom-call(bf16[256,1024]{1,0:T(8,128)(2,1)} %refs_3_.1, bf16[256,1024]{1,0:T(8,128)(2,1)} %refs_4_.1), custom_call_target="tpu_custom_call" | custom-call | tf_op jit(solution)/shard_map/pick/pallas_call | solution.py:64
  2.8 4.8 %collective-permute-start.2 = (bf16[128,1024]{1,0:T(8,128)(2,1)}, bf16[128,1024]{1,0:T(8,128)(2,1)S(1)}, u32[]{:S(2)}, u32[]{:S(2)}) collective-permute-start(bf16[128,1024]{1,0:T(8,128)(2,1)} %pick.1), channel_id=1, source_target_pairs={{0,2},{2,4},{4,6},{6,8},{8,10},{10,12},{12,14},{14,16},{16,18},{18... | collective-permute-start | bytes 786440 | tf_op jit(solution)/shard_map/ppermute | solution.py:30
  7.7 3.5 %collective-permute-start.1 = (bf16[128,1024]{1,0:T(8,128)(2,1)}, bf16[128,1024]{1,0:T(8,128)(2,1)S(1)}, u32[]{:S(2)}, u32[]{:S(2)}) collective-permute-start(bf16[128,1024]{1,0:T(8,128)(2,1)} %pick.1), channel_id=1, source_target_pairs={{0,8},{2,10},{4,12},{6,14},{8,16},{10,18},{12,20},{14,22},{16,24},... | collective-permute-start | bytes 786440 | tf_op jit(solution)/shard_map/ppermute | solution.py:30
  11.3 1.2 %collective-permute-done.2.refs_7_ = bf16[128,1024]{1,0:T(8,128)(2,1)S(1)} collective-permute-done((bf16[128,1024]{1,0:T(8,128)(2,1)}, bf16[128,1024]{1,0:T(8,128)(2,1)S(1)}, u32[]{:S(2)}, u32[]{:S(2)}) %collective-permute-start.2) | collective-permute-done | bytes 262176 | tf_op jit(solution)/shard_map/ppermute | solution.py:30
  12.5 2.8 %collective-permute-done.1.refs_6_ = bf16[128,1024]{1,0:T(8,128)(2,1)S(1)} collective-permute-done((bf16[128,1024]{1,0:T(8,128)(2,1)}, bf16[128,1024]{1,0:T(8,128)(2,1)S(1)}, u32[]{:S(2)}, u32[]{:S(2)}) %collective-permute-start.1) | collective-permute-done | bytes 262176 | tf_op jit(solution)/shard_map/ppermute | solution.py:30
  15.4 1.0 %select_select_fusion = (bf16[128,1024]{1,0:T(8,128)(2,1)S(1)}, bf16[128,1024]{1,0:T(8,128)(2,1)S(1)}) fusion(bf16[128,1024]{1,0:T(8,128)(2,1)} %pick.1, pred[]{:T(512)S(6)} %eq.7, pred[]{:T(512)S(6)} %eq.6, bf16[128,1024]{1,0:T(8,128)(2,1)S(1)} %collective-permute-done.1.refs_6_, bf16[128,1024]{1,0:T(8,128)(2,1)S(1)} %collective-permute-done.2.refs_7_), kind=kLoop, calls=%fused_computation.1 | loop fusion | flops 524288 | bytes 1310722 | tf_op jit(solution)/shard_map/jit(_where)/select_n | solution.py:285
  16.4 2.5 %collective-permute-start.4 = (bf16[128,1024]{1,0:T(8,128)(2,1)S(1)}, bf16[128,1024]{1,0:T(8,128)(2,1)S(1)}, u32[]{:S(2)}, u32[]{:S(2)}) collective-permute-start(bf16[128,1024]{1,0:T(8,128)(2,1)S(1)} %get-tuple-element.26), channel_id=1, source_target_pairs={{0,4},{2,6},{4,0},{6,2},{8,12},{10,14},{12,8},{14,10},{16,20},{18,... | collective-permute-start | bytes 786440 | tf_op jit(solution)/shard_map/ppermute | solution.py:30
  18.8 4.9 %collective-permute-start.3 = (bf16[128,1024]{1,0:T(8,128)(2,1)S(1)}, bf16[128,1024]{1,0:T(8,128)(2,1)S(1)}, u32[]{:S(2)}, u32[]{:S(2)}) collective-permute-start(bf16[128,1024]{1,0:T(8,128)(2,1)S(1)} %get-tuple-element.27), channel_id=1, source_target_pairs={{0,8},{2,10},{4,12},{6,14},{8,16},{10,18},{12,20},{14,22},{16,24},... | collective-permute-start | bytes 786440 | tf_op jit(solution)/shard_map/ppermute | solution.py:30
  24.7 5.0 %grad_attn.1.refs_5_ = bf16[256,1024]{1,0:T(8,128)(2,1)} custom-call(s32[1]{0:T(128)} %bitcast.g_ref, bf16[256,1024]{1,0:T(8,128)(2,1)} %own_ref.1, bf16[256,1024]{1,0:T(8,128)(2,1)} %copy-done.7, bf16[2048,2048]{1,0:T(8,128)(2,1)} %w_other_ref.3, bf16[2048,2048]{1,0:T(8,128)(2,1)} %w_other_ref.3), custom_call_target="tpu_custom_call" | custom-call | flops 1073741824 | bytes 6291456 | tf_op jit(solution)/shard_map/grad_attn/pallas_call | solution.py:82
  30.1 1.0 %copy-done.4 = bf16[256,1024]{1,0:T(8,128)(2,1)S(1)} copy-done((bf16[256,1024]{1,0:T(8,128)(2,1)S(1)}, bf16[256,1024]{1,0:T(8,128)(2,1)}, u32[]{:S(2)}) %copy-start.4) | copy-done | bytes 524312
  31.2 9.4 %attention.1 = (bf16[256,1024]{1,0:T(8,128)(2,1)S(1)}, bf16[256,1024]{1,0:T(8,128)(2,1)}, f32[256,1024]{1,0:T(8,128)S(1)}, f32[256,1024]{1,0:T(8,128)S(1)}, bf16...) custom-call(s32[2]{0:T(128)S(1)} %pad_add_fusion.refs_0_, ...), custom_call_target="tpu_custom_call" | custom-call | flops 1610612736 | bytes 4194304 | tf_op jit(solution)/shard_map/attention/pallas_call | solution.py:213
  40.6 1.3 %collective-permute-start.7 = (bf16[128,1024]{1,0:T(8,128)(2,1)S(1)}, bf16[128,1024]{1,0:T(8,128)(2,1)S(1)}, u32[]{:S(2)}, u32[]{:S(2)}) collective-permute-start(bf16[128,1024]{1,0:T(8,128)(2,1)S(1)} %get-tuple-element.29), channel_id=1, source_target_pairs={{8,0},{10,2},{12,4},{14,6},{16,8},{18,10},{20,12},{22,14},{24,16},... | collective-permute-start | bytes 786440 | tf_op jit(solution)/shard_map/ppermute | solution.py:30
  41.9 3.6 %collective-permute-start.6 = (bf16[128,1024]{1,0:T(8,128)(2,1)S(1)}, bf16[128,1024]{1,0:T(8,128)(2,1)S(1)}, u32[]{:S(2)}, u32[]{:S(2)}) collective-permute-start(bf16[128,1024]{1,0:T(8,128)(2,1)S(1)} %get-tuple-element.30), channel_id=1, source_target_pairs={{0,4},{2,6},{4,0},{6,2},{8,12},{10,14},{12,8},{14,10},{16,20},{18,... | collective-permute-start | bytes 786440 | tf_op jit(solution)/shard_map/ppermute | solution.py:30
  45.5 2.6 %collective-permute-start.5 = (bf16[256,1024]{1,0:T(8,128)(2,1)S(1)}, bf16[256,1024]{1,0:T(8,128)(2,1)S(1)}, u32[]{:S(2)}, u32[]{:S(2)}) collective-permute-start(bf16[256,1024]{1,0:T(8,128)(2,1)S(1)} %get-tuple-element.14.own_ref), channel_id=1, source_target_pairs={{0,1},{1,0},{2,3},{3,2},{4,5},{5,4},{6,7},{7,6},{8,9},{9,8},{10,11... | collective-permute-start | bytes 1572872 | tf_op jit(solution)/shard_map/ppermute | solution.py:34
  48.0 1.3 %collective-permute-done.7 = bf16[128,1024]{1,0:T(8,128)(2,1)S(1)} collective-permute-done((bf16[128,1024]{1,0:T(8,128)(2,1)S(1)}, bf16[128,1024]{1,0:T(8,128)(2,1)S(1)}, u32[]{:S(2)}, u32[]{:S(2)}) %collective-permute-start.7) | collective-permute-done | bytes 262176 | tf_op jit(solution)/shard_map/ppermute | solution.py:30
  49.3 3.3 %collective-permute-done.6 = bf16[128,1024]{1,0:T(8,128)(2,1)S(1)} collective-permute-done((bf16[128,1024]{1,0:T(8,128)(2,1)S(1)}, bf16[128,1024]{1,0:T(8,128)(2,1)S(1)}, u32[]{:S(2)}, u32[]{:S(2)}) %collective-permute-start.6) | collective-permute-done | bytes 262176 | tf_op jit(solution)/shard_map/ppermute | solution.py:30
  52.8 1.3 %collective-permute-start.9 = (bf16[128,1024]{1,0:T(8,128)(2,1)S(1)}, bf16[128,1024]{1,0:T(8,128)(2,1)S(1)}, u32[]{:S(2)}, u32[]{:S(2)}) collective-permute-start(bf16[128,1024]{1,0:T(8,128)(2,1)S(1)} %get-tuple-element.24), channel_id=1, source_target_pairs={{2,0},{4,2},{6,4},{8,6},{10,8},{12,10},{14,12},{16,14},{18,16},{20... | collective-permute-start | bytes 786440 | tf_op jit(solution)/shard_map/ppermute | solution.py:30
  54.1 1.3 %collective-permute-start.8 = (bf16[128,1024]{1,0:T(8,128)(2,1)S(1)}, bf16[128,1024]{1,0:T(8,128)(2,1)S(1)}, u32[]{:S(2)}, u32[]{:S(2)}) collective-permute-start(bf16[128,1024]{1,0:T(8,128)(2,1)S(1)} %get-tuple-element.25), channel_id=1, source_target_pairs={{8,0},{10,2},{12,4},{14,6},{16,8},{18,10},{20,12},{22,14},{24,16},... | collective-permute-start | bytes 786440 | tf_op jit(solution)/shard_map/ppermute | solution.py:30
  55.4 0.8 %copy-done.8 = bf16[256,1024]{1,0:T(8,128)(2,1)} copy-done((bf16[256,1024]{1,0:T(8,128)(2,1)}, bf16[256,1024]{1,0:T(8,128)(2,1)S(1)}, u32[]{:S(2)}) %copy-start.8) | copy-done | bytes 524312
  56.2 5.0 %project.1.refs_5_ = bf16[256,1024]{1,0:T(8,128)(2,1)} custom-call(s32[1]{0:T(128)} %bitcast.g_ref, bf16[256,1024]{1,0:T(8,128)(2,1)} %copy-done.3, bf16[256,1024]{1,0:T(8,128)(2,1)} %copy-done.8, bf16[2048,2048]{1,0:T(8,128)(2,1)} %w_other_ref.3, bf16[2048,2048]{1,0:T(8,128)(2,1)} %w_other_ref.3), custom_call_target="tpu_custom_call" | custom-call | flops 1073741824 | bytes 6291456 | tf_op jit(solution)/shard_map/project/pallas_call | solution.py:114
  61.2 3.4 %collective-permute-done.9.refs_4_ = bf16[128,1024]{1,0:T(8,128)(2,1)S(1)} collective-permute-done((bf16[128,1024]{1,0:T(8,128)(2,1)S(1)}, bf16[128,1024]{1,0:T(8,128)(2,1)S(1)}, u32[]{:S(2)}, u32[]{:S(2)}) %collective-permute-start.9) | collective-permute-done | bytes 262176 | tf_op jit(solution)/shard_map/ppermute | solution.py:30
  64.6 5.1 %collective-permute-done.8.refs_3_ = bf16[128,1024]{1,0:T(8,128)(2,1)S(1)} collective-permute-done((bf16[128,1024]{1,0:T(8,128)(2,1)S(1)}, bf16[128,1024]{1,0:T(8,128)(2,1)S(1)}, u32[]{:S(2)}, u32[]{:S(2)}) %collective-permute-start.8) | collective-permute-done | bytes 262176 | tf_op jit(solution)/shard_map/ppermute | solution.py:30
  69.7 1.0 %copy-done = bf16[256,1024]{1,0:T(8,128)(2,1)S(1)} copy-done((bf16[256,1024]{1,0:T(8,128)(2,1)S(1)}, bf16[256,1024]{1,0:T(8,128)(2,1)}, u32[]{:S(2)}) %copy-start) | copy-done | bytes 524312
  70.7 1.6 %settle.1 = (bf16[256,1024]{1,0:T(8,128)(2,1)}, bf16[256,1024]{1,0:T(8,128)(2,1)}) custom-call(f32[256,1024]{1,0:T(8,128)S(1)} %get-tuple-element.16.refs_0_, f32[256,1024]{1,0:T(8,128)S(1)} %get-tuple-element.17.refs_1_, bf16[128,1024]{1,0:T(8,128)(2,1)S(1)} %get-tuple-element.28.refs_2_, bf16[128,1024]{1,0:T(8,128)(2,1)S(1)} %collective-permute-done.8.refs_3_, ...), custom_call_target="tpu_custom_call" | custom-call | tf_op jit(solution)/shard_map/settle/pallas_call | solution.py:251
  (23 shorter events, 1.5 us)
Async XLA Ops:
  2.8 9.7 %collective-permute-start.2 = (bf16[128,1024]{1,0:T(8,128)(2,1)}, bf16[128,1024]{1,0:T(8,128)(2,1)S(1)}, u32[]{:S(2)}, u32[]{:S(2)}) collective-permute-start(bf16[128,1024]{1,0:T(8,128)(2,1)} %pick.1), channel_id=1, source_target_pairs={{0,2},{2,4},{4,6},{6,8},{8,10},{10,12},{12,14},{14,16},{16,18},{18... | collective-permute-start | bytes 786440 | tf_op jit(solution)/shard_map/ppermute | solution.py:30
  7.7 7.7 %collective-permute-start.1 = (bf16[128,1024]{1,0:T(8,128)(2,1)}, bf16[128,1024]{1,0:T(8,128)(2,1)S(1)}, u32[]{:S(2)}, u32[]{:S(2)}) collective-permute-start(bf16[128,1024]{1,0:T(8,128)(2,1)} %pick.1), channel_id=1, source_target_pairs={{0,8},{2,10},{4,12},{6,14},{8,16},{10,18},{12,20},{14,22},{16,24},... | collective-permute-start | bytes 786440 | tf_op jit(solution)/shard_map/ppermute | solution.py:30
  11.2 12.7 %collective-permute-start = (bf16[256,1024]{1,0:T(8,128)(2,1)}, bf16[256,1024]{1,0:T(8,128)(2,1)S(1)}, u32[]{:S(2)}, u32[]{:S(2)}) collective-permute-start(bf16[256,1024]{1,0:T(8,128)(2,1)} %own_ref.1), channel_id=1, source_target_pairs={{0,1},{1,0},{2,3},{3,2},{4,5},{5,4},{6,7},{7,6},{8,9},{9,8},{10,11... | collective-permute-start | bytes 1572872 | tf_op jit(solution)/shard_map/ppermute | solution.py:34
  16.4 13.4 %collective-permute-start.4 = (bf16[128,1024]{1,0:T(8,128)(2,1)S(1)}, bf16[128,1024]{1,0:T(8,128)(2,1)S(1)}, u32[]{:S(2)}, u32[]{:S(2)}) collective-permute-start(bf16[128,1024]{1,0:T(8,128)(2,1)S(1)} %get-tuple-element.26), channel_id=1, source_target_pairs={{0,4},{2,6},{4,0},{6,2},{8,12},{10,14},{12,8},{14,10},{16,20},{18,... | collective-permute-start | bytes 786440 | tf_op jit(solution)/shard_map/ppermute | solution.py:30
  18.8 11.3 %collective-permute-start.3 = (bf16[128,1024]{1,0:T(8,128)(2,1)S(1)}, bf16[128,1024]{1,0:T(8,128)(2,1)S(1)}, u32[]{:S(2)}, u32[]{:S(2)}) collective-permute-start(bf16[128,1024]{1,0:T(8,128)(2,1)S(1)} %get-tuple-element.27), channel_id=1, source_target_pairs={{0,8},{2,10},{4,12},{6,14},{8,16},{10,18},{12,20},{14,22},{16,24},... | collective-permute-start | bytes 786440 | tf_op jit(solution)/shard_map/ppermute | solution.py:30
  23.9 6.2 %copy-start.1 = (bf16[256,1024]{1,0:T(8,128)(2,1)S(1)}, bf16[256,1024]{1,0:T(8,128)(2,1)}, u32[]{:S(2)}) copy-start(bf16[256,1024]{1,0:T(8,128)(2,1)} %refs_3_.1) | copy-start | bytes 1572868
  23.9 6.2 %copy-start.2 = (bf16[256,1024]{1,0:T(8,128)(2,1)S(1)}, bf16[256,1024]{1,0:T(8,128)(2,1)}, u32[]{:S(2)}) copy-start(bf16[256,1024]{1,0:T(8,128)(2,1)} %refs_4_.1) | copy-start | bytes 1572868
  23.9 6.2 %copy-start.5 = (bf16[256,1024]{1,0:T(8,128)(2,1)S(1)}, bf16[256,1024]{1,0:T(8,128)(2,1)}, u32[]{:S(2)}) copy-start(bf16[256,1024]{1,0:T(8,128)(2,1)} %refs_2_.1) | copy-start | bytes 1572868
  23.9 6.2 %copy-start.6 = (s32[4]{0:T(128)S(1)}, s32[4]{0:T(128)}, u32[]{:S(2)}) copy-start(s32[4]{0:T(128)} %refs_1_.1) | copy-start | bytes 52
  23.9 0.8 %copy-start.7 = (bf16[256,1024]{1,0:T(8,128)(2,1)}, bf16[256,1024]{1,0:T(8,128)(2,1)S(1)}, u32[]{:S(2)}) copy-start(bf16[256,1024]{1,0:T(8,128)(2,1)S(1)} %collective-permute-done.other_ref) | copy-start | bytes 1572868
  30.1 1.0 %copy-start.4 = (bf16[256,1024]{1,0:T(8,128)(2,1)S(1)}, bf16[256,1024]{1,0:T(8,128)(2,1)}, u32[]{:S(2)}) copy-start(bf16[256,1024]{1,0:T(8,128)(2,1)} %grad_attn.1.refs_5_) | copy-start | bytes 1572868
  40.5 14.8 %copy-start.3 = (bf16[256,1024]{1,0:T(8,128)(2,1)}, bf16[256,1024]{1,0:T(8,128)(2,1)S(1)}, u32[]{:S(2)}) copy-start(bf16[256,1024]{1,0:T(8,128)(2,1)S(1)} %get-tuple-element.14.own_ref) | copy-start | bytes 1572868
  40.6 8.7 %collective-permute-start.7 = (bf16[128,1024]{1,0:T(8,128)(2,1)S(1)}, bf16[128,1024]{1,0:T(8,128)(2,1)S(1)}, u32[]{:S(2)}, u32[]{:S(2)}) collective-permute-start(bf16[128,1024]{1,0:T(8,128)(2,1)S(1)} %get-tuple-element.29), channel_id=1, source_target_pairs={{8,0},{10,2},{12,4},{14,6},{16,8},{18,10},{20,12},{22,14},{24,16},... | collective-permute-start | bytes 786440 | tf_op jit(solution)/shard_map/ppermute | solution.py:30
  41.9 10.7 %collective-permute-start.6 = (bf16[128,1024]{1,0:T(8,128)(2,1)S(1)}, bf16[128,1024]{1,0:T(8,128)(2,1)S(1)}, u32[]{:S(2)}, u32[]{:S(2)}) collective-permute-start(bf16[128,1024]{1,0:T(8,128)(2,1)S(1)} %get-tuple-element.30), channel_id=1, source_target_pairs={{0,4},{2,6},{4,0},{6,2},{8,12},{10,14},{12,8},{14,10},{16,20},{18,... | collective-permute-start | bytes 786440 | tf_op jit(solution)/shard_map/ppermute | solution.py:30
  45.5 9.9 %collective-permute-start.5 = (bf16[256,1024]{1,0:T(8,128)(2,1)S(1)}, bf16[256,1024]{1,0:T(8,128)(2,1)S(1)}, u32[]{:S(2)}, u32[]{:S(2)}) collective-permute-start(bf16[256,1024]{1,0:T(8,128)(2,1)S(1)} %get-tuple-element.14.own_ref), channel_id=1, source_target_pairs={{0,1},{1,0},{2,3},{3,2},{4,5},{5,4},{6,7},{7,6},{8,9},{9,8},{10,11... | collective-permute-start | bytes 1572872 | tf_op jit(solution)/shard_map/ppermute | solution.py:34
  52.8 11.8 %collective-permute-start.9 = (bf16[128,1024]{1,0:T(8,128)(2,1)S(1)}, bf16[128,1024]{1,0:T(8,128)(2,1)S(1)}, u32[]{:S(2)}, u32[]{:S(2)}) collective-permute-start(bf16[128,1024]{1,0:T(8,128)(2,1)S(1)} %get-tuple-element.24), channel_id=1, source_target_pairs={{2,0},{4,2},{6,4},{8,6},{10,8},{12,10},{14,12},{16,14},{18,16},{20... | collective-permute-start | bytes 786440 | tf_op jit(solution)/shard_map/ppermute | solution.py:30
  54.1 15.6 %collective-permute-start.8 = (bf16[128,1024]{1,0:T(8,128)(2,1)S(1)}, bf16[128,1024]{1,0:T(8,128)(2,1)S(1)}, u32[]{:S(2)}, u32[]{:S(2)}) collective-permute-start(bf16[128,1024]{1,0:T(8,128)(2,1)S(1)} %get-tuple-element.25), channel_id=1, source_target_pairs={{8,0},{10,2},{12,4},{14,6},{16,8},{18,10},{20,12},{22,14},{24,16},... | collective-permute-start | bytes 786440 | tf_op jit(solution)/shard_map/ppermute | solution.py:30
  55.4 0.8 %copy-start.8 = (bf16[256,1024]{1,0:T(8,128)(2,1)}, bf16[256,1024]{1,0:T(8,128)(2,1)S(1)}, u32[]{:S(2)}) copy-start(bf16[256,1024]{1,0:T(8,128)(2,1)S(1)} %collective-permute-done.5.other_ref) | copy-start | bytes 1572868
  69.7 1.0 %copy-start = (bf16[256,1024]{1,0:T(8,128)(2,1)S(1)}, bf16[256,1024]{1,0:T(8,128)(2,1)}, u32[]{:S(2)}) copy-start(bf16[256,1024]{1,0:T(8,128)(2,1)} %project.1.refs_5_) | copy-start | bytes 1572868

commit v3 on v2

v3 whole, which is shorter than its diff:
```python
import functools
import math

import jax
import jax.numpy as jnp
from jax import lax
from jax.experimental import pallas as pl
from jax.experimental.pallas import tpu as pltpu
from jax.sharding import PartitionSpec as P

DH = 128
STEP = 4
BF16 = jnp.bfloat16
F32 = jnp.float32
HBM_BLOCK = pl.BlockSpec(memory_space=pltpu.HBM)
VMEM_BLOCK = pl.BlockSpec(memory_space=pltpu.VMEM)
SMEM_BLOCK = pl.BlockSpec(memory_space=pltpu.SMEM)


def hop(distance, n):
    return [(i, i + distance) for i in range(n) if 0 <= i + distance < n]


def pairs(n):
    return [(i, i ^ 2) for i in range(n)]


def steps(n):
    return [(i, i - 3 if i % 4 == 3 else i + 1) for i in range(n)]


def turned(route):
    return [(b, a) for a, b in route]


def mixed(block, route_of_core):
    cores = len(route_of_core)
    route = [(a * cores + c, b * cores + c) for c, r in enumerate(route_of_core) for a, b in r]
    return lax.ppermute(block, ("ctx", "head"), route)


def swap(block):
    return lax.ppermute(block, "head", [(0, 1), (1, 0)])


def nt(a, b):
    return lax.dot_general(a, b, (((1,), (1,)), ((), ())), preferred_element_type=F32)


def tn(a, b):
    return lax.dot_general(a, b, (((0,), (0,)), ((), ())), preferred_element_type=F32)


def nn(a, b):
    return jnp.dot(a, b, preferred_element_type=F32)


def params(mib=24):
    return pltpu.CompilerParams(vmem_limit_bytes=int(mib * 1024 * 1024))


def pick_kernel(k_hbm, v_hbm, out_ref, held, sems):
    tokens = k_hbm.shape[0]
    rows = tokens // STEP
    copies = [pltpu.make_async_copy(x, held.at[i], sems.at[i]) for i, x in enumerate((k_hbm, v_hbm))]
    for copy in copies:
        copy.start()
    at = lax.broadcasted_iota(jnp.int32, (rows, tokens), 0) * STEP
    choose = (at == lax.broadcasted_iota(jnp.int32, (rows, tokens), 1)).astype(BF16)
    for i, copy in enumerate(copies):
        copy.wait()
        out_ref[i * rows : (i + 1) * rows] = nn(choose, held[i]).astype(BF16)


def pick(keys, values):
    tokens, width = keys.shape
    return pl.pallas_call(
        pick_kernel,
        in_specs=[HBM_BLOCK, HBM_BLOCK],
        out_shape=jax.ShapeDtypeStruct((2 * tokens // STEP, width), BF16),
        scratch_shapes=[pltpu.VMEM((2, tokens, width), BF16), pltpu.SemaphoreType.DMA((2,))],
        compiler_params=params(63.5),
        name="pick",
    )(keys, values)


def grad_attn_kernel(place_ref, own_ref, other_ref, w_hbm, out_ref, flag_ref, held, sems):
    pieces, tile, _ = held.shape
    core = place_ref[1]
    copies = []
    for i in range(pieces):
        rows = w_hbm.at[pl.ds((core * pieces + i) * tile, tile), :]
        copies.append(pltpu.make_async_copy(rows, held.at[i], sems.at[i]))
        copies[i].start()
    flag_ref[0] = place_ref[0]
    flag_ref[1] = core
    own, other = own_ref[...], other_ref[...]
    whole = jnp.concatenate([jnp.where(core == 0, own, other), jnp.where(core == 0, other, own)], 1)
    for i in range(pieces):
        copies[i].wait()
        out_ref[:, i * tile : (i + 1) * tile] = nt(whole, held[i]).astype(BF16)


def grad_attn(place, own, other, weight):
    tokens, width = own.shape
    pieces = 4
    return pl.pallas_call(
        grad_attn_kernel,
        in_specs=[SMEM_BLOCK, VMEM_BLOCK, VMEM_BLOCK, HBM_BLOCK],
        out_specs=[VMEM_BLOCK, SMEM_BLOCK],
        out_shape=[
            jax.ShapeDtypeStruct((tokens, width), BF16),
            jax.ShapeDtypeStruct(place.shape, jnp.int32),
        ],
        scratch_shapes=[
            pltpu.VMEM((pieces, width // pieces, weight.shape[1]), BF16),
            pltpu.SemaphoreType.DMA((pieces,)),
        ],
        compiler_params=params(57),
        cost_estimate=pl.CostEstimate(
            flops=4 * tokens * width * width, bytes_accessed=6 * width * width, transcendentals=0
        ),
        name="grad_attn",
    )(place, own, other, weight)


def project_kernel(place_ref, own_ref, other_ref, w_hbm, out_ref, flag_ref, held, sems):
    flag_ref[0] = place_ref[0]
    flag_ref[1] = place_ref[1]
    pieces, tile, width = held.shape
    core = place_ref[1]
    columns = pl.ds(pl.multiple_of(core * width, width), width)
    copies = []
    for i in range(pieces):
        part = w_hbm.at[pl.ds(i * tile, tile), columns]
        copies.append(pltpu.make_async_copy(part, held.at[i], sems.at[i]))
        copies[i].start()
    own, other = own_ref[...], other_ref[...]
    whole = jnp.concatenate([jnp.where(core == 0, own, other), jnp.where(core == 0, other, own)], 1)
    total = None
    for i in range(pieces):
        copies[i].wait()
        term = nn(whole[:, i * tile : (i + 1) * tile], held[i])
        total = term if total is None else total + term
    out_ref[...] = total.astype(BF16)


def project(place, own, other, weight):
    tokens, width = own.shape
    pieces = 4
    return pl.pallas_call(
        project_kernel,
        in_specs=[SMEM_BLOCK, VMEM_BLOCK, VMEM_BLOCK, HBM_BLOCK],
        out_specs=[VMEM_BLOCK, SMEM_BLOCK],
        out_shape=[
            jax.ShapeDtypeStruct((tokens, width), BF16),
            jax.ShapeDtypeStruct(place.shape, jnp.int32),
        ],
        scratch_shapes=[
            pltpu.VMEM((pieces, weight.shape[0] // pieces, width), BF16),
            pltpu.SemaphoreType.DMA((pieces,)),
        ],
        compiler_params=params(57),
        cost_estimate=pl.CostEstimate(
            flops=4 * tokens * width * width, bytes_accessed=6 * width * width, transcendentals=0
        ),
        name="project",
    )(place, own, other, weight)


def documents(positions, bounds_ref):
    count = jnp.zeros(positions.shape, jnp.int32)
    for i in range(bounds_ref.shape[0]):
        count = count + (bounds_ref[i] <= positions).astype(jnp.int32)
    return count


def mask_bias(me, bounds_ref, tokens, levels):
    rows = tokens // STEP
    own = lax.broadcasted_iota(jnp.int32, (1, tokens), 1) + me * tokens
    parts = [lax.broadcasted_iota(jnp.int32, (tokens, 1), 0) + me * tokens]
    for i in range(levels):
        at = lax.broadcasted_iota(jnp.int32, (rows, 1), 0) * STEP
        parts.append(at + (me - 2**i) * tokens)
    keys = jnp.concatenate(parts, 0)
    key_doc = jnp.where(keys >= 0, documents(keys, bounds_ref), -1)
    ok = (documents(own, bounds_ref) == key_doc) & (keys <= own)
    return jnp.where(ok, 0.0, -jnp.inf).astype(F32)


def sort_arrived(first, arrived):
    far4, two, three, four, *more = arrived
    far1 = jnp.where(first, three, two)
    far2 = jnp.where(first, four, three)
    far8 = jnp.where(first, two, four)
    return [far1, far2, far4, far8, *more]


def scores_kernel(levels, *refs):
    place_ref, bounds_ref, q_ref, k_ref, v_ref, ga_ref = refs[:6]
    arrived_refs = refs[6 : 6 + levels]
    w_ref, u_ref = refs[6 + levels : 8 + levels]
    gfar_refs = refs[8 + levels : 8 + 2 * levels]
    bias_ref = refs[8 + 2 * levels]
    tokens = q_ref.shape[0]
    rows = tokens // STEP
    scale = 1.0 / math.sqrt(DH)
    first = place_ref[1] == 0

    @pl.when(pl.program_id(0) == 0)
    def _():
        bias_ref[...] = mask_bias(place_ref[0], bounds_ref, tokens, levels)

    for h in range(q_ref.shape[1] // DH):
        cols = slice(h * DH, (h + 1) * DH)
        q, ga = q_ref[:, cols], ga_ref[:, cols]
        far = sort_arrived(first, [r[:, cols] for r in arrived_refs])
        k = jnp.concatenate([k_ref[:, cols]] + [f[:rows] for f in far], 0)
        v = jnp.concatenate([v_ref[:, cols]] + [f[rows:] for f in far], 0)
        scores = nt(k, q) + bias_ref[...]
        top = jnp.max(scores, axis=0, keepdims=True)
        grown = jnp.exp2((scores - top) * (scale * math.log2(math.e)))
        prob = grown * (1.0 / jnp.sum(grown, axis=0, keepdims=True))
        weights = prob.astype(BF16)
        grad_prob = nt(v, ga)
        delta = jnp.sum(prob * grad_prob, axis=0, keepdims=True)
        grad_scores = (prob * (grad_prob - delta)).astype(BF16)
        w_ref[h] = weights
        u_ref[h] = grad_scores
        gk = (nn(grad_scores[tokens:], q) * scale).astype(BF16)
        gv = nn(weights[tokens:], ga).astype(BF16)
        g1, g2, g4, g8, *more = [
            jnp.concatenate([g[i * rows : (i + 1) * rows] for g in (gk, gv)], 0) for i in range(levels)
        ]
        out = [g4, jnp.where(first, g8, g1), jnp.where(first, g1, g2), jnp.where(first, g2, g8)]
        for ref, block in zip(gfar_refs, out + more):
            ref[:, cols] = block


def attention_scores(place, bounds, q, k, v, ga, arrived):
    tokens, width = q.shape
    levels = len(arrived)
    rows = tokens // STEP
    count = tokens + levels * rows
    step = 2
    block = pl.BlockSpec((tokens, step * DH), lambda i: (0, i))
    far_block = pl.BlockSpec((2 * rows, step * DH), lambda i: (0, i))
    prob_block = pl.BlockSpec((step, count, tokens), lambda i: (i, 0, 0))
    prob = jax.ShapeDtypeStruct((width // DH, count, tokens), BF16)
    return pl.pallas_call(
        functools.partial(scores_kernel, levels),
        grid=(width // (step * DH),),
        in_specs=[SMEM_BLOCK, SMEM_BLOCK] + [block] * 4 + [far_block] * levels,
        out_specs=[prob_block] * 2 + [far_block] * levels,
        out_shape=[prob, prob] + [jax.ShapeDtypeStruct((2 * rows, width), BF16)] * levels,
        scratch_shapes=[pltpu.VMEM((count, tokens), F32)],
        compiler_params=params(),
        cost_estimate=pl.CostEstimate(
            flops=6 * tokens * count * width, bytes_accessed=16 * tokens * width, transcendentals=0
        ),
        name="attention_scores",
    )(place, bounds, q, k, v, ga, *arrived)


def local_kernel(levels, *refs):
    place_ref, q_ref, k_ref, v_ref, ga_ref, w_ref, u_ref = refs[:7]
    arrived_refs = refs[7 : 7 + levels]
    attn_ref, gq_ref, gk_ref, gv_ref, flag_ref = refs[7 + levels :]
    tokens = q_ref.shape[0]
    rows = tokens // STEP
    scale = 1.0 / math.sqrt(DH)
    first = place_ref[1] == 0
    flag_ref[0] = place_ref[0]
    flag_ref[1] = place_ref[1]
    for h in range(q_ref.shape[1] // DH):
        cols = slice(h * DH, (h + 1) * DH)
        far = sort_arrived(first, [r[:, cols] for r in arrived_refs])
        k = jnp.concatenate([k_ref[:, cols]] + [f[:rows] for f in far], 0)
        v = jnp.concatenate([v_ref[:, cols]] + [f[rows:] for f in far], 0)
        weights, grad_scores = w_ref[h], u_ref[h]
        attn_ref[:, cols] = tn(weights, v).astype(BF16)
        gq_ref[:, cols] = (tn(grad_scores, k) * scale).astype(BF16)
        gk_ref[:, cols] = nn(grad_scores[:tokens], q_ref[:, cols]) * scale
        gv_ref[:, cols] = nn(weights[:tokens], ga_ref[:, cols])


def attention_local(place, q, k, v, ga, weights, grad_scores, arrived):
    tokens, width = q.shape
    levels = len(arrived)
    rows = tokens // STEP
    count = tokens + levels * rows
    step = 2
    block = pl.BlockSpec((tokens, step * DH), lambda i: (0, i))
    far_block = pl.BlockSpec((2 * rows, step * DH), lambda i: (0, i))
    prob_block = pl.BlockSpec((step, count, tokens), lambda i: (i, 0, 0))
    bf = jax.ShapeDtypeStruct((tokens, width), BF16)
    f32 = jax.ShapeDtypeStruct((tokens, width), F32)
    return pl.pallas_call(
        functools.partial(local_kernel, levels),
        grid=(width // (step * DH),),
        in_specs=[SMEM_BLOCK] + [block] * 4 + [prob_block] * 2 + [far_block] * levels,
        out_specs=[block] * 4 + [SMEM_BLOCK],
        out_shape=[bf, bf, f32, f32, jax.ShapeDtypeStruct(place.shape, jnp.int32)],
        compiler_params=params(),
        cost_estimate=pl.CostEstimate(
            flops=6 * tokens * count * width, bytes_accessed=16 * tokens * width, transcendentals=0
        ),
        name="attention_local",
    )(place, q, k, v, ga, weights, grad_scores, *arrived)


def settle_kernel(count, *refs):
    gk_ref, gv_ref = refs[:2]
    back_refs = refs[2 : 2 + count]
    out_k_ref, out_v_ref = refs[3 + count :]
    tokens = gk_ref.shape[0]
    rows = tokens // STEP
    at = lax.broadcasted_iota(jnp.int32, (tokens, rows), 0)
    place = (at == lax.broadcasted_iota(jnp.int32, (tokens, rows), 1) * STEP).astype(BF16)
    place = jnp.concatenate([place] * count, 1)
    extra_k = nn(place, jnp.concatenate([r[:rows] for r in back_refs], 0))
    extra_v = nn(place, jnp.concatenate([r[rows:] for r in back_refs], 0))
    out_k_ref[...] = (gk_ref[...] + extra_k).astype(BF16)
    out_v_ref[...] = (gv_ref[...] + extra_v).astype(BF16)


def settle(gk, gv, back, after):
    tokens, width = gk.shape
    out = jax.ShapeDtypeStruct((tokens, width), BF16)
    cols = 512
    block = pl.BlockSpec((tokens, cols), lambda i: (0, i))
    back_block = pl.BlockSpec((back[0].shape[0], cols), lambda i: (0, i))
    return pl.pallas_call(
        functools.partial(settle_kernel, len(back)),
        grid=(width // cols,),
        in_specs=[block] * 2 + [back_block] * len(back) + [SMEM_BLOCK],
        out_specs=[block] * 2,
        out_shape=[out, out],
        compiler_params=params(),
        name="settle",
    )(gk, gv, *back, after)


def add(*blocks):
    total = blocks[0].astype(F32)
    for block in blocks[1:]:
        total = total + block.astype(F32)
    return total.astype(BF16)


def per_device(queries, keys, values, out_weight, cotangent, bounds):
    n = lax.axis_size("ctx")
    levels = n.bit_length() - 1
    place = jnp.stack([lax.axis_index("ctx"), lax.axis_index("head")]).astype(jnp.int32)

    other_cot = swap(cotangent)
    picked = pick(keys, values)
    far4 = lax.ppermute(picked, "ctx", hop(4, n))
    ga, flags = grad_attn(place, cotangent, other_cot, out_weight)

    first = flags[1] == 0
    lent1 = jnp.where(flags[0] % 4 == 3, far4, picked)
    lent2 = jnp.where(flags[0] % 4 < 2, picked, far4)
    hops, ones, twos = hop(4, n), steps(n), pairs(n)
    two = mixed(jnp.where(first, far4, lent1), (hops, ones))
    three = mixed(jnp.where(first, lent1, lent2), (ones, twos))
    four = mixed(jnp.where(first, lent2, far4), (twos, hops))
    arrived = [far4, two, three, four]
    farther = jnp.where(first, two, four) if levels > 4 else None
    for i in range(4, levels):
        farther = lax.ppermute(farther, "ctx", hop(2 ** (i - 1), n))
        arrived.append(farther)

    weights, grad_scores, g4, two, three, four, *more = attention_scores(
        place, bounds, queries, keys, values, ga, arrived
    )
    for i in reversed(range(len(more))):
        back = lax.ppermute(more[i], "ctx", hop(-(2 ** (i + 3)), n))
        if i > 0:
            more[i - 1] = add(more[i - 1], back)
        else:
            two = jnp.where(place[1] == 0, add(two, back), two)
            four = jnp.where(place[1] == 0, four, add(four, back))
    hops, ones, twos = hop(-4, n), turned(ones), turned(twos)
    two = mixed(two, (hops, ones))
    three = mixed(three, (ones, twos))
    four = mixed(four, (twos, hops))
    attn, gq, gk, gv, flags = attention_local(
        place, queries, keys, values, ga, weights, grad_scores, arrived
    )
    first = flags[1] == 0
    own1, own2 = flags[0] % 4 != 3, flags[0] % 4 < 2
    back1, back2 = jnp.where(first, three, two), jnp.where(first, four, three)
    back8 = jnp.where(first, two, four)
    zero = jnp.zeros_like(back1)
    g4 = add(g4, back8, jnp.where(own1, zero, back1), jnp.where(own2, zero, back2))
    back4 = lax.ppermute(g4, "ctx", hop(-4, n))
    other_attn = swap(attn)
    output, flags = project(place, attn, other_attn, out_weight)
    back = [back4, jnp.where(own1, back1, zero), jnp.where(own2, back2, zero)]
    gk, gv = settle(gk, gv, back, flags)
    return output, gq, gk, gv


def solution(mesh):
    shared = P("ctx", "head")
    return jax.shard_map(
        per_device,
        mesh=mesh,
        in_specs=(shared, shared, shared, P(), shared, P()),
        out_specs=(shared,) * 4,
        check_vma=False,
    )
```

time: 72.9 us -> 73.6 us (level)
  waiting for transfers between devices: 17.5 us -> 8.72 us
  between operations: 0.79 us -> 5.84 us
  Pallas kernels: 23.3 us -> 27.3 us
  starting transfers between devices: 25.8 us -> 21.8 us
  other arithmetic: 1.27 us -> 3.21 us
  local copies, waits for them, and re-layouts: 3.67 us -> 5.5 us
    ppermute x8 -> x6, waiting for transfers between devices: 17.5 us -> 6.07 us  [mixed(): return lax.ppermute(block, ('ctx', 'head'), route)]
    ppermute x8 -> x6, starting transfers between devices: 23.2 us -> 13.6 us  [mixed(): return lax.ppermute(block, ('ctx', 'head'), route)]
    ppermute x0 -> x2, starting transfers between devices: none -> 5.8 us  [the longest x1 4.51 us: per_device(): far4 = lax.ppermute(picked, 'ctx', hop(4, n))]
    pallas_call x4 -> x5, Pallas kernels: 21.6 us -> 25.2 us  [the longest x1 7.43 us: attention_scores(): pl.pallas_call(functools.partial(scores_kernel, levels), grid=(width // (...]
    ppermute x0 -> x2, waiting for transfers between devices: none -> 2.65 us  [the longest x1 2.65 us: per_device(): back4 = lax.ppermute(g4, 'ctx', hop(-4, n))]
    slice x0 -> x2, local copies, waits for them, and re-layouts: none -> 2.03 us  [the longest x1 1.4 us: per_device(): lent1 = jnp.where(flags[0] % 4 == 3, far4, picked)]
    convert_element_type x0 -> x1, other arithmetic: none -> 1.41 us  [add(): return total.astype(BF16)]
    unnamed x18 -> x26, local copies, waits for them, and re-layouts: 3.67 us -> 3.47 us
  transfers between devices with their start and end apart: 10 -> 10, of which waited for: 7 -> 3; matrix products, arithmetic and copies ran while one was open for 2% -> 7% of each run, Pallas kernels for 14% -> 25%
where the time goes in v3:
time: 73.6 us; the launch traced here: 72.4 us
  Pallas kernels  27.3 us (37%)
  starting transfers between devices  21.8 us (30%)
  waiting for transfers between devices  8.72 us (12%)
  between operations  5.84 us (8%)
  local copies, waits for them, and re-layouts  5.5 us (7%)
  other arithmetic  3.21 us (4%)
    ppermute x6, starting transfers between devices, mixed(): return lax.ppermute(block, ('ctx', 'head'), route)  13.6 us
    pallas_call x1, Pallas kernels, attention_scores(): pl.pallas_call(functools.partial(scores_kernel, levels), grid=(width // (...  7.43 us
    pallas_call x1, Pallas kernels, grad_attn(): pl.pallas_call(grad_attn_kernel, in_specs=[SMEM_BLOCK, VMEM_BLOCK, VMEM_B...  6.3 us
    ppermute x6, waiting for transfers between devices, mixed(): return lax.ppermute(block, ('ctx', 'head'), route)  6.07 us
    pallas_call x1, Pallas kernels, project(): pl.pallas_call(project_kernel, in_specs=[SMEM_BLOCK, VMEM_BLOCK, VMEM_BLO...  4.95 us
    ppermute x1, starting transfers between devices, per_device(): far4 = lax.ppermute(picked, 'ctx', hop(4, n))  4.51 us
    pallas_call x1, Pallas kernels, attention_local(): pl.pallas_call(functools.partial(local_kernel, levels), grid=(width // (s...  4.37 us
    unnamed x26, local copies, waits for them, and re-layouts  3.47 us
  transfers between devices with their start and end apart: 10, of which 3 were waited for; matrix products, arithmetic and copies ran while one was open for 7% of the time, Pallas kernels for 25%

profile of v3, /device:TPU:0, one launch (start us, length us, event | category | flops | bytes accessed | tf_op | source)
XLA Modules:
  0.0 72.4 jit_solution(17092930611803353948)
XLA Ops:
  1.1 2.2 %pick.1 = bf16[128,1024]{1,0:T(8,128)(2,1)} custom-call(bf16[256,1024]{1,0:T(8,128)(2,1)} %refs_2_.3, bf16[256,1024]{1,0:T(8,128)(2,1)} %refs_3_.3), custom_call_target="tpu_custom_call" | custom-call | tf_op jit(solution)/shard_map/pick/pallas_call | solution.py:77
  3.3 4.5 %collective-permute-start.1 = (bf16[128,1024]{1,0:T(8,128)(2,1)}, bf16[128,1024]{1,0:T(8,128)(2,1)S(1)}, u32[]{:S(2)}, u32[]{:S(2)}) collective-permute-start(bf16[128,1024]{1,0:T(8,128)(2,1)} %pick.1), channel_id=1, source_target_pairs={{0,8},{2,10},{4,12},{6,14},{8,16},{10,18},{12,20},{14,22},{16,24},... | collective-permute-start | bytes 786440 | tf_op jit(solution)/shard_map/ppermute | solution.py:358
  7.9 0.6 pad_add_fusion.place_ref.refs_0_
  8.6 6.3 %grad_attn.1 = (bf16[256,1024]{1,0:T(8,128)(2,1)}, s32[2]{0:T(128)}) custom-call(s32[2]{0:T(128)} %pad_add_fusion.place_ref.refs_0_, bf16[256,1024]{1,0:T(8,128)(2,1)} %own_ref.1, bf16[256,1024]{1,0:T(8,128)(2,1)} %collective-permute-done.other_ref, bf16[2048,2048]{1,0:T(8,128)(2,1)} %w_hbm.3), custom_call_target="tpu_custom_call" | custom-call | flops 1073741824 | bytes 6291456 | tf_op jit(solution)/shard_map/grad_attn/pallas_call | solution.py:107
  14.9 1.4 %fusion.1 = (s32[1]{0:T(128)}, s32[1]{0:T(128)}) fusion(s32[2]{0:T(128)} %get-tuple-element.22), kind=kLoop, calls=%fused_computation.12 | loop fusion | bytes 16 | tf_op jit(solution)/shard_map/slice | solution.py:362
  19.0 3.4 %collective-permute-start.4 = (bf16[128,1024]{1,0:T(8,128)(2,1)S(1)}, bf16[128,1024]{1,0:T(8,128)(2,1)S(1)}, u32[]{:S(2)}, u32[]{:S(2)}) collective-permute-start(bf16[128,1024]{1,0:T(8,128)(2,1)S(1)} %get-tuple-element.38), channel_id=1, source_target_pairs={{0,4},{2,6},{4,0},{6,2},{8,12},{10,14},{12,8},{14,10},{16,20},{18,... | collective-permute-start | bytes 786440 | tf_op jit(solution)/shard_map/ppermute | solution.py:39
  22.4 3.5 %collective-permute-start.2 = (bf16[128,1024]{1,0:T(8,128)(2,1)S(1)}, bf16[128,1024]{1,0:T(8,128)(2,1)S(1)}, u32[]{:S(2)}, u32[]{:S(2)}) collective-permute-start(bf16[128,1024]{1,0:T(8,128)(2,1)S(1)} %get-tuple-element.39), channel_id=1, source_target_pairs={{0,8},{2,10},{4,12},{6,14},{8,16},{10,18},{12,20},{14,22},{16,24},... | collective-permute-start | bytes 786440 | tf_op jit(solution)/shard_map/ppermute | solution.py:39
  25.9 1.5 %collective-permute-start.3 = (bf16[128,1024]{1,0:T(8,128)(2,1)S(1)}, bf16[128,1024]{1,0:T(8,128)(2,1)S(1)}, u32[]{:S(2)}, u32[]{:S(2)}) collective-permute-start(bf16[128,1024]{1,0:T(8,128)(2,1)S(1)} %get-tuple-element.40), channel_id=1, source_target_pairs={{0,2},{2,4},{4,6},{6,0},{8,10},{10,12},{12,14},{14,8},{16,18},{18,... | collective-permute-start | bytes 786440 | tf_op jit(solution)/shard_map/ppermute | solution.py:39
  27.5 2.3 %collective-permute-done.2.refs_7_.refs_8_ = bf16[128,1024]{1,0:T(8,128)(2,1)S(1)} collective-permute-done((bf16[128,1024]{1,0:T(8,128)(2,1)S(1)}, bf16[128,1024]{1,0:T(8,128)(2,1)S(1)}, u32[]{:S(2)}, u32[]{:S(2)}) %collective-permute-start.2) | collective-permute-done | bytes 262176 | tf_op jit(solution)/shard_map/ppermute | solution.py:39
  29.8 3.7 %collective-permute-done.3.refs_8_.refs_9_ = bf16[128,1024]{1,0:T(8,128)(2,1)S(1)} collective-permute-done((bf16[128,1024]{1,0:T(8,128)(2,1)S(1)}, bf16[128,1024]{1,0:T(8,128)(2,1)S(1)}, u32[]{:S(2)}, u32[]{:S(2)}) %collective-permute-start.3) | collective-permute-done | bytes 262176 | tf_op jit(solution)/shard_map/ppermute | solution.py:39
  33.6 1.0 %copy-done.3 = bf16[256,1024]{1,0:T(8,128)(2,1)S(1)} copy-done((bf16[256,1024]{1,0:T(8,128)(2,1)S(1)}, bf16[256,1024]{1,0:T(8,128)(2,1)}, u32[]{:S(2)}) %copy-start.3) | copy-done | bytes 524312
  34.6 7.4 %attention_scores.1 = (bf16[8,512,256]{2,1,0:T(8,128)(2,1)S(1)}, bf16[8,512,256]{2,1,0:T(8,128)(2,1)S(1)}, bf16[128,1024]{1,0:T(8,128)(2,1)S(1)}, bf16[128,1024]...) custom-call(s32[2]{0:T(128)S(1)} %copy-done.8, s32[4]{0:T(128)S(1)} %copy-done.9, ...), custom_call_target="tpu_custom_call" | custom-call | flops 805306368 | bytes 4194304 | tf_op jit(solution)/shard_map/attention_scores/pallas_call | solution.py:250
  42.0 1.3 %collective-permute-start.6 = (bf16[128,1024]{1,0:T(8,128)(2,1)}, bf16[128,1024]{1,0:T(8,128)(2,1)}, u32[]{:S(2)}, u32[]{:S(2)}) collective-permute-start(bf16[128,1024]{1,0:T(8,128)(2,1)} %get-tuple-element.32), channel_id=1, source_target_pairs={{8,0},{10,2},{12,4},{14,6},{16,8},{18,10},{20,12},{22,14},{24,16},... | collective-permute-start | bytes 786440 | tf_op jit(solution)/shard_map/ppermute | solution.py:39
  43.3 3.4 %collective-permute-start.7 = (bf16[128,1024]{1,0:T(8,128)(2,1)}, bf16[128,1024]{1,0:T(8,128)(2,1)}, u32[]{:S(2)}, u32[]{:S(2)}) collective-permute-start(bf16[128,1024]{1,0:T(8,128)(2,1)} %get-tuple-element.33), channel_id=1, source_target_pairs={{4,0},{6,2},{0,4},{2,6},{12,8},{14,10},{8,12},{10,14},{20,16},{22,... | collective-permute-start | bytes 786440 | tf_op jit(solution)/shard_map/ppermute | solution.py:39
  47.2 4.4 %attention_local.1 = (bf16[256,1024]{1,0:T(8,128)(2,1)S(1)}, bf16[256,1024]{1,0:T(8,128)(2,1)}, f32[256,1024]{1,0:T(8,128)S(1)}, f32[256,1024]{1,0:T(8,128)S(1)}, s32[2]{0:T(128)S(1)}) custom-call(s32[2]{0:T(128)S(1)} %copy-done.8, bf16[256,1024]{1,0:T(8,128)(2,1)S(1)} %copy-done.2, bf16[256,1024]{1,0:T(8,128)(2,1)S(1)} %copy-done, ...), custom_call_target="tpu_custom_call" | custom-call | flops 805306368 | bytes 4194304 | tf_op jit(solution)/shard_map/attention_local/pallas_call | solution.py:298
  51.6 1.0 %copy-done.4 = f32[256,1024]{1,0:T(8,128)} copy-done((f32[256,1024]{1,0:T(8,128)}, f32[256,1024]{1,0:T(8,128)S(1)}, u32[]{:S(2)}) %copy-start.4) | copy-done | bytes 1048600
  52.6 1.8 %collective-permute-start.5 = (bf16[256,1024]{1,0:T(8,128)(2,1)S(1)}, bf16[256,1024]{1,0:T(8,128)(2,1)S(1)}, u32[]{:S(2)}, u32[]{:S(2)}) collective-permute-start(bf16[256,1024]{1,0:T(8,128)(2,1)S(1)} %get-tuple-element.25.own_ref), channel_id=1, source_target_pairs={{0,1},{1,0},{2,3},{3,2},{4,5},{5,4},{6,7},{7,6},{8,9},{9,8},{10,11... | collective-permute-start | bytes 1572872 | tf_op jit(solution)/shard_map/ppermute | solution.py:43
  57.4 1.4 %add_convert_fusion = bf16[128,1024]{1,0:T(8,128)(2,1)S(1)} fusion(bf16[128,1024]{1,0:T(8,128)(2,1)} %copy-done.7, bf16[128,1024]{1,0:T(8,128)(2,1)} %collective-permute-done.6, bf16[128,1024]{1,0:T(8,128)(2,1)} %collective-permute-done.7, pred[]{:T(512)S(6)} %lt.23, pred[]{:T(512)S(6)} %ne.19, pred[]{:T(512)} %bitcast.4, ...), kind=kLoop, calls=%fused_computation | loop fusion | flops 1703936 | bytes 1310723 | tf_op jit(solution)/shard_map/convert_element_type | solution.py:348
  58.8 1.3 %collective-permute-start.9 = (bf16[128,1024]{1,0:T(8,128)(2,1)S(1)}, bf16[128,1024]{1,0:T(8,128)(2,1)S(1)}, u32[]{:S(2)}, u32[]{:S(2)}) collective-permute-start(bf16[128,1024]{1,0:T(8,128)(2,1)S(1)} %add_convert_fusion), channel_id=1, source_target_pairs={{8,0},{10,2},{12,4},{14,6},{16,8},{18,10},{20,12},{22,14},{24,16},... | collective-permute-start | bytes 786440 | tf_op jit(solution)/shard_map/ppermute | solution.py:397
  60.1 1.1 %broadcast_select_fusion = (bf16[128,1024]{1,0:T(8,128)(2,1)S(1)}, bf16[128,1024]{1,0:T(8,128)(2,1)S(1)}) fusion(pred[]{:T(512)S(6)} %lt.23, bf16[128,1024]{1,0:T(8,128)(2,1)} %collective-permute-done.7, bf16[128,1024]{1,0:T(8,128)(2,1)} %collective-permute-done.8, pred[]{:T(512)} %bitcast.4, bf16[128,1024]{1,0:T(8,128)(2,1)} %collective-permute-done.6, ...), kind=kLoop, calls=%fused_computation.1 | loop fusion | flops 524288 | bytes 1310723 | tf_op jit(solution)/shard_map/jit(_where)/select_n | solution.py:400
  61.3 0.8 %copy-done.12 = bf16[256,1024]{1,0:T(8,128)(2,1)} copy-done((bf16[256,1024]{1,0:T(8,128)(2,1)}, bf16[256,1024]{1,0:T(8,128)(2,1)S(1)}, u32[]{:S(2)}) %copy-start.12) | copy-done | bytes 524312
  62.1 4.9 %project.1 = (bf16[256,1024]{1,0:T(8,128)(2,1)}, s32[2]{0:T(128)}) custom-call(s32[2]{0:T(128)} %pad_add_fusion.place_ref.refs_0_, bf16[256,1024]{1,0:T(8,128)(2,1)} %copy-done.6, bf16[256,1024]{1,0:T(8,128)(2,1)} %copy-done.12, bf16[2048,2048]{1,0:T(8,128)(2,1)} %w_hbm.3), custom_call_target="tpu_custom_call" | custom-call | flops 1073741824 | bytes 6291456 | tf_op jit(solution)/shard_map/project/pallas_call | solution.py:151
  67.0 2.6 %collective-permute-done.9.refs_2_ = bf16[128,1024]{1,0:T(8,128)(2,1)S(1)} collective-permute-done((bf16[128,1024]{1,0:T(8,128)(2,1)S(1)}, bf16[128,1024]{1,0:T(8,128)(2,1)S(1)}, u32[]{:S(2)}, u32[]{:S(2)}) %collective-permute-start.9) | collective-permute-done | bytes 262176 | tf_op jit(solution)/shard_map/ppermute | solution.py:397
  70.3 2.1 %settle.1 = (bf16[256,1024]{1,0:T(8,128)(2,1)}, bf16[256,1024]{1,0:T(8,128)(2,1)}) custom-call(f32[256,1024]{1,0:T(8,128)S(1)} %get-tuple-element.28.refs_0_, f32[256,1024]{1,0:T(8,128)S(1)} %copy-done.5, bf16[128,1024]{1,0:T(8,128)(2,1)S(1)} %collective-permute-done.9.refs_2_, bf16[128,1024]{1,0:T(8,128)(2,1)S(1)} %get-tuple-element.42.refs_3_, ...), custom_call_target="tpu_custom_call" | custom-call | tf_op jit(solution)/shard_map/settle/pallas_call | solution.py:333
  (34 shorter events, 2.4 us)
Async XLA Ops:
  0.6 7.9 %collective-permute-start = (bf16[256,1024]{1,0:T(8,128)(2,1)}, bf16[256,1024]{1,0:T(8,128)(2,1)}, u32[]{:S(2)}, u32[]{:S(2)}) collective-permute-start(bf16[256,1024]{1,0:T(8,128)(2,1)} %own_ref.1), channel_id=1, source_target_pairs={{0,1},{1,0},{2,3},{3,2},{4,5},{5,4},{6,7},{7,6},{8,9},{9,8},{10,11... | collective-permute-start | bytes 1572872 | tf_op jit(solution)/shard_map/ppermute | solution.py:43
  3.3 15.6 %collective-permute-start.1 = (bf16[128,1024]{1,0:T(8,128)(2,1)}, bf16[128,1024]{1,0:T(8,128)(2,1)S(1)}, u32[]{:S(2)}, u32[]{:S(2)}) collective-permute-start(bf16[128,1024]{1,0:T(8,128)(2,1)} %pick.1), channel_id=1, source_target_pairs={{0,8},{2,10},{4,12},{6,14},{8,16},{10,18},{12,20},{14,22},{16,24},... | collective-permute-start | bytes 786440 | tf_op jit(solution)/shard_map/ppermute | solution.py:358
  8.5 10.4 %copy-start.11 = (bf16[128,1024]{1,0:T(8,128)(2,1)S(1)}, bf16[128,1024]{1,0:T(8,128)(2,1)}, u32[]{:S(2)}) copy-start(bf16[128,1024]{1,0:T(8,128)(2,1)} %pick.1) | copy-start | bytes 786436
  8.5 25.0 %copy-start = (bf16[256,1024]{1,0:T(8,128)(2,1)S(1)}, bf16[256,1024]{1,0:T(8,128)(2,1)}, u32[]{:S(2)}) copy-start(bf16[256,1024]{1,0:T(8,128)(2,1)} %refs_2_.3) | copy-start | bytes 1572868
  8.5 25.0 %copy-start.1 = (bf16[256,1024]{1,0:T(8,128)(2,1)S(1)}, bf16[256,1024]{1,0:T(8,128)(2,1)}, u32[]{:S(2)}) copy-start(bf16[256,1024]{1,0:T(8,128)(2,1)} %refs_3_.3) | copy-start | bytes 1572868
  8.5 25.0 %copy-start.2 = (bf16[256,1024]{1,0:T(8,128)(2,1)S(1)}, bf16[256,1024]{1,0:T(8,128)(2,1)}, u32[]{:S(2)}) copy-start(bf16[256,1024]{1,0:T(8,128)(2,1)} %refs_1_.3) | copy-start | bytes 1572868
  8.5 25.0 %copy-start.8 = (s32[2]{0:T(128)S(1)}, s32[2]{0:T(128)}, u32[]{:S(2)}) copy-start(s32[2]{0:T(128)} %pad_add_fusion.place_ref.refs_0_) | copy-start | bytes 28
  8.5 25.0 %copy-start.9 = (s32[4]{0:T(128)S(1)}, s32[4]{0:T(128)}, u32[]{:S(2)}) copy-start(s32[4]{0:T(128)} %refs_1_.2) | copy-start | bytes 52
  19.0 8.5 %collective-permute-start.4 = (bf16[128,1024]{1,0:T(8,128)(2,1)S(1)}, bf16[128,1024]{1,0:T(8,128)(2,1)S(1)}, u32[]{:S(2)}, u32[]{:S(2)}) collective-permute-start(bf16[128,1024]{1,0:T(8,128)(2,1)S(1)} %get-tuple-element.38), channel_id=1, source_target_pairs={{0,4},{2,6},{4,0},{6,2},{8,12},{10,14},{12,8},{14,10},{16,20},{18,... | collective-permute-start | bytes 786440 | tf_op jit(solution)/shard_map/ppermute | solution.py:39
  22.4 7.3 %collective-permute-start.2 = (bf16[128,1024]{1,0:T(8,128)(2,1)S(1)}, bf16[128,1024]{1,0:T(8,128)(2,1)S(1)}, u32[]{:S(2)}, u32[]{:S(2)}) collective-permute-start(bf16[128,1024]{1,0:T(8,128)(2,1)S(1)} %get-tuple-element.39), channel_id=1, source_target_pairs={{0,8},{2,10},{4,12},{6,14},{8,16},{10,18},{12,20},{14,22},{16,24},... | collective-permute-start | bytes 786440 | tf_op jit(solution)/shard_map/ppermute | solution.py:39
  25.9 7.6 %collective-permute-start.3 = (bf16[128,1024]{1,0:T(8,128)(2,1)S(1)}, bf16[128,1024]{1,0:T(8,128)(2,1)S(1)}, u32[]{:S(2)}, u32[]{:S(2)}) collective-permute-start(bf16[128,1024]{1,0:T(8,128)(2,1)S(1)} %get-tuple-element.40), channel_id=1, source_target_pairs={{0,2},{2,4},{4,6},{6,0},{8,10},{10,12},{12,14},{14,8},{16,18},{18,... | collective-permute-start | bytes 786440 | tf_op jit(solution)/shard_map/ppermute | solution.py:39
  33.6 1.0 %copy-start.3 = (bf16[256,1024]{1,0:T(8,128)(2,1)S(1)}, bf16[256,1024]{1,0:T(8,128)(2,1)}, u32[]{:S(2)}) copy-start(bf16[256,1024]{1,0:T(8,128)(2,1)} %get-tuple-element.21.refs_5_.refs_4_) | copy-start | bytes 1572868
  42.0 9.6 %copy-start.7 = (bf16[128,1024]{1,0:T(8,128)(2,1)}, bf16[128,1024]{1,0:T(8,128)(2,1)S(1)}, u32[]{:S(2)}) copy-start(bf16[128,1024]{1,0:T(8,128)(2,1)S(1)} %get-tuple-element.30) | copy-start | bytes 786436
  42.0 15.4 %collective-permute-start.6 = (bf16[128,1024]{1,0:T(8,128)(2,1)}, bf16[128,1024]{1,0:T(8,128)(2,1)}, u32[]{:S(2)}, u32[]{:S(2)}) collective-permute-start(bf16[128,1024]{1,0:T(8,128)(2,1)} %get-tuple-element.32), channel_id=1, source_target_pairs={{8,0},{10,2},{12,4},{14,6},{16,8},{18,10},{20,12},{22,14},{24,16},... | collective-permute-start | bytes 786440 | tf_op jit(solution)/shard_map/ppermute | solution.py:39
  43.3 14.1 %collective-permute-start.7 = (bf16[128,1024]{1,0:T(8,128)(2,1)}, bf16[128,1024]{1,0:T(8,128)(2,1)}, u32[]{:S(2)}, u32[]{:S(2)}) collective-permute-start(bf16[128,1024]{1,0:T(8,128)(2,1)} %get-tuple-element.33), channel_id=1, source_target_pairs={{4,0},{6,2},{0,4},{2,6},{12,8},{14,10},{8,12},{10,14},{20,16},{22,... | collective-permute-start | bytes 786440 | tf_op jit(solution)/shard_map/ppermute | solution.py:39
  46.8 10.7 %collective-permute-start.8 = (bf16[128,1024]{1,0:T(8,128)(2,1)}, bf16[128,1024]{1,0:T(8,128)(2,1)}, u32[]{:S(2)}, u32[]{:S(2)}) collective-permute-start(bf16[128,1024]{1,0:T(8,128)(2,1)} %get-tuple-element.34), channel_id=1, source_target_pairs={{2,0},{4,2},{6,4},{0,6},{10,8},{12,10},{14,12},{8,14},{18,16},{20,... | collective-permute-start | bytes 786440 | tf_op jit(solution)/shard_map/ppermute | solution.py:39
  51.6 1.0 %copy-start.4 = (f32[256,1024]{1,0:T(8,128)}, f32[256,1024]{1,0:T(8,128)S(1)}, u32[]{:S(2)}) copy-start(f32[256,1024]{1,0:T(8,128)S(1)} %get-tuple-element.29.refs_1_) | copy-start | bytes 3145732
  52.6 8.6 %copy-start.6 = (bf16[256,1024]{1,0:T(8,128)(2,1)}, bf16[256,1024]{1,0:T(8,128)(2,1)S(1)}, u32[]{:S(2)}) copy-start(bf16[256,1024]{1,0:T(8,128)(2,1)S(1)} %get-tuple-element.25.own_ref) | copy-start | bytes 1572868
  52.6 8.6 %collective-permute-start.5 = (bf16[256,1024]{1,0:T(8,128)(2,1)S(1)}, bf16[256,1024]{1,0:T(8,128)(2,1)S(1)}, u32[]{:S(2)}, u32[]{:S(2)}) collective-permute-start(bf16[256,1024]{1,0:T(8,128)(2,1)S(1)} %get-tuple-element.25.own_ref), channel_id=1, source_target_pairs={{0,1},{1,0},{2,3},{3,2},{4,5},{5,4},{6,7},{7,6},{8,9},{9,8},{10,11... | collective-permute-start | bytes 1572872 | tf_op jit(solution)/shard_map/ppermute | solution.py:43
  58.8 10.8 %collective-permute-start.9 = (bf16[128,1024]{1,0:T(8,128)(2,1)S(1)}, bf16[128,1024]{1,0:T(8,128)(2,1)S(1)}, u32[]{:S(2)}, u32[]{:S(2)}) collective-permute-start(bf16[128,1024]{1,0:T(8,128)(2,1)S(1)} %add_convert_fusion), channel_id=1, source_target_pairs={{8,0},{10,2},{12,4},{14,6},{16,8},{18,10},{20,12},{22,14},{24,16},... | collective-permute-start | bytes 786440 | tf_op jit(solution)/shard_map/ppermute | solution.py:397
  61.2 8.4 %copy-start.5 = (f32[256,1024]{1,0:T(8,128)S(1)}, f32[256,1024]{1,0:T(8,128)}, u32[]{:S(2)}) copy-start(f32[256,1024]{1,0:T(8,128)} %copy-done.4) | copy-start | bytes 3145732
  61.3 0.8 %copy-start.12 = (bf16[256,1024]{1,0:T(8,128)(2,1)}, bf16[256,1024]{1,0:T(8,128)(2,1)S(1)}, u32[]{:S(2)}) copy-start(bf16[256,1024]{1,0:T(8,128)(2,1)S(1)} %collective-permute-done.5.other_ref) | copy-start | bytes 1572868
  69.7 0.6 copy-start.10

commit v4 on v3

--- a/solution.py
+++ b/solution.py
@@ -84,7 +84,7 @@
     )(keys, values)
 
 
-def grad_attn_kernel(place_ref, own_ref, other_ref, w_hbm, out_ref, flag_ref, held, sems):
+def grad_attn_kernel(place_ref, own_ref, other_ref, w_hbm, out_ref, held, sems):
     pieces, tile, _ = held.shape
     core = place_ref[1]
     copies = []
@@ -92,8 +92,6 @@
         rows = w_hbm.at[pl.ds((core * pieces + i) * tile, tile), :]
         copies.append(pltpu.make_async_copy(rows, held.at[i], sems.at[i]))
         copies[i].start()
-    flag_ref[0] = place_ref[0]
-    flag_ref[1] = core
     own, other = own_ref[...], other_ref[...]
     whole = jnp.concatenate([jnp.where(core == 0, own, other), jnp.where(core == 0, other, own)], 1)
     for i in range(pieces):
@@ -107,11 +105,8 @@
     return pl.pallas_call(
         grad_attn_kernel,
         in_specs=[SMEM_BLOCK, VMEM_BLOCK, VMEM_BLOCK, HBM_BLOCK],
-        out_specs=[VMEM_BLOCK, SMEM_BLOCK],
-        out_shape=[
-            jax.ShapeDtypeStruct((tokens, width), BF16),
-            jax.ShapeDtypeStruct(place.shape, jnp.int32),
-        ],
+        out_specs=VMEM_BLOCK,
+        out_shape=jax.ShapeDtypeStruct((tokens, width), BF16),
         scratch_shapes=[
             pltpu.VMEM((pieces, width // pieces, weight.shape[1]), BF16),
             pltpu.SemaphoreType.DMA((pieces,)),
@@ -124,9 +119,7 @@
     )(place, own, other, weight)
 
 
-def project_kernel(place_ref, own_ref, other_ref, w_hbm, out_ref, flag_ref, held, sems):
-    flag_ref[0] = place_ref[0]
-    flag_ref[1] = place_ref[1]
+def project_kernel(place_ref, own_ref, other_ref, w_hbm, out_ref, held, sems):
     pieces, tile, width = held.shape
     core = place_ref[1]
     columns = pl.ds(pl.multiple_of(core * width, width), width)
@@ -151,11 +144,8 @@
     return pl.pallas_call(
         project_kernel,
         in_specs=[SMEM_BLOCK, VMEM_BLOCK, VMEM_BLOCK, HBM_BLOCK],
-        out_specs=[VMEM_BLOCK, SMEM_BLOCK],
-        out_shape=[
-            jax.ShapeDtypeStruct((tokens, width), BF16),
-            jax.ShapeDtypeStruct(place.shape, jnp.int32),
-        ],
+        out_specs=VMEM_BLOCK,
+        out_shape=jax.ShapeDtypeStruct((tokens, width), BF16),
         scratch_shapes=[
             pltpu.VMEM((pieces, weight.shape[0] // pieces, width), BF16),
             pltpu.SemaphoreType.DMA((pieces,)),
@@ -206,11 +196,7 @@
     rows = tokens // STEP
     scale = 1.0 / math.sqrt(DH)
     first = place_ref[1] == 0
-
-    @pl.when(pl.program_id(0) == 0)
-    def _():
-        bias_ref[...] = mask_bias(place_ref[0], bounds_ref, tokens, levels)
-
+    bias_ref[...] = mask_bias(place_ref[0], bounds_ref, tokens, levels)
     for h in range(q_ref.shape[1] // DH):
         cols = slice(h * DH, (h + 1) * DH)
         q, ga = q_ref[:, cols], ga_ref[:, cols]
@@ -242,16 +228,11 @@
     levels = len(arrived)
     rows = tokens // STEP
     count = tokens + levels * rows
-    step = 2
-    block = pl.BlockSpec((tokens, step * DH), lambda i: (0, i))
-    far_block = pl.BlockSpec((2 * rows, step * DH), lambda i: (0, i))
-    prob_block = pl.BlockSpec((step, count, tokens), lambda i: (i, 0, 0))
     prob = jax.ShapeDtypeStruct((width // DH, count, tokens), BF16)
     return pl.pallas_call(
         functools.partial(scores_kernel, levels),
-        grid=(width // (step * DH),),
-        in_specs=[SMEM_BLOCK, SMEM_BLOCK] + [block] * 4 + [far_block] * levels,
-        out_specs=[prob_block] * 2 + [far_block] * levels,
+        in_specs=[SMEM_BLOCK, SMEM_BLOCK] + [VMEM_BLOCK] * (4 + levels),
+        out_specs=[VMEM_BLOCK] * (2 + levels),
         out_shape=[prob, prob] + [jax.ShapeDtypeStruct((2 * rows, width), BF16)] * levels,
         scratch_shapes=[pltpu.VMEM((count, tokens), F32)],
         compiler_params=params(),
@@ -265,13 +246,11 @@
 def local_kernel(levels, *refs):
     place_ref, q_ref, k_ref, v_ref, ga_ref, w_ref, u_ref = refs[:7]
     arrived_refs = refs[7 : 7 + levels]
-    attn_ref, gq_ref, gk_ref, gv_ref, flag_ref = refs[7 + levels :]
+    attn_ref, gq_ref, gk_ref, gv_ref = refs[7 + levels :]
     tokens = q_ref.shape[0]
     rows = tokens // STEP
     scale = 1.0 / math.sqrt(DH)
     first = place_ref[1] == 0
-    flag_ref[0] = place_ref[0]
-    flag_ref[1] = place_ref[1]
     for h in range(q_ref.shape[1] // DH):
         cols = slice(h * DH, (h + 1) * DH)
         far = sort_arrived(first, [r[:, cols] for r in arrived_refs])
@@ -287,20 +266,14 @@
 def attention_local(place, q, k, v, ga, weights, grad_scores, arrived):
     tokens, width = q.shape
     levels = len(arrived)
-    rows = tokens // STEP
-    count = tokens + levels * rows
-    step = 2
-    block = pl.BlockSpec((tokens, step * DH), lambda i: (0, i))
-    far_block = pl.BlockSpec((2 * rows, step * DH), lambda i: (0, i))
-    prob_block = pl.BlockSpec((step, count, tokens), lambda i: (i, 0, 0))
+    count = weights.shape[1]
     bf = jax.ShapeDtypeStruct((tokens, width), BF16)
     f32 = jax.ShapeDtypeStruct((tokens, width), F32)
     return pl.pallas_call(
         functools.partial(local_kernel, levels),
-        grid=(width // (step * DH),),
-        in_specs=[SMEM_BLOCK] + [block] * 4 + [prob_block] * 2 + [far_block] * levels,
-        out_specs=[block] * 4 + [SMEM_BLOCK],
-        out_shape=[bf, bf, f32, f32, jax.ShapeDtypeStruct(place.shape, jnp.int32)],
+        in_specs=[SMEM_BLOCK] + [VMEM_BLOCK] * (6 + levels),
+        out_specs=[VMEM_BLOCK] * 4,
+        out_shape=[bf, bf, f32, f32],
         compiler_params=params(),
         cost_estimate=pl.CostEstimate(
             flops=6 * tokens * count * width, bytes_accessed=16 * tokens * width, transcendentals=0
@@ -309,36 +282,38 @@
     )(place, q, k, v, ga, weights, grad_scores, *arrived)
 
 
-def settle_kernel(count, *refs):
-    gk_ref, gv_ref = refs[:2]
-    back_refs = refs[2 : 2 + count]
-    out_k_ref, out_v_ref = refs[3 + count :]
+def lends_own(index):
+    return index % 4 != 3, index % 4 < 2
+
+
+def settle_kernel(place_ref, gk_ref, gv_ref, four_ref, one_ref, two_ref, three_ref, *out_refs):
     tokens = gk_ref.shape[0]
     rows = tokens // STEP
+    first = place_ref[1] == 0
+    own1, own2 = lends_own(place_ref[0])
+    back1 = jnp.where(first, two_ref[...], one_ref[...])
+    back2 = jnp.where(first, three_ref[...], two_ref[...])
+    back1 = jnp.where(own1, back1, jnp.zeros_like(back1))
+    back2 = jnp.where(own2, back2, jnp.zeros_like(back2))
+    back = (four_ref[...], back1, back2)
     at = lax.broadcasted_iota(jnp.int32, (tokens, rows), 0)
-    place = (at == lax.broadcasted_iota(jnp.int32, (tokens, rows), 1) * STEP).astype(BF16)
-    place = jnp.concatenate([place] * count, 1)
-    extra_k = nn(place, jnp.concatenate([r[:rows] for r in back_refs], 0))
-    extra_v = nn(place, jnp.concatenate([r[rows:] for r in back_refs], 0))
-    out_k_ref[...] = (gk_ref[...] + extra_k).astype(BF16)
-    out_v_ref[...] = (gv_ref[...] + extra_v).astype(BF16)
-
-
-def settle(gk, gv, back, after):
-    tokens, width = gk.shape
-    out = jax.ShapeDtypeStruct((tokens, width), BF16)
-    cols = 512
-    block = pl.BlockSpec((tokens, cols), lambda i: (0, i))
-    back_block = pl.BlockSpec((back[0].shape[0], cols), lambda i: (0, i))
-    return pl.pallas_call(
-        functools.partial(settle_kernel, len(back)),
-        grid=(width // cols,),
-        in_specs=[block] * 2 + [back_block] * len(back) + [SMEM_BLOCK],
-        out_specs=[block] * 2,
+    spot = (at == lax.broadcasted_iota(jnp.int32, (tokens, rows), 1) * STEP).astype(BF16)
+    spot = jnp.concatenate([spot] * len(back), 1)
+    for i, (near_ref, out_ref) in enumerate(zip((gk_ref, gv_ref), out_refs)):
+        extra = nn(spot, jnp.concatenate([b[i * rows : (i + 1) * rows] for b in back], 0))
+        out_ref[...] = (near_ref[...] + extra).astype(BF16)
+
+
+def settle(place, gk, gv, back4, one, two, three):
+    out = jax.ShapeDtypeStruct(gk.shape, BF16)
+    return pl.pallas_call(
+        settle_kernel,
+        in_specs=[SMEM_BLOCK] + [VMEM_BLOCK] * 6,
+        out_specs=[VMEM_BLOCK] * 2,
         out_shape=[out, out],
         compiler_params=params(),
         name="settle",
-    )(gk, gv, *back, after)
+    )(place, gk, gv, back4, one, two, three)
 
 
 def add(*blocks):
@@ -356,11 +331,11 @@
     other_cot = swap(cotangent)
     picked = pick(keys, values)
     far4 = lax.ppermute(picked, "ctx", hop(4, n))
-    ga, flags = grad_attn(place, cotangent, other_cot, out_weight)
-
-    first = flags[1] == 0
-    lent1 = jnp.where(flags[0] % 4 == 3, far4, picked)
-    lent2 = jnp.where(flags[0] % 4 < 2, picked, far4)
+    ga = grad_attn(place, cotangent, other_cot, out_weight)
+
+    first = lax.axis_index("head") == 0
+    own1, own2 = lends_own(lax.axis_index("ctx"))
+    lent1, lent2 = jnp.where(own1, picked, far4), jnp.where(own2, picked, far4)
     hops, ones, twos = hop(4, n), steps(n), pairs(n)
     two = mixed(jnp.where(first, far4, lent1), (hops, ones))
     three = mixed(jnp.where(first, lent1, lent2), (ones, twos))
@@ -379,26 +354,23 @@
         if i > 0:
             more[i - 1] = add(more[i - 1], back)
         else:
-            two = jnp.where(place[1] == 0, add(two, back), two)
-            four = jnp.where(place[1] == 0, four, add(four, back))
+            two = jnp.where(first, add(two, back), two)
+            four = jnp.where(first, four, add(four, back))
     hops, ones, twos = hop(-4, n), turned(ones), turned(twos)
     two = mixed(two, (hops, ones))
     three = mixed(three, (ones, twos))
     four = mixed(four, (twos, hops))
-    attn, gq, gk, gv, flags = attention_local(
+    attn, gq, gk, gv = attention_local(
         place, queries, keys, values, ga, weights, grad_scores, arrived
     )
-    first = flags[1] == 0
-    own1, own2 = flags[0] % 4 != 3, flags[0] % 4 < 2
     back1, back2 = jnp.where(first, three, two), jnp.where(first, four, three)
     back8 = jnp.where(first, two, four)
     zero = jnp.zeros_like(back1)
     g4 = add(g4, back8, jnp.where(own1, zero, back1), jnp.where(own2, zero, back2))
     back4 = lax.ppermute(g4, "ctx", hop(-4, n))
     other_attn = swap(attn)
-    output, flags = project(place, attn, other_attn, out_weight)
-    back = [back4, jnp.where(own1, back1, zero), jnp.where(own2, back2, zero)]
-    gk, gv = settle(gk, gv, back, flags)
+    output = project(place, attn, other_attn, out_weight)
+    gk, gv = settle(place, gk, gv, back4, two, three, four)
     return output, gq, gk, gv
 
 

time: 73.6 us -> 63.3 us (0.86)
  between operations: 5.84 us -> 0.89 us
  Pallas kernels: 27.3 us -> 23.7 us
  waiting for transfers between devices: 8.72 us -> 10.1 us
  other arithmetic: 3.21 us -> 1.88 us
  starting transfers between devices: 21.8 us -> 20.8 us
    ppermute x1, waiting for transfers between devices: 0.01 us -> 5.74 us  [per_device(): far4 = lax.ppermute(picked, 'ctx', hop(4, n))]
    ppermute x6, waiting for transfers between devices: 6.07 us -> 0.61 us  [mixed(): return lax.ppermute(block, ('ctx', 'head'), route)]
    pallas_call x3, Pallas kernels: 13.9 us -> 10.4 us  [the longest x1 5.4 us: attention_scores(): pl.pallas_call(functools.partial(scores_kernel, levels), in_specs=[SMEM_B...]
    ppermute x2, starting transfers between devices: 2.35 us -> 0.08 us  [swap(): return lax.ppermute(block, 'head', [(0, 1), (1, 0)])]
    slice x2 -> x0, local copies, waits for them, and re-layouts: 2.03 us -> none  [the longest x1 1.4 us: per_device(): lent1 = jnp.where(flags[0] % 4 == 3, far4, picked)]
    unnamed x26 -> x28, local copies, waits for them, and re-layouts: 3.47 us -> 4.77 us
    convert_element_type x1, other arithmetic: 1.41 us -> 0.22 us  [add(): return total.astype(BF16)]
    select_n x1 -> x0, other arithmetic: 1.09 us -> none  [per_device(): back = [back4, jnp.where(own1, back1, zero), jnp.where(own2, back2, zero)]]
  transfers between devices with their start and end apart: 10 -> 10, of which waited for: 3 -> 3; matrix products, arithmetic and copies ran while one was open for 7% -> 3% of each run, Pallas kernels for 25% -> 23%
where the time goes in v4:
time: 63.3 us; the launch traced here: 62 us
  Pallas kernels  23.7 us (37%)
  starting transfers between devices  20.8 us (33%)
  waiting for transfers between devices  10.1 us (16%)
  local copies, waits for them, and re-layouts  4.77 us (8%)
  other arithmetic  1.88 us (3%)
  between operations  0.89 us (1%)
    ppermute x6, starting transfers between devices, mixed(): return lax.ppermute(block, ('ctx', 'head'), route)  14.4 us
    pallas_call x1, Pallas kernels, grad_attn(): pl.pallas_call(grad_attn_kernel, in_specs=[SMEM_BLOCK, VMEM_BLOCK, VMEM_B...  6.16 us
    ppermute x1, waiting for transfers between devices, per_device(): far4 = lax.ppermute(picked, 'ctx', hop(4, n))  5.74 us
    pallas_call x1, Pallas kernels, attention_scores(): pl.pallas_call(functools.partial(scores_kernel, levels), in_specs=[SMEM_B...  5.4 us
    ppermute x1, starting transfers between devices, per_device(): far4 = lax.ppermute(picked, 'ctx', hop(4, n))  4.94 us
    pallas_call x1, Pallas kernels, project(): pl.pallas_call(project_kernel, in_specs=[SMEM_BLOCK, VMEM_BLOCK, VMEM_BLO...  4.94 us
    unnamed x28, local copies, waits for them, and re-layouts  4.77 us
    ppermute x1, waiting for transfers between devices, per_device(): back4 = lax.ppermute(g4, 'ctx', hop(-4, n))  3.71 us
  transfers between devices with their start and end apart: 10, of which 3 were waited for; matrix products, arithmetic and copies ran while one was open for 3% of the time, Pallas kernels for 23%

profile of v4, /device:TPU:0, one launch (start us, length us, event | category | flops | bytes accessed | tf_op | source)
XLA Modules:
  0.0 62.0 jit_solution(13084523548760531385)
XLA Ops:
  0.6 2.2 %pick.1 = bf16[128,1024]{1,0:T(8,128)(2,1)} custom-call(bf16[256,1024]{1,0:T(8,128)(2,1)} %refs_2_.3, bf16[256,1024]{1,0:T(8,128)(2,1)} %refs_3_.3), custom_call_target="tpu_custom_call" | custom-call | tf_op jit(solution)/shard_map/pick/pallas_call | solution.py:77
  2.8 4.9 %collective-permute-start.1 = (bf16[128,1024]{1,0:T(8,128)(2,1)}, bf16[128,1024]{1,0:T(8,128)(2,1)S(1)}, u32[]{:S(2)}, u32[]{:S(2)}) collective-permute-start(bf16[128,1024]{1,0:T(8,128)(2,1)} %pick.1), channel_id=1, source_target_pairs={{0,8},{2,10},{4,12},{6,14},{8,16},{10,18},{12,20},{14,22},{16,24},... | collective-permute-start | bytes 786440 | tf_op jit(solution)/shard_map/ppermute | solution.py:333
  7.9 5.7 %collective-permute-done.1.refs_6_.refs_7_ = bf16[128,1024]{1,0:T(8,128)(2,1)S(1)} collective-permute-done((bf16[128,1024]{1,0:T(8,128)(2,1)}, bf16[128,1024]{1,0:T(8,128)(2,1)S(1)}, u32[]{:S(2)}, u32[]{:S(2)}) %collective-permute-start.1) | collective-permute-done | bytes 262176 | tf_op jit(solution)/shard_map/ppermute | solution.py:333
  13.6 1.0 %broadcast_select_fusion.2 = (bf16[128,1024]{1,0:T(8,128)(2,1)S(1)}, bf16[128,1024]{1,0:T(8,128)(2,1)S(1)}, bf16[128,1024]{1,0:T(8,128)(2,1)S(1)}) fusion(bf16[128,1024]{1,0:T(8,128)(2,1)S(1)} %collective-permute-done.1.refs_6_.refs_7_, pred[]{:T(512)S(6)} %eq.6, bf16[128,1024]{1,0:T(8,128)(2,1)} %pick.1, pred[]{:T(512)S(6)} %lt.12, pred[]{:T(512)S(6)} %ne.12), kind=kLoop, calls=%fused_computation.3 | loop fusion | flops 655360 | bytes 1310723 | tf_op jit(solution)/shard_map/jit(_where)/select_n | solution.py:342
  14.6 4.3 %collective-permute-start.2 = (bf16[128,1024]{1,0:T(8,128)(2,1)S(1)}, bf16[128,1024]{1,0:T(8,128)(2,1)S(1)}, u32[]{:S(2)}, u32[]{:S(2)}) collective-permute-start(bf16[128,1024]{1,0:T(8,128)(2,1)S(1)} %get-tuple-element.29), channel_id=1, source_target_pairs={{0,8},{2,10},{4,12},{6,14},{8,16},{10,18},{12,20},{14,22},{16,24},... | collective-permute-start | bytes 786440 | tf_op jit(solution)/shard_map/ppermute | solution.py:39
  18.9 1.5 %collective-permute-start.3 = (bf16[128,1024]{1,0:T(8,128)(2,1)S(1)}, bf16[128,1024]{1,0:T(8,128)(2,1)S(1)}, u32[]{:S(2)}, u32[]{:S(2)}) collective-permute-start(bf16[128,1024]{1,0:T(8,128)(2,1)S(1)} %get-tuple-element.30), channel_id=1, source_target_pairs={{0,2},{2,4},{4,6},{6,0},{8,10},{10,12},{12,14},{14,8},{16,18},{18,... | collective-permute-start | bytes 786440 | tf_op jit(solution)/shard_map/ppermute | solution.py:39
  20.5 3.4 %collective-permute-start.4 = (bf16[128,1024]{1,0:T(8,128)(2,1)S(1)}, bf16[128,1024]{1,0:T(8,128)(2,1)S(1)}, u32[]{:S(2)}, u32[]{:S(2)}) collective-permute-start(bf16[128,1024]{1,0:T(8,128)(2,1)S(1)} %get-tuple-element.28), channel_id=1, source_target_pairs={{0,4},{2,6},{4,0},{6,2},{8,12},{10,14},{12,8},{14,10},{16,20},{18,... | collective-permute-start | bytes 786440 | tf_op jit(solution)/shard_map/ppermute | solution.py:39
  23.9 0.7 %pad_add_fusion.place_ref.refs_0_ = s32[2]{0:T(128)} fusion(s32[1]{0:T(128)} %bitcast.1, s32[1]{0:T(128)} %bitcast), kind=kLoop, calls=%fused_computation.6 | loop fusion | flops 2 | bytes 16 | tf_op jit(solution)/shard_map/stack | solution.py:329
  24.6 0.8 %copy-done.12 = bf16[256,1024]{1,0:T(8,128)(2,1)} copy-done((bf16[256,1024]{1,0:T(8,128)(2,1)}, bf16[256,1024]{1,0:T(8,128)(2,1)S(1)}, u32[]{:S(2)}) %copy-start.12) | copy-done | bytes 524312
  25.4 6.2 %grad_attn.1.refs_5_.refs_4_ = bf16[256,1024]{1,0:T(8,128)(2,1)} custom-call(s32[2]{0:T(128)} %pad_add_fusion.place_ref.refs_0_, bf16[256,1024]{1,0:T(8,128)(2,1)} %own_ref.1, bf16[256,1024]{1,0:T(8,128)(2,1)} %copy-done.12, bf16[2048,2048]{1,0:T(8,128)(2,1)} %w_hbm.3), custom_call_target="tpu_custom_call" | custom-call | flops 1073741824 | bytes 6291456 | tf_op jit(solution)/shard_map/grad_attn/pallas_call | solution.py:105
  31.7 1.1 %copy-done = bf16[256,1024]{1,0:T(8,128)(2,1)S(1)} copy-done((bf16[256,1024]{1,0:T(8,128)(2,1)S(1)}, bf16[256,1024]{1,0:T(8,128)(2,1)}, u32[]{:S(2)}) %copy-start) | copy-done | bytes 524312
  32.7 5.4 %attention_scores.1 = (bf16[8,512,256]{2,1,0:T(8,128)(2,1)S(1)}, bf16[8,512,256]{2,1,0:T(8,128)(2,1)S(1)}, bf16[128,1024]{1,0:T(8,128)(2,1)S(1)}, bf16[128,1024]...) custom-call(s32[2]{0:T(128)S(1)} %copy-done.9, s32[4]{0:T(128)S(1)} %copy-done.11, ...), custom_call_target="tpu_custom_call" | custom-call | flops 805306368 | bytes 4194304 | tf_op jit(solution)/shard_map/attention_scores/pallas_call | solution.py:232
  38.1 1.3 %collective-permute-start.6 = (bf16[128,1024]{1,0:T(8,128)(2,1)S(1)}, bf16[128,1024]{1,0:T(8,128)(2,1)S(1)}, u32[]{:S(2)}, u32[]{:S(2)}) collective-permute-start(bf16[128,1024]{1,0:T(8,128)(2,1)S(1)} %get-tuple-element.23), channel_id=1, source_target_pairs={{8,0},{10,2},{12,4},{14,6},{16,8},{18,10},{20,12},{22,14},{24,16},... | collective-permute-start | bytes 786440 | tf_op jit(solution)/shard_map/ppermute | solution.py:39
  39.4 2.4 %collective-permute-start.7 = (bf16[128,1024]{1,0:T(8,128)(2,1)S(1)}, bf16[128,1024]{1,0:T(8,128)(2,1)S(1)}, u32[]{:S(2)}, u32[]{:S(2)}) collective-permute-start(bf16[128,1024]{1,0:T(8,128)(2,1)S(1)} %get-tuple-element.24), channel_id=1, source_target_pairs={{4,0},{6,2},{0,4},{2,6},{12,8},{14,10},{8,12},{10,14},{20,16},{22,... | collective-permute-start | bytes 786440 | tf_op jit(solution)/shard_map/ppermute | solution.py:39
  41.9 1.5 %collective-permute-start.8 = (bf16[128,1024]{1,0:T(8,128)(2,1)S(1)}, bf16[128,1024]{1,0:T(8,128)(2,1)S(1)}, u32[]{:S(2)}, u32[]{:S(2)}) collective-permute-start(bf16[128,1024]{1,0:T(8,128)(2,1)S(1)} %get-tuple-element.25), channel_id=1, source_target_pairs={{2,0},{4,2},{6,4},{0,6},{10,8},{12,10},{14,12},{8,14},{18,16},{20,... | collective-permute-start | bytes 786440 | tf_op jit(solution)/shard_map/ppermute | solution.py:39
  43.4 0.9 %copy-done.5 = bf16[128,1024]{1,0:T(8,128)(2,1)S(1)} copy-done((bf16[128,1024]{1,0:T(8,128)(2,1)S(1)}, bf16[128,1024]{1,0:T(8,128)(2,1)}, u32[]{:S(2)}) %copy-start.5) | copy-done | bytes 262168
  44.3 0.9 %copy-done.7 = bf16[128,1024]{1,0:T(8,128)(2,1)S(1)} copy-done((bf16[128,1024]{1,0:T(8,128)(2,1)S(1)}, bf16[128,1024]{1,0:T(8,128)(2,1)}, u32[]{:S(2)}) %copy-start.7) | copy-done | bytes 262168
  45.3 3.1 %attention_local.1 = (bf16[256,1024]{1,0:T(8,128)(2,1)S(1)}, bf16[256,1024]{1,0:T(8,128)(2,1)}, f32[256,1024]{1,0:T(8,128)S(1)}, f32[256,1024]{1,0:T(8,128)S(1)}) custom-call(s32[2]{0:T(128)S(1)} %copy-done.9, bf16[256,1024]{1,0:T(8,128)(2,1)S(1)} %copy-done.3, bf16[256,1024]{1,0:T(8,128)(2,1)S(1)} %copy-done.1, bf16[256,1024]{1,0:T(8,128)(2,1)S(1)} %copy-done.2, ...), custom_call_target="tpu_custom_call" | custom-call | flops 805306368 | bytes 4194304 | tf_op jit(solution)/shard_map/attention_local/pallas_call | solution.py:272
  48.4 0.6 collective-permute-done.6.one_ref
  49.4 1.3 %collective-permute-start.9 = (bf16[128,1024]{1,0:T(8,128)(2,1)S(1)}, bf16[128,1024]{1,0:T(8,128)(2,1)S(1)}, u32[]{:S(2)}, u32[]{:S(2)}) collective-permute-start(bf16[128,1024]{1,0:T(8,128)(2,1)S(1)} %add_convert_fusion), channel_id=1, source_target_pairs={{8,0},{10,2},{12,4},{14,6},{16,8},{18,10},{20,12},{22,14},{24,16},... | collective-permute-start | bytes 786440 | tf_op jit(solution)/shard_map/ppermute | solution.py:370
  50.7 0.8 %copy-done.13 = bf16[256,1024]{1,0:T(8,128)(2,1)} copy-done((bf16[256,1024]{1,0:T(8,128)(2,1)}, bf16[256,1024]{1,0:T(8,128)(2,1)S(1)}, u32[]{:S(2)}) %copy-start.13) | copy-done | bytes 524312
  51.5 4.9 %project.1 = bf16[256,1024]{1,0:T(8,128)(2,1)} custom-call(s32[2]{0:T(128)} %pad_add_fusion.place_ref.refs_0_, bf16[256,1024]{1,0:T(8,128)(2,1)} %copy-done.8, bf16[256,1024]{1,0:T(8,128)(2,1)} %copy-done.13, bf16[2048,2048]{1,0:T(8,128)(2,1)} %w_hbm.3), custom_call_target="tpu_custom_call" | custom-call | flops 1073741824 | bytes 6291456 | tf_op jit(solution)/shard_map/project/pallas_call | solution.py:144
  56.5 3.7 %collective-permute-done.9.four_ref = bf16[128,1024]{1,0:T(8,128)(2,1)S(1)} collective-permute-done((bf16[128,1024]{1,0:T(8,128)(2,1)S(1)}, bf16[128,1024]{1,0:T(8,128)(2,1)S(1)}, u32[]{:S(2)}, u32[]{:S(2)}) %collective-permute-start.9) | collective-permute-done | bytes 262176 | tf_op jit(solution)/shard_map/ppermute | solution.py:370
  60.2 1.9 %settle.1 = (bf16[256,1024]{1,0:T(8,128)(2,1)}, bf16[256,1024]{1,0:T(8,128)(2,1)}) custom-call(s32[2]{0:T(128)S(1)} %copy-done.10, f32[256,1024]{1,0:T(8,128)S(1)} %get-tuple-element.20.gk_ref, f32[256,1024]{1,0:T(8,128)S(1)} %get-tuple-element.21.gv_ref, bf16[128,1024]{1,0:T(8,128)(2,1)S(1)} %collective-permute-done.9.four_ref, ...), custom_call_target="tpu_custom_call" | custom-call | tf_op jit(solution)/shard_map/settle/pallas_call | solution.py:309
  (33 shorter events, 0.6 us)
Async XLA Ops:
  2.8 10.8 %collective-permute-start.1 = (bf16[128,1024]{1,0:T(8,128)(2,1)}, bf16[128,1024]{1,0:T(8,128)(2,1)S(1)}, u32[]{:S(2)}, u32[]{:S(2)}) collective-permute-start(bf16[128,1024]{1,0:T(8,128)(2,1)} %pick.1), channel_id=1, source_target_pairs={{0,8},{2,10},{4,12},{6,14},{8,16},{10,18},{12,20},{14,22},{16,24},... | collective-permute-start | bytes 786440 | tf_op jit(solution)/shard_map/ppermute | solution.py:333
  7.8 16.8 %collective-permute-start = (bf16[256,1024]{1,0:T(8,128)(2,1)}, bf16[256,1024]{1,0:T(8,128)(2,1)S(1)}, u32[]{:S(2)}, u32[]{:S(2)}) collective-permute-start(bf16[256,1024]{1,0:T(8,128)(2,1)} %own_ref.1), channel_id=1, source_target_pairs={{0,1},{1,0},{2,3},{3,2},{4,5},{5,4},{6,7},{7,6},{8,9},{9,8},{10,11... | collective-permute-start | bytes 1572872 | tf_op jit(solution)/shard_map/ppermute | solution.py:43
  14.6 16.9 %collective-permute-start.2 = (bf16[128,1024]{1,0:T(8,128)(2,1)S(1)}, bf16[128,1024]{1,0:T(8,128)(2,1)S(1)}, u32[]{:S(2)}, u32[]{:S(2)}) collective-permute-start(bf16[128,1024]{1,0:T(8,128)(2,1)S(1)} %get-tuple-element.29), channel_id=1, source_target_pairs={{0,8},{2,10},{4,12},{6,14},{8,16},{10,18},{12,20},{14,22},{16,24},... | collective-permute-start | bytes 786440 | tf_op jit(solution)/shard_map/ppermute | solution.py:39
  18.9 12.6 %collective-permute-start.3 = (bf16[128,1024]{1,0:T(8,128)(2,1)S(1)}, bf16[128,1024]{1,0:T(8,128)(2,1)S(1)}, u32[]{:S(2)}, u32[]{:S(2)}) collective-permute-start(bf16[128,1024]{1,0:T(8,128)(2,1)S(1)} %get-tuple-element.30), channel_id=1, source_target_pairs={{0,2},{2,4},{4,6},{6,0},{8,10},{10,12},{12,14},{14,8},{16,18},{18,... | collective-permute-start | bytes 786440 | tf_op jit(solution)/shard_map/ppermute | solution.py:39
  20.5 11.1 %collective-permute-start.4 = (bf16[128,1024]{1,0:T(8,128)(2,1)S(1)}, bf16[128,1024]{1,0:T(8,128)(2,1)S(1)}, u32[]{:S(2)}, u32[]{:S(2)}) collective-permute-start(bf16[128,1024]{1,0:T(8,128)(2,1)S(1)} %get-tuple-element.28), channel_id=1, source_target_pairs={{0,4},{2,6},{4,0},{6,2},{8,12},{10,14},{12,8},{14,10},{16,20},{18,... | collective-permute-start | bytes 786440 | tf_op jit(solution)/shard_map/ppermute | solution.py:39
  24.6 7.0 %copy-start.1 = (bf16[256,1024]{1,0:T(8,128)(2,1)S(1)}, bf16[256,1024]{1,0:T(8,128)(2,1)}, u32[]{:S(2)}) copy-start(bf16[256,1024]{1,0:T(8,128)(2,1)} %refs_2_.3) | copy-start | bytes 1572868
  24.6 7.0 %copy-start.2 = (bf16[256,1024]{1,0:T(8,128)(2,1)S(1)}, bf16[256,1024]{1,0:T(8,128)(2,1)}, u32[]{:S(2)}) copy-start(bf16[256,1024]{1,0:T(8,128)(2,1)} %refs_3_.3) | copy-start | bytes 1572868
  24.6 7.1 %copy-start.3 = (bf16[256,1024]{1,0:T(8,128)(2,1)S(1)}, bf16[256,1024]{1,0:T(8,128)(2,1)}, u32[]{:S(2)}) copy-start(bf16[256,1024]{1,0:T(8,128)(2,1)} %refs_1_.3) | copy-start | bytes 1572868
  24.6 7.1 %copy-start.9 = (s32[2]{0:T(128)S(1)}, s32[2]{0:T(128)}, u32[]{:S(2)}) copy-start(s32[2]{0:T(128)} %pad_add_fusion.place_ref.refs_0_) | copy-start | bytes 28
  24.6 7.1 %copy-start.11 = (s32[4]{0:T(128)S(1)}, s32[4]{0:T(128)}, u32[]{:S(2)}) copy-start(s32[4]{0:T(128)} %refs_1_.2) | copy-start | bytes 52
  24.6 0.8 %copy-start.12 = (bf16[256,1024]{1,0:T(8,128)(2,1)}, bf16[256,1024]{1,0:T(8,128)(2,1)S(1)}, u32[]{:S(2)}) copy-start(bf16[256,1024]{1,0:T(8,128)(2,1)S(1)} %collective-permute-done.other_ref) | copy-start | bytes 1572868
  31.6 11.8 %copy-start.4 = (bf16[128,1024]{1,0:T(8,128)(2,1)}, bf16[128,1024]{1,0:T(8,128)(2,1)S(1)}, u32[]{:S(2)}) copy-start(bf16[128,1024]{1,0:T(8,128)(2,1)S(1)} %collective-permute-done.3.refs_8_.refs_9_) | copy-start | bytes 786436
  31.6 1.1 %copy-start = (bf16[256,1024]{1,0:T(8,128)(2,1)S(1)}, bf16[256,1024]{1,0:T(8,128)(2,1)}, u32[]{:S(2)}) copy-start(bf16[256,1024]{1,0:T(8,128)(2,1)} %grad_attn.1.refs_5_.refs_4_) | copy-start | bytes 1572868
  32.7 10.6 %copy-start.6 = (bf16[128,1024]{1,0:T(8,128)(2,1)}, bf16[128,1024]{1,0:T(8,128)(2,1)S(1)}, u32[]{:S(2)}) copy-start(bf16[128,1024]{1,0:T(8,128)(2,1)S(1)} %collective-permute-done.4.refs_9_.refs_10_) | copy-start | bytes 786436
  38.1 10.8 %collective-permute-start.6 = (bf16[128,1024]{1,0:T(8,128)(2,1)S(1)}, bf16[128,1024]{1,0:T(8,128)(2,1)S(1)}, u32[]{:S(2)}, u32[]{:S(2)}) collective-permute-start(bf16[128,1024]{1,0:T(8,128)(2,1)S(1)} %get-tuple-element.23), channel_id=1, source_target_pairs={{8,0},{10,2},{12,4},{14,6},{16,8},{18,10},{20,12},{22,14},{24,16},... | collective-permute-start | bytes 786440 | tf_op jit(solution)/shard_map/ppermute | solution.py:39
  39.4 9.6 %collective-permute-start.7 = (bf16[128,1024]{1,0:T(8,128)(2,1)S(1)}, bf16[128,1024]{1,0:T(8,128)(2,1)S(1)}, u32[]{:S(2)}, u32[]{:S(2)}) collective-permute-start(bf16[128,1024]{1,0:T(8,128)(2,1)S(1)} %get-tuple-element.24), channel_id=1, source_target_pairs={{4,0},{6,2},{0,4},{2,6},{12,8},{14,10},{8,12},{10,14},{20,16},{22,... | collective-permute-start | bytes 786440 | tf_op jit(solution)/shard_map/ppermute | solution.py:39
  41.9 7.1 %collective-permute-start.8 = (bf16[128,1024]{1,0:T(8,128)(2,1)S(1)}, bf16[128,1024]{1,0:T(8,128)(2,1)S(1)}, u32[]{:S(2)}, u32[]{:S(2)}) collective-permute-start(bf16[128,1024]{1,0:T(8,128)(2,1)S(1)} %get-tuple-element.25), channel_id=1, source_target_pairs={{2,0},{4,2},{6,4},{0,6},{10,8},{12,10},{14,12},{8,14},{18,16},{20,... | collective-permute-start | bytes 786440 | tf_op jit(solution)/shard_map/ppermute | solution.py:39
  43.4 1.0 %copy-start.5 = (bf16[128,1024]{1,0:T(8,128)(2,1)S(1)}, bf16[128,1024]{1,0:T(8,128)(2,1)}, u32[]{:S(2)}) copy-start(bf16[128,1024]{1,0:T(8,128)(2,1)} %copy-done.4) | copy-start | bytes 786436
  44.3 0.9 %copy-start.7 = (bf16[128,1024]{1,0:T(8,128)(2,1)S(1)}, bf16[128,1024]{1,0:T(8,128)(2,1)}, u32[]{:S(2)}) copy-start(bf16[128,1024]{1,0:T(8,128)(2,1)} %copy-done.6) | copy-start | bytes 786436
  48.4 0.8 %copy-start.8 = (bf16[256,1024]{1,0:T(8,128)(2,1)}, bf16[256,1024]{1,0:T(8,128)(2,1)S(1)}, u32[]{:S(2)}) copy-start(bf16[256,1024]{1,0:T(8,128)(2,1)S(1)} %get-tuple-element.18.own_ref) | copy-start | bytes 1572868
  48.4 2.3 %collective-permute-start.5 = (bf16[256,1024]{1,0:T(8,128)(2,1)S(1)}, bf16[256,1024]{1,0:T(8,128)(2,1)S(1)}, u32[]{:S(2)}, u32[]{:S(2)}) collective-permute-start(bf16[256,1024]{1,0:T(8,128)(2,1)S(1)} %get-tuple-element.18.own_ref), channel_id=1, source_target_pairs={{0,1},{1,0},{2,3},{3,2},{4,5},{5,4},{6,7},{7,6},{8,9},{9,8},{10,11... | collective-permute-start | bytes 1572872 | tf_op jit(solution)/shard_map/ppermute | solution.py:43
  49.4 10.8 %copy-start.10 = (s32[2]{0:T(128)S(1)}, s32[2]{0:T(128)}, u32[]{:S(2)}) copy-start(s32[2]{0:T(128)} %pad_add_fusion.place_ref.refs_0_) | copy-start | bytes 28
  49.4 10.8 %collective-permute-start.9 = (bf16[128,1024]{1,0:T(8,128)(2,1)S(1)}, bf16[128,1024]{1,0:T(8,128)(2,1)S(1)}, u32[]{:S(2)}, u32[]{:S(2)}) collective-permute-start(bf16[128,1024]{1,0:T(8,128)(2,1)S(1)} %add_convert_fusion), channel_id=1, source_target_pairs={{8,0},{10,2},{12,4},{14,6},{16,8},{18,10},{20,12},{22,14},{24,16},... | collective-permute-start | bytes 786440 | tf_op jit(solution)/shard_map/ppermute | solution.py:370
  50.7 0.8 %copy-start.13 = (bf16[256,1024]{1,0:T(8,128)(2,1)}, bf16[256,1024]{1,0:T(8,128)(2,1)S(1)}, u32[]{:S(2)}) copy-start(bf16[256,1024]{1,0:T(8,128)(2,1)S(1)} %collective-permute-done.5.other_ref) | copy-start | bytes 1572868

commit v5 on v4

v5 whole, which is shorter than its diff:
```python
import functools
import math

import jax
import jax.numpy as jnp
from jax import lax
from jax.experimental import pallas as pl
from jax.experimental.pallas import tpu as pltpu
from jax.sharding import PartitionSpec as P

DH = 128
STEP = 4
BF16 = jnp.bfloat16
F32 = jnp.float32
HBM_BLOCK = pl.BlockSpec(memory_space=pltpu.HBM)
VMEM_BLOCK = pl.BlockSpec(memory_space=pltpu.VMEM)
SMEM_BLOCK = pl.BlockSpec(memory_space=pltpu.SMEM)


def hop(distance, n):
    return [(i, i + distance) for i in range(n) if 0 <= i + distance < n]


def pairs(n):
    return [(i, i ^ 2) for i in range(n)]


def steps(n):
    return [(i, i - 3 if i % 4 == 3 else i + 1) for i in range(n)]


def turned(route):
    return [(b, a) for a, b in route]


def mixed(block, route_of_core):
    cores = len(route_of_core)
    route = [(a * cores + c, b * cores + c) for c, r in enumerate(route_of_core) for a, b in r]
    return lax.ppermute(block, ("ctx", "head"), route)


def swap(block):
    return lax.ppermute(block, "head", [(0, 1), (1, 0)])


def nt(a, b):
    return lax.dot_general(a, b, (((1,), (1,)), ((), ())), preferred_element_type=F32)


def tn(a, b):
    return lax.dot_general(a, b, (((0,), (0,)), ((), ())), preferred_element_type=F32)


def nn(a, b):
    return jnp.dot(a, b, preferred_element_type=F32)


def params(mib=24):
    return pltpu.CompilerParams(vmem_limit_bytes=int(mib * 1024 * 1024))


def pick_kernel(k_hbm, v_hbm, out_ref, held, sems):
    tokens = k_hbm.shape[0]
    rows = tokens // STEP
    copies = [pltpu.make_async_copy(x, held.at[i], sems.at[i]) for i, x in enumerate((k_hbm, v_hbm))]
    for copy in copies:
        copy.start()
    at = lax.broadcasted_iota(jnp.int32, (rows, tokens), 0) * STEP
    choose = (at == lax.broadcasted_iota(jnp.int32, (rows, tokens), 1)).astype(BF16)
    for i, copy in enumerate(copies):
        copy.wait()
        out_ref[i * rows : (i + 1) * rows] = nn(choose, held[i]).astype(BF16)


def pick(keys, values):
    tokens, width = keys.shape
    return pl.pallas_call(
        pick_kernel,
        in_specs=[HBM_BLOCK, HBM_BLOCK],
        out_shape=jax.ShapeDtypeStruct((2 * tokens // STEP, width), BF16),
        scratch_shapes=[pltpu.VMEM((2, tokens, width), BF16), pltpu.SemaphoreType.DMA((2,))],
        compiler_params=params(63.5),
        name="pick",
    )(keys, values)


def grad_attn_kernel(
    core_ref, own_hbm, other_hbm, picked_ref, w_hbm, out_ref, handed_ref, cot, held, cot_sems, sems
):
    pieces, tile, _ = held.shape
    width = own_hbm.shape[1]
    core = core_ref[0]
    copies = []
    for source, at, i in ((own_hbm, core, 0), (other_hbm, 1 - core, 1)):
        columns = pl.ds(pl.multiple_of(at * width, width), width)
        copies.append(pltpu.make_async_copy(source, cot.at[:, columns], cot_sems.at[i]))
    for i in range(pieces):
        rows = w_hbm.at[pl.ds((core * pieces + i) * tile, tile), :]
        copies.append(pltpu.make_async_copy(rows, held.at[i], sems.at[i]))
    for copy in copies:
        copy.start()
    handed_ref[...] = picked_ref[...]
    copies[0].wait()
    copies[1].wait()
    for i in range(pieces):
        copies[2 + i].wait()
        out_ref[:, i * tile : (i + 1) * tile] = nt(cot[...], held[i]).astype(BF16)


def grad_attn(core, own, other, picked, weight):
    tokens, width = own.shape
    pieces = 4
    return pl.pallas_call(
        grad_attn_kernel,
        in_specs=[SMEM_BLOCK, HBM_BLOCK, HBM_BLOCK, VMEM_BLOCK, HBM_BLOCK],
        out_specs=[VMEM_BLOCK] * 2,
        out_shape=[
            jax.ShapeDtypeStruct((tokens, width), BF16),
            jax.ShapeDtypeStruct(picked.shape, BF16),
        ],
        scratch_shapes=[
            pltpu.VMEM((tokens, weight.shape[1]), BF16),
            pltpu.VMEM((pieces, width // pieces, weight.shape[1]), BF16),
            pltpu.SemaphoreType.DMA((2,)),
            pltpu.SemaphoreType.DMA((pieces,)),
        ],
        compiler_params=params(57),
        cost_estimate=pl.CostEstimate(
            flops=4 * tokens * width * width, bytes_accessed=6 * width * width, transcendentals=0
        ),
        name="grad_attn",
    )(core, own, other, picked, weight)


def project_kernel(core_ref, own_ref, other_ref, w_hbm, out_ref, held, sems):
    pieces, tile, width = held.shape
    core = core_ref[0]
    columns = pl.ds(pl.multiple_of(core * width, width), width)
    copies = []
    for i in range(pieces):
        part = w_hbm.at[pl.ds(i * tile, tile), columns]
        copies.append(pltpu.make_async_copy(part, held.at[i], sems.at[i]))
        copies[i].start()
    own, other = own_ref[...], other_ref[...]
    whole = jnp.concatenate([jnp.where(core == 0, own, other), jnp.where(core == 0, other, own)], 1)
    total = None
    for i in range(pieces):
        copies[i].wait()
        term = nn(whole[:, i * tile : (i + 1) * tile], held[i])
        total = term if total is None else total + term
    out_ref[...] = total.astype(BF16)


def project(core, own, other, weight):
    tokens, width = own.shape
    pieces = 4
    return pl.pallas_call(
        project_kernel,
        in_specs=[SMEM_BLOCK, VMEM_BLOCK, VMEM_BLOCK, HBM_BLOCK],
        out_specs=VMEM_BLOCK,
        out_shape=jax.ShapeDtypeStruct((tokens, width), BF16),
        scratch_shapes=[
            pltpu.VMEM((pieces, weight.shape[0] // pieces, width), BF16),
            pltpu.SemaphoreType.DMA((pieces,)),
        ],
        compiler_params=params(57),
        cost_estimate=pl.CostEstimate(
            flops=4 * tokens * width * width, bytes_accessed=6 * width * width, transcendentals=0
        ),
        name="project",
    )(core, own, other, weight)


def documents(positions, bounds_ref):
    count = jnp.zeros(positions.shape, jnp.int32)
    for i in range(bounds_ref.shape[0]):
        count = count + (bounds_ref[i] <= positions).astype(jnp.int32)
    return count


def mask_bias(me, bounds_ref, tokens, order):
    rows = tokens // STEP
    own = lax.broadcasted_iota(jnp.int32, (1, tokens), 1) + me * tokens
    parts = [lax.broadcasted_iota(jnp.int32, (tokens, 1), 0) + me * tokens]
    for distance in order:
        at = lax.broadcasted_iota(jnp.int32, (rows, 1), 0) * STEP
        parts.append(at + (me - distance) * tokens)
    keys = jnp.concatenate(parts, 0)
    key_doc = jnp.where(keys >= 0, documents(keys, bounds_ref), -1)
    ok = (documents(own, bounds_ref) == key_doc) & (keys <= own)
    return jnp.where(ok, 0.0, -jnp.inf).astype(F32)


def sort_arrived(first, two, three, four, *more):
    return [jnp.where(first, three, two), jnp.where(first, four, three), jnp.where(first, two, four), *more]


def distances(levels):
    return [4, 1, 2] + [2**i for i in range(3, levels)]


SCALE = 1.0 / math.sqrt(DH)
POWER = SCALE * math.log2(math.e)


def near_kernel(
    levels, me_ref, bounds_ref, q_ref, k_ref, v_ref, ga_ref, far4_ref, grown_ref, gp_ref, stat_ref, bias_ref
):
    tokens = q_ref.shape[0]
    rows = tokens // STEP
    near = tokens + rows
    bias_ref[...] = mask_bias(me_ref[0], bounds_ref, tokens, distances(levels))
    for h in range(q_ref.shape[1] // DH):
        cols = slice(h * DH, (h + 1) * DH)
        k = jnp.concatenate([k_ref[:, cols], far4_ref[:rows, cols]], 0)
        v = jnp.concatenate([v_ref[:, cols], far4_ref[rows:, cols]], 0)
        scores = nt(k, q_ref[:, cols]) + bias_ref[:near]
        top = jnp.max(scores, axis=0, keepdims=True)
        grown = jnp.exp2((scores - top) * POWER)
        grad_prob = nt(v, ga_ref[:, cols])
        grown_ref[h] = grown
        gp_ref[h] = grad_prob
        stat_ref[h, 0:1] = top
        stat_ref[h, 1:2] = jnp.sum(grown, axis=0, keepdims=True)
        stat_ref[h, 2:3] = jnp.sum(grown * grad_prob, axis=0, keepdims=True)


def attention_near(me, bounds, q, k, v, ga, far4, levels):
    tokens, width = q.shape
    heads, rows = width // DH, tokens // STEP
    near, count = tokens + rows, tokens + levels * rows
    early = jax.ShapeDtypeStruct((heads, near, tokens), F32)
    return pl.pallas_call(
        functools.partial(near_kernel, levels),
        in_specs=[SMEM_BLOCK, SMEM_BLOCK] + [VMEM_BLOCK] * 5,
        out_specs=[VMEM_BLOCK] * 4,
        out_shape=[
            early,
            early,
            jax.ShapeDtypeStruct((heads, 8, tokens), F32),
            jax.ShapeDtypeStruct((count, tokens), F32),
        ],
        compiler_params=params(),
        cost_estimate=pl.CostEstimate(
            flops=4 * tokens * near * width, bytes_accessed=16 * tokens * width, transcendentals=0
        ),
        name="attention_near",
    )(me, bounds, q, k, v, ga, far4)


def far_kernel(levels, *refs):
    core_ref, q_ref, ga_ref, grown_ref, gp_ref, stat_ref, bias_ref = refs[:7]
    arrived_refs = refs[7 : 6 + levels]
    w_ref, u_ref, use_ref, far_ref = refs[6 + levels : 10 + levels]
    gfar_refs = refs[10 + levels :]
    tokens = q_ref.shape[0]
    rows = tokens // STEP
    near = tokens + rows
    first = core_ref[0] == 0
    for h in range(q_ref.shape[1] // DH):
        cols = slice(h * DH, (h + 1) * DH)
        q, ga = q_ref[:, cols], ga_ref[:, cols]
        far = sort_arrived(first, *[r[:, cols] for r in arrived_refs])
        k = jnp.concatenate([f[:rows] for f in far], 0)
        v = jnp.concatenate([f[rows:] for f in far], 0)
        far_ref[0, :, cols] = k
        far_ref[1, :, cols] = v
        scores = nt(k, q) + bias_ref[near:]
        early_top = stat_ref[h, 0:1]
        top = jnp.maximum(early_top, jnp.max(scores, axis=0, keepdims=True))
        shrink = jnp.exp2((early_top - top) * POWER)
        grown = jnp.exp2((scores - top) * POWER)
        grad_prob = nt(v, ga)
        total = stat_ref[h, 1:2] * shrink + jnp.sum(grown, axis=0, keepdims=True)
        weighted = stat_ref[h, 2:3] * shrink + jnp.sum(grown * grad_prob, axis=0, keepdims=True)
        part = 1.0 / total
        delta = weighted * part
        early_part = shrink * part
        use_ref[h, 0:1] = early_part
        use_ref[h, 1:2] = delta
        prob = jnp.concatenate([grown_ref[h, tokens:] * early_part, grown * part], 0)
        grad_prob = jnp.concatenate([gp_ref[h, tokens:], grad_prob], 0)
        weights = prob.astype(BF16)
        grad_scores = (prob * (grad_prob - delta)).astype(BF16)
        w_ref[h] = weights
        u_ref[h] = grad_scores
        gk = (nn(grad_scores, q) * SCALE).astype(BF16)
        gv = nn(weights, ga).astype(BF16)
        g4, g1, g2, g8, *more = [
            jnp.concatenate([g[i * rows : (i + 1) * rows] for g in (gk, gv)], 0) for i in range(levels)
        ]
        out = [g4, jnp.where(first, g8, g1), jnp.where(first, g1, g2), jnp.where(first, g2, g8)]
        for ref, block in zip(gfar_refs, out + more):
            ref[:, cols] = block


def attention_far(core, q, ga, grown, grad_prob, stats, bias, arrived):
    tokens, width = q.shape
    levels = 1 + len(arrived)
    heads, rows = width // DH, tokens // STEP
    prob = jax.ShapeDtypeStruct((heads, levels * rows, tokens), BF16)
    return pl.pallas_call(
        functools.partial(far_kernel, levels),
        in_specs=[SMEM_BLOCK] + [VMEM_BLOCK] * (6 + len(arrived)),
        out_specs=[VMEM_BLOCK] * (4 + levels),
        out_shape=[
            prob,
            prob,
            jax.ShapeDtypeStruct(stats.shape, F32),
            jax.ShapeDtypeStruct((2, (levels - 1) * rows, width), BF16),
        ]
        + [jax.ShapeDtypeStruct((2 * rows, width), BF16)] * levels,
        compiler_params=params(),
        cost_estimate=pl.CostEstimate(
            flops=8 * tokens * levels * rows * width, bytes_accessed=16 * tokens * width, transcendentals=0
        ),
        name="attention_far",
    )(core, q, ga, grown, grad_prob, stats, bias, *arrived)


def local_kernel(
    q_ref, k_ref, v_ref, ga_ref, far4_ref, far_ref, grown_ref, gp_ref, use_ref, w_ref, u_ref,
    attn_ref, gq_ref, gk_ref, gv_ref,
):
    tokens = q_ref.shape[0]
    rows = tokens // STEP
    for h in range(q_ref.shape[1] // DH):
        cols = slice(h * DH, (h + 1) * DH)
        k = jnp.concatenate([k_ref[:, cols], far4_ref[:rows, cols], far_ref[0, :, cols]], 0)
        v = jnp.concatenate([v_ref[:, cols], far4_ref[rows:, cols], far_ref[1, :, cols]], 0)
        prob = grown_ref[h, :tokens] * use_ref[h, 0:1]
        near_weights = prob.astype(BF16)
        near_scores = (prob * (gp_ref[h, :tokens] - use_ref[h, 1:2])).astype(BF16)
        weights = jnp.concatenate([near_weights, w_ref[h]], 0)
        grad_scores = jnp.concatenate([near_scores, u_ref[h]], 0)
        attn_ref[:, cols] = tn(weights, v).astype(BF16)
        gq_ref[:, cols] = (tn(grad_scores, k) * SCALE).astype(BF16)
        gk_ref[:, cols] = nn(near_scores, q_ref[:, cols]) * SCALE
        gv_ref[:, cols] = nn(near_weights, ga_ref[:, cols])


def attention_local(q, *operands):
    tokens, width = q.shape
    bf = jax.ShapeDtypeStruct((tokens, width), BF16)
    f32 = jax.ShapeDtypeStruct((tokens, width), F32)
    return pl.pallas_call(
        local_kernel,
        in_specs=[VMEM_BLOCK] * (1 + len(operands)),
        out_specs=[VMEM_BLOCK] * 4,
        out_shape=[bf, bf, f32, f32],
        compiler_params=params(),
        cost_estimate=pl.CostEstimate(
            flops=12 * tokens * tokens * width, bytes_accessed=16 * tokens * width, transcendentals=0
        ),
        name="attention_local",
    )(q, *operands)


def lends_own(index):
    return index % 4 != 3, index % 4 < 2


def settle_kernel(me_ref, core_ref, gk_ref, gv_ref, four_ref, one_ref, two_ref, three_ref, *out_refs):
    tokens = gk_ref.shape[0]
    rows = tokens // STEP
    first = core_ref[0] == 0
    own1, own2 = lends_own(me_ref[0])
    back1 = jnp.where(first, two_ref[...], one_ref[...])
    back2 = jnp.where(first, three_ref[...], two_ref[...])
    back1 = jnp.where(own1, back1, jnp.zeros_like(back1))
    back2 = jnp.where(own2, back2, jnp.zeros_like(back2))
    back = (four_ref[...], back1, back2)
    at = lax.broadcasted_iota(jnp.int32, (tokens, rows), 0)
    spot = (at == lax.broadcasted_iota(jnp.int32, (tokens, rows), 1) * STEP).astype(BF16)
    spot = jnp.concatenate([spot] * len(back), 1)
    for i, (near_ref, out_ref) in enumerate(zip((gk_ref, gv_ref), out_refs)):
        extra = nn(spot, jnp.concatenate([b[i * rows : (i + 1) * rows] for b in back], 0))
        out_ref[...] = (near_ref[...] + extra).astype(BF16)


def settle(me, core, gk, gv, back4, one, two, three):
    out = jax.ShapeDtypeStruct(gk.shape, BF16)
    return pl.pallas_call(
        settle_kernel,
        in_specs=[SMEM_BLOCK] * 2 + [VMEM_BLOCK] * 6,
        out_specs=[VMEM_BLOCK] * 2,
        out_shape=[out, out],
        compiler_params=params(),
        name="settle",
    )(me, core, gk, gv, back4, one, two, three)


def add(*blocks):
    total = blocks[0].astype(F32)
    for block in blocks[1:]:
        total = total + block.astype(F32)
    return total.astype(BF16)


def per_device(queries, keys, values, out_weight, cotangent, bounds):
    n = lax.axis_size("ctx")
    levels = n.bit_length() - 1
    me = lax.axis_index("ctx").astype(jnp.int32).reshape(1)
    core = lax.axis_index("head").astype(jnp.int32).reshape(1)

    other_cot = swap(cotangent)
    picked = pick(keys, values)
    far4 = lax.ppermute(picked, "ctx", hop(4, n))
    ga, picked = grad_attn(core, cotangent, other_cot, picked, out_weight)

    first = lax.axis_index("head") == 0
    own1, own2 = lends_own(lax.axis_index("ctx"))
    lent1, lent2 = jnp.where(own1, picked, far4), jnp.where(own2, picked, far4)
    hops, ones, twos = hop(4, n), steps(n), pairs(n)
    two = mixed(jnp.where(first, far4, lent1), (hops, ones))
    three = mixed(jnp.where(first, lent1, lent2), (ones, twos))
    four = mixed(jnp.where(first, lent2, far4), (twos, hops))
    arrived = [two, three, four]
    farther = jnp.where(first, two, four) if levels > 4 else None
    for i in range(4, levels):
        farther = lax.ppermute(farther, "ctx", hop(2 ** (i - 1), n))
        arrived.append(farther)

    grown, grad_prob, stats, bias = attention_near(me, bounds, queries, keys, values, ga, far4, levels)
    weights, grad_scores, use, far, g4, two, three, four, *more = attention_far(
        core, queries, ga, grown, grad_prob, stats, bias, arrived
    )
    for i in reversed(range(len(more))):
        back = lax.ppermute(more[i], "ctx", hop(-(2 ** (i + 3)), n))
        if i > 0:
            more[i - 1] = add(more[i - 1], back)
        else:
            two = jnp.where(first, add(two, back), two)
            four = jnp.where(first, four, add(four, back))
    hops, ones, twos = hop(-4, n), turned(ones), turned(twos)
    two = mixed(two, (hops, ones))
    three = mixed(three, (ones, twos))
    four = mixed(four, (twos, hops))
    attn, gq, gk, gv = attention_local(
        queries, keys, values, ga, far4, far, grown, grad_prob, use, weights, grad_scores
    )
    back1, back2 = jnp.where(first, three, two), jnp.where(first, four, three)
    back8 = jnp.where(first, two, four)
    zero = jnp.zeros_like(back1)
    g4 = add(g4, back8, jnp.where(own1, zero, back1), jnp.where(own2, zero, back2))
    back4 = lax.ppermute(g4, "ctx", hop(-4, n))
    other_attn = swap(attn)
    output = project(core, attn, other_attn, out_weight)
    gk, gv = settle(me, core, gk, gv, back4, two, three, four)
    return output, gq, gk, gv


def solution(mesh):
    shared = P("ctx", "head")
    return jax.shard_map(
        per_device,
        mesh=mesh,
        in_specs=(shared, shared, shared, P(), shared, P()),
        out_specs=(shared,) * 4,
        check_vma=False,
    )
```

time: 63.3 us -> 62 us (0.979)
  the two profiles are of different devices: /device:TPU:0 before, /device:TPU:18 now
where the time goes in v5:
time: 62 us; the launch traced here: 61.6 us
  Pallas kernels  23.1 us (37%)
  starting transfers between devices  23 us (37%)
  waiting for transfers between devices  11.5 us (19%)
  local copies, waits for them, and re-layouts  1.86 us (3%)
  other arithmetic  1.23 us (2%)
  between operations  0.88 us (1%)
    ppermute x6, starting transfers between devices, mixed(): return lax.ppermute(block, ('ctx', 'head'), route)  17.1 us
    ppermute x6, waiting for transfers between devices, mixed(): return lax.ppermute(block, ('ctx', 'head'), route)  9.12 us
    pallas_call x1, Pallas kernels, grad_attn(): pl.pallas_call(grad_attn_kernel, in_specs=[SMEM_BLOCK, HBM_BLOCK, HBM_BLO...  6.95 us
    pallas_call x1, Pallas kernels, project(): pl.pallas_call(project_kernel, in_specs=[SMEM_BLOCK, VMEM_BLOCK, VMEM_BLO...  4.93 us
    ppermute x1, starting transfers between devices, per_device(): far4 = lax.ppermute(picked, 'ctx', hop(4, n))  3.48 us
    pallas_call x1, Pallas kernels, attention_far(): pl.pallas_call(functools.partial(far_kernel, levels), in_specs=[SMEM_BLOC...  3.12 us
    pallas_call x1, Pallas kernels, attention_local(): pl.pallas_call(local_kernel, in_specs=[VMEM_BLOCK] * (1 + len(operands)),...  2.67 us
    ppermute x1, starting transfers between devices, per_device(): back4 = lax.ppermute(g4, 'ctx', hop(-4, n))  2.36 us
  transfers between devices with their start and end apart: 10, of which 4 were waited for; matrix products, arithmetic and copies ran while one was open for 0% of the time, Pallas kernels for 30%

profile of v5, /device:TPU:18, one launch (start us, length us, event | category | flops | bytes accessed | tf_op | source)
XLA Modules:
  0.0 61.6 jit_solution(11573914276006767836)
XLA Ops:
  0.6 0.1 collective-permute-start
  0.7 2.2 %pick.1.picked_ref = bf16[128,1024]{1,0:T(8,128)(2,1)} custom-call(bf16[256,1024]{1,0:T(8,128)(2,1)} %k_ref.3, bf16[256,1024]{1,0:T(8,128)(2,1)} %v_ref.3), custom_call_target="tpu_custom_call" | custom-call | tf_op jit(solution)/shard_map/pick/pallas_call | solution.py:77
  2.9 3.5 %collective-permute-start.1 = (bf16[128,1024]{1,0:T(8,128)(2,1)}, bf16[128,1024]{1,0:T(8,128)(2,1)S(1)}, u32[]{:S(2)}, u32[]{:S(2)}) collective-permute-start(bf16[128,1024]{1,0:T(8,128)(2,1)} %pick.1.picked_ref), channel_id=1, source_target_pairs={{0,8},{2,10},{4,12},{6,14},{8,16},{10,18},{12,20},{14,22},{16,24},... | collective-permute-start | bytes 786440 | tf_op jit(solution)/shard_map/ppermute | solution.py:408
  6.5 7.0 %grad_attn.1 = (bf16[256,1024]{1,0:T(8,128)(2,1)}, bf16[128,1024]{1,0:T(8,128)(2,1)}) custom-call(s32[1]{0:T(128)} %bitcast.core_ref.refs_0_, bf16[256,1024]{1,0:T(8,128)(2,1)} %own_hbm.1, bf16[256,1024]{1,0:T(8,128)(2,1)} %collective-permute-done.other_hbm, bf16[128,1024]{1,0:T(8,128)(2,1)} %pick.1.picked_ref, bf16[2048,2048]{1,0:T(8,128)(2,1)} %w_hbm.3), custom_call_target="tpu_custom_call" | custom-call | flops 1073741824 | bytes 6291456 | tf_op jit(solution)/shard_map/grad_attn/pallas_call | solution.py:113
  13.4 0.3 collective-permute-done.1.far4_ref
  13.7 1.0 %broadcast_select_fusion.2 = (bf16[128,1024]{1,0:T(8,128)(2,1)S(1)}, bf16[128,1024]{1,0:T(8,128)(2,1)S(1)}, bf16[128,1024]{1,0:T(8,128)(2,1)S(1)}) fusion(bf16[128,1024]{1,0:T(8,128)(2,1)S(1)} %collective-permute-done.1.far4_ref, pred[]{:T(512)S(6)} %eq.6, bf16[128,1024]{1,0:T(8,128)(2,1)} %get-tuple-element.29, pred[]{:T(512)S(6)} %lt.12, pred[]{:T(512)S(6)} %ne.12), kind=kLoop, calls=%fused_computation.3 | loop fusion | flops 655360 | bytes 1310723 | tf_op jit(solution)/shard_map/jit(_where)/select_n | solution.py:417
  14.7 3.5 %collective-permute-start.2 = (bf16[128,1024]{1,0:T(8,128)(2,1)S(1)}, bf16[128,1024]{1,0:T(8,128)(2,1)S(1)}, u32[]{:S(2)}, u32[]{:S(2)}) collective-permute-start(bf16[128,1024]{1,0:T(8,128)(2,1)S(1)} %get-tuple-element.45), channel_id=1, source_target_pairs={{0,8},{2,10},{4,12},{6,14},{8,16},{10,18},{12,20},{14,22},{16,24},... | collective-permute-start | bytes 786440 | tf_op jit(solution)/shard_map/ppermute | solution.py:39
  18.2 1.5 %collective-permute-start.3 = (bf16[128,1024]{1,0:T(8,128)(2,1)S(1)}, bf16[128,1024]{1,0:T(8,128)(2,1)S(1)}, u32[]{:S(2)}, u32[]{:S(2)}) collective-permute-start(bf16[128,1024]{1,0:T(8,128)(2,1)S(1)} %get-tuple-element.46), channel_id=1, source_target_pairs={{0,2},{2,4},{4,6},{6,0},{8,10},{10,12},{12,14},{14,8},{16,18},{18,... | collective-permute-start | bytes 786440 | tf_op jit(solution)/shard_map/ppermute | solution.py:39
  19.8 2.4 %collective-permute-start.4 = (bf16[128,1024]{1,0:T(8,128)(2,1)S(1)}, bf16[128,1024]{1,0:T(8,128)(2,1)S(1)}, u32[]{:S(2)}, u32[]{:S(2)}) collective-permute-start(bf16[128,1024]{1,0:T(8,128)(2,1)S(1)} %get-tuple-element.44), channel_id=1, source_target_pairs={{0,4},{2,6},{4,0},{6,2},{8,12},{10,14},{12,8},{14,10},{16,20},{18,... | collective-permute-start | bytes 786440 | tf_op jit(solution)/shard_map/ppermute | solution.py:39
  22.2 1.0 %copy-done.3 = bf16[256,1024]{1,0:T(8,128)(2,1)S(1)} copy-done((bf16[256,1024]{1,0:T(8,128)(2,1)S(1)}, bf16[256,1024]{1,0:T(8,128)(2,1)}, u32[]{:S(2)}) %copy-start.3) | copy-done | bytes 524312
  23.3 2.0 %attention_near.1 = (f32[8,320,256]{2,1,0:T(8,128)S(1)}, f32[8,320,256]{2,1,0:T(8,128)S(1)}, f32[8,8,256]{2,1,0:T(8,128)S(1)}, f32[512,256]{1,0:T(8,128)S(1)}) custom-call(s32[1]{0:T(128)} %bitcast.1.me_ref, s32[4]{0:T(128)S(1)} %copy-done.6, bf16[256,1024]{1,0:T(8,128)(2,1)S(1)} %copy-done.2, bf16[256,1024]{1,0:T(8,128)(2,1)S(1)} %copy-done, ...), custom_call_target="tpu_custom_call" | custom-call | flops 335544320 | bytes 4194304 | tf_op jit(solution)/shard_map/attention_near/pallas_call | solution.py:233
  25.2 2.8 %collective-permute-done.4.refs_9_ = bf16[128,1024]{1,0:T(8,128)(2,1)S(1)} collective-permute-done((bf16[128,1024]{1,0:T(8,128)(2,1)S(1)}, bf16[128,1024]{1,0:T(8,128)(2,1)S(1)}, u32[]{:S(2)}, u32[]{:S(2)}) %collective-permute-start.4) | collective-permute-done | bytes 262176 | tf_op jit(solution)/shard_map/ppermute | solution.py:39
  28.0 3.1 %attention_far.1 = (bf16[8,256,256]{2,1,0:T(8,128)(2,1)S(1)}, bf16[8,256,256]{2,1,0:T(8,128)(2,1)S(1)}, f32[8,8,256]{2,1,0:T(8,128)S(1)}, bf16[2,192,1024]{2,1,0...) custom-call(s32[1]{0:T(128)} %bitcast.core_ref.refs_0_, ...), custom_call_target="tpu_custom_call" | custom-call | flops 536870912 | bytes 4194304 | tf_op jit(solution)/shard_map/attention_far/pallas_call | solution.py:302
  31.1 2.4 %collective-permute-start.6 = (bf16[128,1024]{1,0:T(8,128)(2,1)S(1)}, bf16[128,1024]{1,0:T(8,128)(2,1)S(1)}, u32[]{:S(2)}, u32[]{:S(2)}) collective-permute-start(bf16[128,1024]{1,0:T(8,128)(2,1)S(1)} %get-tuple-element.39), channel_id=1, source_target_pairs={{8,0},{10,2},{12,4},{14,6},{16,8},{18,10},{20,12},{22,14},{24,16},... | collective-permute-start | bytes 786440 | tf_op jit(solution)/shard_map/ppermute | solution.py:39
  33.5 2.4 %collective-permute-start.7 = (bf16[128,1024]{1,0:T(8,128)(2,1)S(1)}, bf16[128,1024]{1,0:T(8,128)(2,1)S(1)}, u32[]{:S(2)}, u32[]{:S(2)}) collective-permute-start(bf16[128,1024]{1,0:T(8,128)(2,1)S(1)} %get-tuple-element.40), channel_id=1, source_target_pairs={{4,0},{6,2},{0,4},{2,6},{12,8},{14,10},{8,12},{10,14},{20,16},{22,... | collective-permute-start | bytes 786440 | tf_op jit(solution)/shard_map/ppermute | solution.py:39
  35.9 4.9 %collective-permute-start.8 = (bf16[128,1024]{1,0:T(8,128)(2,1)S(1)}, bf16[128,1024]{1,0:T(8,128)(2,1)S(1)}, u32[]{:S(2)}, u32[]{:S(2)}) collective-permute-start(bf16[128,1024]{1,0:T(8,128)(2,1)S(1)} %get-tuple-element.41), channel_id=1, source_target_pairs={{2,0},{4,2},{6,4},{0,6},{10,8},{12,10},{14,12},{8,14},{18,16},{20,... | collective-permute-start | bytes 786440 | tf_op jit(solution)/shard_map/ppermute | solution.py:39
  40.8 2.7 %attention_local.1 = (bf16[256,1024]{1,0:T(8,128)(2,1)S(1)}, bf16[256,1024]{1,0:T(8,128)(2,1)}, f32[256,1024]{1,0:T(8,128)S(1)}, f32[256,1024]{1,0:T(8,128)S(1)}) custom-call(bf16[256,1024]{1,0:T(8,128)(2,1)S(1)} %copy-done.2, bf16[256,1024]{1,0:T(8,128)(2,1)S(1)} %copy-done, bf16[256,1024]{1,0:T(8,128)(2,1)S(1)} %copy-done.1, ...), custom_call_target="tpu_custom_call" | custom-call | flops 805306368 | bytes 4194304 | tf_op jit(solution)/shard_map/attention_local/pallas_call | solution.py:346
  43.5 6.3 %collective-permute-done.7.three_ref = bf16[128,1024]{1,0:T(8,128)(2,1)S(1)} collective-permute-done((bf16[128,1024]{1,0:T(8,128)(2,1)S(1)}, bf16[128,1024]{1,0:T(8,128)(2,1)S(1)}, u32[]{:S(2)}, u32[]{:S(2)}) %collective-permute-start.7) | collective-permute-done | bytes 262176 | tf_op jit(solution)/shard_map/ppermute | solution.py:39
  49.8 0.2 add_convert_fusion
  50.0 2.4 %collective-permute-start.9 = (bf16[128,1024]{1,0:T(8,128)(2,1)S(1)}, bf16[128,1024]{1,0:T(8,128)(2,1)S(1)}, u32[]{:S(2)}, u32[]{:S(2)}) collective-permute-start(bf16[128,1024]{1,0:T(8,128)(2,1)S(1)} %add_convert_fusion), channel_id=1, source_target_pairs={{8,0},{10,2},{12,4},{14,6},{16,8},{18,10},{20,12},{22,14},{24,16},... | collective-permute-start | bytes 786440 | tf_op jit(solution)/shard_map/ppermute | solution.py:446
  52.4 0.8 %copy-done.7 = bf16[256,1024]{1,0:T(8,128)(2,1)} copy-done((bf16[256,1024]{1,0:T(8,128)(2,1)}, bf16[256,1024]{1,0:T(8,128)(2,1)S(1)}, u32[]{:S(2)}) %copy-start.7) | copy-done | bytes 524312
  53.2 4.9 %project.1 = bf16[256,1024]{1,0:T(8,128)(2,1)} custom-call(s32[1]{0:T(128)} %bitcast.core_ref.refs_0_, bf16[256,1024]{1,0:T(8,128)(2,1)} %copy-done.5, bf16[256,1024]{1,0:T(8,128)(2,1)} %copy-done.7, bf16[2048,2048]{1,0:T(8,128)(2,1)} %w_hbm.3), custom_call_target="tpu_custom_call" | custom-call | flops 1073741824 | bytes 6291456 | tf_op jit(solution)/shard_map/project/pallas_call | solution.py:157
  58.2 2.1 %collective-permute-done.9.four_ref = bf16[128,1024]{1,0:T(8,128)(2,1)S(1)} collective-permute-done((bf16[128,1024]{1,0:T(8,128)(2,1)S(1)}, bf16[128,1024]{1,0:T(8,128)(2,1)S(1)}, u32[]{:S(2)}, u32[]{:S(2)}) %collective-permute-start.9) | collective-permute-done | bytes 262176 | tf_op jit(solution)/shard_map/ppermute | solution.py:446
  60.3 1.3 %settle.1 = (bf16[256,1024]{1,0:T(8,128)(2,1)}, bf16[256,1024]{1,0:T(8,128)(2,1)}) custom-call(s32[1]{0:T(128)} %bitcast.1.me_ref, s32[1]{0:T(128)} %bitcast.core_ref.refs_0_, f32[256,1024]{1,0:T(8,128)S(1)} %get-tuple-element.36.gk_ref, f32[256,1024]{1,0:T(8,128)S(1)} %get-tuple-element.37.gv_ref, bf16[128,1024]{1,0:T(8,128)(2,1)S(1)} %collective-permute-done.9.four_ref, ...), custom_call_target="tpu_custom_call" | custom-call | tf_op jit(solution)/shard_map/settle/pallas_call | solution.py:383
  (21 shorter events, 0.1 us)
Async XLA Ops:
  0.6 5.8 %collective-permute-start = (bf16[256,1024]{1,0:T(8,128)(2,1)}, bf16[256,1024]{1,0:T(8,128)(2,1)}, u32[]{:S(2)}, u32[]{:S(2)}) collective-permute-start(bf16[256,1024]{1,0:T(8,128)(2,1)} %own_hbm.1), channel_id=1, source_target_pairs={{0,1},{1,0},{2,3},{3,2},{4,5},{5,4},{6,7},{7,6},{8,9},{9,8},{10,11... | collective-permute-start | bytes 1572872 | tf_op jit(solution)/shard_map/ppermute | solution.py:43
  2.9 10.8 %collective-permute-start.1 = (bf16[128,1024]{1,0:T(8,128)(2,1)}, bf16[128,1024]{1,0:T(8,128)(2,1)S(1)}, u32[]{:S(2)}, u32[]{:S(2)}) collective-permute-start(bf16[128,1024]{1,0:T(8,128)(2,1)} %pick.1.picked_ref), channel_id=1, source_target_pairs={{0,8},{2,10},{4,12},{6,14},{8,16},{10,18},{12,20},{14,22},{16,24},... | collective-permute-start | bytes 786440 | tf_op jit(solution)/shard_map/ppermute | solution.py:408
  6.4 15.7 %copy-start = (bf16[256,1024]{1,0:T(8,128)(2,1)S(1)}, bf16[256,1024]{1,0:T(8,128)(2,1)}, u32[]{:S(2)}) copy-start(bf16[256,1024]{1,0:T(8,128)(2,1)} %k_ref.3) | copy-start | bytes 1572868
  6.4 15.7 %copy-start.1 = (bf16[256,1024]{1,0:T(8,128)(2,1)S(1)}, bf16[256,1024]{1,0:T(8,128)(2,1)}, u32[]{:S(2)}) copy-start(bf16[256,1024]{1,0:T(8,128)(2,1)} %v_ref.3) | copy-start | bytes 1572868
  6.5 15.7 %copy-start.2 = (bf16[256,1024]{1,0:T(8,128)(2,1)S(1)}, bf16[256,1024]{1,0:T(8,128)(2,1)}, u32[]{:S(2)}) copy-start(bf16[256,1024]{1,0:T(8,128)(2,1)} %q_ref.3) | copy-start | bytes 1572868
  6.5 15.7 %copy-start.6 = (s32[4]{0:T(128)S(1)}, s32[4]{0:T(128)}, u32[]{:S(2)}) copy-start(s32[4]{0:T(128)} %bounds_ref.1) | copy-start | bytes 52
  14.7 10.5 %collective-permute-start.2 = (bf16[128,1024]{1,0:T(8,128)(2,1)S(1)}, bf16[128,1024]{1,0:T(8,128)(2,1)S(1)}, u32[]{:S(2)}, u32[]{:S(2)}) collective-permute-start(bf16[128,1024]{1,0:T(8,128)(2,1)S(1)} %get-tuple-element.45), channel_id=1, source_target_pairs={{0,8},{2,10},{4,12},{6,14},{8,16},{10,18},{12,20},{14,22},{16,24},... | collective-permute-start | bytes 786440 | tf_op jit(solution)/shard_map/ppermute | solution.py:39
  18.2 7.0 %collective-permute-start.3 = (bf16[128,1024]{1,0:T(8,128)(2,1)S(1)}, bf16[128,1024]{1,0:T(8,128)(2,1)S(1)}, u32[]{:S(2)}, u32[]{:S(2)}) collective-permute-start(bf16[128,1024]{1,0:T(8,128)(2,1)S(1)} %get-tuple-element.46), channel_id=1, source_target_pairs={{0,2},{2,4},{4,6},{6,0},{8,10},{10,12},{12,14},{14,8},{16,18},{18,... | collective-permute-start | bytes 786440 | tf_op jit(solution)/shard_map/ppermute | solution.py:39
  19.8 8.3 %collective-permute-start.4 = (bf16[128,1024]{1,0:T(8,128)(2,1)S(1)}, bf16[128,1024]{1,0:T(8,128)(2,1)S(1)}, u32[]{:S(2)}, u32[]{:S(2)}) collective-permute-start(bf16[128,1024]{1,0:T(8,128)(2,1)S(1)} %get-tuple-element.44), channel_id=1, source_target_pairs={{0,4},{2,6},{4,0},{6,2},{8,12},{10,14},{12,8},{14,10},{16,20},{18,... | collective-permute-start | bytes 786440 | tf_op jit(solution)/shard_map/ppermute | solution.py:39
  22.2 1.0 %copy-start.3 = (bf16[256,1024]{1,0:T(8,128)(2,1)S(1)}, bf16[256,1024]{1,0:T(8,128)(2,1)}, u32[]{:S(2)}) copy-start(bf16[256,1024]{1,0:T(8,128)(2,1)} %get-tuple-element.24.ga_ref.refs_2_) | copy-start | bytes 1572868
  28.0 12.8 %copy-start.4 = (bf16[256,1024]{1,0:T(8,128)(2,1)S(1)}, bf16[256,1024]{1,0:T(8,128)(2,1)}, u32[]{:S(2)}) copy-start(bf16[256,1024]{1,0:T(8,128)(2,1)} %get-tuple-element.24.ga_ref.refs_2_) | copy-start | bytes 1572868
  31.1 12.3 %collective-permute-start.6 = (bf16[128,1024]{1,0:T(8,128)(2,1)S(1)}, bf16[128,1024]{1,0:T(8,128)(2,1)S(1)}, u32[]{:S(2)}, u32[]{:S(2)}) collective-permute-start(bf16[128,1024]{1,0:T(8,128)(2,1)S(1)} %get-tuple-element.39), channel_id=1, source_target_pairs={{8,0},{10,2},{12,4},{14,6},{16,8},{18,10},{20,12},{22,14},{24,16},... | collective-permute-start | bytes 786440 | tf_op jit(solution)/shard_map/ppermute | solution.py:39
  33.5 16.3 %collective-permute-start.7 = (bf16[128,1024]{1,0:T(8,128)(2,1)S(1)}, bf16[128,1024]{1,0:T(8,128)(2,1)S(1)}, u32[]{:S(2)}, u32[]{:S(2)}) collective-permute-start(bf16[128,1024]{1,0:T(8,128)(2,1)S(1)} %get-tuple-element.40), channel_id=1, source_target_pairs={{4,0},{6,2},{0,4},{2,6},{12,8},{14,10},{8,12},{10,14},{20,16},{22,... | collective-permute-start | bytes 786440 | tf_op jit(solution)/shard_map/ppermute | solution.py:39
  35.9 13.9 %collective-permute-start.8 = (bf16[128,1024]{1,0:T(8,128)(2,1)S(1)}, bf16[128,1024]{1,0:T(8,128)(2,1)S(1)}, u32[]{:S(2)}, u32[]{:S(2)}) collective-permute-start(bf16[128,1024]{1,0:T(8,128)(2,1)S(1)} %get-tuple-element.41), channel_id=1, source_target_pairs={{2,0},{4,2},{6,4},{0,6},{10,8},{12,10},{14,12},{8,14},{18,16},{20,... | collective-permute-start | bytes 786440 | tf_op jit(solution)/shard_map/ppermute | solution.py:39
  43.5 8.9 %copy-start.5 = (bf16[256,1024]{1,0:T(8,128)(2,1)}, bf16[256,1024]{1,0:T(8,128)(2,1)S(1)}, u32[]{:S(2)}) copy-start(bf16[256,1024]{1,0:T(8,128)(2,1)S(1)} %get-tuple-element.34.own_ref) | copy-start | bytes 1572868
  43.5 8.9 %collective-permute-start.5 = (bf16[256,1024]{1,0:T(8,128)(2,1)S(1)}, bf16[256,1024]{1,0:T(8,128)(2,1)S(1)}, u32[]{:S(2)}, u32[]{:S(2)}) collective-permute-start(bf16[256,1024]{1,0:T(8,128)(2,1)S(1)} %get-tuple-element.34.own_ref), channel_id=1, source_target_pairs={{0,1},{1,0},{2,3},{3,2},{4,5},{5,4},{6,7},{7,6},{8,9},{9,8},{10,11... | collective-permute-start | bytes 1572872 | tf_op jit(solution)/shard_map/ppermute | solution.py:43
  50.0 10.2 %collective-permute-start.9 = (bf16[128,1024]{1,0:T(8,128)(2,1)S(1)}, bf16[128,1024]{1,0:T(8,128)(2,1)S(1)}, u32[]{:S(2)}, u32[]{:S(2)}) collective-permute-start(bf16[128,1024]{1,0:T(8,128)(2,1)S(1)} %add_convert_fusion), channel_id=1, source_target_pairs={{8,0},{10,2},{12,4},{14,6},{16,8},{18,10},{20,12},{22,14},{24,16},... | collective-permute-start | bytes 786440 | tf_op jit(solution)/shard_map/ppermute | solution.py:446
  52.4 0.8 %copy-start.7 = (bf16[256,1024]{1,0:T(8,128)(2,1)}, bf16[256,1024]{1,0:T(8,128)(2,1)S(1)}, u32[]{:S(2)}) copy-start(bf16[256,1024]{1,0:T(8,128)(2,1)S(1)} %collective-permute-done.5.other_ref) | copy-start | bytes 1572868

commit v6 on v5

--- a/solution.py
+++ b/solution.py
@@ -27,6 +27,10 @@
 
 def steps(n):
     return [(i, i - 3 if i % 4 == 3 else i + 1) for i in range(n)]
+
+
+def neighbours(n):
+    return [(i, i ^ 1) for i in range(n)]
 
 
 def turned(route):
@@ -84,47 +88,29 @@
     )(keys, values)
 
 
-def grad_attn_kernel(
-    core_ref, own_hbm, other_hbm, picked_ref, w_hbm, out_ref, handed_ref, cot, held, cot_sems, sems
-):
-    pieces, tile, _ = held.shape
-    width = own_hbm.shape[1]
+def grad_attn_kernel(core_ref, own_ref, other_ref, picked_ref, w_ref, out_ref, handed_ref):
+    width = own_ref.shape[1]
+    tile = 256
     core = core_ref[0]
-    copies = []
-    for source, at, i in ((own_hbm, core, 0), (other_hbm, 1 - core, 1)):
-        columns = pl.ds(pl.multiple_of(at * width, width), width)
-        copies.append(pltpu.make_async_copy(source, cot.at[:, columns], cot_sems.at[i]))
-    for i in range(pieces):
-        rows = w_hbm.at[pl.ds((core * pieces + i) * tile, tile), :]
-        copies.append(pltpu.make_async_copy(rows, held.at[i], sems.at[i]))
-    for copy in copies:
-        copy.start()
     handed_ref[...] = picked_ref[...]
-    copies[0].wait()
-    copies[1].wait()
-    for i in range(pieces):
-        copies[2 + i].wait()
-        out_ref[:, i * tile : (i + 1) * tile] = nt(cot[...], held[i]).astype(BF16)
+    own, other = own_ref[...], other_ref[...]
+    cot = jnp.concatenate([jnp.where(core == 0, own, other), jnp.where(core == 0, other, own)], 1)
+    for i in range(width // tile):
+        rows = pl.ds(pl.multiple_of(core * width + i * tile, tile), tile)
+        out_ref[:, i * tile : (i + 1) * tile] = nt(cot, w_ref[rows, :]).astype(BF16)
 
 
 def grad_attn(core, own, other, picked, weight):
     tokens, width = own.shape
-    pieces = 4
     return pl.pallas_call(
         grad_attn_kernel,
-        in_specs=[SMEM_BLOCK, HBM_BLOCK, HBM_BLOCK, VMEM_BLOCK, HBM_BLOCK],
+        in_specs=[SMEM_BLOCK] + [VMEM_BLOCK] * 4,
         out_specs=[VMEM_BLOCK] * 2,
         out_shape=[
             jax.ShapeDtypeStruct((tokens, width), BF16),
             jax.ShapeDtypeStruct(picked.shape, BF16),
         ],
-        scratch_shapes=[
-            pltpu.VMEM((tokens, weight.shape[1]), BF16),
-            pltpu.VMEM((pieces, width // pieces, weight.shape[1]), BF16),
-            pltpu.SemaphoreType.DMA((2,)),
-            pltpu.SemaphoreType.DMA((pieces,)),
-        ],
-        compiler_params=params(57),
+        compiler_params=params(),
         cost_estimate=pl.CostEstimate(
             flops=4 * tokens * width * width, bytes_accessed=6 * width * width, transcendentals=0
         ),
@@ -132,38 +118,25 @@
     )(core, own, other, picked, weight)
 
 
-def project_kernel(core_ref, own_ref, other_ref, w_hbm, out_ref, held, sems):
-    pieces, tile, width = held.shape
+def project_kernel(core_ref, own_ref, other_ref, w_ref, out_ref):
+    width = own_ref.shape[1]
+    tile = 256
     core = core_ref[0]
-    columns = pl.ds(pl.multiple_of(core * width, width), width)
-    copies = []
-    for i in range(pieces):
-        part = w_hbm.at[pl.ds(i * tile, tile), columns]
-        copies.append(pltpu.make_async_copy(part, held.at[i], sems.at[i]))
-        copies[i].start()
     own, other = own_ref[...], other_ref[...]
-    whole = jnp.concatenate([jnp.where(core == 0, own, other), jnp.where(core == 0, other, own)], 1)
-    total = None
-    for i in range(pieces):
-        copies[i].wait()
-        term = nn(whole[:, i * tile : (i + 1) * tile], held[i])
-        total = term if total is None else total + term
-    out_ref[...] = total.astype(BF16)
+    heads = jnp.concatenate([jnp.where(core == 0, own, other), jnp.where(core == 0, other, own)], 1)
+    for i in range(width // tile):
+        columns = pl.ds(pl.multiple_of(core * width + i * tile, tile), tile)
+        out_ref[:, i * tile : (i + 1) * tile] = nn(heads, w_ref[:, columns]).astype(BF16)
 
 
 def project(core, own, other, weight):
     tokens, width = own.shape
-    pieces = 4
     return pl.pallas_call(
         project_kernel,
-        in_specs=[SMEM_BLOCK, VMEM_BLOCK, VMEM_BLOCK, HBM_BLOCK],
+        in_specs=[SMEM_BLOCK] + [VMEM_BLOCK] * 3,
         out_specs=VMEM_BLOCK,
         out_shape=jax.ShapeDtypeStruct((tokens, width), BF16),
-        scratch_shapes=[
-            pltpu.VMEM((pieces, weight.shape[0] // pieces, width), BF16),
-            pltpu.SemaphoreType.DMA((pieces,)),
-        ],
-        compiler_params=params(57),
+        compiler_params=params(),
         cost_estimate=pl.CostEstimate(
             flops=4 * tokens * width * width, bytes_accessed=6 * width * width, transcendentals=0
         ),
@@ -192,7 +165,7 @@
 
 
 def sort_arrived(first, two, three, four, *more):
-    return [jnp.where(first, three, two), jnp.where(first, four, three), jnp.where(first, two, four), *more]
+    return [jnp.where(first, three, four), jnp.where(first, four, two), jnp.where(first, two, three), *more]
 
 
 def distances(levels):
@@ -289,7 +262,7 @@
         g4, g1, g2, g8, *more = [
             jnp.concatenate([g[i * rows : (i + 1) * rows] for g in (gk, gv)], 0) for i in range(levels)
         ]
-        out = [g4, jnp.where(first, g8, g1), jnp.where(first, g1, g2), jnp.where(first, g2, g8)]
+        out = [g4, jnp.where(first, g2, g1), jnp.where(first, g1, g8), jnp.where(first, g8, g2)]
         for ref, block in zip(gfar_refs, out + more):
             ref[:, cols] = block
 
@@ -360,16 +333,25 @@
     return index % 4 != 3, index % 4 < 2
 
 
-def settle_kernel(me_ref, core_ref, gk_ref, gv_ref, four_ref, one_ref, two_ref, three_ref, *out_refs):
+def returns_own(index, first):
+    own1, own2 = lends_own(index)
+    rest = jnp.logical_not(first)
+    return (first & own2) | (rest & (index % 2 == 0)), first & own1, rest & own2
+
+
+def returns_lent(index, first):
+    own1, own2 = lends_own(index)
+    rest = jnp.logical_not(first)
+    return first & jnp.logical_not(own2), rest | jnp.logical_not(own1), first | jnp.logical_not(own2)
+
+
+def settle_kernel(me_ref, core_ref, gk_ref, gv_ref, last_ref, one_ref, two_ref, three_ref, *out_refs):
     tokens = gk_ref.shape[0]
     rows = tokens // STEP
-    first = core_ref[0] == 0
-    own1, own2 = lends_own(me_ref[0])
-    back1 = jnp.where(first, two_ref[...], one_ref[...])
-    back2 = jnp.where(first, three_ref[...], two_ref[...])
-    back1 = jnp.where(own1, back1, jnp.zeros_like(back1))
-    back2 = jnp.where(own2, back2, jnp.zeros_like(back2))
-    back = (four_ref[...], back1, back2)
+    back = [last_ref[...]]
+    for ref, own in zip((one_ref, two_ref, three_ref), returns_own(me_ref[0], core_ref[0] == 0)):
+        block = ref[...]
+        back.append(jnp.where(own, block, jnp.zeros_like(block)))
     at = lax.broadcasted_iota(jnp.int32, (tokens, rows), 0)
     spot = (at == lax.broadcasted_iota(jnp.int32, (tokens, rows), 1) * STEP).astype(BF16)
     spot = jnp.concatenate([spot] * len(back), 1)
@@ -378,7 +360,7 @@
         out_ref[...] = (near_ref[...] + extra).astype(BF16)
 
 
-def settle(me, core, gk, gv, back4, one, two, three):
+def settle(me, core, gk, gv, last, one, two, three):
     out = jax.ShapeDtypeStruct(gk.shape, BF16)
     return pl.pallas_call(
         settle_kernel,
@@ -387,7 +369,7 @@
         out_shape=[out, out],
         compiler_params=params(),
         name="settle",
-    )(me, core, gk, gv, back4, one, two, three)
+    )(me, core, gk, gv, last, one, two, three)
 
 
 def add(*blocks):
@@ -408,15 +390,19 @@
     far4 = lax.ppermute(picked, "ctx", hop(4, n))
     ga, picked = grad_attn(core, cotangent, other_cot, picked, out_weight)
 
-    first = lax.axis_index("head") == 0
-    own1, own2 = lends_own(lax.axis_index("ctx"))
+    index, first = lax.axis_index("ctx"), lax.axis_index("head") == 0
+    own1, own2 = lends_own(index)
+    even = index % 2 == 0
     lent1, lent2 = jnp.where(own1, picked, far4), jnp.where(own2, picked, far4)
-    hops, ones, twos = hop(4, n), steps(n), pairs(n)
-    two = mixed(jnp.where(first, far4, lent1), (hops, ones))
-    three = mixed(jnp.where(first, lent1, lent2), (ones, twos))
-    four = mixed(jnp.where(first, lent2, far4), (twos, hops))
+    hops, ones, twos, nexts = hop(4, n), steps(n), pairs(n), neighbours(n)
+    two, three = lax.optimization_barrier(
+        (jnp.where(first, far4, lent2), jnp.where(first, lent1, far4))
+    )
+    two = mixed(two, (hops, twos))
+    three = mixed(three, (ones, hops))
+    four = mixed(jnp.where(first, lent2, jnp.where(even, picked, two)), (twos, nexts))
     arrived = [two, three, four]
-    farther = jnp.where(first, two, four) if levels > 4 else None
+    farther = jnp.where(first, two, three) if levels > 4 else None
     for i in range(4, levels):
         farther = lax.ppermute(farther, "ctx", hop(2 ** (i - 1), n))
         arrived.append(farther)
@@ -430,23 +416,22 @@
         if i > 0:
             more[i - 1] = add(more[i - 1], back)
         else:
-            two = jnp.where(first, add(two, back), two)
-            four = jnp.where(first, four, add(four, back))
+            three = jnp.where(first, three, add(three, back))
+            four = jnp.where(first, add(four, back), four)
     hops, ones, twos = hop(-4, n), turned(ones), turned(twos)
-    two = mixed(two, (hops, ones))
-    three = mixed(three, (ones, twos))
-    four = mixed(four, (twos, hops))
+    one = mixed(two, (twos, nexts))
+    two = mixed(three, (ones, hops))
+    zero = jnp.zeros_like(one)
+    three = mixed(add(four, jnp.where(first | even, zero, one)), (hops, twos))
     attn, gq, gk, gv = attention_local(
         queries, keys, values, ga, far4, far, grown, grad_prob, use, weights, grad_scores
     )
-    back1, back2 = jnp.where(first, three, two), jnp.where(first, four, three)
-    back8 = jnp.where(first, two, four)
-    zero = jnp.zeros_like(back1)
-    g4 = add(g4, back8, jnp.where(own1, zero, back1), jnp.where(own2, zero, back2))
-    back4 = lax.ppermute(g4, "ctx", hop(-4, n))
+    back = (one, two, three)
+    lent = [jnp.where(w, b, zero) for w, b in zip(returns_lent(index, first), back)]
+    last = lax.ppermute(add(g4, *lent), "ctx", hop(-4, n))
     other_attn = swap(attn)
     output = project(core, attn, other_attn, out_weight)
-    gk, gv = settle(me, core, gk, gv, back4, two, three, four)
+    gk, gv = settle(me, core, gk, gv, last, *back)
     return output, gq, gk, gv
 
 

time: 62 us -> 83.6 us (1.35)
  the two profiles are of different devices: /device:TPU:18 before, /device:TPU:0 now
where the time goes in v6:
time: 83.6 us; the launch traced here: 82.6 us
  local copies, waits for them, and re-layouts  30.2 us (36%)
  starting transfers between devices  21.5 us (26%)
  Pallas kernels  18.8 us (22%)
  waiting for transfers between devices  7.38 us (9%)
  other arithmetic  3.88 us (5%)
  between operations  0.85 us (1%)
    unnamed x62, local copies, waits for them, and re-layouts  30.2 us
    ppermute x6, starting transfers between devices, mixed(): return lax.ppermute(block, ('ctx', 'head'), route)  15.1 us
    ppermute x1, starting transfers between devices, per_device(): far4 = lax.ppermute(picked, 'ctx', hop(4, n))  4.51 us
    pallas_call x1, Pallas kernels, attention_far(): pl.pallas_call(functools.partial(far_kernel, levels), in_specs=[SMEM_BLOC...  3.81 us
    ppermute x6, waiting for transfers between devices, mixed(): return lax.ppermute(block, ('ctx', 'head'), route)  3.77 us
    ppermute x1, waiting for transfers between devices, per_device(): last = lax.ppermute(add(g4, *lent), 'ctx', hop(-4, n))  3.6 us
    pallas_call x1, Pallas kernels, project(): pl.pallas_call(project_kernel, in_specs=[SMEM_BLOCK] + [VMEM_BLOCK] * 3,...  3.24 us
    convert_element_type x2, other arithmetic, add(): return total.astype(BF16)  3.05 us
  transfers between devices with their start and end apart: 10, of which 4 were waited for; matrix products, arithmetic and copies ran while one was open for 4% of the time, Pallas kernels for 15%

profile of v6, /device:TPU:0, one launch (start us, length us, event | category | flops | bytes accessed | tf_op | source)
XLA Modules:
  0.0 82.6 jit_solution(15399500907481390209)
XLA Ops:
  1.1 2.2 %pick.1.picked_ref = bf16[128,1024]{1,0:T(8,128)(2,1)} custom-call(bf16[256,1024]{1,0:T(8,128)(2,1)} %k_ref.3, bf16[256,1024]{1,0:T(8,128)(2,1)} %v_ref.3), custom_call_target="tpu_custom_call" | custom-call | tf_op jit(solution)/shard_map/pick/pallas_call | solution.py:81
  3.3 4.5 %collective-permute-start.1 = (bf16[128,1024]{1,0:T(8,128)(2,1)}, bf16[128,1024]{1,0:T(8,128)(2,1)S(1)}, u32[]{:S(2)}, u32[]{:S(2)}) collective-permute-start(bf16[128,1024]{1,0:T(8,128)(2,1)} %pick.1.picked_ref), channel_id=1, source_target_pairs={{0,8},{2,10},{4,12},{6,14},{8,16},{10,18},{12,20},{14,22},{16,24},... | collective-permute-start | bytes 786440 | tf_op jit(solution)/shard_map/ppermute | solution.py:390
  7.9 3.4 %copy-done = bf16[2048,2048]{1,0:T(8,128)(2,1)S(1)} copy-done((bf16[2048,2048]{1,0:T(8,128)(2,1)S(1)}, bf16[2048,2048]{1,0:T(8,128)(2,1)}, u32[]{:S(2)}) %copy-start) | copy-done | bytes 8388632
  13.3 2.4 %grad_attn.1 = (bf16[256,1024]{1,0:T(8,128)(2,1)S(1)}, bf16[128,1024]{1,0:T(8,128)(2,1)S(1)}) custom-call(s32[1]{0:T(128)} %bitcast.core_ref.refs_0_, bf16[256,1024]{1,0:T(8,128)(2,1)S(1)} %copy-done.26, bf16[256,1024]{1,0:T(8,128)(2,1)} %collective-permute-done.other_ref, bf16[128,1024]{1,0:T(8,128)(2,1)S(1)} %copy-done.19, bf16[2048,2048]{1,0:T(8,128)(2,1)S(1)} %copy-done), custom_call_target="tpu_custom_call" | custom-call | flops 1073741824 | bytes 6291456 | tf_op jit(solution)/shard_map/grad_attn/pallas_call | solution.py:105
  17.2 3.5 %collective-permute-start.2 = (bf16[128,1024]{1,0:T(8,128)(2,1)S(1)}, bf16[128,1024]{1,0:T(8,128)(2,1)S(1)}, u32[]{:S(2)}, u32[]{:S(2)}) collective-permute-start(bf16[128,1024]{1,0:T(8,128)(2,1)S(1)} %get-tuple-element.32), channel_id=1, source_target_pairs={{0,8},{2,10},{4,12},{6,14},{8,16},{10,18},{12,20},{14,22},{16,24},... | collective-permute-start | bytes 786440 | tf_op jit(solution)/shard_map/ppermute | solution.py:43
  20.7 3.4 %collective-permute-start.3 = (bf16[128,1024]{1,0:T(8,128)(2,1)}, bf16[128,1024]{1,0:T(8,128)(2,1)S(1)}, u32[]{:S(2)}, u32[]{:S(2)}) collective-permute-start(bf16[128,1024]{1,0:T(8,128)(2,1)} %get-tuple-element.33), channel_id=1, source_target_pairs={{0,2},{2,4},{4,6},{6,0},{8,10},{10,12},{12,14},{14,8},{16,18},{18,... | collective-permute-start | bytes 786440 | tf_op jit(solution)/shard_map/ppermute | solution.py:43
  24.8 2.6 %collective-permute-start.4 = (bf16[128,1024]{1,0:T(8,128)(2,1)S(1)}, bf16[128,1024]{1,0:T(8,128)(2,1)S(1)}, u32[]{:S(2)}, u32[]{:S(2)}) collective-permute-start(bf16[128,1024]{1,0:T(8,128)(2,1)S(1)} %select_select_fusion.1), channel_id=1, source_target_pairs={{0,4},{2,6},{4,0},{6,2},{8,12},{10,14},{12,8},{14,10},{16,20},{18,... | collective-permute-start | bytes 786440 | tf_op jit(solution)/shard_map/ppermute | solution.py:43
  30.5 1.9 %attention_near.1 = (f32[8,320,256]{2,1,0:T(8,128)S(1)}, f32[8,320,256]{2,1,0:T(8,128)S(1)}, f32[8,8,256]{2,1,0:T(8,128)S(1)}, f32[512,256]{1,0:T(8,128)S(1)}) custom-call(s32[1]{0:T(128)} %bitcast.1.me_ref, s32[4]{0:T(128)S(1)} %copy-done.29, bf16[256,1024]{1,0:T(8,128)(2,1)S(1)} %copy-done.7, bf16[256,1024]{1,0:T(8,128)(2,1)S(1)} %copy-done.4, ...), custom_call_target="tpu_custom_call" | custom-call | flops 335544320 | bytes 4194304 | tf_op jit(solution)/shard_map/attention_near/pallas_call | solution.py:206
  35.3 3.8 %attention_far.1 = (bf16[8,256,256]{2,1,0:T(8,128)(2,1)S(1)}, bf16[8,256,256]{2,1,0:T(8,128)(2,1)S(1)}, f32[8,8,256]{2,1,0:T(8,128)S(1)}, bf16[2,192,1024]{2,1,0...) custom-call(s32[1]{0:T(128)} %bitcast.core_ref.refs_0_, ...), custom_call_target="tpu_custom_call" | custom-call | flops 536870912 | bytes 4194304 | tf_op jit(solution)/shard_map/attention_far/pallas_call | solution.py:275
  44.2 2.1 %collective-permute-start.6 = (bf16[128,1024]{1,0:T(8,128)(2,1)}, bf16[128,1024]{1,0:T(8,128)(2,1)}, u32[]{:S(2)}, u32[]{:S(2)}) collective-permute-start(bf16[128,1024]{1,0:T(8,128)(2,1)} %get-tuple-element.43), channel_id=1, source_target_pairs={{4,0},{6,2},{0,4},{2,6},{12,8},{14,10},{8,12},{10,14},{20,16},{22,... | collective-permute-start | bytes 786440 | tf_op jit(solution)/shard_map/ppermute | solution.py:43
  46.3 2.2 %collective-permute-start.7 = (bf16[128,1024]{1,0:T(8,128)(2,1)}, bf16[128,1024]{1,0:T(8,128)(2,1)}, u32[]{:S(2)}, u32[]{:S(2)}) collective-permute-start(bf16[128,1024]{1,0:T(8,128)(2,1)} %copy-done.30), channel_id=1, source_target_pairs={{2,0},{4,2},{6,4},{0,6},{10,8},{12,10},{14,12},{8,14},{18,16},{20,... | collective-permute-start | bytes 786440 | tf_op jit(solution)/shard_map/ppermute | solution.py:43
  48.6 2.4 %collective-permute-done.6.one_ref = bf16[128,1024]{1,0:T(8,128)(2,1)} collective-permute-done((bf16[128,1024]{1,0:T(8,128)(2,1)}, bf16[128,1024]{1,0:T(8,128)(2,1)}, u32[]{:S(2)}, u32[]{:S(2)}) %collective-permute-start.6) | collective-permute-done | bytes 262176 | tf_op jit(solution)/shard_map/ppermute | solution.py:43
  51.0 1.7 %add_convert_fusion.1 = bf16[128,1024]{1,0:T(8,128)(2,1)} fusion(bf16[128,1024]{1,0:T(8,128)(2,1)} %copy-done.28, bf16[128,1024]{1,0:T(8,128)(2,1)} %collective-permute-done.6.one_ref, pred[]{:T(512)S(6)} %or.11), kind=kLoop, calls=%fused_computation.1 | loop fusion | flops 655360 | bytes 786433 | tf_op jit(solution)/shard_map/convert_element_type | solution.py:379
  52.7 1.3 %collective-permute-start.8 = (bf16[128,1024]{1,0:T(8,128)(2,1)}, bf16[128,1024]{1,0:T(8,128)(2,1)}, u32[]{:S(2)}, u32[]{:S(2)}) collective-permute-start(bf16[128,1024]{1,0:T(8,128)(2,1)} %add_convert_fusion.1), channel_id=1, source_target_pairs={{8,0},{10,2},{12,4},{14,6},{16,8},{18,10},{20,12},{22,14},{24,16},... | collective-permute-start | bytes 786440 | tf_op jit(solution)/shard_map/ppermute | solution.py:43
  54.0 1.7 %copy-done.3 = f32[8,320,256]{2,1,0:T(8,128)S(1)} copy-done((f32[8,320,256]{2,1,0:T(8,128)S(1)}, f32[8,320,256]{2,1,0:T(8,128)}, u32[]{:S(2)}) %copy-start.3) | copy-done | bytes 2621464
  58.9 1.2 %copy-done.14 = bf16[8,256,256]{2,1,0:T(8,128)(2,1)S(1)} copy-done((bf16[8,256,256]{2,1,0:T(8,128)(2,1)S(1)}, bf16[8,256,256]{2,1,0:T(8,128)(2,1)}, u32[]{:S(2)}) %copy-start.14) | copy-done | bytes 1048600
  60.1 1.2 %copy-done.16 = bf16[8,256,256]{2,1,0:T(8,128)(2,1)S(1)} copy-done((bf16[8,256,256]{2,1,0:T(8,128)(2,1)S(1)}, bf16[8,256,256]{2,1,0:T(8,128)(2,1)}, u32[]{:S(2)}) %copy-start.16) | copy-done | bytes 1048600
  62.4 2.8 %attention_local.1 = (bf16[256,1024]{1,0:T(8,128)(2,1)}, bf16[256,1024]{1,0:T(8,128)(2,1)}, f32[256,1024]{1,0:T(8,128)S(1)}, f32[256,1024]{1,0:T(8,128)S(1)}) custom-call(bf16[256,1024]{1,0:T(8,128)(2,1)S(1)} %copy-done.9, bf16[256,1024]{1,0:T(8,128)(2,1)S(1)} %copy-done.4, bf16[256,1024]{1,0:T(8,128)(2,1)S(1)} %copy-done.6, ...), custom_call_target="tpu_custom_call" | custom-call | flops 805306368 | bytes 4194304 | tf_op jit(solution)/shard_map/attention_local/pallas_call | solution.py:319
  67.3 1.3 %add_convert_fusion = bf16[128,1024]{1,0:T(8,128)(2,1)S(1)} fusion(bf16[128,1024]{1,0:T(8,128)(2,1)} %copy-done.27, bf16[128,1024]{1,0:T(8,128)(2,1)} %collective-permute-done.8.three_ref, bf16[128,1024]{1,0:T(8,128)(2,1)} %collective-permute-done.7.two_ref, bf16[128,1024]{1,0:T(8,128)(2,1)} %collective-permute-done.6.one_ref, pred[]{:T(512)S(6)} %or.10, ...), kind=kLoop, calls=%fused_computation | loop fusion | flops 1441792 | bytes 1310723 | tf_op jit(solution)/shard_map/convert_element_type | solution.py:379
  68.6 1.3 %collective-permute-start.9 = (bf16[128,1024]{1,0:T(8,128)(2,1)S(1)}, bf16[128,1024]{1,0:T(8,128)(2,1)S(1)}, u32[]{:S(2)}, u32[]{:S(2)}) collective-permute-start(bf16[128,1024]{1,0:T(8,128)(2,1)S(1)} %add_convert_fusion), channel_id=1, source_target_pairs={{8,0},{10,2},{12,4},{14,6},{16,8},{18,10},{20,12},{22,14},{24,16},... | collective-permute-start | bytes 786440 | tf_op jit(solution)/shard_map/ppermute | solution.py:431
  69.9 3.4 %copy-done.1 = bf16[2048,2048]{1,0:T(8,128)(2,1)S(1)} copy-done((bf16[2048,2048]{1,0:T(8,128)(2,1)S(1)}, bf16[2048,2048]{1,0:T(8,128)(2,1)}, u32[]{:S(2)}) %copy-start.1) | copy-done | bytes 8388632
  73.3 3.2 %project.1 = bf16[256,1024]{1,0:T(8,128)(2,1)} custom-call(s32[1]{0:T(128)} %bitcast.core_ref.refs_0_, bf16[256,1024]{1,0:T(8,128)(2,1)} %get-tuple-element.38.own_ref, bf16[256,1024]{1,0:T(8,128)(2,1)S(1)} %collective-permute-done.5.other_ref, bf16[2048,2048]{1,0:T(8,128)(2,1)S(1)} %copy-done.1), custom_call_target="tpu_custom_call" | custom-call | flops 1073741824 | bytes 6291456 | tf_op jit(solution)/shard_map/project/pallas_call | solution.py:134
  76.5 3.6 %collective-permute-done.9.last_ref = bf16[128,1024]{1,0:T(8,128)(2,1)S(1)} collective-permute-done((bf16[128,1024]{1,0:T(8,128)(2,1)S(1)}, bf16[128,1024]{1,0:T(8,128)(2,1)S(1)}, u32[]{:S(2)}, u32[]{:S(2)}) %collective-permute-start.9) | collective-permute-done | bytes 262176 | tf_op jit(solution)/shard_map/ppermute | solution.py:431
  80.1 2.4 %settle.1 = (bf16[256,1024]{1,0:T(8,128)(2,1)}, bf16[256,1024]{1,0:T(8,128)(2,1)}) custom-call(s32[1]{0:T(128)} %bitcast.1.me_ref, s32[1]{0:T(128)} %bitcast.core_ref.refs_0_, f32[256,1024]{1,0:T(8,128)S(1)} %copy-done.21, f32[256,1024]{1,0:T(8,128)S(1)} %copy-done.23, bf16[128,1024]{1,0:T(8,128)(2,1)S(1)} %collective-permute-done.9.last_ref, ...), custom_call_target="tpu_custom_call" | custom-call | tf_op jit(solution)/shard_map/settle/pallas_call | solution.py:365
  (69 shorter events, 22.0 us)
Async XLA Ops:
  0.6 7.2 %collective-permute-start = (bf16[256,1024]{1,0:T(8,128)(2,1)}, bf16[256,1024]{1,0:T(8,128)(2,1)}, u32[]{:S(2)}, u32[]{:S(2)}) collective-permute-start(bf16[256,1024]{1,0:T(8,128)(2,1)} %own_ref.1), channel_id=1, source_target_pairs={{0,1},{1,0},{2,3},{3,2},{4,5},{5,4},{6,7},{7,6},{8,9},{9,8},{10,11... | collective-permute-start | bytes 1572872 | tf_op jit(solution)/shard_map/ppermute | solution.py:47
  3.3 13.1 %collective-permute-start.1 = (bf16[128,1024]{1,0:T(8,128)(2,1)}, bf16[128,1024]{1,0:T(8,128)(2,1)S(1)}, u32[]{:S(2)}, u32[]{:S(2)}) collective-permute-start(bf16[128,1024]{1,0:T(8,128)(2,1)} %pick.1.picked_ref), channel_id=1, source_target_pairs={{0,8},{2,10},{4,12},{6,14},{8,16},{10,18},{12,20},{14,22},{16,24},... | collective-permute-start | bytes 786440 | tf_op jit(solution)/shard_map/ppermute | solution.py:390
  7.9 3.4 %copy-start = (bf16[2048,2048]{1,0:T(8,128)(2,1)S(1)}, bf16[2048,2048]{1,0:T(8,128)(2,1)}, u32[]{:S(2)}) copy-start(bf16[2048,2048]{1,0:T(8,128)(2,1)} %w_ref.3) | copy-start | bytes 25165828
  13.3 14.1 %copy-start.4 = (bf16[256,1024]{1,0:T(8,128)(2,1)S(1)}, bf16[256,1024]{1,0:T(8,128)(2,1)}, u32[]{:S(2)}) copy-start(bf16[256,1024]{1,0:T(8,128)(2,1)} %k_ref.3) | copy-start | bytes 1572868
  13.3 14.1 %copy-start.29 = (s32[4]{0:T(128)S(1)}, s32[4]{0:T(128)}, u32[]{:S(2)}) copy-start(s32[4]{0:T(128)} %bounds_ref.1) | copy-start | bytes 52
  17.2 7.5 %collective-permute-start.2 = (bf16[128,1024]{1,0:T(8,128)(2,1)S(1)}, bf16[128,1024]{1,0:T(8,128)(2,1)S(1)}, u32[]{:S(2)}, u32[]{:S(2)}) collective-permute-start(bf16[128,1024]{1,0:T(8,128)(2,1)S(1)} %get-tuple-element.32), channel_id=1, source_target_pairs={{0,8},{2,10},{4,12},{6,14},{8,16},{10,18},{12,20},{14,22},{16,24},... | collective-permute-start | bytes 786440 | tf_op jit(solution)/shard_map/ppermute | solution.py:43
  20.7 11.7 %collective-permute-start.3 = (bf16[128,1024]{1,0:T(8,128)(2,1)}, bf16[128,1024]{1,0:T(8,128)(2,1)S(1)}, u32[]{:S(2)}, u32[]{:S(2)}) collective-permute-start(bf16[128,1024]{1,0:T(8,128)(2,1)} %get-tuple-element.33), channel_id=1, source_target_pairs={{0,2},{2,4},{4,6},{6,0},{8,10},{10,12},{12,14},{14,8},{16,18},{18,... | collective-permute-start | bytes 786440 | tf_op jit(solution)/shard_map/ppermute | solution.py:43
  24.7 2.7 %copy-start.17 = (bf16[128,1024]{1,0:T(8,128)(2,1)}, bf16[128,1024]{1,0:T(8,128)(2,1)S(1)}, u32[]{:S(2)}) copy-start(bf16[128,1024]{1,0:T(8,128)(2,1)S(1)} %collective-permute-done.2.refs_7_) | copy-start | bytes 786436
  24.8 8.5 %collective-permute-start.4 = (bf16[128,1024]{1,0:T(8,128)(2,1)S(1)}, bf16[128,1024]{1,0:T(8,128)(2,1)S(1)}, u32[]{:S(2)}, u32[]{:S(2)}) collective-permute-start(bf16[128,1024]{1,0:T(8,128)(2,1)S(1)} %select_select_fusion.1), channel_id=1, source_target_pairs={{0,4},{2,6},{4,0},{6,2},{8,12},{10,14},{12,8},{14,10},{16,20},{18,... | collective-permute-start | bytes 786440 | tf_op jit(solution)/shard_map/ppermute | solution.py:43
  27.4 1.0 %copy-start.5 = (bf16[256,1024]{1,0:T(8,128)(2,1)S(1)}, bf16[256,1024]{1,0:T(8,128)(2,1)}, u32[]{:S(2)}) copy-start(bf16[256,1024]{1,0:T(8,128)(2,1)} %v_ref.3) | copy-start | bytes 1572868
  32.4 6.7 %copy-start.2 = (f32[8,320,256]{2,1,0:T(8,128)}, f32[8,320,256]{2,1,0:T(8,128)S(1)}, u32[]{:S(2)}) copy-start(f32[8,320,256]{2,1,0:T(8,128)S(1)} %get-tuple-element.28.refs_4_.gp_ref) | copy-start | bytes 7864324
  33.3 1.1 %copy-start.8 = (bf16[256,1024]{1,0:T(8,128)(2,1)S(1)}, bf16[256,1024]{1,0:T(8,128)(2,1)}, u32[]{:S(2)}) copy-start(bf16[256,1024]{1,0:T(8,128)(2,1)} %q_ref.3) | copy-start | bytes 1572868
  44.2 6.8 %collective-permute-start.6 = (bf16[128,1024]{1,0:T(8,128)(2,1)}, bf16[128,1024]{1,0:T(8,128)(2,1)}, u32[]{:S(2)}, u32[]{:S(2)}) collective-permute-start(bf16[128,1024]{1,0:T(8,128)(2,1)} %get-tuple-element.43), channel_id=1, source_target_pairs={{4,0},{6,2},{0,4},{2,6},{12,8},{14,10},{8,12},{10,14},{20,16},{22,... | collective-permute-start | bytes 786440 | tf_op jit(solution)/shard_map/ppermute | solution.py:43
  46.3 21.0 %collective-permute-start.7 = (bf16[128,1024]{1,0:T(8,128)(2,1)}, bf16[128,1024]{1,0:T(8,128)(2,1)}, u32[]{:S(2)}, u32[]{:S(2)}) collective-permute-start(bf16[128,1024]{1,0:T(8,128)(2,1)} %copy-done.30), channel_id=1, source_target_pairs={{2,0},{4,2},{6,4},{0,6},{10,8},{12,10},{14,12},{8,14},{18,16},{20,... | collective-permute-start | bytes 786440 | tf_op jit(solution)/shard_map/ppermute | solution.py:43
  52.7 14.6 %collective-permute-start.8 = (bf16[128,1024]{1,0:T(8,128)(2,1)}, bf16[128,1024]{1,0:T(8,128)(2,1)}, u32[]{:S(2)}, u32[]{:S(2)}) collective-permute-start(bf16[128,1024]{1,0:T(8,128)(2,1)} %add_convert_fusion.1), channel_id=1, source_target_pairs={{8,0},{10,2},{12,4},{14,6},{16,8},{18,10},{20,12},{22,14},{24,16},... | collective-permute-start | bytes 786440 | tf_op jit(solution)/shard_map/ppermute | solution.py:43
  54.0 1.7 %copy-start.3 = (f32[8,320,256]{2,1,0:T(8,128)S(1)}, f32[8,320,256]{2,1,0:T(8,128)}, u32[]{:S(2)}) copy-start(f32[8,320,256]{2,1,0:T(8,128)} %copy-done.2) | copy-start | bytes 7864324
  58.9 1.2 %copy-start.14 = (bf16[8,256,256]{2,1,0:T(8,128)(2,1)S(1)}, bf16[8,256,256]{2,1,0:T(8,128)(2,1)}, u32[]{:S(2)}) copy-start(bf16[8,256,256]{2,1,0:T(8,128)(2,1)} %copy-done.13) | copy-start | bytes 3145732
  60.1 1.2 %copy-start.16 = (bf16[8,256,256]{2,1,0:T(8,128)(2,1)S(1)}, bf16[8,256,256]{2,1,0:T(8,128)(2,1)}, u32[]{:S(2)}) copy-start(bf16[8,256,256]{2,1,0:T(8,128)(2,1)} %copy-done.15) | copy-start | bytes 3145732
  61.3 1.1 %copy-start.25 = (bf16[2,192,1024]{2,1,0:T(8,128)(2,1)S(1)}, bf16[2,192,1024]{2,1,0:T(8,128)(2,1)}, u32[]{:S(2)}) copy-start(bf16[2,192,1024]{2,1,0:T(8,128)(2,1)} %copy-done.24) | copy-start | bytes 2359300
  67.3 2.6 %collective-permute-start.5 = (bf16[256,1024]{1,0:T(8,128)(2,1)}, bf16[256,1024]{1,0:T(8,128)(2,1)S(1)}, u32[]{:S(2)}, u32[]{:S(2)}) collective-permute-start(bf16[256,1024]{1,0:T(8,128)(2,1)} %get-tuple-element.38.own_ref), channel_id=1, source_target_pairs={{0,1},{1,0},{2,3},{3,2},{4,5},{5,4},{6,7},{7,6},{8,9},{9,8},{10,11... | collective-permute-start | bytes 1572872 | tf_op jit(solution)/shard_map/ppermute | solution.py:47
  67.3 12.9 %copy-start.21 = (f32[256,1024]{1,0:T(8,128)S(1)}, f32[256,1024]{1,0:T(8,128)}, u32[]{:S(2)}) copy-start(f32[256,1024]{1,0:T(8,128)} %copy-done.20) | copy-start | bytes 3145732
  68.6 11.5 %collective-permute-start.9 = (bf16[128,1024]{1,0:T(8,128)(2,1)S(1)}, bf16[128,1024]{1,0:T(8,128)(2,1)S(1)}, u32[]{:S(2)}, u32[]{:S(2)}) collective-permute-start(bf16[128,1024]{1,0:T(8,128)(2,1)S(1)} %add_convert_fusion), channel_id=1, source_target_pairs={{8,0},{10,2},{12,4},{14,6},{16,8},{18,10},{20,12},{22,14},{24,16},... | collective-permute-start | bytes 786440 | tf_op jit(solution)/shard_map/ppermute | solution.py:431
  69.9 3.4 %copy-start.1 = (bf16[2048,2048]{1,0:T(8,128)(2,1)S(1)}, bf16[2048,2048]{1,0:T(8,128)(2,1)}, u32[]{:S(2)}) copy-start(bf16[2048,2048]{1,0:T(8,128)(2,1)} %w_ref.3) | copy-start | bytes 25165828
  73.3 6.9 %copy-start.23 = (f32[256,1024]{1,0:T(8,128)S(1)}, f32[256,1024]{1,0:T(8,128)}, u32[]{:S(2)}) copy-start(f32[256,1024]{1,0:T(8,128)} %copy-done.22) | copy-start | bytes 3145732
  (17 other events, 15.9 us)

commit v7 on v6

--- a/solution.py
+++ b/solution.py
@@ -88,29 +88,47 @@
     )(keys, values)
 
 
-def grad_attn_kernel(core_ref, own_ref, other_ref, picked_ref, w_ref, out_ref, handed_ref):
-    width = own_ref.shape[1]
-    tile = 256
+def grad_attn_kernel(
+    core_ref, own_hbm, other_hbm, picked_ref, w_hbm, out_ref, handed_ref, cot, held, cot_sems, sems
+):
+    pieces, tile, _ = held.shape
+    width = own_hbm.shape[1]
     core = core_ref[0]
+    copies = []
+    for source, at, i in ((own_hbm, core, 0), (other_hbm, 1 - core, 1)):
+        columns = pl.ds(pl.multiple_of(at * width, width), width)
+        copies.append(pltpu.make_async_copy(source, cot.at[:, columns], cot_sems.at[i]))
+    for i in range(pieces):
+        rows = w_hbm.at[pl.ds((core * pieces + i) * tile, tile), :]
+        copies.append(pltpu.make_async_copy(rows, held.at[i], sems.at[i]))
+    for copy in copies:
+        copy.start()
     handed_ref[...] = picked_ref[...]
-    own, other = own_ref[...], other_ref[...]
-    cot = jnp.concatenate([jnp.where(core == 0, own, other), jnp.where(core == 0, other, own)], 1)
-    for i in range(width // tile):
-        rows = pl.ds(pl.multiple_of(core * width + i * tile, tile), tile)
-        out_ref[:, i * tile : (i + 1) * tile] = nt(cot, w_ref[rows, :]).astype(BF16)
+    copies[0].wait()
+    copies[1].wait()
+    for i in range(pieces):
+        copies[2 + i].wait()
+        out_ref[:, i * tile : (i + 1) * tile] = nt(cot[...], held[i]).astype(BF16)
 
 
 def grad_attn(core, own, other, picked, weight):
     tokens, width = own.shape
+    pieces = 4
     return pl.pallas_call(
         grad_attn_kernel,
-        in_specs=[SMEM_BLOCK] + [VMEM_BLOCK] * 4,
+        in_specs=[SMEM_BLOCK, HBM_BLOCK, HBM_BLOCK, VMEM_BLOCK, HBM_BLOCK],
         out_specs=[VMEM_BLOCK] * 2,
         out_shape=[
             jax.ShapeDtypeStruct((tokens, width), BF16),
             jax.ShapeDtypeStruct(picked.shape, BF16),
         ],
-        compiler_params=params(),
+        scratch_shapes=[
+            pltpu.VMEM((tokens, weight.shape[1]), BF16),
+            pltpu.VMEM((pieces, width // pieces, weight.shape[1]), BF16),
+            pltpu.SemaphoreType.DMA((2,)),
+            pltpu.SemaphoreType.DMA((pieces,)),
+        ],
+        compiler_params=params(57),
         cost_estimate=pl.CostEstimate(
             flops=4 * tokens * width * width, bytes_accessed=6 * width * width, transcendentals=0
         ),
@@ -118,25 +136,38 @@
     )(core, own, other, picked, weight)
 
 
-def project_kernel(core_ref, own_ref, other_ref, w_ref, out_ref):
-    width = own_ref.shape[1]
-    tile = 256
+def project_kernel(core_ref, own_ref, other_ref, w_hbm, out_ref, held, sems):
+    pieces, tile, width = held.shape
     core = core_ref[0]
+    columns = pl.ds(pl.multiple_of(core * width, width), width)
+    copies = []
+    for i in range(pieces):
+        part = w_hbm.at[pl.ds(i * tile, tile), columns]
+        copies.append(pltpu.make_async_copy(part, held.at[i], sems.at[i]))
+        copies[i].start()
     own, other = own_ref[...], other_ref[...]
-    heads = jnp.concatenate([jnp.where(core == 0, own, other), jnp.where(core == 0, other, own)], 1)
-    for i in range(width // tile):
-        columns = pl.ds(pl.multiple_of(core * width + i * tile, tile), tile)
-        out_ref[:, i * tile : (i + 1) * tile] = nn(heads, w_ref[:, columns]).astype(BF16)
+    whole = jnp.concatenate([jnp.where(core == 0, own, other), jnp.where(core == 0, other, own)], 1)
+    total = None
+    for i in range(pieces):
+        copies[i].wait()
+        term = nn(whole[:, i * tile : (i + 1) * tile], held[i])
+        total = term if total is None else total + term
+    out_ref[...] = total.astype(BF16)
 
 
 def project(core, own, other, weight):
     tokens, width = own.shape
+    pieces = 4
     return pl.pallas_call(
         project_kernel,
-        in_specs=[SMEM_BLOCK] + [VMEM_BLOCK] * 3,
+        in_specs=[SMEM_BLOCK, VMEM_BLOCK, VMEM_BLOCK, HBM_BLOCK],
         out_specs=VMEM_BLOCK,
         out_shape=jax.ShapeDtypeStruct((tokens, width), BF16),
-        compiler_params=params(),
+        scratch_shapes=[
+            pltpu.VMEM((pieces, weight.shape[0] // pieces, width), BF16),
+            pltpu.SemaphoreType.DMA((pieces,)),
+        ],
+        compiler_params=params(57),
         cost_estimate=pl.CostEstimate(
             flops=4 * tokens * width * width, bytes_accessed=6 * width * width, transcendentals=0
         ),

time: 83.6 us -> 84.4 us (level)
  local copies, waits for them, and re-layouts: 30.2 us -> 21.7 us
  Pallas kernels: 18.8 us -> 25 us
  other arithmetic: 3.88 us -> 5.76 us
  starting transfers between devices: 21.5 us -> 22.4 us
    unnamed x62 -> x54, local copies, waits for them, and re-layouts: 30.2 us -> 21.7 us
    pallas_call x2, Pallas kernels: 5.63 us -> 11.8 us  [the longest x1 6.9 us: grad_attn(): pl.pallas_call(grad_attn_kernel, in_specs=[SMEM_BLOCK, HBM_BLOCK, HBM_BLO...]
    ppermute x1, waiting for transfers between devices: 3.6 us -> 4.94 us  [per_device(): last = lax.ppermute(add(g4, *lent), 'ctx', hop(-4, n))]
    select_n x1, other arithmetic: 0.06 us -> 1.09 us  [per_device(): jnp.where(first, lent2, jnp.where(even, picked, two))]
    ppermute x6, waiting for transfers between devices: 3.77 us -> 2.76 us  [mixed(): return lax.ppermute(block, ('ctx', 'head'), route)]
    select_n x1, other arithmetic: 0.76 us -> 1.7 us  [per_device(): jnp.where(first, lent1, far4)]
  transfers between devices with their start and end apart: 10 -> 10, of which waited for: 4 -> 3; matrix products, arithmetic and copies ran while one was open for 4% -> 5% of each run, Pallas kernels for 15% -> 23%
where the time goes in v7:
time: 84.4 us; the launch traced here: 83.5 us
  Pallas kernels  25 us (30%)
  starting transfers between devices  22.4 us (27%)
  local copies, waits for them, and re-layouts  21.7 us (26%)
  waiting for transfers between devices  7.7 us (9%)
  other arithmetic  5.76 us (7%)
  between operations  0.89 us (1%)
    unnamed x54, local copies, waits for them, and re-layouts  21.7 us
    ppermute x6, starting transfers between devices, mixed(): return lax.ppermute(block, ('ctx', 'head'), route)  16 us
    pallas_call x1, Pallas kernels, grad_attn(): pl.pallas_call(grad_attn_kernel, in_specs=[SMEM_BLOCK, HBM_BLOCK, HBM_BLO...  6.9 us
    ppermute x1, waiting for transfers between devices, per_device(): last = lax.ppermute(add(g4, *lent), 'ctx', hop(-4, n))  4.94 us
    pallas_call x1, Pallas kernels, project(): pl.pallas_call(project_kernel, in_specs=[SMEM_BLOCK, VMEM_BLOCK, VMEM_BLO...  4.93 us
    ppermute x1, starting transfers between devices, per_device(): far4 = lax.ppermute(picked, 'ctx', hop(4, n))  4.51 us
    pallas_call x1, Pallas kernels, attention_far(): pl.pallas_call(functools.partial(far_kernel, levels), in_specs=[SMEM_BLOC...  3.81 us
    convert_element_type x2, other arithmetic, add(): return total.astype(BF16)  2.97 us
  transfers between devices with their start and end apart: 10, of which 3 were waited for; matrix products, arithmetic and copies ran while one was open for 5% of the time, Pallas kernels for 23%

profile of v7, /device:TPU:0, one launch (start us, length us, event | category | flops | bytes accessed | tf_op | source)
XLA Modules:
  0.0 83.5 jit_solution(16201212338675014115)
XLA Ops:
  1.1 2.2 %pick.1.picked_ref = bf16[128,1024]{1,0:T(8,128)(2,1)} custom-call(bf16[256,1024]{1,0:T(8,128)(2,1)} %k_ref.3, bf16[256,1024]{1,0:T(8,128)(2,1)} %v_ref.3), custom_call_target="tpu_custom_call" | custom-call | tf_op jit(solution)/shard_map/pick/pallas_call | solution.py:81
  3.3 4.5 %collective-permute-start.1 = (bf16[128,1024]{1,0:T(8,128)(2,1)}, bf16[128,1024]{1,0:T(8,128)(2,1)S(1)}, u32[]{:S(2)}, u32[]{:S(2)}) collective-permute-start(bf16[128,1024]{1,0:T(8,128)(2,1)} %pick.1.picked_ref), channel_id=1, source_target_pairs={{0,8},{2,10},{4,12},{6,14},{8,16},{10,18},{12,20},{14,22},{16,24},... | collective-permute-start | bytes 786440 | tf_op jit(solution)/shard_map/ppermute | solution.py:421
  7.9 6.9 %grad_attn.1 = (bf16[256,1024]{1,0:T(8,128)(2,1)}, bf16[128,1024]{1,0:T(8,128)(2,1)}) custom-call(s32[1]{0:T(128)} %bitcast.core_ref.refs_0_, bf16[256,1024]{1,0:T(8,128)(2,1)} %own_hbm.1, bf16[256,1024]{1,0:T(8,128)(2,1)} %collective-permute-done.other_hbm, bf16[128,1024]{1,0:T(8,128)(2,1)} %pick.1.picked_ref, bf16[2048,2048]{1,0:T(8,128)(2,1)} %w_hbm.3), custom_call_target="tpu_custom_call" | custom-call | flops 1073741824 | bytes 6291456 | tf_op jit(solution)/shard_map/grad_attn/pallas_call | solution.py:117
  14.8 1.7 %select_select_fusion = (bf16[128,1024]{1,0:T(8,128)(2,1)}, bf16[128,1024]{1,0:T(8,128)(2,1)S(1)}) fusion(bf16[128,1024]{1,0:T(8,128)(2,1)S(1)} %collective-permute-done.1.far4_ref, bf16[128,1024]{1,0:T(8,128)(2,1)} %get-tuple-element.31, pred[]{:T(512)S(6)} %ne.21, pred[]{:T(512)S(6)} %eq.12, pred[]{:T(512)S(6)} %lt.21), kind=kLoop, calls=%fused_computation.2 | loop fusion | flops 524288 | bytes 1048579 | tf_op jit(solution)/shard_map/jit(_where)/select_n | solution.py:430
  16.5 3.8 %collective-permute-start.2 = (bf16[128,1024]{1,0:T(8,128)(2,1)S(1)}, bf16[128,1024]{1,0:T(8,128)(2,1)S(1)}, u32[]{:S(2)}, u32[]{:S(2)}) collective-permute-start(bf16[128,1024]{1,0:T(8,128)(2,1)S(1)} %get-tuple-element.32), channel_id=1, source_target_pairs={{0,8},{2,10},{4,12},{6,14},{8,16},{10,18},{12,20},{14,22},{16,24},... | collective-permute-start | bytes 786440 | tf_op jit(solution)/shard_map/ppermute | solution.py:43
  20.4 3.4 %collective-permute-start.3 = (bf16[128,1024]{1,0:T(8,128)(2,1)}, bf16[128,1024]{1,0:T(8,128)(2,1)S(1)}, u32[]{:S(2)}, u32[]{:S(2)}) collective-permute-start(bf16[128,1024]{1,0:T(8,128)(2,1)} %get-tuple-element.33), channel_id=1, source_target_pairs={{0,2},{2,4},{4,6},{6,0},{8,10},{10,12},{12,14},{14,8},{16,18},{18,... | collective-permute-start | bytes 786440 | tf_op jit(solution)/shard_map/ppermute | solution.py:43
  25.8 2.6 %collective-permute-start.4 = (bf16[128,1024]{1,0:T(8,128)(2,1)S(1)}, bf16[128,1024]{1,0:T(8,128)(2,1)S(1)}, u32[]{:S(2)}, u32[]{:S(2)}) collective-permute-start(bf16[128,1024]{1,0:T(8,128)(2,1)S(1)} %select_select_fusion.1), channel_id=1, source_target_pairs={{0,4},{2,6},{4,0},{6,2},{8,12},{10,14},{12,8},{14,10},{16,20},{18,... | collective-permute-start | bytes 786440 | tf_op jit(solution)/shard_map/ppermute | solution.py:43
  31.5 2.0 %attention_near.1 = (f32[8,320,256]{2,1,0:T(8,128)S(1)}, f32[8,320,256]{2,1,0:T(8,128)S(1)}, f32[8,8,256]{2,1,0:T(8,128)S(1)}, f32[512,256]{1,0:T(8,128)S(1)}) custom-call(s32[1]{0:T(128)} %bitcast.1.me_ref, s32[4]{0:T(128)S(1)} %copy-done.24, bf16[256,1024]{1,0:T(8,128)(2,1)S(1)} %copy-done.5, bf16[256,1024]{1,0:T(8,128)(2,1)S(1)} %copy-done.2, ...), custom_call_target="tpu_custom_call" | custom-call | flops 335544320 | bytes 4194304 | tf_op jit(solution)/shard_map/attention_near/pallas_call | solution.py:237
  33.5 1.4 %copy-done.6 = bf16[256,1024]{1,0:T(8,128)(2,1)S(1)} copy-done((bf16[256,1024]{1,0:T(8,128)(2,1)S(1)}, bf16[256,1024]{1,0:T(8,128)(2,1)}, u32[]{:S(2)}) %copy-start.6) | copy-done | bytes 524312
  35.9 3.8 %attention_far.1 = (bf16[8,256,256]{2,1,0:T(8,128)(2,1)S(1)}, bf16[8,256,256]{2,1,0:T(8,128)(2,1)S(1)}, f32[8,8,256]{2,1,0:T(8,128)S(1)}, bf16[2,192,1024]{2,1,0...) custom-call(s32[1]{0:T(128)} %bitcast.core_ref.refs_0_, ...), custom_call_target="tpu_custom_call" | custom-call | flops 536870912 | bytes 4194304 | tf_op jit(solution)/shard_map/attention_far/pallas_call | solution.py:306
  44.7 1.6 %collective-permute-start.6 = (bf16[128,1024]{1,0:T(8,128)(2,1)}, bf16[128,1024]{1,0:T(8,128)(2,1)}, u32[]{:S(2)}, u32[]{:S(2)}) collective-permute-start(bf16[128,1024]{1,0:T(8,128)(2,1)} %get-tuple-element.43), channel_id=1, source_target_pairs={{4,0},{6,2},{0,4},{2,6},{12,8},{14,10},{8,12},{10,14},{20,16},{22,... | collective-permute-start | bytes 786440 | tf_op jit(solution)/shard_map/ppermute | solution.py:43
  46.3 3.2 %collective-permute-start.7 = (bf16[128,1024]{1,0:T(8,128)(2,1)}, bf16[128,1024]{1,0:T(8,128)(2,1)}, u32[]{:S(2)}, u32[]{:S(2)}) collective-permute-start(bf16[128,1024]{1,0:T(8,128)(2,1)} %copy-done.25), channel_id=1, source_target_pairs={{2,0},{4,2},{6,4},{0,6},{10,8},{12,10},{14,12},{8,14},{18,16},{20,... | collective-permute-start | bytes 786440 | tf_op jit(solution)/shard_map/ppermute | solution.py:43
  49.5 1.8 %collective-permute-done.6.one_ref = bf16[128,1024]{1,0:T(8,128)(2,1)} collective-permute-done((bf16[128,1024]{1,0:T(8,128)(2,1)}, bf16[128,1024]{1,0:T(8,128)(2,1)}, u32[]{:S(2)}, u32[]{:S(2)}) %collective-permute-start.6) | collective-permute-done | bytes 262176 | tf_op jit(solution)/shard_map/ppermute | solution.py:43
  51.4 1.7 %add_convert_fusion.1 = bf16[128,1024]{1,0:T(8,128)(2,1)} fusion(bf16[128,1024]{1,0:T(8,128)(2,1)} %copy-done.23, bf16[128,1024]{1,0:T(8,128)(2,1)} %collective-permute-done.6.one_ref, pred[]{:T(512)S(6)} %or.11), kind=kLoop, calls=%fused_computation.1 | loop fusion | flops 655360 | bytes 786433 | tf_op jit(solution)/shard_map/convert_element_type | solution.py:410
  53.1 1.3 %collective-permute-start.8 = (bf16[128,1024]{1,0:T(8,128)(2,1)}, bf16[128,1024]{1,0:T(8,128)(2,1)}, u32[]{:S(2)}, u32[]{:S(2)}) collective-permute-start(bf16[128,1024]{1,0:T(8,128)(2,1)} %add_convert_fusion.1), channel_id=1, source_target_pairs={{8,0},{10,2},{12,4},{14,6},{16,8},{18,10},{20,12},{22,14},{24,16},... | collective-permute-start | bytes 786440 | tf_op jit(solution)/shard_map/ppermute | solution.py:43
  54.4 1.7 %copy-done.1 = f32[8,320,256]{2,1,0:T(8,128)S(1)} copy-done((f32[8,320,256]{2,1,0:T(8,128)S(1)}, f32[8,320,256]{2,1,0:T(8,128)}, u32[]{:S(2)}) %copy-start.1) | copy-done | bytes 2621464
  59.3 1.2 %copy-done.11 = bf16[8,256,256]{2,1,0:T(8,128)(2,1)S(1)} copy-done((bf16[8,256,256]{2,1,0:T(8,128)(2,1)S(1)}, bf16[8,256,256]{2,1,0:T(8,128)(2,1)}, u32[]{:S(2)}) %copy-start.11) | copy-done | bytes 1048600
  60.5 1.2 %copy-done.13 = bf16[8,256,256]{2,1,0:T(8,128)(2,1)S(1)} copy-done((bf16[8,256,256]{2,1,0:T(8,128)(2,1)S(1)}, bf16[8,256,256]{2,1,0:T(8,128)(2,1)}, u32[]{:S(2)}) %copy-start.13) | copy-done | bytes 1048600
  62.9 2.8 %attention_local.1 = (bf16[256,1024]{1,0:T(8,128)(2,1)}, bf16[256,1024]{1,0:T(8,128)(2,1)}, f32[256,1024]{1,0:T(8,128)S(1)}, f32[256,1024]{1,0:T(8,128)S(1)}) custom-call(bf16[256,1024]{1,0:T(8,128)(2,1)S(1)} %copy-done.7, bf16[256,1024]{1,0:T(8,128)(2,1)S(1)} %copy-done.2, bf16[256,1024]{1,0:T(8,128)(2,1)S(1)} %copy-done.4, ...), custom_call_target="tpu_custom_call" | custom-call | flops 805306368 | bytes 4194304 | tf_op jit(solution)/shard_map/attention_local/pallas_call | solution.py:350
  67.7 1.2 %add_convert_fusion = bf16[128,1024]{1,0:T(8,128)(2,1)S(1)} fusion(bf16[128,1024]{1,0:T(8,128)(2,1)} %copy-done.22, bf16[128,1024]{1,0:T(8,128)(2,1)} %collective-permute-done.8.three_ref, bf16[128,1024]{1,0:T(8,128)(2,1)} %collective-permute-done.7.two_ref, bf16[128,1024]{1,0:T(8,128)(2,1)} %collective-permute-done.6.one_ref, pred[]{:T(512)S(6)} %or.10, ...), kind=kLoop, calls=%fused_computation | loop fusion | flops 1441792 | bytes 1310723 | tf_op jit(solution)/shard_map/convert_element_type | solution.py:410
  68.9 1.4 %collective-permute-start.9 = (bf16[128,1024]{1,0:T(8,128)(2,1)S(1)}, bf16[128,1024]{1,0:T(8,128)(2,1)S(1)}, u32[]{:S(2)}, u32[]{:S(2)}) collective-permute-start(bf16[128,1024]{1,0:T(8,128)(2,1)S(1)} %add_convert_fusion), channel_id=1, source_target_pairs={{8,0},{10,2},{12,4},{14,6},{16,8},{18,10},{20,12},{22,14},{24,16},... | collective-permute-start | bytes 786440 | tf_op jit(solution)/shard_map/ppermute | solution.py:462
  71.2 4.9 %project.1 = bf16[256,1024]{1,0:T(8,128)(2,1)} custom-call(s32[1]{0:T(128)} %bitcast.core_ref.refs_0_, bf16[256,1024]{1,0:T(8,128)(2,1)} %get-tuple-element.38.own_ref, bf16[256,1024]{1,0:T(8,128)(2,1)} %copy-done.26, bf16[2048,2048]{1,0:T(8,128)(2,1)} %w_hbm.3), custom_call_target="tpu_custom_call" | custom-call | flops 1073741824 | bytes 6291456 | tf_op jit(solution)/shard_map/project/pallas_call | solution.py:161
  76.1 4.9 %collective-permute-done.9.last_ref = bf16[128,1024]{1,0:T(8,128)(2,1)S(1)} collective-permute-done((bf16[128,1024]{1,0:T(8,128)(2,1)S(1)}, bf16[128,1024]{1,0:T(8,128)(2,1)S(1)}, u32[]{:S(2)}, u32[]{:S(2)}) %collective-permute-start.9) | collective-permute-done | bytes 262176 | tf_op jit(solution)/shard_map/ppermute | solution.py:462
  81.0 2.4 %settle.1 = (bf16[256,1024]{1,0:T(8,128)(2,1)}, bf16[256,1024]{1,0:T(8,128)(2,1)}) custom-call(s32[1]{0:T(128)} %bitcast.1.me_ref, s32[1]{0:T(128)} %bitcast.core_ref.refs_0_, f32[256,1024]{1,0:T(8,128)S(1)} %copy-done.17, f32[256,1024]{1,0:T(8,128)S(1)} %copy-done.19, bf16[128,1024]{1,0:T(8,128)(2,1)S(1)} %collective-permute-done.9.last_ref, ...), custom_call_target="tpu_custom_call" | custom-call | tf_op jit(solution)/shard_map/settle/pallas_call | solution.py:396
  (61 shorter events, 18.6 us)
Async XLA Ops:
  0.6 7.2 %collective-permute-start = (bf16[256,1024]{1,0:T(8,128)(2,1)}, bf16[256,1024]{1,0:T(8,128)(2,1)}, u32[]{:S(2)}, u32[]{:S(2)}) collective-permute-start(bf16[256,1024]{1,0:T(8,128)(2,1)} %own_hbm.1), channel_id=1, source_target_pairs={{0,1},{1,0},{2,3},{3,2},{4,5},{5,4},{6,7},{7,6},{8,9},{9,8},{10,11... | collective-permute-start | bytes 1572872 | tf_op jit(solution)/shard_map/ppermute | solution.py:47
  3.3 11.5 %collective-permute-start.1 = (bf16[128,1024]{1,0:T(8,128)(2,1)}, bf16[128,1024]{1,0:T(8,128)(2,1)S(1)}, u32[]{:S(2)}, u32[]{:S(2)}) collective-permute-start(bf16[128,1024]{1,0:T(8,128)(2,1)} %pick.1.picked_ref), channel_id=1, source_target_pairs={{0,8},{2,10},{4,12},{6,14},{8,16},{10,18},{12,20},{14,22},{16,24},... | collective-permute-start | bytes 786440 | tf_op jit(solution)/shard_map/ppermute | solution.py:421
  7.9 20.5 %copy-start.2 = (bf16[256,1024]{1,0:T(8,128)(2,1)S(1)}, bf16[256,1024]{1,0:T(8,128)(2,1)}, u32[]{:S(2)}) copy-start(bf16[256,1024]{1,0:T(8,128)(2,1)} %k_ref.3) | copy-start | bytes 1572868
  7.9 20.5 %copy-start.24 = (s32[4]{0:T(128)S(1)}, s32[4]{0:T(128)}, u32[]{:S(2)}) copy-start(s32[4]{0:T(128)} %bounds_ref.1) | copy-start | bytes 52
  16.5 8.1 %collective-permute-start.2 = (bf16[128,1024]{1,0:T(8,128)(2,1)S(1)}, bf16[128,1024]{1,0:T(8,128)(2,1)S(1)}, u32[]{:S(2)}, u32[]{:S(2)}) collective-permute-start(bf16[128,1024]{1,0:T(8,128)(2,1)S(1)} %get-tuple-element.32), channel_id=1, source_target_pairs={{0,8},{2,10},{4,12},{6,14},{8,16},{10,18},{12,20},{14,22},{16,24},... | collective-permute-start | bytes 786440 | tf_op jit(solution)/shard_map/ppermute | solution.py:43
  20.4 13.1 %collective-permute-start.3 = (bf16[128,1024]{1,0:T(8,128)(2,1)}, bf16[128,1024]{1,0:T(8,128)(2,1)S(1)}, u32[]{:S(2)}, u32[]{:S(2)}) collective-permute-start(bf16[128,1024]{1,0:T(8,128)(2,1)} %get-tuple-element.33), channel_id=1, source_target_pairs={{0,2},{2,4},{4,6},{6,0},{8,10},{10,12},{12,14},{14,8},{16,18},{18,... | collective-permute-start | bytes 786440 | tf_op jit(solution)/shard_map/ppermute | solution.py:43
  24.7 3.7 %copy-start.14 = (bf16[128,1024]{1,0:T(8,128)(2,1)}, bf16[128,1024]{1,0:T(8,128)(2,1)S(1)}, u32[]{:S(2)}) copy-start(bf16[128,1024]{1,0:T(8,128)(2,1)S(1)} %collective-permute-done.2.refs_7_) | copy-start | bytes 786436
  25.8 7.8 %collective-permute-start.4 = (bf16[128,1024]{1,0:T(8,128)(2,1)S(1)}, bf16[128,1024]{1,0:T(8,128)(2,1)S(1)}, u32[]{:S(2)}, u32[]{:S(2)}) collective-permute-start(bf16[128,1024]{1,0:T(8,128)(2,1)S(1)} %select_select_fusion.1), channel_id=1, source_target_pairs={{0,4},{2,6},{4,0},{6,2},{8,12},{10,14},{12,8},{14,10},{16,20},{18,... | collective-permute-start | bytes 786440 | tf_op jit(solution)/shard_map/ppermute | solution.py:43
  28.4 1.0 %copy-start.3 = (bf16[256,1024]{1,0:T(8,128)(2,1)S(1)}, bf16[256,1024]{1,0:T(8,128)(2,1)}, u32[]{:S(2)}) copy-start(bf16[256,1024]{1,0:T(8,128)(2,1)} %v_ref.3) | copy-start | bytes 1572868
  29.4 1.0 %copy-start.5 = (bf16[256,1024]{1,0:T(8,128)(2,1)S(1)}, bf16[256,1024]{1,0:T(8,128)(2,1)}, u32[]{:S(2)}) copy-start(bf16[256,1024]{1,0:T(8,128)(2,1)} %q_ref.3) | copy-start | bytes 1572868
  30.5 1.0 %copy-start.8 = (bf16[256,1024]{1,0:T(8,128)(2,1)S(1)}, bf16[256,1024]{1,0:T(8,128)(2,1)}, u32[]{:S(2)}) copy-start(bf16[256,1024]{1,0:T(8,128)(2,1)} %get-tuple-element.26.ga_ref.refs_2_) | copy-start | bytes 1572868
  33.5 6.2 %copy-start = (f32[8,320,256]{2,1,0:T(8,128)}, f32[8,320,256]{2,1,0:T(8,128)S(1)}, u32[]{:S(2)}) copy-start(f32[8,320,256]{2,1,0:T(8,128)S(1)} %get-tuple-element.28.refs_4_.gp_ref) | copy-start | bytes 7864324
  33.5 1.4 %copy-start.6 = (bf16[256,1024]{1,0:T(8,128)(2,1)S(1)}, bf16[256,1024]{1,0:T(8,128)(2,1)}, u32[]{:S(2)}) copy-start(bf16[256,1024]{1,0:T(8,128)(2,1)} %q_ref.3) | copy-start | bytes 1572868
  44.7 6.7 %collective-permute-start.6 = (bf16[128,1024]{1,0:T(8,128)(2,1)}, bf16[128,1024]{1,0:T(8,128)(2,1)}, u32[]{:S(2)}, u32[]{:S(2)}) collective-permute-start(bf16[128,1024]{1,0:T(8,128)(2,1)} %get-tuple-element.43), channel_id=1, source_target_pairs={{4,0},{6,2},{0,4},{2,6},{12,8},{14,10},{8,12},{10,14},{20,16},{22,... | collective-permute-start | bytes 786440 | tf_op jit(solution)/shard_map/ppermute | solution.py:43
  46.3 21.4 %collective-permute-start.7 = (bf16[128,1024]{1,0:T(8,128)(2,1)}, bf16[128,1024]{1,0:T(8,128)(2,1)}, u32[]{:S(2)}, u32[]{:S(2)}) collective-permute-start(bf16[128,1024]{1,0:T(8,128)(2,1)} %copy-done.25), channel_id=1, source_target_pairs={{2,0},{4,2},{6,4},{0,6},{10,8},{12,10},{14,12},{8,14},{18,16},{20,... | collective-permute-start | bytes 786440 | tf_op jit(solution)/shard_map/ppermute | solution.py:43
  53.1 14.6 %collective-permute-start.8 = (bf16[128,1024]{1,0:T(8,128)(2,1)}, bf16[128,1024]{1,0:T(8,128)(2,1)}, u32[]{:S(2)}, u32[]{:S(2)}) collective-permute-start(bf16[128,1024]{1,0:T(8,128)(2,1)} %add_convert_fusion.1), channel_id=1, source_target_pairs={{8,0},{10,2},{12,4},{14,6},{16,8},{18,10},{20,12},{22,14},{24,16},... | collective-permute-start | bytes 786440 | tf_op jit(solution)/shard_map/ppermute | solution.py:43
  54.4 1.7 %copy-start.1 = (f32[8,320,256]{2,1,0:T(8,128)S(1)}, f32[8,320,256]{2,1,0:T(8,128)}, u32[]{:S(2)}) copy-start(f32[8,320,256]{2,1,0:T(8,128)} %copy-done) | copy-start | bytes 7864324
  59.3 1.2 %copy-start.11 = (bf16[8,256,256]{2,1,0:T(8,128)(2,1)S(1)}, bf16[8,256,256]{2,1,0:T(8,128)(2,1)}, u32[]{:S(2)}) copy-start(bf16[8,256,256]{2,1,0:T(8,128)(2,1)} %copy-done.10) | copy-start | bytes 3145732
  60.5 1.2 %copy-start.13 = (bf16[8,256,256]{2,1,0:T(8,128)(2,1)S(1)}, bf16[8,256,256]{2,1,0:T(8,128)(2,1)}, u32[]{:S(2)}) copy-start(bf16[8,256,256]{2,1,0:T(8,128)(2,1)} %copy-done.12) | copy-start | bytes 3145732
  61.7 1.1 %copy-start.21 = (bf16[2,192,1024]{2,1,0:T(8,128)(2,1)S(1)}, bf16[2,192,1024]{2,1,0:T(8,128)(2,1)}, u32[]{:S(2)}) copy-start(bf16[2,192,1024]{2,1,0:T(8,128)(2,1)} %copy-done.20) | copy-start | bytes 2359300
  67.7 2.7 %collective-permute-start.5 = (bf16[256,1024]{1,0:T(8,128)(2,1)}, bf16[256,1024]{1,0:T(8,128)(2,1)S(1)}, u32[]{:S(2)}, u32[]{:S(2)}) collective-permute-start(bf16[256,1024]{1,0:T(8,128)(2,1)} %get-tuple-element.38.own_ref), channel_id=1, source_target_pairs={{0,1},{1,0},{2,3},{3,2},{4,5},{5,4},{6,7},{7,6},{8,9},{9,8},{10,11... | collective-permute-start | bytes 1572872 | tf_op jit(solution)/shard_map/ppermute | solution.py:47
  68.9 12.1 %copy-start.17 = (f32[256,1024]{1,0:T(8,128)S(1)}, f32[256,1024]{1,0:T(8,128)}, u32[]{:S(2)}) copy-start(f32[256,1024]{1,0:T(8,128)} %copy-done.16) | copy-start | bytes 3145732
  68.9 12.1 %copy-start.19 = (f32[256,1024]{1,0:T(8,128)S(1)}, f32[256,1024]{1,0:T(8,128)}, u32[]{:S(2)}) copy-start(f32[256,1024]{1,0:T(8,128)} %copy-done.18) | copy-start | bytes 3145732
  68.9 12.1 %collective-permute-start.9 = (bf16[128,1024]{1,0:T(8,128)(2,1)S(1)}, bf16[128,1024]{1,0:T(8,128)(2,1)S(1)}, u32[]{:S(2)}, u32[]{:S(2)}) collective-permute-start(bf16[128,1024]{1,0:T(8,128)(2,1)S(1)} %add_convert_fusion), channel_id=1, source_target_pairs={{8,0},{10,2},{12,4},{14,6},{16,8},{18,10},{20,12},{22,14},{24,16},... | collective-permute-start | bytes 786440 | tf_op jit(solution)/shard_map/ppermute | solution.py:462
  (13 other events, 11.8 us)

commit v8 on v7

--- a/solution.py
+++ b/solution.py
@@ -376,6 +376,53 @@
     return first & jnp.logical_not(own2), rest | jnp.logical_not(own1), first | jnp.logical_not(own2)
 
 
+def choose_kernel(me_ref, core_ref, picked_ref, far4_ref, two_ref, three_ref):
+    first = core_ref[0] == 0
+    own1, own2 = lends_own(me_ref[0])
+    picked, far4 = picked_ref[...], far4_ref[...]
+    two_ref[...] = jnp.where(first, far4, jnp.where(own2, picked, far4))
+    three_ref[...] = jnp.where(first, jnp.where(own1, picked, far4), far4)
+
+
+def choose_last_kernel(me_ref, core_ref, picked_ref, far4_ref, two_ref, out_ref):
+    first = core_ref[0] == 0
+    own2 = lends_own(me_ref[0])[1]
+    picked = picked_ref[...]
+    ahead = jnp.where(own2, picked, far4_ref[...])
+    out_ref[...] = jnp.where(first, ahead, jnp.where(me_ref[0] % 2 == 0, picked, two_ref[...]))
+
+
+def include(total, block, use):
+    block = block.astype(F32)
+    return total + jnp.where(use, block, jnp.zeros_like(block))
+
+
+def pass_on_kernel(me_ref, core_ref, own_ref, one_ref, out_ref):
+    use = jnp.logical_not((core_ref[0] == 0) | (me_ref[0] % 2 == 0))
+    out_ref[...] = include(own_ref[...].astype(F32), one_ref[...], use).astype(BF16)
+
+
+def collect_kernel(me_ref, core_ref, own_ref, one_ref, two_ref, three_ref, out_ref):
+    total = own_ref[...].astype(F32)
+    uses = returns_lent(me_ref[0], core_ref[0] == 0)
+    for ref, use in zip((one_ref, two_ref, three_ref), uses):
+        total = include(total, ref[...], use)
+    out_ref[...] = total.astype(BF16)
+
+
+def small(kernel, name, count, me, core, *blocks):
+    shape = jax.ShapeDtypeStruct(blocks[0].shape, BF16)
+    out = pl.pallas_call(
+        kernel,
+        in_specs=[SMEM_BLOCK] * 2 + [VMEM_BLOCK] * len(blocks),
+        out_specs=[VMEM_BLOCK] * count,
+        out_shape=[shape] * count,
+        compiler_params=params(8),
+        name=name,
+    )(me, core, *blocks)
+    return out if count > 1 else out[0]
+
+
 def settle_kernel(me_ref, core_ref, gk_ref, gv_ref, last_ref, one_ref, two_ref, three_ref, *out_refs):
     tokens = gk_ref.shape[0]
     rows = tokens // STEP
@@ -421,17 +468,12 @@
     far4 = lax.ppermute(picked, "ctx", hop(4, n))
     ga, picked = grad_attn(core, cotangent, other_cot, picked, out_weight)
 
-    index, first = lax.axis_index("ctx"), lax.axis_index("head") == 0
-    own1, own2 = lends_own(index)
-    even = index % 2 == 0
-    lent1, lent2 = jnp.where(own1, picked, far4), jnp.where(own2, picked, far4)
     hops, ones, twos, nexts = hop(4, n), steps(n), pairs(n), neighbours(n)
-    two, three = lax.optimization_barrier(
-        (jnp.where(first, far4, lent2), jnp.where(first, lent1, far4))
-    )
+    two, three = small(choose_kernel, "choose", 2, me, core, picked, far4)
     two = mixed(two, (hops, twos))
     three = mixed(three, (ones, hops))
-    four = mixed(jnp.where(first, lent2, jnp.where(even, picked, two)), (twos, nexts))
+    four = mixed(small(choose_last_kernel, "choose_last", 1, me, core, picked, far4, two), (twos, nexts))
+    first = lax.axis_index("head") == 0 if levels > 4 else None
     arrived = [two, three, four]
     farther = jnp.where(first, two, three) if levels > 4 else None
     for i in range(4, levels):
@@ -452,14 +494,13 @@
     hops, ones, twos = hop(-4, n), turned(ones), turned(twos)
     one = mixed(two, (twos, nexts))
     two = mixed(three, (ones, hops))
-    zero = jnp.zeros_like(one)
-    three = mixed(add(four, jnp.where(first | even, zero, one)), (hops, twos))
+    three = mixed(small(pass_on_kernel, "pass_on", 1, me, core, four, one), (hops, twos))
     attn, gq, gk, gv = attention_local(
         queries, keys, values, ga, far4, far, grown, grad_prob, use, weights, grad_scores
     )
     back = (one, two, three)
-    lent = [jnp.where(w, b, zero) for w, b in zip(returns_lent(index, first), back)]
-    last = lax.ppermute(add(g4, *lent), "ctx", hop(-4, n))
+    g4 = small(collect_kernel, "collect", 1, me, core, g4, *back)
+    last = lax.ppermute(g4, "ctx", hop(-4, n))
     other_attn = swap(attn)
     output = project(core, attn, other_attn, out_weight)
     gk, gv = settle(me, core, gk, gv, last, *back)

time: 84.4 us -> 62.6 us (0.74)
  local copies, waits for them, and re-layouts: 21.7 us -> 2.8 us
  waiting for transfers between devices: 7.7 us -> 13.5 us
  other arithmetic: 5.76 us -> 0 us
  Pallas kernels: 25 us -> 23.5 us
    unnamed x54 -> x18, local copies, waits for them, and re-layouts: 21.7 us -> 2.8 us
    ppermute x6, waiting for transfers between devices: 2.76 us -> 11.1 us  [mixed(): return lax.ppermute(block, ('ctx', 'head'), route)]
    convert_element_type x2 -> x0, other arithmetic: 2.97 us -> none  [add(): return total.astype(BF16)]
    select_n x2 -> x0, other arithmetic: 2.79 us -> none  [the longest x1 1.7 us: per_device(): jnp.where(first, lent1, far4)]
    ppermute x1, waiting for transfers between devices: 4.94 us -> 2.39 us  [per_device(): last = lax.ppermute(g4, 'ctx', hop(-4, n))]
    pallas_call x1, Pallas kernels: 2.42 us -> 1.31 us  [settle(): pl.pallas_call(settle_kernel, in_specs=[SMEM_BLOCK] * 2 + [VMEM_BLOCK] *...]
  transfers between devices with their start and end apart: 10 -> 10, of which waited for: 3 -> 6; matrix products, arithmetic and copies ran while one was open for 5% -> 0% of each run, Pallas kernels for 23% -> 31%
where the time goes in v8:
time: 62.6 us; the launch traced here: 62.2 us
  Pallas kernels  23.5 us (38%)
  starting transfers between devices  21.6 us (35%)
  waiting for transfers between devices  13.5 us (22%)
  local copies, waits for them, and re-layouts  2.8 us (4%)
  between operations  0.85 us (1%)
    ppermute x6, starting transfers between devices, mixed(): return lax.ppermute(block, ('ctx', 'head'), route)  15.3 us
    ppermute x6, waiting for transfers between devices, mixed(): return lax.ppermute(block, ('ctx', 'head'), route)  11.1 us
    pallas_call x1, Pallas kernels, grad_attn(): pl.pallas_call(grad_attn_kernel, in_specs=[SMEM_BLOCK, HBM_BLOCK, HBM_BLO...  6.95 us
    pallas_call x1, Pallas kernels, project(): pl.pallas_call(project_kernel, in_specs=[SMEM_BLOCK, VMEM_BLOCK, VMEM_BLO...  4.93 us
    ppermute x1, starting transfers between devices, per_device(): far4 = lax.ppermute(picked, 'ctx', hop(4, n))  4.51 us
    pallas_call x1, Pallas kernels, attention_far(): pl.pallas_call(functools.partial(far_kernel, levels), in_specs=[SMEM_BLOC...  3.11 us
    unnamed x18, local copies, waits for them, and re-layouts  2.8 us
    pallas_call x1, Pallas kernels, attention_local(): pl.pallas_call(local_kernel, in_specs=[VMEM_BLOCK] * (1 + len(operands)),...  2.67 us
  transfers between devices with their start and end apart: 10, of which 6 were waited for; matrix products, arithmetic and copies ran while one was open for 0% of the time, Pallas kernels for 31%

profile of v8, /device:TPU:0, one launch (start us, length us, event | category | flops | bytes accessed | tf_op | source)
XLA Modules:
  0.0 62.2 jit_solution(9105962193531434886)
XLA Ops:
  1.1 2.2 %pick.1.picked_ref = bf16[128,1024]{1,0:T(8,128)(2,1)} custom-call(bf16[256,1024]{1,0:T(8,128)(2,1)} %k_ref.3, bf16[256,1024]{1,0:T(8,128)(2,1)} %v_ref.3), custom_call_target="tpu_custom_call" | custom-call | tf_op jit(solution)/shard_map/pick/pallas_call | solution.py:81
  3.3 4.5 %collective-permute-start.1 = (bf16[128,1024]{1,0:T(8,128)(2,1)}, bf16[128,1024]{1,0:T(8,128)(2,1)S(1)}, u32[]{:S(2)}, u32[]{:S(2)}) collective-permute-start(bf16[128,1024]{1,0:T(8,128)(2,1)} %pick.1.picked_ref), channel_id=1, source_target_pairs={{0,8},{2,10},{4,12},{6,14},{8,16},{10,18},{12,20},{14,22},{16,24},... | collective-permute-start | bytes 786440 | tf_op jit(solution)/shard_map/ppermute | solution.py:468
  7.9 7.0 %grad_attn.1 = (bf16[256,1024]{1,0:T(8,128)(2,1)}, bf16[128,1024]{1,0:T(8,128)(2,1)}) custom-call(s32[1]{0:T(128)} %bitcast.core_ref.refs_0_, bf16[256,1024]{1,0:T(8,128)(2,1)} %own_hbm.1, bf16[256,1024]{1,0:T(8,128)(2,1)} %collective-permute-done.other_hbm, bf16[128,1024]{1,0:T(8,128)(2,1)} %pick.1.picked_ref, bf16[2048,2048]{1,0:T(8,128)(2,1)} %w_hbm.3), custom_call_target="tpu_custom_call" | custom-call | flops 1073741824 | bytes 6291456 | tf_op jit(solution)/shard_map/grad_attn/pallas_call | solution.py:117
  14.9 0.9 %copy-done.5 = bf16[128,1024]{1,0:T(8,128)(2,1)S(1)} copy-done((bf16[128,1024]{1,0:T(8,128)(2,1)S(1)}, bf16[128,1024]{1,0:T(8,128)(2,1)}, u32[]{:S(2)}) %copy-start.5) | copy-done | bytes 262168
  15.9 3.8 %collective-permute-start.2 = (bf16[128,1024]{1,0:T(8,128)(2,1)S(1)}, bf16[128,1024]{1,0:T(8,128)(2,1)S(1)}, u32[]{:S(2)}, u32[]{:S(2)}) collective-permute-start(bf16[128,1024]{1,0:T(8,128)(2,1)S(1)} %get-tuple-element.32), channel_id=1, source_target_pairs={{0,8},{2,10},{4,12},{6,14},{8,16},{10,18},{12,20},{14,22},{16,24},... | collective-permute-start | bytes 786440 | tf_op jit(solution)/shard_map/ppermute | solution.py:43
  19.7 3.4 %collective-permute-start.3 = (bf16[128,1024]{1,0:T(8,128)(2,1)S(1)}, bf16[128,1024]{1,0:T(8,128)(2,1)S(1)}, u32[]{:S(2)}, u32[]{:S(2)}) collective-permute-start(bf16[128,1024]{1,0:T(8,128)(2,1)S(1)} %get-tuple-element.33), channel_id=1, source_target_pairs={{0,2},{2,4},{4,6},{6,0},{8,10},{10,12},{12,14},{14,8},{16,18},{18,... | collective-permute-start | bytes 786440 | tf_op jit(solution)/shard_map/ppermute | solution.py:43
  23.1 1.1 %collective-permute-done.2.two_ref.refs_7_ = bf16[128,1024]{1,0:T(8,128)(2,1)S(1)} collective-permute-done((bf16[128,1024]{1,0:T(8,128)(2,1)S(1)}, bf16[128,1024]{1,0:T(8,128)(2,1)S(1)}, u32[]{:S(2)}, u32[]{:S(2)}) %collective-permute-start.2) | collective-permute-done | bytes 262176 | tf_op jit(solution)/shard_map/ppermute | solution.py:43
  24.2 2.7 %collective-permute-start.4 = (bf16[128,1024]{1,0:T(8,128)(2,1)S(1)}, bf16[128,1024]{1,0:T(8,128)(2,1)S(1)}, u32[]{:S(2)}, u32[]{:S(2)}) collective-permute-start(bf16[128,1024]{1,0:T(8,128)(2,1)S(1)} %choose_last.1), channel_id=1, source_target_pairs={{0,4},{2,6},{4,0},{6,2},{8,12},{10,14},{12,8},{14,10},{16,20},{18,... | collective-permute-start | bytes 786440 | tf_op jit(solution)/shard_map/ppermute | solution.py:43
  26.9 1.0 %copy-done.3 = bf16[256,1024]{1,0:T(8,128)(2,1)S(1)} copy-done((bf16[256,1024]{1,0:T(8,128)(2,1)S(1)}, bf16[256,1024]{1,0:T(8,128)(2,1)}, u32[]{:S(2)}) %copy-start.3) | copy-done | bytes 524312
  27.9 2.0 %attention_near.1 = (f32[8,320,256]{2,1,0:T(8,128)S(1)}, f32[8,320,256]{2,1,0:T(8,128)S(1)}, f32[8,8,256]{2,1,0:T(8,128)S(1)}, f32[512,256]{1,0:T(8,128)S(1)}) custom-call(s32[1]{0:T(128)} %bitcast.1.me_ref, s32[4]{0:T(128)S(1)} %copy-done.7, bf16[256,1024]{1,0:T(8,128)(2,1)S(1)} %copy-done.2, bf16[256,1024]{1,0:T(8,128)(2,1)S(1)} %copy-done, ...), custom_call_target="tpu_custom_call" | custom-call | flops 335544320 | bytes 4194304 | tf_op jit(solution)/shard_map/attention_near/pallas_call | solution.py:237
  29.9 0.9 %collective-permute-done.3.refs_8_ = bf16[128,1024]{1,0:T(8,128)(2,1)S(1)} collective-permute-done((bf16[128,1024]{1,0:T(8,128)(2,1)S(1)}, bf16[128,1024]{1,0:T(8,128)(2,1)S(1)}, u32[]{:S(2)}, u32[]{:S(2)}) %collective-permute-start.3) | collective-permute-done | bytes 262176 | tf_op jit(solution)/shard_map/ppermute | solution.py:43
  30.8 1.6 %collective-permute-done.4.refs_9_ = bf16[128,1024]{1,0:T(8,128)(2,1)S(1)} collective-permute-done((bf16[128,1024]{1,0:T(8,128)(2,1)S(1)}, bf16[128,1024]{1,0:T(8,128)(2,1)S(1)}, u32[]{:S(2)}, u32[]{:S(2)}) %collective-permute-start.4) | collective-permute-done | bytes 262176 | tf_op jit(solution)/shard_map/ppermute | solution.py:43
  32.4 3.1 %attention_far.1 = (bf16[8,256,256]{2,1,0:T(8,128)(2,1)S(1)}, bf16[8,256,256]{2,1,0:T(8,128)(2,1)S(1)}, f32[8,8,256]{2,1,0:T(8,128)S(1)}, bf16[2,192,1024]{2,1,0...) custom-call(s32[1]{0:T(128)} %bitcast.core_ref.refs_0_, ...), custom_call_target="tpu_custom_call" | custom-call | flops 536870912 | bytes 4194304 | tf_op jit(solution)/shard_map/attention_far/pallas_call | solution.py:306
  35.5 2.3 %collective-permute-start.6 = (bf16[128,1024]{1,0:T(8,128)(2,1)S(1)}, bf16[128,1024]{1,0:T(8,128)(2,1)S(1)}, u32[]{:S(2)}, u32[]{:S(2)}) collective-permute-start(bf16[128,1024]{1,0:T(8,128)(2,1)S(1)} %get-tuple-element.43), channel_id=1, source_target_pairs={{4,0},{6,2},{0,4},{2,6},{12,8},{14,10},{8,12},{10,14},{20,16},{22,... | collective-permute-start | bytes 786440 | tf_op jit(solution)/shard_map/ppermute | solution.py:43
  37.8 2.7 %attention_local.1 = (bf16[256,1024]{1,0:T(8,128)(2,1)S(1)}, bf16[256,1024]{1,0:T(8,128)(2,1)}, f32[256,1024]{1,0:T(8,128)S(1)}, f32[256,1024]{1,0:T(8,128)S(1)}) custom-call(bf16[256,1024]{1,0:T(8,128)(2,1)S(1)} %copy-done.2, bf16[256,1024]{1,0:T(8,128)(2,1)S(1)} %copy-done, bf16[256,1024]{1,0:T(8,128)(2,1)S(1)} %copy-done.1, ...), custom_call_target="tpu_custom_call" | custom-call | flops 805306368 | bytes 4194304 | tf_op jit(solution)/shard_map/attention_local/pallas_call | solution.py:350
  40.5 1.9 %collective-permute-start.7 = (bf16[128,1024]{1,0:T(8,128)(2,1)S(1)}, bf16[128,1024]{1,0:T(8,128)(2,1)S(1)}, u32[]{:S(2)}, u32[]{:S(2)}) collective-permute-start(bf16[128,1024]{1,0:T(8,128)(2,1)S(1)} %get-tuple-element.44), channel_id=1, source_target_pairs={{2,0},{4,2},{6,4},{0,6},{10,8},{12,10},{14,12},{8,14},{18,16},{20,... | collective-permute-start | bytes 786440 | tf_op jit(solution)/shard_map/ppermute | solution.py:43
  42.5 1.3 %collective-permute-start.8 = (bf16[128,1024]{1,0:T(8,128)(2,1)S(1)}, bf16[128,1024]{1,0:T(8,128)(2,1)S(1)}, u32[]{:S(2)}, u32[]{:S(2)}) collective-permute-start(bf16[128,1024]{1,0:T(8,128)(2,1)S(1)} %pass_on.1), channel_id=1, source_target_pairs={{8,0},{10,2},{12,4},{14,6},{16,8},{18,10},{20,12},{22,14},{24,16},... | collective-permute-start | bytes 786440 | tf_op jit(solution)/shard_map/ppermute | solution.py:43
  43.8 4.9 %collective-permute-done.7.two_ref = bf16[128,1024]{1,0:T(8,128)(2,1)S(1)} collective-permute-done((bf16[128,1024]{1,0:T(8,128)(2,1)S(1)}, bf16[128,1024]{1,0:T(8,128)(2,1)S(1)}, u32[]{:S(2)}, u32[]{:S(2)}) %collective-permute-start.7) | collective-permute-done | bytes 262176 | tf_op jit(solution)/shard_map/ppermute | solution.py:43
  48.7 2.6 %collective-permute-done.8.three_ref = bf16[128,1024]{1,0:T(8,128)(2,1)S(1)} collective-permute-done((bf16[128,1024]{1,0:T(8,128)(2,1)S(1)}, bf16[128,1024]{1,0:T(8,128)(2,1)S(1)}, u32[]{:S(2)}, u32[]{:S(2)}) %collective-permute-start.8) | collective-permute-done | bytes 262176 | tf_op jit(solution)/shard_map/ppermute | solution.py:43
  51.5 1.3 %collective-permute-start.9 = (bf16[128,1024]{1,0:T(8,128)(2,1)S(1)}, bf16[128,1024]{1,0:T(8,128)(2,1)S(1)}, u32[]{:S(2)}, u32[]{:S(2)}) collective-permute-start(bf16[128,1024]{1,0:T(8,128)(2,1)S(1)} %collect.1), channel_id=1, source_target_pairs={{8,0},{10,2},{12,4},{14,6},{16,8},{18,10},{20,12},{22,14},{24,16},... | collective-permute-start | bytes 786440 | tf_op jit(solution)/shard_map/ppermute | solution.py:503
  52.8 0.8 %copy-done.8 = bf16[256,1024]{1,0:T(8,128)(2,1)} copy-done((bf16[256,1024]{1,0:T(8,128)(2,1)}, bf16[256,1024]{1,0:T(8,128)(2,1)S(1)}, u32[]{:S(2)}) %copy-start.8) | copy-done | bytes 524312
  53.6 4.9 %project.1 = bf16[256,1024]{1,0:T(8,128)(2,1)} custom-call(s32[1]{0:T(128)} %bitcast.core_ref.refs_0_, bf16[256,1024]{1,0:T(8,128)(2,1)} %copy-done.6, bf16[256,1024]{1,0:T(8,128)(2,1)} %copy-done.8, bf16[2048,2048]{1,0:T(8,128)(2,1)} %w_hbm.3), custom_call_target="tpu_custom_call" | custom-call | flops 1073741824 | bytes 6291456 | tf_op jit(solution)/shard_map/project/pallas_call | solution.py:161
  58.5 2.4 %collective-permute-done.9.last_ref = bf16[128,1024]{1,0:T(8,128)(2,1)S(1)} collective-permute-done((bf16[128,1024]{1,0:T(8,128)(2,1)S(1)}, bf16[128,1024]{1,0:T(8,128)(2,1)S(1)}, u32[]{:S(2)}, u32[]{:S(2)}) %collective-permute-start.9) | collective-permute-done | bytes 262176 | tf_op jit(solution)/shard_map/ppermute | solution.py:503
  60.9 1.3 %settle.1 = (bf16[256,1024]{1,0:T(8,128)(2,1)}, bf16[256,1024]{1,0:T(8,128)(2,1)}) custom-call(s32[1]{0:T(128)} %bitcast.1.me_ref, s32[1]{0:T(128)} %bitcast.core_ref.refs_0_, f32[256,1024]{1,0:T(8,128)S(1)} %get-tuple-element.40.gk_ref, f32[256,1024]{1,0:T(8,128)S(1)} %get-tuple-element.41.gv_ref, bf16[128,1024]{1,0:T(8,128)(2,1)S(1)} %collective-permute-done.9.last_ref, ...), custom_call_target="tpu_custom_call" | custom-call | tf_op jit(solution)/shard_map/settle/pallas_call | solution.py:443
  (25 shorter events, 1.0 us)
Async XLA Ops:
  0.6 7.2 %collective-permute-start = (bf16[256,1024]{1,0:T(8,128)(2,1)}, bf16[256,1024]{1,0:T(8,128)(2,1)}, u32[]{:S(2)}, u32[]{:S(2)}) collective-permute-start(bf16[256,1024]{1,0:T(8,128)(2,1)} %own_hbm.1), channel_id=1, source_target_pairs={{0,1},{1,0},{2,3},{3,2},{4,5},{5,4},{6,7},{7,6},{8,9},{9,8},{10,11... | collective-permute-start | bytes 1572872 | tf_op jit(solution)/shard_map/ppermute | solution.py:47
  3.3 11.5 %collective-permute-start.1 = (bf16[128,1024]{1,0:T(8,128)(2,1)}, bf16[128,1024]{1,0:T(8,128)(2,1)S(1)}, u32[]{:S(2)}, u32[]{:S(2)}) collective-permute-start(bf16[128,1024]{1,0:T(8,128)(2,1)} %pick.1.picked_ref), channel_id=1, source_target_pairs={{0,8},{2,10},{4,12},{6,14},{8,16},{10,18},{12,20},{14,22},{16,24},... | collective-permute-start | bytes 786440 | tf_op jit(solution)/shard_map/ppermute | solution.py:468
  7.9 19.0 %copy-start = (bf16[256,1024]{1,0:T(8,128)(2,1)S(1)}, bf16[256,1024]{1,0:T(8,128)(2,1)}, u32[]{:S(2)}) copy-start(bf16[256,1024]{1,0:T(8,128)(2,1)} %k_ref.3) | copy-start | bytes 1572868
  7.9 19.0 %copy-start.1 = (bf16[256,1024]{1,0:T(8,128)(2,1)S(1)}, bf16[256,1024]{1,0:T(8,128)(2,1)}, u32[]{:S(2)}) copy-start(bf16[256,1024]{1,0:T(8,128)(2,1)} %v_ref.3) | copy-start | bytes 1572868
  7.9 19.0 %copy-start.2 = (bf16[256,1024]{1,0:T(8,128)(2,1)S(1)}, bf16[256,1024]{1,0:T(8,128)(2,1)}, u32[]{:S(2)}) copy-start(bf16[256,1024]{1,0:T(8,128)(2,1)} %q_ref.3) | copy-start | bytes 1572868
  7.9 19.0 %copy-start.7 = (s32[4]{0:T(128)S(1)}, s32[4]{0:T(128)}, u32[]{:S(2)}) copy-start(s32[4]{0:T(128)} %bounds_ref.1) | copy-start | bytes 52
  14.9 1.0 %copy-start.5 = (bf16[128,1024]{1,0:T(8,128)(2,1)S(1)}, bf16[128,1024]{1,0:T(8,128)(2,1)}, u32[]{:S(2)}) copy-start(bf16[128,1024]{1,0:T(8,128)(2,1)} %get-tuple-element.31.picked_ref) | copy-start | bytes 786436
  15.9 8.2 %collective-permute-start.2 = (bf16[128,1024]{1,0:T(8,128)(2,1)S(1)}, bf16[128,1024]{1,0:T(8,128)(2,1)S(1)}, u32[]{:S(2)}, u32[]{:S(2)}) collective-permute-start(bf16[128,1024]{1,0:T(8,128)(2,1)S(1)} %get-tuple-element.32), channel_id=1, source_target_pairs={{0,8},{2,10},{4,12},{6,14},{8,16},{10,18},{12,20},{14,22},{16,24},... | collective-permute-start | bytes 786440 | tf_op jit(solution)/shard_map/ppermute | solution.py:43
  19.7 11.1 %collective-permute-start.3 = (bf16[128,1024]{1,0:T(8,128)(2,1)S(1)}, bf16[128,1024]{1,0:T(8,128)(2,1)S(1)}, u32[]{:S(2)}, u32[]{:S(2)}) collective-permute-start(bf16[128,1024]{1,0:T(8,128)(2,1)S(1)} %get-tuple-element.33), channel_id=1, source_target_pairs={{0,2},{2,4},{4,6},{6,0},{8,10},{10,12},{12,14},{14,8},{16,18},{18,... | collective-permute-start | bytes 786440 | tf_op jit(solution)/shard_map/ppermute | solution.py:43
  24.2 8.2 %collective-permute-start.4 = (bf16[128,1024]{1,0:T(8,128)(2,1)S(1)}, bf16[128,1024]{1,0:T(8,128)(2,1)S(1)}, u32[]{:S(2)}, u32[]{:S(2)}) collective-permute-start(bf16[128,1024]{1,0:T(8,128)(2,1)S(1)} %choose_last.1), channel_id=1, source_target_pairs={{0,4},{2,6},{4,0},{6,2},{8,12},{10,14},{12,8},{14,10},{16,20},{18,... | collective-permute-start | bytes 786440 | tf_op jit(solution)/shard_map/ppermute | solution.py:43
  26.9 1.0 %copy-start.3 = (bf16[256,1024]{1,0:T(8,128)(2,1)S(1)}, bf16[256,1024]{1,0:T(8,128)(2,1)}, u32[]{:S(2)}) copy-start(bf16[256,1024]{1,0:T(8,128)(2,1)} %get-tuple-element.26.ga_ref.refs_2_) | copy-start | bytes 1572868
  32.4 5.4 %copy-start.4 = (bf16[256,1024]{1,0:T(8,128)(2,1)S(1)}, bf16[256,1024]{1,0:T(8,128)(2,1)}, u32[]{:S(2)}) copy-start(bf16[256,1024]{1,0:T(8,128)(2,1)} %get-tuple-element.26.ga_ref.refs_2_) | copy-start | bytes 1572868
  35.5 6.8 %collective-permute-start.6 = (bf16[128,1024]{1,0:T(8,128)(2,1)S(1)}, bf16[128,1024]{1,0:T(8,128)(2,1)S(1)}, u32[]{:S(2)}, u32[]{:S(2)}) collective-permute-start(bf16[128,1024]{1,0:T(8,128)(2,1)S(1)} %get-tuple-element.43), channel_id=1, source_target_pairs={{4,0},{6,2},{0,4},{2,6},{12,8},{14,10},{8,12},{10,14},{20,16},{22,... | collective-permute-start | bytes 786440 | tf_op jit(solution)/shard_map/ppermute | solution.py:43
  40.5 12.3 %copy-start.6 = (bf16[256,1024]{1,0:T(8,128)(2,1)}, bf16[256,1024]{1,0:T(8,128)(2,1)S(1)}, u32[]{:S(2)}) copy-start(bf16[256,1024]{1,0:T(8,128)(2,1)S(1)} %get-tuple-element.38.own_ref) | copy-start | bytes 1572868
  40.5 12.3 %collective-permute-start.5 = (bf16[256,1024]{1,0:T(8,128)(2,1)S(1)}, bf16[256,1024]{1,0:T(8,128)(2,1)S(1)}, u32[]{:S(2)}, u32[]{:S(2)}) collective-permute-start(bf16[256,1024]{1,0:T(8,128)(2,1)S(1)} %get-tuple-element.38.own_ref), channel_id=1, source_target_pairs={{0,1},{1,0},{2,3},{3,2},{4,5},{5,4},{6,7},{7,6},{8,9},{9,8},{10,11... | collective-permute-start | bytes 1572872 | tf_op jit(solution)/shard_map/ppermute | solution.py:47
  40.5 8.3 %collective-permute-start.7 = (bf16[128,1024]{1,0:T(8,128)(2,1)S(1)}, bf16[128,1024]{1,0:T(8,128)(2,1)S(1)}, u32[]{:S(2)}, u32[]{:S(2)}) collective-permute-start(bf16[128,1024]{1,0:T(8,128)(2,1)S(1)} %get-tuple-element.44), channel_id=1, source_target_pairs={{2,0},{4,2},{6,4},{0,6},{10,8},{12,10},{14,12},{8,14},{18,16},{20,... | collective-permute-start | bytes 786440 | tf_op jit(solution)/shard_map/ppermute | solution.py:43
  42.5 8.8 %collective-permute-start.8 = (bf16[128,1024]{1,0:T(8,128)(2,1)S(1)}, bf16[128,1024]{1,0:T(8,128)(2,1)S(1)}, u32[]{:S(2)}, u32[]{:S(2)}) collective-permute-start(bf16[128,1024]{1,0:T(8,128)(2,1)S(1)} %pass_on.1), channel_id=1, source_target_pairs={{8,0},{10,2},{12,4},{14,6},{16,8},{18,10},{20,12},{22,14},{24,16},... | collective-permute-start | bytes 786440 | tf_op jit(solution)/shard_map/ppermute | solution.py:43
  51.5 9.4 %collective-permute-start.9 = (bf16[128,1024]{1,0:T(8,128)(2,1)S(1)}, bf16[128,1024]{1,0:T(8,128)(2,1)S(1)}, u32[]{:S(2)}, u32[]{:S(2)}) collective-permute-start(bf16[128,1024]{1,0:T(8,128)(2,1)S(1)} %collect.1), channel_id=1, source_target_pairs={{8,0},{10,2},{12,4},{14,6},{16,8},{18,10},{20,12},{22,14},{24,16},... | collective-permute-start | bytes 786440 | tf_op jit(solution)/shard_map/ppermute | solution.py:503
  52.8 0.8 %copy-start.8 = (bf16[256,1024]{1,0:T(8,128)(2,1)}, bf16[256,1024]{1,0:T(8,128)(2,1)S(1)}, u32[]{:S(2)}) copy-start(bf16[256,1024]{1,0:T(8,128)(2,1)S(1)} %collective-permute-done.5.other_ref) | copy-start | bytes 1572868

commit v9 on v8

--- a/solution.py
+++ b/solution.py
@@ -128,7 +128,7 @@
             pltpu.SemaphoreType.DMA((2,)),
             pltpu.SemaphoreType.DMA((pieces,)),
         ],
-        compiler_params=params(57),
+        compiler_params=params(52),
         cost_estimate=pl.CostEstimate(
             flops=4 * tokens * width * width, bytes_accessed=6 * width * width, transcendentals=0
         ),
@@ -167,7 +167,7 @@
             pltpu.VMEM((pieces, weight.shape[0] // pieces, width), BF16),
             pltpu.SemaphoreType.DMA((pieces,)),
         ],
-        compiler_params=params(57),
+        compiler_params=params(52),
         cost_estimate=pl.CostEstimate(
             flops=4 * tokens * width * width, bytes_accessed=6 * width * width, transcendentals=0
         ),
@@ -253,14 +253,16 @@
 
 
 def far_kernel(levels, *refs):
-    core_ref, q_ref, ga_ref, grown_ref, gp_ref, stat_ref, bias_ref = refs[:7]
-    arrived_refs = refs[7 : 6 + levels]
-    w_ref, u_ref, use_ref, far_ref = refs[6 + levels : 10 + levels]
-    gfar_refs = refs[10 + levels :]
+    me_ref, core_ref, q_ref, ga_ref, grown_ref, gp_ref, stat_ref, bias_ref = refs[:8]
+    arrived_refs = refs[8 : 7 + levels]
+    w_ref, u_ref, use_ref, far_ref, pass_ref = refs[7 + levels : 12 + levels]
+    gfar_refs = refs[12 + levels :]
     tokens = q_ref.shape[0]
     rows = tokens // STEP
     near = tokens + rows
     first = core_ref[0] == 0
+    passes = (core_ref[0] * (me_ref[0] % 2)).astype(F32)
+    pass_ref[...] = jnp.full(pass_ref.shape, passes, F32)
     for h in range(q_ref.shape[1] // DH):
         cols = slice(h * DH, (h + 1) * DH)
         q, ga = q_ref[:, cols], ga_ref[:, cols]
@@ -298,20 +300,21 @@
             ref[:, cols] = block
 
 
-def attention_far(core, q, ga, grown, grad_prob, stats, bias, arrived):
+def attention_far(me, core, q, ga, grown, grad_prob, stats, bias, arrived):
     tokens, width = q.shape
     levels = 1 + len(arrived)
     heads, rows = width // DH, tokens // STEP
     prob = jax.ShapeDtypeStruct((heads, levels * rows, tokens), BF16)
     return pl.pallas_call(
         functools.partial(far_kernel, levels),
-        in_specs=[SMEM_BLOCK] + [VMEM_BLOCK] * (6 + len(arrived)),
-        out_specs=[VMEM_BLOCK] * (4 + levels),
+        in_specs=[SMEM_BLOCK] * 2 + [VMEM_BLOCK] * (6 + len(arrived)),
+        out_specs=[VMEM_BLOCK] * (5 + levels),
         out_shape=[
             prob,
             prob,
             jax.ShapeDtypeStruct(stats.shape, F32),
             jax.ShapeDtypeStruct((2, (levels - 1) * rows, width), BF16),
+            jax.ShapeDtypeStruct((1, width), F32),
         ]
         + [jax.ShapeDtypeStruct((2 * rows, width), BF16)] * levels,
         compiler_params=params(),
@@ -319,7 +322,7 @@
             flops=8 * tokens * levels * rows * width, bytes_accessed=16 * tokens * width, transcendentals=0
         ),
         name="attention_far",
-    )(core, q, ga, grown, grad_prob, stats, bias, *arrived)
+    )(me, core, q, ga, grown, grad_prob, stats, bias, *arrived)
 
 
 def local_kernel(
@@ -397,11 +400,6 @@
     return total + jnp.where(use, block, jnp.zeros_like(block))
 
 
-def pass_on_kernel(me_ref, core_ref, own_ref, one_ref, out_ref):
-    use = jnp.logical_not((core_ref[0] == 0) | (me_ref[0] % 2 == 0))
-    out_ref[...] = include(own_ref[...].astype(F32), one_ref[...], use).astype(BF16)
-
-
 def collect_kernel(me_ref, core_ref, own_ref, one_ref, two_ref, three_ref, out_ref):
     total = own_ref[...].astype(F32)
     uses = returns_lent(me_ref[0], core_ref[0] == 0)
@@ -418,6 +416,9 @@
         out_specs=[VMEM_BLOCK] * count,
         out_shape=[shape] * count,
         compiler_params=params(8),
+        cost_estimate=pl.CostEstimate(
+            flops=blocks[0].size, bytes_accessed=2 * blocks[0].size, transcendentals=0
+        ),
         name=name,
     )(me, core, *blocks)
     return out if count > 1 else out[0]
@@ -481,8 +482,8 @@
         arrived.append(farther)
 
     grown, grad_prob, stats, bias = attention_near(me, bounds, queries, keys, values, ga, far4, levels)
-    weights, grad_scores, use, far, g4, two, three, four, *more = attention_far(
-        core, queries, ga, grown, grad_prob, stats, bias, arrived
+    weights, grad_scores, use, far, passes, g4, two, three, four, *more = attention_far(
+        me, core, queries, ga, grown, grad_prob, stats, bias, arrived
     )
     for i in reversed(range(len(more))):
         back = lax.ppermute(more[i], "ctx", hop(-(2 ** (i + 3)), n))
@@ -494,7 +495,7 @@
     hops, ones, twos = hop(-4, n), turned(ones), turned(twos)
     one = mixed(two, (twos, nexts))
     two = mixed(three, (ones, hops))
-    three = mixed(small(pass_on_kernel, "pass_on", 1, me, core, four, one), (hops, twos))
+    three = mixed((four.astype(F32) + one.astype(F32) * passes).astype(BF16), (hops, twos))
     attn, gq, gk, gv = attention_local(
         queries, keys, values, ga, far4, far, grown, grad_prob, use, weights, grad_scores
     )

time: 62.6 us -> 61.8 us (0.987)
  waiting for transfers between devices: 13.5 us -> 16.6 us
  Pallas kernels: 23.5 us -> 20.7 us
  local copies, waits for them, and re-layouts: 2.8 us -> 2.02 us
    ppermute x1, waiting for transfers between devices: 2.39 us -> 5.19 us  [per_device(): last = lax.ppermute(g4, 'ctx', hop(-4, n))]
    pallas_call x1, Pallas kernels: 6.95 us -> 5.41 us  [grad_attn(): pl.pallas_call(grad_attn_kernel, in_specs=[SMEM_BLOCK, HBM_BLOCK, HBM_BLO...]
    pallas_call x1, Pallas kernels: 4.93 us -> 3.73 us  [project(): pl.pallas_call(project_kernel, in_specs=[SMEM_BLOCK, VMEM_BLOCK, VMEM_BLO...]
    unnamed x18 -> x12, local copies, waits for them, and re-layouts: 2.8 us -> 2.02 us
  transfers between devices with their start and end apart: 10 -> 10, of which waited for: 6 -> 6; matrix products, arithmetic and copies ran while one was open for 0% -> 0% of each run, Pallas kernels for 31% -> 26%
where the time goes in v9:
time: 61.8 us; the launch traced here: 61.5 us
  starting transfers between devices  21.4 us (35%)
  Pallas kernels  20.7 us (33%)
  waiting for transfers between devices  16.6 us (27%)
  local copies, waits for them, and re-layouts  2.02 us (3%)
  between operations  0.79 us (1%)
    ppermute x6, starting transfers between devices, mixed(): return lax.ppermute(block, ('ctx', 'head'), route)  15.1 us
    ppermute x6, waiting for transfers between devices, mixed(): return lax.ppermute(block, ('ctx', 'head'), route)  11.4 us
    pallas_call x1, Pallas kernels, grad_attn(): pl.pallas_call(grad_attn_kernel, in_specs=[SMEM_BLOCK, HBM_BLOCK, HBM_BLO...  5.41 us
    ppermute x1, waiting for transfers between devices, per_device(): last = lax.ppermute(g4, 'ctx', hop(-4, n))  5.19 us
    ppermute x1, starting transfers between devices, per_device(): far4 = lax.ppermute(picked, 'ctx', hop(4, n))  4.51 us
    pallas_call x1, Pallas kernels, project(): pl.pallas_call(project_kernel, in_specs=[SMEM_BLOCK, VMEM_BLOCK, VMEM_BLO...  3.73 us
    pallas_call x1, Pallas kernels, attention_far(): pl.pallas_call(functools.partial(far_kernel, levels), in_specs=[SMEM_BLOC...  3.11 us
    pallas_call x1, Pallas kernels, attention_local(): pl.pallas_call(local_kernel, in_specs=[VMEM_BLOCK] * (1 + len(operands)),...  2.67 us
  transfers between devices with their start and end apart: 10, of which 6 were waited for; matrix products, arithmetic and copies ran while one was open for 0% of the time, Pallas kernels for 26%

profile of v9, /device:TPU:0, one launch (start us, length us, event | category | flops | bytes accessed | tf_op | source)
XLA Modules:
  0.0 61.5 jit_solution(18160979238490191766)
XLA Ops:
  0.6 0.5 collective-permute-start
  1.1 2.2 %pick.1.picked_ref = bf16[128,1024]{1,0:T(8,128)(2,1)} custom-call(bf16[256,1024]{1,0:T(8,128)(2,1)} %k_ref.3, bf16[256,1024]{1,0:T(8,128)(2,1)} %v_ref.3), custom_call_target="tpu_custom_call" | custom-call | tf_op jit(solution)/shard_map/pick/pallas_call | solution.py:81
  3.3 4.5 %collective-permute-start.1 = (bf16[128,1024]{1,0:T(8,128)(2,1)}, bf16[128,1024]{1,0:T(8,128)(2,1)S(1)}, u32[]{:S(2)}, u32[]{:S(2)}) collective-permute-start(bf16[128,1024]{1,0:T(8,128)(2,1)} %pick.1.picked_ref), channel_id=1, source_target_pairs={{0,8},{2,10},{4,12},{6,14},{8,16},{10,18},{12,20},{14,22},{16,24},... | collective-permute-start | bytes 786440 | tf_op jit(solution)/shard_map/ppermute | solution.py:469
  7.9 1.0 %copy-done.3 = bf16[128,1024]{1,0:T(8,128)(2,1)S(1)} copy-done((bf16[128,1024]{1,0:T(8,128)(2,1)S(1)}, bf16[128,1024]{1,0:T(8,128)(2,1)}, u32[]{:S(2)}) %copy-start.3) | copy-done | bytes 262168
  8.8 1.0 %copy-done.4 = bf16[256,1024]{1,0:T(8,128)(2,1)S(1)} copy-done((bf16[256,1024]{1,0:T(8,128)(2,1)S(1)}, bf16[256,1024]{1,0:T(8,128)(2,1)}, u32[]{:S(2)}) %copy-start.4) | copy-done | bytes 524312
  9.9 5.4 %grad_attn.1 = (bf16[256,1024]{1,0:T(8,128)(2,1)S(1)}, bf16[128,1024]{1,0:T(8,128)(2,1)S(1)}) custom-call(s32[1]{0:T(128)} %bitcast.core_ref.refs_1_, bf16[256,1024]{1,0:T(8,128)(2,1)S(1)} %copy-done.4, bf16[256,1024]{1,0:T(8,128)(2,1)} %collective-permute-done.other_hbm, bf16[128,1024]{1,0:T(8,128)(2,1)S(1)} %copy-done.3, bf16[2048,2048]{1,0:T(8,128)(2,1)} %w_hbm.3), custom_call_target="tpu_custom_call" | custom-call | flops 1073741824 | bytes 6291456 | tf_op jit(solution)/shard_map/grad_attn/pallas_call | solution.py:117
  15.4 3.5 %collective-permute-start.2 = (bf16[128,1024]{1,0:T(8,128)(2,1)S(1)}, bf16[128,1024]{1,0:T(8,128)(2,1)S(1)}, u32[]{:S(2)}, u32[]{:S(2)}) collective-permute-start(bf16[128,1024]{1,0:T(8,128)(2,1)S(1)} %get-tuple-element.33), channel_id=1, source_target_pairs={{0,8},{2,10},{4,12},{6,14},{8,16},{10,18},{12,20},{14,22},{16,24},... | collective-permute-start | bytes 786440 | tf_op jit(solution)/shard_map/ppermute | solution.py:43
  18.9 3.4 %collective-permute-start.3 = (bf16[128,1024]{1,0:T(8,128)(2,1)S(1)}, bf16[128,1024]{1,0:T(8,128)(2,1)S(1)}, u32[]{:S(2)}, u32[]{:S(2)}) collective-permute-start(bf16[128,1024]{1,0:T(8,128)(2,1)S(1)} %get-tuple-element.34), channel_id=1, source_target_pairs={{0,2},{2,4},{4,6},{6,0},{8,10},{10,12},{12,14},{14,8},{16,18},{18,... | collective-permute-start | bytes 786440 | tf_op jit(solution)/shard_map/ppermute | solution.py:43
  22.3 0.8 %collective-permute-done.2.two_ref.refs_8_ = bf16[128,1024]{1,0:T(8,128)(2,1)S(1)} collective-permute-done((bf16[128,1024]{1,0:T(8,128)(2,1)S(1)}, bf16[128,1024]{1,0:T(8,128)(2,1)S(1)}, u32[]{:S(2)}, u32[]{:S(2)}) %collective-permute-start.2) | collective-permute-done | bytes 262176 | tf_op jit(solution)/shard_map/ppermute | solution.py:43
  23.2 2.6 %collective-permute-start.4 = (bf16[128,1024]{1,0:T(8,128)(2,1)S(1)}, bf16[128,1024]{1,0:T(8,128)(2,1)S(1)}, u32[]{:S(2)}, u32[]{:S(2)}) collective-permute-start(bf16[128,1024]{1,0:T(8,128)(2,1)S(1)} %choose_last.1), channel_id=1, source_target_pairs={{0,4},{2,6},{4,0},{6,2},{8,12},{10,14},{12,8},{14,10},{16,20},{18,... | collective-permute-start | bytes 786440 | tf_op jit(solution)/shard_map/ppermute | solution.py:43
  25.8 1.9 %attention_near.1 = (f32[8,320,256]{2,1,0:T(8,128)S(1)}, f32[8,320,256]{2,1,0:T(8,128)S(1)}, f32[8,8,256]{2,1,0:T(8,128)S(1)}, f32[512,256]{1,0:T(8,128)S(1)}) custom-call(s32[1]{0:T(128)} %bitcast.1.me_ref.refs_0_, s32[4]{0:T(128)S(1)} %copy-done.5, bf16[256,1024]{1,0:T(8,128)(2,1)S(1)} %copy-done, bf16[256,1024]{1,0:T(8,128)(2,1)S(1)} %copy-done.1, ...), custom_call_target="tpu_custom_call" | custom-call | flops 335544320 | bytes 4194304 | tf_op jit(solution)/shard_map/attention_near/pallas_call | solution.py:237
  27.7 2.0 %collective-permute-done.3.refs_9_ = bf16[128,1024]{1,0:T(8,128)(2,1)S(1)} collective-permute-done((bf16[128,1024]{1,0:T(8,128)(2,1)S(1)}, bf16[128,1024]{1,0:T(8,128)(2,1)S(1)}, u32[]{:S(2)}, u32[]{:S(2)}) %collective-permute-start.3) | collective-permute-done | bytes 262176 | tf_op jit(solution)/shard_map/ppermute | solution.py:43
  29.7 1.6 %collective-permute-done.4.refs_10_ = bf16[128,1024]{1,0:T(8,128)(2,1)S(1)} collective-permute-done((bf16[128,1024]{1,0:T(8,128)(2,1)S(1)}, bf16[128,1024]{1,0:T(8,128)(2,1)S(1)}, u32[]{:S(2)}, u32[]{:S(2)}) %collective-permute-start.4) | collective-permute-done | bytes 262176 | tf_op jit(solution)/shard_map/ppermute | solution.py:43
  31.3 3.1 %attention_far.1 = (bf16[8,256,256]{2,1,0:T(8,128)(2,1)S(1)}, bf16[8,256,256]{2,1,0:T(8,128)(2,1)S(1)}, f32[8,8,256]{2,1,0:T(8,128)S(1)}, bf16[2,192,1024]{2,1,0...) custom-call(s32[1]{0:T(128)} %bitcast.1.me_ref.refs_0_, ...), custom_call_target="tpu_custom_call" | custom-call | flops 536870912 | bytes 4194304 | tf_op jit(solution)/shard_map/attention_far/pallas_call | solution.py:308
  34.5 2.4 %collective-permute-start.6 = (bf16[128,1024]{1,0:T(8,128)(2,1)S(1)}, bf16[128,1024]{1,0:T(8,128)(2,1)S(1)}, u32[]{:S(2)}, u32[]{:S(2)}) collective-permute-start(bf16[128,1024]{1,0:T(8,128)(2,1)S(1)} %get-tuple-element.44), channel_id=1, source_target_pairs={{4,0},{6,2},{0,4},{2,6},{12,8},{14,10},{8,12},{10,14},{20,16},{22,... | collective-permute-start | bytes 786440 | tf_op jit(solution)/shard_map/ppermute | solution.py:43
  36.8 1.9 %collective-permute-start.7 = (bf16[128,1024]{1,0:T(8,128)(2,1)S(1)}, bf16[128,1024]{1,0:T(8,128)(2,1)S(1)}, u32[]{:S(2)}, u32[]{:S(2)}) collective-permute-start(bf16[128,1024]{1,0:T(8,128)(2,1)S(1)} %get-tuple-element.45), channel_id=1, source_target_pairs={{2,0},{4,2},{6,4},{0,6},{10,8},{12,10},{14,12},{8,14},{18,16},{20,... | collective-permute-start | bytes 786440 | tf_op jit(solution)/shard_map/ppermute | solution.py:43
  38.7 2.7 %attention_local.1 = (bf16[256,1024]{1,0:T(8,128)(2,1)S(1)}, bf16[256,1024]{1,0:T(8,128)(2,1)}, f32[256,1024]{1,0:T(8,128)S(1)}, f32[256,1024]{1,0:T(8,128)S(1)}) custom-call(bf16[256,1024]{1,0:T(8,128)(2,1)S(1)} %copy-done, bf16[256,1024]{1,0:T(8,128)(2,1)S(1)} %copy-done.1, bf16[256,1024]{1,0:T(8,128)(2,1)S(1)} %copy-done.2, ...), custom_call_target="tpu_custom_call" | custom-call | flops 805306368 | bytes 4194304 | tf_op jit(solution)/shard_map/attention_local/pallas_call | solution.py:353
  41.5 1.3 %collective-permute-start.8 = (bf16[128,1024]{1,0:T(8,128)(2,1)S(1)}, bf16[128,1024]{1,0:T(8,128)(2,1)S(1)}, u32[]{:S(2)}, u32[]{:S(2)}) collective-permute-start(bf16[128,1024]{1,0:T(8,128)(2,1)S(1)} %add_convert_fusion), channel_id=1, source_target_pairs={{8,0},{10,2},{12,4},{14,6},{16,8},{18,10},{20,12},{22,14},{24,16},... | collective-permute-start | bytes 786440 | tf_op jit(solution)/shard_map/ppermute | solution.py:43
  42.8 2.3 %collective-permute-done.7.two_ref = bf16[128,1024]{1,0:T(8,128)(2,1)S(1)} collective-permute-done((bf16[128,1024]{1,0:T(8,128)(2,1)S(1)}, bf16[128,1024]{1,0:T(8,128)(2,1)S(1)}, u32[]{:S(2)}, u32[]{:S(2)}) %collective-permute-start.7) | collective-permute-done | bytes 262176 | tf_op jit(solution)/shard_map/ppermute | solution.py:43
  45.1 4.7 %collective-permute-done.8.three_ref = bf16[128,1024]{1,0:T(8,128)(2,1)S(1)} collective-permute-done((bf16[128,1024]{1,0:T(8,128)(2,1)S(1)}, bf16[128,1024]{1,0:T(8,128)(2,1)S(1)}, u32[]{:S(2)}, u32[]{:S(2)}) %collective-permute-start.8) | collective-permute-done | bytes 262176 | tf_op jit(solution)/shard_map/ppermute | solution.py:43
  49.9 1.3 %collective-permute-start.9 = (bf16[128,1024]{1,0:T(8,128)(2,1)S(1)}, bf16[128,1024]{1,0:T(8,128)(2,1)S(1)}, u32[]{:S(2)}, u32[]{:S(2)}) collective-permute-start(bf16[128,1024]{1,0:T(8,128)(2,1)S(1)} %collect.1), channel_id=1, source_target_pairs={{8,0},{10,2},{12,4},{14,6},{16,8},{18,10},{20,12},{22,14},{24,16},... | collective-permute-start | bytes 786440 | tf_op jit(solution)/shard_map/ppermute | solution.py:504
  51.3 3.7 %project.1 = bf16[256,1024]{1,0:T(8,128)(2,1)} custom-call(s32[1]{0:T(128)} %bitcast.core_ref.refs_1_, bf16[256,1024]{1,0:T(8,128)(2,1)S(1)} %get-tuple-element.39.own_ref, bf16[256,1024]{1,0:T(8,128)(2,1)S(1)} %collective-permute-done.5.other_ref, bf16[2048,2048]{1,0:T(8,128)(2,1)} %w_hbm.3), custom_call_target="tpu_custom_call" | custom-call | flops 1073741824 | bytes 6291456 | tf_op jit(solution)/shard_map/project/pallas_call | solution.py:161
  55.0 5.2 %collective-permute-done.9.last_ref = bf16[128,1024]{1,0:T(8,128)(2,1)S(1)} collective-permute-done((bf16[128,1024]{1,0:T(8,128)(2,1)S(1)}, bf16[128,1024]{1,0:T(8,128)(2,1)S(1)}, u32[]{:S(2)}, u32[]{:S(2)}) %collective-permute-start.9) | collective-permute-done | bytes 262176 | tf_op jit(solution)/shard_map/ppermute | solution.py:504
  60.2 1.3 %settle.1 = (bf16[256,1024]{1,0:T(8,128)(2,1)}, bf16[256,1024]{1,0:T(8,128)(2,1)}) custom-call(s32[1]{0:T(128)} %bitcast.1.me_ref.refs_0_, s32[1]{0:T(128)} %bitcast.core_ref.refs_1_, f32[256,1024]{1,0:T(8,128)S(1)} %get-tuple-element.41.gk_ref, f32[256,1024]{1,0:T(8,128)S(1)} %get-tuple-element.42.gv_ref, ...), custom_call_target="tpu_custom_call" | custom-call | tf_op jit(solution)/shard_map/settle/pallas_call | solution.py:444
  (19 shorter events, 0.4 us)
Async XLA Ops:
  0.6 7.2 %collective-permute-start = (bf16[256,1024]{1,0:T(8,128)(2,1)}, bf16[256,1024]{1,0:T(8,128)(2,1)}, u32[]{:S(2)}, u32[]{:S(2)}) collective-permute-start(bf16[256,1024]{1,0:T(8,128)(2,1)} %own_hbm.1), channel_id=1, source_target_pairs={{0,1},{1,0},{2,3},{3,2},{4,5},{5,4},{6,7},{7,6},{8,9},{9,8},{10,11... | collective-permute-start | bytes 1572872 | tf_op jit(solution)/shard_map/ppermute | solution.py:47
  3.3 12.0 %collective-permute-start.1 = (bf16[128,1024]{1,0:T(8,128)(2,1)}, bf16[128,1024]{1,0:T(8,128)(2,1)S(1)}, u32[]{:S(2)}, u32[]{:S(2)}) collective-permute-start(bf16[128,1024]{1,0:T(8,128)(2,1)} %pick.1.picked_ref), channel_id=1, source_target_pairs={{0,8},{2,10},{4,12},{6,14},{8,16},{10,18},{12,20},{14,22},{16,24},... | collective-permute-start | bytes 786440 | tf_op jit(solution)/shard_map/ppermute | solution.py:469
  7.9 1.0 %copy-start.3 = (bf16[128,1024]{1,0:T(8,128)(2,1)S(1)}, bf16[128,1024]{1,0:T(8,128)(2,1)}, u32[]{:S(2)}) copy-start(bf16[128,1024]{1,0:T(8,128)(2,1)} %pick.1.picked_ref) | copy-start | bytes 786436
  8.8 1.0 %copy-start.4 = (bf16[256,1024]{1,0:T(8,128)(2,1)S(1)}, bf16[256,1024]{1,0:T(8,128)(2,1)}, u32[]{:S(2)}) copy-start(bf16[256,1024]{1,0:T(8,128)(2,1)} %own_hbm.1) | copy-start | bytes 1572868
  9.9 15.9 %copy-start = (bf16[256,1024]{1,0:T(8,128)(2,1)S(1)}, bf16[256,1024]{1,0:T(8,128)(2,1)}, u32[]{:S(2)}) copy-start(bf16[256,1024]{1,0:T(8,128)(2,1)} %q_ref.3) | copy-start | bytes 1572868
  9.9 15.9 %copy-start.1 = (bf16[256,1024]{1,0:T(8,128)(2,1)S(1)}, bf16[256,1024]{1,0:T(8,128)(2,1)}, u32[]{:S(2)}) copy-start(bf16[256,1024]{1,0:T(8,128)(2,1)} %k_ref.3) | copy-start | bytes 1572868
  9.9 15.9 %copy-start.2 = (bf16[256,1024]{1,0:T(8,128)(2,1)S(1)}, bf16[256,1024]{1,0:T(8,128)(2,1)}, u32[]{:S(2)}) copy-start(bf16[256,1024]{1,0:T(8,128)(2,1)} %v_ref.3) | copy-start | bytes 1572868
  9.9 15.9 %copy-start.5 = (s32[4]{0:T(128)S(1)}, s32[4]{0:T(128)}, u32[]{:S(2)}) copy-start(s32[4]{0:T(128)} %bounds_ref.1) | copy-start | bytes 52
  15.4 7.7 %collective-permute-start.2 = (bf16[128,1024]{1,0:T(8,128)(2,1)S(1)}, bf16[128,1024]{1,0:T(8,128)(2,1)S(1)}, u32[]{:S(2)}, u32[]{:S(2)}) collective-permute-start(bf16[128,1024]{1,0:T(8,128)(2,1)S(1)} %get-tuple-element.33), channel_id=1, source_target_pairs={{0,8},{2,10},{4,12},{6,14},{8,16},{10,18},{12,20},{14,22},{16,24},... | collective-permute-start | bytes 786440 | tf_op jit(solution)/shard_map/ppermute | solution.py:43
  18.9 10.8 %collective-permute-start.3 = (bf16[128,1024]{1,0:T(8,128)(2,1)S(1)}, bf16[128,1024]{1,0:T(8,128)(2,1)S(1)}, u32[]{:S(2)}, u32[]{:S(2)}) collective-permute-start(bf16[128,1024]{1,0:T(8,128)(2,1)S(1)} %get-tuple-element.34), channel_id=1, source_target_pairs={{0,2},{2,4},{4,6},{6,0},{8,10},{10,12},{12,14},{14,8},{16,18},{18,... | collective-permute-start | bytes 786440 | tf_op jit(solution)/shard_map/ppermute | solution.py:43
  23.2 8.2 %collective-permute-start.4 = (bf16[128,1024]{1,0:T(8,128)(2,1)S(1)}, bf16[128,1024]{1,0:T(8,128)(2,1)S(1)}, u32[]{:S(2)}, u32[]{:S(2)}) collective-permute-start(bf16[128,1024]{1,0:T(8,128)(2,1)S(1)} %choose_last.1), channel_id=1, source_target_pairs={{0,4},{2,6},{4,0},{6,2},{8,12},{10,14},{12,8},{14,10},{16,20},{18,... | collective-permute-start | bytes 786440 | tf_op jit(solution)/shard_map/ppermute | solution.py:43
  34.5 6.9 %collective-permute-start.6 = (bf16[128,1024]{1,0:T(8,128)(2,1)S(1)}, bf16[128,1024]{1,0:T(8,128)(2,1)S(1)}, u32[]{:S(2)}, u32[]{:S(2)}) collective-permute-start(bf16[128,1024]{1,0:T(8,128)(2,1)S(1)} %get-tuple-element.44), channel_id=1, source_target_pairs={{4,0},{6,2},{0,4},{2,6},{12,8},{14,10},{8,12},{10,14},{20,16},{22,... | collective-permute-start | bytes 786440 | tf_op jit(solution)/shard_map/ppermute | solution.py:43
  36.8 8.3 %collective-permute-start.7 = (bf16[128,1024]{1,0:T(8,128)(2,1)S(1)}, bf16[128,1024]{1,0:T(8,128)(2,1)S(1)}, u32[]{:S(2)}, u32[]{:S(2)}) collective-permute-start(bf16[128,1024]{1,0:T(8,128)(2,1)S(1)} %get-tuple-element.45), channel_id=1, source_target_pairs={{2,0},{4,2},{6,4},{0,6},{10,8},{12,10},{14,12},{8,14},{18,16},{20,... | collective-permute-start | bytes 786440 | tf_op jit(solution)/shard_map/ppermute | solution.py:43
  41.4 9.9 %collective-permute-start.5 = (bf16[256,1024]{1,0:T(8,128)(2,1)S(1)}, bf16[256,1024]{1,0:T(8,128)(2,1)S(1)}, u32[]{:S(2)}, u32[]{:S(2)}) collective-permute-start(bf16[256,1024]{1,0:T(8,128)(2,1)S(1)} %get-tuple-element.39.own_ref), channel_id=1, source_target_pairs={{0,1},{1,0},{2,3},{3,2},{4,5},{5,4},{6,7},{7,6},{8,9},{9,8},{10,11... | collective-permute-start | bytes 1572872 | tf_op jit(solution)/shard_map/ppermute | solution.py:47
  41.5 8.3 %collective-permute-start.8 = (bf16[128,1024]{1,0:T(8,128)(2,1)S(1)}, bf16[128,1024]{1,0:T(8,128)(2,1)S(1)}, u32[]{:S(2)}, u32[]{:S(2)}) collective-permute-start(bf16[128,1024]{1,0:T(8,128)(2,1)S(1)} %add_convert_fusion), channel_id=1, source_target_pairs={{8,0},{10,2},{12,4},{14,6},{16,8},{18,10},{20,12},{22,14},{24,16},... | collective-permute-start | bytes 786440 | tf_op jit(solution)/shard_map/ppermute | solution.py:43
  49.9 10.2 %collective-permute-start.9 = (bf16[128,1024]{1,0:T(8,128)(2,1)S(1)}, bf16[128,1024]{1,0:T(8,128)(2,1)S(1)}, u32[]{:S(2)}, u32[]{:S(2)}) collective-permute-start(bf16[128,1024]{1,0:T(8,128)(2,1)S(1)} %collect.1), channel_id=1, source_target_pairs={{8,0},{10,2},{12,4},{14,6},{16,8},{18,10},{20,12},{22,14},{24,16},... | collective-permute-start | bytes 786440 | tf_op jit(solution)/shard_map/ppermute | solution.py:504

commit v10 on v9

--- a/solution.py
+++ b/solution.py
@@ -195,8 +195,8 @@
     return jnp.where(ok, 0.0, -jnp.inf).astype(F32)
 
 
-def sort_arrived(first, two, three, four, *more):
-    return [jnp.where(first, three, four), jnp.where(first, four, two), jnp.where(first, two, three), *more]
+def sort_arrived(first, two, three, *more):
+    return [jnp.where(first, three, two), jnp.where(first, two, three), *more]
 
 
 def distances(levels):
@@ -208,16 +208,17 @@
 
 
 def near_kernel(
-    levels, me_ref, bounds_ref, q_ref, k_ref, v_ref, ga_ref, far4_ref, grown_ref, gp_ref, stat_ref, bias_ref
+    levels, me_ref, bounds_ref, q_ref, k_ref, v_ref, ga_ref, far4_ref, far1_ref,
+    grown_ref, gp_ref, stat_ref, bias_ref,
 ):
     tokens = q_ref.shape[0]
     rows = tokens // STEP
-    near = tokens + rows
+    near = tokens + 2 * rows
     bias_ref[...] = mask_bias(me_ref[0], bounds_ref, tokens, distances(levels))
     for h in range(q_ref.shape[1] // DH):
         cols = slice(h * DH, (h + 1) * DH)
-        k = jnp.concatenate([k_ref[:, cols], far4_ref[:rows, cols]], 0)
-        v = jnp.concatenate([v_ref[:, cols], far4_ref[rows:, cols]], 0)
+        k = jnp.concatenate([k_ref[:, cols], far4_ref[:rows, cols], far1_ref[:rows, cols]], 0)
+        v = jnp.concatenate([v_ref[:, cols], far4_ref[rows:, cols], far1_ref[rows:, cols]], 0)
         scores = nt(k, q_ref[:, cols]) + bias_ref[:near]
         top = jnp.max(scores, axis=0, keepdims=True)
         grown = jnp.exp2((scores - top) * POWER)
@@ -229,14 +230,14 @@
         stat_ref[h, 2:3] = jnp.sum(grown * grad_prob, axis=0, keepdims=True)
 
 
-def attention_near(me, bounds, q, k, v, ga, far4, levels):
+def attention_near(me, bounds, q, k, v, ga, far4, far1, levels):
     tokens, width = q.shape
     heads, rows = width // DH, tokens // STEP
-    near, count = tokens + rows, tokens + levels * rows
+    near, count = tokens + 2 * rows, tokens + levels * rows
     early = jax.ShapeDtypeStruct((heads, near, tokens), F32)
     return pl.pallas_call(
         functools.partial(near_kernel, levels),
-        in_specs=[SMEM_BLOCK, SMEM_BLOCK] + [VMEM_BLOCK] * 5,
+        in_specs=[SMEM_BLOCK, SMEM_BLOCK] + [VMEM_BLOCK] * 6,
         out_specs=[VMEM_BLOCK] * 4,
         out_shape=[
             early,
@@ -249,17 +250,17 @@
             flops=4 * tokens * near * width, bytes_accessed=16 * tokens * width, transcendentals=0
         ),
         name="attention_near",
-    )(me, bounds, q, k, v, ga, far4)
+    )(me, bounds, q, k, v, ga, far4, far1)
 
 
 def far_kernel(levels, *refs):
     me_ref, core_ref, q_ref, ga_ref, grown_ref, gp_ref, stat_ref, bias_ref = refs[:8]
-    arrived_refs = refs[8 : 7 + levels]
-    w_ref, u_ref, use_ref, far_ref, pass_ref = refs[7 + levels : 12 + levels]
-    gfar_refs = refs[12 + levels :]
+    arrived_refs = refs[8 : 6 + levels]
+    w_ref, u_ref, use_ref, far_ref, pass_ref = refs[6 + levels : 11 + levels]
+    gfar_refs = refs[11 + levels :]
     tokens = q_ref.shape[0]
     rows = tokens // STEP
-    near = tokens + rows
+    near = tokens + 2 * rows
     first = core_ref[0] == 0
     passes = (core_ref[0] * (me_ref[0] % 2)).astype(F32)
     pass_ref[...] = jnp.full(pass_ref.shape, passes, F32)
@@ -302,7 +303,7 @@
 
 def attention_far(me, core, q, ga, grown, grad_prob, stats, bias, arrived):
     tokens, width = q.shape
-    levels = 1 + len(arrived)
+    levels = 2 + len(arrived)
     heads, rows = width // DH, tokens // STEP
     prob = jax.ShapeDtypeStruct((heads, levels * rows, tokens), BF16)
     return pl.pallas_call(
@@ -313,7 +314,7 @@
             prob,
             prob,
             jax.ShapeDtypeStruct(stats.shape, F32),
-            jax.ShapeDtypeStruct((2, (levels - 1) * rows, width), BF16),
+            jax.ShapeDtypeStruct((2, (levels - 2) * rows, width), BF16),
             jax.ShapeDtypeStruct((1, width), F32),
         ]
         + [jax.ShapeDtypeStruct((2 * rows, width), BF16)] * levels,
@@ -326,15 +327,19 @@
 
 
 def local_kernel(
-    q_ref, k_ref, v_ref, ga_ref, far4_ref, far_ref, grown_ref, gp_ref, use_ref, w_ref, u_ref,
+    q_ref, k_ref, v_ref, ga_ref, far4_ref, far1_ref, far_ref, grown_ref, gp_ref, use_ref, w_ref, u_ref,
     attn_ref, gq_ref, gk_ref, gv_ref,
 ):
     tokens = q_ref.shape[0]
     rows = tokens // STEP
     for h in range(q_ref.shape[1] // DH):
         cols = slice(h * DH, (h + 1) * DH)
-        k = jnp.concatenate([k_ref[:, cols], far4_ref[:rows, cols], far_ref[0, :, cols]], 0)
-        v = jnp.concatenate([v_ref[:, cols], far4_ref[rows:, cols], far_ref[1, :, cols]], 0)
+        k = jnp.concatenate(
+            [k_ref[:, cols], far4_ref[:rows, cols], far1_ref[:rows, cols], far_ref[0, :, cols]], 0
+        )
+        v = jnp.concatenate(
+            [v_ref[:, cols], far4_ref[rows:, cols], far1_ref[rows:, cols], far_ref[1, :, cols]], 0
+        )
         prob = grown_ref[h, :tokens] * use_ref[h, 0:1]
         near_weights = prob.astype(BF16)
         near_scores = (prob * (gp_ref[h, :tokens] - use_ref[h, 1:2])).astype(BF16)
@@ -381,18 +386,10 @@
 
 def choose_kernel(me_ref, core_ref, picked_ref, far4_ref, two_ref, three_ref):
     first = core_ref[0] == 0
-    own1, own2 = lends_own(me_ref[0])
     picked, far4 = picked_ref[...], far4_ref[...]
-    two_ref[...] = jnp.where(first, far4, jnp.where(own2, picked, far4))
-    three_ref[...] = jnp.where(first, jnp.where(own1, picked, far4), far4)
-
-
-def choose_last_kernel(me_ref, core_ref, picked_ref, far4_ref, two_ref, out_ref):
-    first = core_ref[0] == 0
-    own2 = lends_own(me_ref[0])[1]
-    picked = picked_ref[...]
-    ahead = jnp.where(own2, picked, far4_ref[...])
-    out_ref[...] = jnp.where(first, ahead, jnp.where(me_ref[0] % 2 == 0, picked, two_ref[...]))
+    lent = jnp.where(lends_own(me_ref[0])[1], picked, far4)
+    two_ref[...] = jnp.where(first, far4, lent)
+    three_ref[...] = jnp.where(first, lent, far4)
 
 
 def include(total, block, use):
@@ -467,21 +464,23 @@
     other_cot = swap(cotangent)
     picked = pick(keys, values)
     far4 = lax.ppermute(picked, "ctx", hop(4, n))
+    far1 = lax.ppermute(picked, "ctx", hop(1, n))
     ga, picked = grad_attn(core, cotangent, other_cot, picked, out_weight)
 
-    hops, ones, twos, nexts = hop(4, n), steps(n), pairs(n), neighbours(n)
+    hops, twos = hop(4, n), pairs(n)
     two, three = small(choose_kernel, "choose", 2, me, core, picked, far4)
     two = mixed(two, (hops, twos))
-    three = mixed(three, (ones, hops))
-    four = mixed(small(choose_last_kernel, "choose_last", 1, me, core, picked, far4, two), (twos, nexts))
+    three = mixed(three, (twos, hops))
+    arrived = [two, three]
     first = lax.axis_index("head") == 0 if levels > 4 else None
-    arrived = [two, three, four]
     farther = jnp.where(first, two, three) if levels > 4 else None
     for i in range(4, levels):
         farther = lax.ppermute(farther, "ctx", hop(2 ** (i - 1), n))
         arrived.append(farther)
 
-    grown, grad_prob, stats, bias = attention_near(me, bounds, queries, keys, values, ga, far4, levels)
+    grown, grad_prob, stats, bias = attention_near(
+        me, bounds, queries, keys, values, ga, far4, far1, levels
+    )
     weights, grad_scores, use, far, passes, g4, two, three, four, *more = attention_far(
         me, core, queries, ga, grown, grad_prob, stats, bias, arrived
     )
@@ -492,12 +491,12 @@
         else:
             three = jnp.where(first, three, add(three, back))
             four = jnp.where(first, add(four, back), four)
-    hops, ones, twos = hop(-4, n), turned(ones), turned(twos)
+    hops, ones, twos, nexts = hop(-4, n), turned(steps(n)), turned(twos), neighbours(n)
     one = mixed(two, (twos, nexts))
     two = mixed(three, (ones, hops))
     three = mixed((four.astype(F32) + one.astype(F32) * passes).astype(BF16), (hops, twos))
     attn, gq, gk, gv = attention_local(
-        queries, keys, values, ga, far4, far, grown, grad_prob, use, weights, grad_scores
+        queries, keys, values, ga, far4, far1, far, grown, grad_prob, use, weights, grad_scores
     )
     back = (one, two, three)
     g4 = small(collect_kernel, "collect", 1, me, core, g4, *back)

time: 61.8 us -> 61 us (0.987)
  waiting for transfers between devices: 16.6 us -> 14.3 us
  starting transfers between devices: 21.4 us -> 22.9 us
    ppermute x0 -> x1, starting transfers between devices: none -> 3.41 us  [per_device(): far1 = lax.ppermute(picked, 'ctx', hop(1, n))]
    ppermute x6 -> x5, starting transfers between devices: 15.1 us -> 13.1 us  [mixed(): return lax.ppermute(block, ('ctx', 'head'), route)]
    ppermute x6 -> x5, waiting for transfers between devices: 11.4 us -> 9.62 us  [mixed(): return lax.ppermute(block, ('ctx', 'head'), route)]
  transfers between devices with their start and end apart: 10 -> 10, of which waited for: 6 -> 4; matrix products, arithmetic and copies ran while one was open for 0% -> 0% of each run, Pallas kernels for 26% -> 27%
where the time goes in v10:
time: 61 us; the launch traced here: 60.6 us
  starting transfers between devices  22.9 us (38%)
  Pallas kernels  20.5 us (34%)
  waiting for transfers between devices  14.3 us (23%)
  local copies, waits for them, and re-layouts  2.02 us (3%)
  between operations  0.83 us (1%)
    ppermute x5, starting transfers between devices, mixed(): return lax.ppermute(block, ('ctx', 'head'), route)  13.1 us
    ppermute x5, waiting for transfers between devices, mixed(): return lax.ppermute(block, ('ctx', 'head'), route)  9.62 us
    pallas_call x1, Pallas kernels, grad_attn(): pl.pallas_call(grad_attn_kernel, in_specs=[SMEM_BLOCK, HBM_BLOCK, HBM_BLO...  5.41 us
    ppermute x1, waiting for transfers between devices, per_device(): last = lax.ppermute(g4, 'ctx', hop(-4, n))  4.71 us
    ppermute x1, starting transfers between devices, per_device(): far4 = lax.ppermute(picked, 'ctx', hop(4, n))  4.51 us
    pallas_call x1, Pallas kernels, project(): pl.pallas_call(project_kernel, in_specs=[SMEM_BLOCK, VMEM_BLOCK, VMEM_BLO...  3.73 us
    ppermute x1, starting transfers between devices, per_device(): far1 = lax.ppermute(picked, 'ctx', hop(1, n))  3.41 us
    pallas_call x1, Pallas kernels, attention_far(): pl.pallas_call(functools.partial(far_kernel, levels), in_specs=[SMEM_BLOC...  2.78 us
  transfers between devices with their start and end apart: 10, of which 4 were waited for; matrix products, arithmetic and copies ran while one was open for 0% of the time, Pallas kernels for 27%

profile of v10, /device:TPU:0, one launch (start us, length us, event | category | flops | bytes accessed | tf_op | source)
XLA Modules:
  0.0 60.6 jit_solution(2051961028016181028)
XLA Ops:
  0.6 0.5 collective-permute-start
  1.1 2.2 %pick.1.picked_ref = bf16[128,1024]{1,0:T(8,128)(2,1)} custom-call(bf16[256,1024]{1,0:T(8,128)(2,1)} %k_ref.3, bf16[256,1024]{1,0:T(8,128)(2,1)} %v_ref.3), custom_call_target="tpu_custom_call" | custom-call | tf_op jit(solution)/shard_map/pick/pallas_call | solution.py:81
  3.3 4.5 %collective-permute-start.1 = (bf16[128,1024]{1,0:T(8,128)(2,1)}, bf16[128,1024]{1,0:T(8,128)(2,1)S(1)}, u32[]{:S(2)}, u32[]{:S(2)}) collective-permute-start(bf16[128,1024]{1,0:T(8,128)(2,1)} %pick.1.picked_ref), channel_id=1, source_target_pairs={{0,8},{2,10},{4,12},{6,14},{8,16},{10,18},{12,20},{14,22},{16,24},... | collective-permute-start | bytes 786440 | tf_op jit(solution)/shard_map/ppermute | solution.py:466
  7.9 3.4 %collective-permute-start.2 = (bf16[128,1024]{1,0:T(8,128)(2,1)}, bf16[128,1024]{1,0:T(8,128)(2,1)S(1)}, u32[]{:S(2)}, u32[]{:S(2)}) collective-permute-start(bf16[128,1024]{1,0:T(8,128)(2,1)} %pick.1.picked_ref), channel_id=1, source_target_pairs={{0,2},{2,4},{4,6},{6,8},{8,10},{10,12},{12,14},{14,16},{16,18},{18... | collective-permute-start | bytes 786440 | tf_op jit(solution)/shard_map/ppermute | solution.py:467
  11.3 1.0 %copy-done.3 = bf16[128,1024]{1,0:T(8,128)(2,1)S(1)} copy-done((bf16[128,1024]{1,0:T(8,128)(2,1)S(1)}, bf16[128,1024]{1,0:T(8,128)(2,1)}, u32[]{:S(2)}) %copy-start.3) | copy-done | bytes 262168
  12.3 1.0 %copy-done.4 = bf16[256,1024]{1,0:T(8,128)(2,1)S(1)} copy-done((bf16[256,1024]{1,0:T(8,128)(2,1)S(1)}, bf16[256,1024]{1,0:T(8,128)(2,1)}, u32[]{:S(2)}) %copy-start.4) | copy-done | bytes 524312
  13.3 5.4 %grad_attn.1 = (bf16[256,1024]{1,0:T(8,128)(2,1)S(1)}, bf16[128,1024]{1,0:T(8,128)(2,1)S(1)}) custom-call(s32[1]{0:T(128)} %bitcast.core_ref.refs_1_, bf16[256,1024]{1,0:T(8,128)(2,1)S(1)} %copy-done.4, bf16[256,1024]{1,0:T(8,128)(2,1)} %collective-permute-done.other_hbm, bf16[128,1024]{1,0:T(8,128)(2,1)S(1)} %copy-done.3, bf16[2048,2048]{1,0:T(8,128)(2,1)} %w_hbm.3), custom_call_target="tpu_custom_call" | custom-call | flops 1073741824 | bytes 6291456 | tf_op jit(solution)/shard_map/grad_attn/pallas_call | solution.py:117
  18.8 3.5 %collective-permute-start.3 = (bf16[128,1024]{1,0:T(8,128)(2,1)S(1)}, bf16[128,1024]{1,0:T(8,128)(2,1)S(1)}, u32[]{:S(2)}, u32[]{:S(2)}) collective-permute-start(bf16[128,1024]{1,0:T(8,128)(2,1)S(1)} %get-tuple-element.33), channel_id=1, source_target_pairs={{0,8},{2,10},{4,12},{6,14},{8,16},{10,18},{12,20},{14,22},{16,24},... | collective-permute-start | bytes 786440 | tf_op jit(solution)/shard_map/ppermute | solution.py:43
  22.3 3.4 %collective-permute-start.4 = (bf16[128,1024]{1,0:T(8,128)(2,1)S(1)}, bf16[128,1024]{1,0:T(8,128)(2,1)S(1)}, u32[]{:S(2)}, u32[]{:S(2)}) collective-permute-start(bf16[128,1024]{1,0:T(8,128)(2,1)S(1)} %get-tuple-element.34), channel_id=1, source_target_pairs={{0,4},{2,6},{4,0},{6,2},{8,12},{10,14},{12,8},{14,10},{16,20},{18,... | collective-permute-start | bytes 786440 | tf_op jit(solution)/shard_map/ppermute | solution.py:43
  25.8 2.1 %attention_near.1 = (f32[8,384,256]{2,1,0:T(8,128)S(1)}, f32[8,384,256]{2,1,0:T(8,128)S(1)}, f32[8,8,256]{2,1,0:T(8,128)S(1)}, f32[512,256]{1,0:T(8,128)S(1)}) custom-call(s32[1]{0:T(128)} %bitcast.1.me_ref.refs_0_, s32[4]{0:T(128)S(1)} %copy-done.5, bf16[256,1024]{1,0:T(8,128)(2,1)S(1)} %copy-done, bf16[256,1024]{1,0:T(8,128)(2,1)S(1)} %copy-done.1, ...), custom_call_target="tpu_custom_call" | custom-call | flops 402653184 | bytes 4194304 | tf_op jit(solution)/shard_map/attention_near/pallas_call | solution.py:238
  27.9 2.6 %collective-permute-done.4.refs_9_ = bf16[128,1024]{1,0:T(8,128)(2,1)S(1)} collective-permute-done((bf16[128,1024]{1,0:T(8,128)(2,1)S(1)}, bf16[128,1024]{1,0:T(8,128)(2,1)S(1)}, u32[]{:S(2)}, u32[]{:S(2)}) %collective-permute-start.4) | collective-permute-done | bytes 262176 | tf_op jit(solution)/shard_map/ppermute | solution.py:43
  30.6 2.8 %attention_far.1 = (bf16[8,256,256]{2,1,0:T(8,128)(2,1)S(1)}, bf16[8,256,256]{2,1,0:T(8,128)(2,1)S(1)}, f32[8,8,256]{2,1,0:T(8,128)S(1)}, bf16[2,128,1024]{2,1,0...) custom-call(s32[1]{0:T(128)} %bitcast.1.me_ref.refs_0_, ...), custom_call_target="tpu_custom_call" | custom-call | flops 536870912 | bytes 4194304 | tf_op jit(solution)/shard_map/attention_far/pallas_call | solution.py:309
  33.4 1.6 %collective-permute-start.6 = (bf16[128,1024]{1,0:T(8,128)(2,1)S(1)}, bf16[128,1024]{1,0:T(8,128)(2,1)S(1)}, u32[]{:S(2)}, u32[]{:S(2)}) collective-permute-start(bf16[128,1024]{1,0:T(8,128)(2,1)S(1)} %get-tuple-element.44), channel_id=1, source_target_pairs={{4,0},{6,2},{0,4},{2,6},{12,8},{14,10},{8,12},{10,14},{20,16},{22,... | collective-permute-start | bytes 786440 | tf_op jit(solution)/shard_map/ppermute | solution.py:43
  35.0 3.3 %collective-permute-start.7 = (bf16[128,1024]{1,0:T(8,128)(2,1)S(1)}, bf16[128,1024]{1,0:T(8,128)(2,1)S(1)}, u32[]{:S(2)}, u32[]{:S(2)}) collective-permute-start(bf16[128,1024]{1,0:T(8,128)(2,1)S(1)} %get-tuple-element.45), channel_id=1, source_target_pairs={{2,0},{4,2},{6,4},{0,6},{10,8},{12,10},{14,12},{8,14},{18,16},{20,... | collective-permute-start | bytes 786440 | tf_op jit(solution)/shard_map/ppermute | solution.py:43
  38.3 2.7 %attention_local.1 = (bf16[256,1024]{1,0:T(8,128)(2,1)S(1)}, bf16[256,1024]{1,0:T(8,128)(2,1)}, f32[256,1024]{1,0:T(8,128)S(1)}, f32[256,1024]{1,0:T(8,128)S(1)}) custom-call(bf16[256,1024]{1,0:T(8,128)(2,1)S(1)} %copy-done, bf16[256,1024]{1,0:T(8,128)(2,1)S(1)} %copy-done.1, bf16[256,1024]{1,0:T(8,128)(2,1)S(1)} %copy-done.2, ...), custom_call_target="tpu_custom_call" | custom-call | flops 805306368 | bytes 4194304 | tf_op jit(solution)/shard_map/attention_local/pallas_call | solution.py:358
  41.0 0.1 add_convert_fusion
  41.1 1.3 %collective-permute-start.8 = (bf16[128,1024]{1,0:T(8,128)(2,1)S(1)}, bf16[128,1024]{1,0:T(8,128)(2,1)S(1)}, u32[]{:S(2)}, u32[]{:S(2)}) collective-permute-start(bf16[128,1024]{1,0:T(8,128)(2,1)S(1)} %add_convert_fusion), channel_id=1, source_target_pairs={{8,0},{10,2},{12,4},{14,6},{16,8},{18,10},{20,12},{22,14},{24,16},... | collective-permute-start | bytes 786440 | tf_op jit(solution)/shard_map/ppermute | solution.py:43
  42.4 0.8 %collective-permute-done.7.two_ref = bf16[128,1024]{1,0:T(8,128)(2,1)S(1)} collective-permute-done((bf16[128,1024]{1,0:T(8,128)(2,1)S(1)}, bf16[128,1024]{1,0:T(8,128)(2,1)S(1)}, u32[]{:S(2)}, u32[]{:S(2)}) %collective-permute-start.7) | collective-permute-done | bytes 262176 | tf_op jit(solution)/shard_map/ppermute | solution.py:43
  43.2 6.1 %collective-permute-done.8.three_ref = bf16[128,1024]{1,0:T(8,128)(2,1)S(1)} collective-permute-done((bf16[128,1024]{1,0:T(8,128)(2,1)S(1)}, bf16[128,1024]{1,0:T(8,128)(2,1)S(1)}, u32[]{:S(2)}, u32[]{:S(2)}) %collective-permute-start.8) | collective-permute-done | bytes 262176 | tf_op jit(solution)/shard_map/ppermute | solution.py:43
  49.3 0.2 collect.1
  49.5 1.3 %collective-permute-start.9 = (bf16[128,1024]{1,0:T(8,128)(2,1)S(1)}, bf16[128,1024]{1,0:T(8,128)(2,1)S(1)}, u32[]{:S(2)}, u32[]{:S(2)}) collective-permute-start(bf16[128,1024]{1,0:T(8,128)(2,1)S(1)} %collect.1), channel_id=1, source_target_pairs={{8,0},{10,2},{12,4},{14,6},{16,8},{18,10},{20,12},{22,14},{24,16},... | collective-permute-start | bytes 786440 | tf_op jit(solution)/shard_map/ppermute | solution.py:503
  50.8 3.7 %project.1 = bf16[256,1024]{1,0:T(8,128)(2,1)} custom-call(s32[1]{0:T(128)} %bitcast.core_ref.refs_1_, bf16[256,1024]{1,0:T(8,128)(2,1)S(1)} %get-tuple-element.39.own_ref, bf16[256,1024]{1,0:T(8,128)(2,1)S(1)} %collective-permute-done.5.other_ref, bf16[2048,2048]{1,0:T(8,128)(2,1)} %w_hbm.3), custom_call_target="tpu_custom_call" | custom-call | flops 1073741824 | bytes 6291456 | tf_op jit(solution)/shard_map/project/pallas_call | solution.py:161
  54.6 4.7 %collective-permute-done.9.last_ref = bf16[128,1024]{1,0:T(8,128)(2,1)S(1)} collective-permute-done((bf16[128,1024]{1,0:T(8,128)(2,1)S(1)}, bf16[128,1024]{1,0:T(8,128)(2,1)S(1)}, u32[]{:S(2)}, u32[]{:S(2)}) %collective-permute-start.9) | collective-permute-done | bytes 262176 | tf_op jit(solution)/shard_map/ppermute | solution.py:503
  59.3 1.3 %settle.1 = (bf16[256,1024]{1,0:T(8,128)(2,1)}, bf16[256,1024]{1,0:T(8,128)(2,1)}) custom-call(s32[1]{0:T(128)} %bitcast.1.me_ref.refs_0_, s32[1]{0:T(128)} %bitcast.core_ref.refs_1_, f32[256,1024]{1,0:T(8,128)S(1)} %get-tuple-element.41.gk_ref, f32[256,1024]{1,0:T(8,128)S(1)} %get-tuple-element.42.gv_ref, ...), custom_call_target="tpu_custom_call" | custom-call | tf_op jit(solution)/shard_map/settle/pallas_call | solution.py:441
  (18 shorter events, 0.1 us)
Async XLA Ops:
  0.6 10.7 %collective-permute-start = (bf16[256,1024]{1,0:T(8,128)(2,1)}, bf16[256,1024]{1,0:T(8,128)(2,1)}, u32[]{:S(2)}, u32[]{:S(2)}) collective-permute-start(bf16[256,1024]{1,0:T(8,128)(2,1)} %own_hbm.1), channel_id=1, source_target_pairs={{0,1},{1,0},{2,3},{3,2},{4,5},{5,4},{6,7},{7,6},{8,9},{9,8},{10,11... | collective-permute-start | bytes 1572872 | tf_op jit(solution)/shard_map/ppermute | solution.py:47
  3.3 15.4 %collective-permute-start.1 = (bf16[128,1024]{1,0:T(8,128)(2,1)}, bf16[128,1024]{1,0:T(8,128)(2,1)S(1)}, u32[]{:S(2)}, u32[]{:S(2)}) collective-permute-start(bf16[128,1024]{1,0:T(8,128)(2,1)} %pick.1.picked_ref), channel_id=1, source_target_pairs={{0,8},{2,10},{4,12},{6,14},{8,16},{10,18},{12,20},{14,22},{16,24},... | collective-permute-start | bytes 786440 | tf_op jit(solution)/shard_map/ppermute | solution.py:466
  7.9 17.9 %collective-permute-start.2 = (bf16[128,1024]{1,0:T(8,128)(2,1)}, bf16[128,1024]{1,0:T(8,128)(2,1)S(1)}, u32[]{:S(2)}, u32[]{:S(2)}) collective-permute-start(bf16[128,1024]{1,0:T(8,128)(2,1)} %pick.1.picked_ref), channel_id=1, source_target_pairs={{0,2},{2,4},{4,6},{6,8},{8,10},{10,12},{12,14},{14,16},{16,18},{18... | collective-permute-start | bytes 786440 | tf_op jit(solution)/shard_map/ppermute | solution.py:467
  11.3 1.0 %copy-start.3 = (bf16[128,1024]{1,0:T(8,128)(2,1)S(1)}, bf16[128,1024]{1,0:T(8,128)(2,1)}, u32[]{:S(2)}) copy-start(bf16[128,1024]{1,0:T(8,128)(2,1)} %pick.1.picked_ref) | copy-start | bytes 786436
  12.3 1.0 %copy-start.4 = (bf16[256,1024]{1,0:T(8,128)(2,1)S(1)}, bf16[256,1024]{1,0:T(8,128)(2,1)}, u32[]{:S(2)}) copy-start(bf16[256,1024]{1,0:T(8,128)(2,1)} %own_hbm.1) | copy-start | bytes 1572868
  13.3 12.5 %copy-start = (bf16[256,1024]{1,0:T(8,128)(2,1)S(1)}, bf16[256,1024]{1,0:T(8,128)(2,1)}, u32[]{:S(2)}) copy-start(bf16[256,1024]{1,0:T(8,128)(2,1)} %q_ref.3) | copy-start | bytes 1572868
  13.3 12.5 %copy-start.1 = (bf16[256,1024]{1,0:T(8,128)(2,1)S(1)}, bf16[256,1024]{1,0:T(8,128)(2,1)}, u32[]{:S(2)}) copy-start(bf16[256,1024]{1,0:T(8,128)(2,1)} %k_ref.3) | copy-start | bytes 1572868
  13.3 12.5 %copy-start.2 = (bf16[256,1024]{1,0:T(8,128)(2,1)S(1)}, bf16[256,1024]{1,0:T(8,128)(2,1)}, u32[]{:S(2)}) copy-start(bf16[256,1024]{1,0:T(8,128)(2,1)} %v_ref.3) | copy-start | bytes 1572868
  13.3 12.5 %copy-start.5 = (s32[4]{0:T(128)S(1)}, s32[4]{0:T(128)}, u32[]{:S(2)}) copy-start(s32[4]{0:T(128)} %bounds_ref.1) | copy-start | bytes 52
  18.8 9.1 %collective-permute-start.3 = (bf16[128,1024]{1,0:T(8,128)(2,1)S(1)}, bf16[128,1024]{1,0:T(8,128)(2,1)S(1)}, u32[]{:S(2)}, u32[]{:S(2)}) collective-permute-start(bf16[128,1024]{1,0:T(8,128)(2,1)S(1)} %get-tuple-element.33), channel_id=1, source_target_pairs={{0,8},{2,10},{4,12},{6,14},{8,16},{10,18},{12,20},{14,22},{16,24},... | collective-permute-start | bytes 786440 | tf_op jit(solution)/shard_map/ppermute | solution.py:43
  22.3 8.3 %collective-permute-start.4 = (bf16[128,1024]{1,0:T(8,128)(2,1)S(1)}, bf16[128,1024]{1,0:T(8,128)(2,1)S(1)}, u32[]{:S(2)}, u32[]{:S(2)}) collective-permute-start(bf16[128,1024]{1,0:T(8,128)(2,1)S(1)} %get-tuple-element.34), channel_id=1, source_target_pairs={{0,4},{2,6},{4,0},{6,2},{8,12},{10,14},{12,8},{14,10},{16,20},{18,... | collective-permute-start | bytes 786440 | tf_op jit(solution)/shard_map/ppermute | solution.py:43
  33.4 7.6 %collective-permute-start.6 = (bf16[128,1024]{1,0:T(8,128)(2,1)S(1)}, bf16[128,1024]{1,0:T(8,128)(2,1)S(1)}, u32[]{:S(2)}, u32[]{:S(2)}) collective-permute-start(bf16[128,1024]{1,0:T(8,128)(2,1)S(1)} %get-tuple-element.44), channel_id=1, source_target_pairs={{4,0},{6,2},{0,4},{2,6},{12,8},{14,10},{8,12},{10,14},{20,16},{22,... | collective-permute-start | bytes 786440 | tf_op jit(solution)/shard_map/ppermute | solution.py:43
  35.0 8.3 %collective-permute-start.7 = (bf16[128,1024]{1,0:T(8,128)(2,1)S(1)}, bf16[128,1024]{1,0:T(8,128)(2,1)S(1)}, u32[]{:S(2)}, u32[]{:S(2)}) collective-permute-start(bf16[128,1024]{1,0:T(8,128)(2,1)S(1)} %get-tuple-element.45), channel_id=1, source_target_pairs={{2,0},{4,2},{6,4},{0,6},{10,8},{12,10},{14,12},{8,14},{18,16},{20,... | collective-permute-start | bytes 786440 | tf_op jit(solution)/shard_map/ppermute | solution.py:43
  41.0 9.9 %collective-permute-start.5 = (bf16[256,1024]{1,0:T(8,128)(2,1)S(1)}, bf16[256,1024]{1,0:T(8,128)(2,1)S(1)}, u32[]{:S(2)}, u32[]{:S(2)}) collective-permute-start(bf16[256,1024]{1,0:T(8,128)(2,1)S(1)} %get-tuple-element.39.own_ref), channel_id=1, source_target_pairs={{0,1},{1,0},{2,3},{3,2},{4,5},{5,4},{6,7},{7,6},{8,9},{9,8},{10,11... | collective-permute-start | bytes 1572872 | tf_op jit(solution)/shard_map/ppermute | solution.py:47
  41.1 8.3 %collective-permute-start.8 = (bf16[128,1024]{1,0:T(8,128)(2,1)S(1)}, bf16[128,1024]{1,0:T(8,128)(2,1)S(1)}, u32[]{:S(2)}, u32[]{:S(2)}) collective-permute-start(bf16[128,1024]{1,0:T(8,128)(2,1)S(1)} %add_convert_fusion), channel_id=1, source_target_pairs={{8,0},{10,2},{12,4},{14,6},{16,8},{18,10},{20,12},{22,14},{24,16},... | collective-permute-start | bytes 786440 | tf_op jit(solution)/shard_map/ppermute | solution.py:43
  49.5 9.8 %collective-permute-start.9 = (bf16[128,1024]{1,0:T(8,128)(2,1)S(1)}, bf16[128,1024]{1,0:T(8,128)(2,1)S(1)}, u32[]{:S(2)}, u32[]{:S(2)}) collective-permute-start(bf16[128,1024]{1,0:T(8,128)(2,1)S(1)} %collect.1), channel_id=1, source_target_pairs={{8,0},{10,2},{12,4},{14,6},{16,8},{18,10},{20,12},{22,14},{24,16},... | collective-permute-start | bytes 786440 | tf_op jit(solution)/shard_map/ppermute | solution.py:503

commit v11 on v10

--- a/solution.py
+++ b/solution.py
@@ -88,44 +88,40 @@
     )(keys, values)
 
 
-def grad_attn_kernel(
-    core_ref, own_hbm, other_hbm, picked_ref, w_hbm, out_ref, handed_ref, cot, held, cot_sems, sems
-):
+def grad_attn_kernel(core_ref, own_ref, other_hbm, w_hbm, out_ref, done_ref, got, held, got_sem, sems):
     pieces, tile, _ = held.shape
-    width = own_hbm.shape[1]
     core = core_ref[0]
+    fetch = pltpu.make_async_copy(other_hbm, got, got_sem)
+    fetch.start()
     copies = []
-    for source, at, i in ((own_hbm, core, 0), (other_hbm, 1 - core, 1)):
-        columns = pl.ds(pl.multiple_of(at * width, width), width)
-        copies.append(pltpu.make_async_copy(source, cot.at[:, columns], cot_sems.at[i]))
     for i in range(pieces):
         rows = w_hbm.at[pl.ds((core * pieces + i) * tile, tile), :]
         copies.append(pltpu.make_async_copy(rows, held.at[i], sems.at[i]))
-    for copy in copies:
-        copy.start()
-    handed_ref[...] = picked_ref[...]
-    copies[0].wait()
-    copies[1].wait()
+        copies[i].start()
+    done_ref[...] = jnp.zeros_like(done_ref)
+    fetch.wait()
+    own, other = own_ref[...], got[...]
+    cot = jnp.concatenate([jnp.where(core == 0, own, other), jnp.where(core == 0, other, own)], 1)
     for i in range(pieces):
-        copies[2 + i].wait()
-        out_ref[:, i * tile : (i + 1) * tile] = nt(cot[...], held[i]).astype(BF16)
-
-
-def grad_attn(core, own, other, picked, weight):
+        copies[i].wait()
+        out_ref[:, i * tile : (i + 1) * tile] = nt(cot, held[i]).astype(BF16)
+
+
+def grad_attn(core, own, other, weight):
     tokens, width = own.shape
     pieces = 4
     return pl.pallas_call(
         grad_attn_kernel,
-        in_specs=[SMEM_BLOCK, HBM_BLOCK, HBM_BLOCK, VMEM_BLOCK, HBM_BLOCK],
+        in_specs=[SMEM_BLOCK, VMEM_BLOCK, HBM_BLOCK, HBM_BLOCK],
         out_specs=[VMEM_BLOCK] * 2,
         out_shape=[
             jax.ShapeDtypeStruct((tokens, width), BF16),
-            jax.ShapeDtypeStruct(picked.shape, BF16),
+            jax.ShapeDtypeStruct((8, DH), F32),
         ],
         scratch_shapes=[
-            pltpu.VMEM((tokens, weight.shape[1]), BF16),
+            pltpu.VMEM((tokens, width), BF16),
             pltpu.VMEM((pieces, width // pieces, weight.shape[1]), BF16),
-            pltpu.SemaphoreType.DMA((2,)),
+            pltpu.SemaphoreType.DMA,
             pltpu.SemaphoreType.DMA((pieces,)),
         ],
         compiler_params=params(52),
@@ -133,7 +129,7 @@
             flops=4 * tokens * width * width, bytes_accessed=6 * width * width, transcendentals=0
         ),
         name="grad_attn",
-    )(core, own, other, picked, weight)
+    )(core, own, other, weight)
 
 
 def project_kernel(core_ref, own_ref, other_ref, w_hbm, out_ref, held, sems):
@@ -384,7 +380,7 @@
     return first & jnp.logical_not(own2), rest | jnp.logical_not(own1), first | jnp.logical_not(own2)
 
 
-def choose_kernel(me_ref, core_ref, picked_ref, far4_ref, two_ref, three_ref):
+def choose_kernel(me_ref, core_ref, picked_ref, far4_ref, after, two_ref, three_ref):
     first = core_ref[0] == 0
     picked, far4 = picked_ref[...], far4_ref[...]
     lent = jnp.where(lends_own(me_ref[0])[1], picked, far4)
@@ -465,10 +461,10 @@
     picked = pick(keys, values)
     far4 = lax.ppermute(picked, "ctx", hop(4, n))
     far1 = lax.ppermute(picked, "ctx", hop(1, n))
-    ga, picked = grad_attn(core, cotangent, other_cot, picked, out_weight)
+    ga, done = grad_attn(core, cotangent, other_cot, out_weight)
 
     hops, twos = hop(4, n), pairs(n)
-    two, three = small(choose_kernel, "choose", 2, me, core, picked, far4)
+    two, three = small(choose_kernel, "choose", 2, me, core, picked, far4, done)
     two = mixed(two, (hops, twos))
     three = mixed(three, (twos, hops))
     arrived = [two, three]

time: 61 us -> 59.8 us (0.980)
  local copies, waits for them, and re-layouts: 2.02 us -> 1.06 us
    unnamed x12, local copies, waits for them, and re-layouts: 2.02 us -> 1.06 us
where the time goes in v11:
time: 59.8 us; the launch traced here: 59.5 us
  starting transfers between devices  22.8 us (38%)
  Pallas kernels  20.3 us (34%)
  waiting for transfers between devices  14.3 us (24%)
  local copies, waits for them, and re-layouts  1.06 us (2%)
  between operations  0.84 us (1%)
    ppermute x5, starting transfers between devices, mixed(): return lax.ppermute(block, ('ctx', 'head'), route)  13.1 us
    ppermute x5, waiting for transfers between devices, mixed(): return lax.ppermute(block, ('ctx', 'head'), route)  9.61 us
    pallas_call x1, Pallas kernels, grad_attn(): pl.pallas_call(grad_attn_kernel, in_specs=[SMEM_BLOCK, VMEM_BLOCK, HBM_BL...  5.23 us
    ppermute x1, waiting for transfers between devices, per_device(): last = lax.ppermute(g4, 'ctx', hop(-4, n))  4.71 us
    ppermute x1, starting transfers between devices, per_device(): far4 = lax.ppermute(picked, 'ctx', hop(4, n))  4.51 us
    pallas_call x1, Pallas kernels, project(): pl.pallas_call(project_kernel, in_specs=[SMEM_BLOCK, VMEM_BLOCK, VMEM_BLO...  3.73 us
    ppermute x1, starting transfers between devices, per_device(): far1 = lax.ppermute(picked, 'ctx', hop(1, n))  3.41 us
    pallas_call x1, Pallas kernels, attention_far(): pl.pallas_call(functools.partial(far_kernel, levels), in_specs=[SMEM_BLOC...  2.78 us
  transfers between devices with their start and end apart: 10, of which 4 were waited for; matrix products, arithmetic and copies ran while one was open for 0% of the time, Pallas kernels for 27%

profile of v11, /device:TPU:0, one launch (start us, length us, event | category | flops | bytes accessed | tf_op | source)
XLA Modules:
  0.0 59.5 jit_solution(5307175639964584518)
XLA Ops:
  0.6 0.5 collective-permute-start
  1.1 2.2 %pick.1.picked_ref = bf16[128,1024]{1,0:T(8,128)(2,1)} custom-call(bf16[256,1024]{1,0:T(8,128)(2,1)} %k_ref.3, bf16[256,1024]{1,0:T(8,128)(2,1)} %v_ref.3), custom_call_target="tpu_custom_call" | custom-call | tf_op jit(solution)/shard_map/pick/pallas_call | solution.py:81
  3.3 4.5 %collective-permute-start.1 = (bf16[128,1024]{1,0:T(8,128)(2,1)}, bf16[128,1024]{1,0:T(8,128)(2,1)S(1)}, u32[]{:S(2)}, u32[]{:S(2)}) collective-permute-start(bf16[128,1024]{1,0:T(8,128)(2,1)} %pick.1.picked_ref), channel_id=1, source_target_pairs={{0,8},{2,10},{4,12},{6,14},{8,16},{10,18},{12,20},{14,22},{16,24},... | collective-permute-start | bytes 786440 | tf_op jit(solution)/shard_map/ppermute | solution.py:462
  7.9 3.4 %collective-permute-start.2 = (bf16[128,1024]{1,0:T(8,128)(2,1)}, bf16[128,1024]{1,0:T(8,128)(2,1)S(1)}, u32[]{:S(2)}, u32[]{:S(2)}) collective-permute-start(bf16[128,1024]{1,0:T(8,128)(2,1)} %pick.1.picked_ref), channel_id=1, source_target_pairs={{0,2},{2,4},{4,6},{6,8},{8,10},{10,12},{12,14},{14,16},{16,18},{18... | collective-permute-start | bytes 786440 | tf_op jit(solution)/shard_map/ppermute | solution.py:463
  11.3 1.0 %copy-done.4 = bf16[256,1024]{1,0:T(8,128)(2,1)S(1)} copy-done((bf16[256,1024]{1,0:T(8,128)(2,1)S(1)}, bf16[256,1024]{1,0:T(8,128)(2,1)}, u32[]{:S(2)}) %copy-start.4) | copy-done | bytes 524312
  12.4 5.2 %grad_attn.1 = (bf16[256,1024]{1,0:T(8,128)(2,1)S(1)}, f32[8,128]{1,0:T(8,128)S(1)}) custom-call(s32[1]{0:T(128)} %bitcast.core_ref.refs_1_, bf16[256,1024]{1,0:T(8,128)(2,1)S(1)} %copy-done.4, bf16[256,1024]{1,0:T(8,128)(2,1)} %collective-permute-done.other_hbm, bf16[2048,2048]{1,0:T(8,128)(2,1)} %w_hbm.3), custom_call_target="tpu_custom_call" | custom-call | flops 1073741824 | bytes 6291456 | tf_op jit(solution)/shard_map/grad_attn/pallas_call | solution.py:113
  17.6 0.1 choose.1
  17.7 3.5 %collective-permute-start.3 = (bf16[128,1024]{1,0:T(8,128)(2,1)S(1)}, bf16[128,1024]{1,0:T(8,128)(2,1)S(1)}, u32[]{:S(2)}, u32[]{:S(2)}) collective-permute-start(bf16[128,1024]{1,0:T(8,128)(2,1)S(1)} %get-tuple-element.33), channel_id=1, source_target_pairs={{0,8},{2,10},{4,12},{6,14},{8,16},{10,18},{12,20},{14,22},{16,24},... | collective-permute-start | bytes 786440 | tf_op jit(solution)/shard_map/ppermute | solution.py:43
  21.2 3.4 %collective-permute-start.4 = (bf16[128,1024]{1,0:T(8,128)(2,1)S(1)}, bf16[128,1024]{1,0:T(8,128)(2,1)S(1)}, u32[]{:S(2)}, u32[]{:S(2)}) collective-permute-start(bf16[128,1024]{1,0:T(8,128)(2,1)S(1)} %get-tuple-element.34), channel_id=1, source_target_pairs={{0,4},{2,6},{4,0},{6,2},{8,12},{10,14},{12,8},{14,10},{16,20},{18,... | collective-permute-start | bytes 786440 | tf_op jit(solution)/shard_map/ppermute | solution.py:43
  24.7 2.1 %attention_near.1 = (f32[8,384,256]{2,1,0:T(8,128)S(1)}, f32[8,384,256]{2,1,0:T(8,128)S(1)}, f32[8,8,256]{2,1,0:T(8,128)S(1)}, f32[512,256]{1,0:T(8,128)S(1)}) custom-call(s32[1]{0:T(128)} %bitcast.1.me_ref.refs_0_, s32[4]{0:T(128)S(1)} %copy-done.5, bf16[256,1024]{1,0:T(8,128)(2,1)S(1)} %copy-done, bf16[256,1024]{1,0:T(8,128)(2,1)S(1)} %copy-done.1, ...), custom_call_target="tpu_custom_call" | custom-call | flops 402653184 | bytes 4194304 | tf_op jit(solution)/shard_map/attention_near/pallas_call | solution.py:234
  26.8 2.6 %collective-permute-done.4.refs_9_ = bf16[128,1024]{1,0:T(8,128)(2,1)S(1)} collective-permute-done((bf16[128,1024]{1,0:T(8,128)(2,1)S(1)}, bf16[128,1024]{1,0:T(8,128)(2,1)S(1)}, u32[]{:S(2)}, u32[]{:S(2)}) %collective-permute-start.4) | collective-permute-done | bytes 262176 | tf_op jit(solution)/shard_map/ppermute | solution.py:43
  29.4 2.8 %attention_far.1 = (bf16[8,256,256]{2,1,0:T(8,128)(2,1)S(1)}, bf16[8,256,256]{2,1,0:T(8,128)(2,1)S(1)}, f32[8,8,256]{2,1,0:T(8,128)S(1)}, bf16[2,128,1024]{2,1,0...) custom-call(s32[1]{0:T(128)} %bitcast.1.me_ref.refs_0_, ...), custom_call_target="tpu_custom_call" | custom-call | flops 536870912 | bytes 4194304 | tf_op jit(solution)/shard_map/attention_far/pallas_call | solution.py:305
  32.2 1.6 %collective-permute-start.6 = (bf16[128,1024]{1,0:T(8,128)(2,1)S(1)}, bf16[128,1024]{1,0:T(8,128)(2,1)S(1)}, u32[]{:S(2)}, u32[]{:S(2)}) collective-permute-start(bf16[128,1024]{1,0:T(8,128)(2,1)S(1)} %get-tuple-element.44), channel_id=1, source_target_pairs={{4,0},{6,2},{0,4},{2,6},{12,8},{14,10},{8,12},{10,14},{20,16},{22,... | collective-permute-start | bytes 786440 | tf_op jit(solution)/shard_map/ppermute | solution.py:43
  33.8 3.3 %collective-permute-start.7 = (bf16[128,1024]{1,0:T(8,128)(2,1)S(1)}, bf16[128,1024]{1,0:T(8,128)(2,1)S(1)}, u32[]{:S(2)}, u32[]{:S(2)}) collective-permute-start(bf16[128,1024]{1,0:T(8,128)(2,1)S(1)} %get-tuple-element.45), channel_id=1, source_target_pairs={{2,0},{4,2},{6,4},{0,6},{10,8},{12,10},{14,12},{8,14},{18,16},{20,... | collective-permute-start | bytes 786440 | tf_op jit(solution)/shard_map/ppermute | solution.py:43
  37.2 2.7 %attention_local.1 = (bf16[256,1024]{1,0:T(8,128)(2,1)S(1)}, bf16[256,1024]{1,0:T(8,128)(2,1)}, f32[256,1024]{1,0:T(8,128)S(1)}, f32[256,1024]{1,0:T(8,128)S(1)}) custom-call(bf16[256,1024]{1,0:T(8,128)(2,1)S(1)} %copy-done, bf16[256,1024]{1,0:T(8,128)(2,1)S(1)} %copy-done.1, bf16[256,1024]{1,0:T(8,128)(2,1)S(1)} %copy-done.2, ...), custom_call_target="tpu_custom_call" | custom-call | flops 805306368 | bytes 4194304 | tf_op jit(solution)/shard_map/attention_local/pallas_call | solution.py:354
  39.8 0.1 add_convert_fusion
  39.9 1.3 %collective-permute-start.8 = (bf16[128,1024]{1,0:T(8,128)(2,1)S(1)}, bf16[128,1024]{1,0:T(8,128)(2,1)S(1)}, u32[]{:S(2)}, u32[]{:S(2)}) collective-permute-start(bf16[128,1024]{1,0:T(8,128)(2,1)S(1)} %add_convert_fusion), channel_id=1, source_target_pairs={{8,0},{10,2},{12,4},{14,6},{16,8},{18,10},{20,12},{22,14},{24,16},... | collective-permute-start | bytes 786440 | tf_op jit(solution)/shard_map/ppermute | solution.py:43
  41.2 0.8 %collective-permute-done.7.two_ref = bf16[128,1024]{1,0:T(8,128)(2,1)S(1)} collective-permute-done((bf16[128,1024]{1,0:T(8,128)(2,1)S(1)}, bf16[128,1024]{1,0:T(8,128)(2,1)S(1)}, u32[]{:S(2)}, u32[]{:S(2)}) %collective-permute-start.7) | collective-permute-done | bytes 262176 | tf_op jit(solution)/shard_map/ppermute | solution.py:43
  42.1 6.1 %collective-permute-done.8.three_ref = bf16[128,1024]{1,0:T(8,128)(2,1)S(1)} collective-permute-done((bf16[128,1024]{1,0:T(8,128)(2,1)S(1)}, bf16[128,1024]{1,0:T(8,128)(2,1)S(1)}, u32[]{:S(2)}, u32[]{:S(2)}) %collective-permute-start.8) | collective-permute-done | bytes 262176 | tf_op jit(solution)/shard_map/ppermute | solution.py:43
  48.2 0.2 collect.1
  48.4 1.3 %collective-permute-start.9 = (bf16[128,1024]{1,0:T(8,128)(2,1)S(1)}, bf16[128,1024]{1,0:T(8,128)(2,1)S(1)}, u32[]{:S(2)}, u32[]{:S(2)}) collective-permute-start(bf16[128,1024]{1,0:T(8,128)(2,1)S(1)} %collect.1), channel_id=1, source_target_pairs={{8,0},{10,2},{12,4},{14,6},{16,8},{18,10},{20,12},{22,14},{24,16},... | collective-permute-start | bytes 786440 | tf_op jit(solution)/shard_map/ppermute | solution.py:499
  49.7 3.7 %project.1 = bf16[256,1024]{1,0:T(8,128)(2,1)} custom-call(s32[1]{0:T(128)} %bitcast.core_ref.refs_1_, bf16[256,1024]{1,0:T(8,128)(2,1)S(1)} %get-tuple-element.39.own_ref, bf16[256,1024]{1,0:T(8,128)(2,1)S(1)} %collective-permute-done.5.other_ref, bf16[2048,2048]{1,0:T(8,128)(2,1)} %w_hbm.3), custom_call_target="tpu_custom_call" | custom-call | flops 1073741824 | bytes 6291456 | tf_op jit(solution)/shard_map/project/pallas_call | solution.py:157
  53.4 4.7 %collective-permute-done.9.last_ref = bf16[128,1024]{1,0:T(8,128)(2,1)S(1)} collective-permute-done((bf16[128,1024]{1,0:T(8,128)(2,1)S(1)}, bf16[128,1024]{1,0:T(8,128)(2,1)S(1)}, u32[]{:S(2)}, u32[]{:S(2)}) %collective-permute-start.9) | collective-permute-done | bytes 262176 | tf_op jit(solution)/shard_map/ppermute | solution.py:499
  58.1 1.3 %settle.1 = (bf16[256,1024]{1,0:T(8,128)(2,1)}, bf16[256,1024]{1,0:T(8,128)(2,1)}) custom-call(s32[1]{0:T(128)} %bitcast.1.me_ref.refs_0_, s32[1]{0:T(128)} %bitcast.core_ref.refs_1_, f32[256,1024]{1,0:T(8,128)S(1)} %get-tuple-element.41.gk_ref, f32[256,1024]{1,0:T(8,128)S(1)} %get-tuple-element.42.gv_ref, ...), custom_call_target="tpu_custom_call" | custom-call | tf_op jit(solution)/shard_map/settle/pallas_call | solution.py:437
  (18 shorter events, 0.0 us)
Async XLA Ops:
  0.6 10.7 %collective-permute-start = (bf16[256,1024]{1,0:T(8,128)(2,1)}, bf16[256,1024]{1,0:T(8,128)(2,1)}, u32[]{:S(2)}, u32[]{:S(2)}) collective-permute-start(bf16[256,1024]{1,0:T(8,128)(2,1)} %own_ref.1), channel_id=1, source_target_pairs={{0,1},{1,0},{2,3},{3,2},{4,5},{5,4},{6,7},{7,6},{8,9},{9,8},{10,11... | collective-permute-start | bytes 1572872 | tf_op jit(solution)/shard_map/ppermute | solution.py:47
  3.3 14.3 %collective-permute-start.1 = (bf16[128,1024]{1,0:T(8,128)(2,1)}, bf16[128,1024]{1,0:T(8,128)(2,1)S(1)}, u32[]{:S(2)}, u32[]{:S(2)}) collective-permute-start(bf16[128,1024]{1,0:T(8,128)(2,1)} %pick.1.picked_ref), channel_id=1, source_target_pairs={{0,8},{2,10},{4,12},{6,14},{8,16},{10,18},{12,20},{14,22},{16,24},... | collective-permute-start | bytes 786440 | tf_op jit(solution)/shard_map/ppermute | solution.py:462
  7.9 16.8 %collective-permute-start.2 = (bf16[128,1024]{1,0:T(8,128)(2,1)}, bf16[128,1024]{1,0:T(8,128)(2,1)S(1)}, u32[]{:S(2)}, u32[]{:S(2)}) collective-permute-start(bf16[128,1024]{1,0:T(8,128)(2,1)} %pick.1.picked_ref), channel_id=1, source_target_pairs={{0,2},{2,4},{4,6},{6,8},{8,10},{10,12},{12,14},{14,16},{16,18},{18... | collective-permute-start | bytes 786440 | tf_op jit(solution)/shard_map/ppermute | solution.py:463
  11.3 1.0 %copy-start.4 = (bf16[256,1024]{1,0:T(8,128)(2,1)S(1)}, bf16[256,1024]{1,0:T(8,128)(2,1)}, u32[]{:S(2)}) copy-start(bf16[256,1024]{1,0:T(8,128)(2,1)} %own_ref.1) | copy-start | bytes 1572868
  12.3 5.3 %copy-start.3 = (bf16[128,1024]{1,0:T(8,128)(2,1)S(1)}, bf16[128,1024]{1,0:T(8,128)(2,1)}, u32[]{:S(2)}) copy-start(bf16[128,1024]{1,0:T(8,128)(2,1)} %pick.1.picked_ref) | copy-start | bytes 786436
  12.3 12.3 %copy-start = (bf16[256,1024]{1,0:T(8,128)(2,1)S(1)}, bf16[256,1024]{1,0:T(8,128)(2,1)}, u32[]{:S(2)}) copy-start(bf16[256,1024]{1,0:T(8,128)(2,1)} %q_ref.3) | copy-start | bytes 1572868
  12.3 12.3 %copy-start.1 = (bf16[256,1024]{1,0:T(8,128)(2,1)S(1)}, bf16[256,1024]{1,0:T(8,128)(2,1)}, u32[]{:S(2)}) copy-start(bf16[256,1024]{1,0:T(8,128)(2,1)} %k_ref.3) | copy-start | bytes 1572868
  12.3 12.3 %copy-start.2 = (bf16[256,1024]{1,0:T(8,128)(2,1)S(1)}, bf16[256,1024]{1,0:T(8,128)(2,1)}, u32[]{:S(2)}) copy-start(bf16[256,1024]{1,0:T(8,128)(2,1)} %v_ref.3) | copy-start | bytes 1572868
  12.3 12.3 %copy-start.5 = (s32[4]{0:T(128)S(1)}, s32[4]{0:T(128)}, u32[]{:S(2)}) copy-start(s32[4]{0:T(128)} %bounds_ref.1) | copy-start | bytes 52
  17.7 9.1 %collective-permute-start.3 = (bf16[128,1024]{1,0:T(8,128)(2,1)S(1)}, bf16[128,1024]{1,0:T(8,128)(2,1)S(1)}, u32[]{:S(2)}, u32[]{:S(2)}) collective-permute-start(bf16[128,1024]{1,0:T(8,128)(2,1)S(1)} %get-tuple-element.33), channel_id=1, source_target_pairs={{0,8},{2,10},{4,12},{6,14},{8,16},{10,18},{12,20},{14,22},{16,24},... | collective-permute-start | bytes 786440 | tf_op jit(solution)/shard_map/ppermute | solution.py:43
  21.2 8.3 %collective-permute-start.4 = (bf16[128,1024]{1,0:T(8,128)(2,1)S(1)}, bf16[128,1024]{1,0:T(8,128)(2,1)S(1)}, u32[]{:S(2)}, u32[]{:S(2)}) collective-permute-start(bf16[128,1024]{1,0:T(8,128)(2,1)S(1)} %get-tuple-element.34), channel_id=1, source_target_pairs={{0,4},{2,6},{4,0},{6,2},{8,12},{10,14},{12,8},{14,10},{16,20},{18,... | collective-permute-start | bytes 786440 | tf_op jit(solution)/shard_map/ppermute | solution.py:43
  32.2 7.6 %collective-permute-start.6 = (bf16[128,1024]{1,0:T(8,128)(2,1)S(1)}, bf16[128,1024]{1,0:T(8,128)(2,1)S(1)}, u32[]{:S(2)}, u32[]{:S(2)}) collective-permute-start(bf16[128,1024]{1,0:T(8,128)(2,1)S(1)} %get-tuple-element.44), channel_id=1, source_target_pairs={{4,0},{6,2},{0,4},{2,6},{12,8},{14,10},{8,12},{10,14},{20,16},{22,... | collective-permute-start | bytes 786440 | tf_op jit(solution)/shard_map/ppermute | solution.py:43
  33.8 8.3 %collective-permute-start.7 = (bf16[128,1024]{1,0:T(8,128)(2,1)S(1)}, bf16[128,1024]{1,0:T(8,128)(2,1)S(1)}, u32[]{:S(2)}, u32[]{:S(2)}) collective-permute-start(bf16[128,1024]{1,0:T(8,128)(2,1)S(1)} %get-tuple-element.45), channel_id=1, source_target_pairs={{2,0},{4,2},{6,4},{0,6},{10,8},{12,10},{14,12},{8,14},{18,16},{20,... | collective-permute-start | bytes 786440 | tf_op jit(solution)/shard_map/ppermute | solution.py:43
  39.8 9.9 %collective-permute-start.5 = (bf16[256,1024]{1,0:T(8,128)(2,1)S(1)}, bf16[256,1024]{1,0:T(8,128)(2,1)S(1)}, u32[]{:S(2)}, u32[]{:S(2)}) collective-permute-start(bf16[256,1024]{1,0:T(8,128)(2,1)S(1)} %get-tuple-element.39.own_ref), channel_id=1, source_target_pairs={{0,1},{1,0},{2,3},{3,2},{4,5},{5,4},{6,7},{7,6},{8,9},{9,8},{10,11... | collective-permute-start | bytes 1572872 | tf_op jit(solution)/shard_map/ppermute | solution.py:47
  39.9 8.3 %collective-permute-start.8 = (bf16[128,1024]{1,0:T(8,128)(2,1)S(1)}, bf16[128,1024]{1,0:T(8,128)(2,1)S(1)}, u32[]{:S(2)}, u32[]{:S(2)}) collective-permute-start(bf16[128,1024]{1,0:T(8,128)(2,1)S(1)} %add_convert_fusion), channel_id=1, source_target_pairs={{8,0},{10,2},{12,4},{14,6},{16,8},{18,10},{20,12},{22,14},{24,16},... | collective-permute-start | bytes 786440 | tf_op jit(solution)/shard_map/ppermute | solution.py:43
  48.4 9.8 %collective-permute-start.9 = (bf16[128,1024]{1,0:T(8,128)(2,1)S(1)}, bf16[128,1024]{1,0:T(8,128)(2,1)S(1)}, u32[]{:S(2)}, u32[]{:S(2)}) collective-permute-start(bf16[128,1024]{1,0:T(8,128)(2,1)S(1)} %collect.1), channel_id=1, source_target_pairs={{8,0},{10,2},{12,4},{14,6},{16,8},{18,10},{20,12},{22,14},{24,16},... | collective-permute-start | bytes 786440 | tf_op jit(solution)/shard_map/ppermute | solution.py:499

commit v12 on v11

--- a/solution.py
+++ b/solution.py
@@ -63,26 +63,41 @@
     return pltpu.CompilerParams(vmem_limit_bytes=int(mib * 1024 * 1024))
 
 
-def pick_kernel(k_hbm, v_hbm, out_ref, held, sems):
-    tokens = k_hbm.shape[0]
-    rows = tokens // STEP
-    copies = [pltpu.make_async_copy(x, held.at[i], sems.at[i]) for i, x in enumerate((k_hbm, v_hbm))]
-    for copy in copies:
-        copy.start()
+def pick_kernel(k_hbm, v_hbm, out_hbm, held, ready, in_sems, out_sems):
+    tokens, width = k_hbm.shape
+    rows, half = tokens // STEP, width // 2
+    parts = [(i, x, slice(c * half, (c + 1) * half)) for i, x in enumerate((k_hbm, v_hbm)) for c in (0, 1)]
+    copies = []
+    for n, (i, x, cols) in enumerate(parts):
+        copies.append(pltpu.make_async_copy(x.at[:, cols], held.at[i, :, cols], in_sems.at[n]))
+        copies[n].start()
     at = lax.broadcasted_iota(jnp.int32, (rows, tokens), 0) * STEP
     choose = (at == lax.broadcasted_iota(jnp.int32, (rows, tokens), 1)).astype(BF16)
-    for i, copy in enumerate(copies):
+    sent = []
+    for n, (i, x, cols) in enumerate(parts):
+        copies[n].wait()
+        ready[i * rows : (i + 1) * rows, cols] = nn(choose, held[i, :, cols]).astype(BF16)
+        block = pl.ds(i * rows, rows), cols
+        sent.append(pltpu.make_async_copy(ready.at[block], out_hbm.at[block], out_sems.at[n]))
+        sent[n].start()
+    for copy in sent:
         copy.wait()
-        out_ref[i * rows : (i + 1) * rows] = nn(choose, held[i]).astype(BF16)
 
 
 def pick(keys, values):
     tokens, width = keys.shape
+    shape = (2 * tokens // STEP, width)
     return pl.pallas_call(
         pick_kernel,
         in_specs=[HBM_BLOCK, HBM_BLOCK],
-        out_shape=jax.ShapeDtypeStruct((2 * tokens // STEP, width), BF16),
-        scratch_shapes=[pltpu.VMEM((2, tokens, width), BF16), pltpu.SemaphoreType.DMA((2,))],
+        out_specs=HBM_BLOCK,
+        out_shape=jax.ShapeDtypeStruct(shape, BF16),
+        scratch_shapes=[
+            pltpu.VMEM((2, tokens, width), BF16),
+            pltpu.VMEM(shape, BF16),
+            pltpu.SemaphoreType.DMA((4,)),
+            pltpu.SemaphoreType.DMA((4,)),
+        ],
         compiler_params=params(63.5),
         name="pick",
     )(keys, values)
@@ -281,18 +296,18 @@
         early_part = shrink * part
         use_ref[h, 0:1] = early_part
         use_ref[h, 1:2] = delta
-        prob = jnp.concatenate([grown_ref[h, tokens:] * early_part, grown * part], 0)
-        grad_prob = jnp.concatenate([gp_ref[h, tokens:], grad_prob], 0)
+        prob = jnp.concatenate([grown_ref[h, tokens + rows :] * early_part, grown * part], 0)
+        grad_prob = jnp.concatenate([gp_ref[h, tokens + rows :], grad_prob], 0)
         weights = prob.astype(BF16)
         grad_scores = (prob * (grad_prob - delta)).astype(BF16)
         w_ref[h] = weights
         u_ref[h] = grad_scores
         gk = (nn(grad_scores, q) * SCALE).astype(BF16)
         gv = nn(weights, ga).astype(BF16)
-        g4, g1, g2, g8, *more = [
-            jnp.concatenate([g[i * rows : (i + 1) * rows] for g in (gk, gv)], 0) for i in range(levels)
+        g1, g2, g8, *more = [
+            jnp.concatenate([g[i * rows : (i + 1) * rows] for g in (gk, gv)], 0) for i in range(levels - 1)
         ]
-        out = [g4, jnp.where(first, g2, g1), jnp.where(first, g1, g8), jnp.where(first, g8, g2)]
+        out = [jnp.where(first, g2, g1), jnp.where(first, g1, g8), jnp.where(first, g8, g2)]
         for ref, block in zip(gfar_refs, out + more):
             ref[:, cols] = block
 
@@ -301,11 +316,11 @@
     tokens, width = q.shape
     levels = 2 + len(arrived)
     heads, rows = width // DH, tokens // STEP
-    prob = jax.ShapeDtypeStruct((heads, levels * rows, tokens), BF16)
+    prob = jax.ShapeDtypeStruct((heads, (levels - 1) * rows, tokens), BF16)
     return pl.pallas_call(
         functools.partial(far_kernel, levels),
         in_specs=[SMEM_BLOCK] * 2 + [VMEM_BLOCK] * (6 + len(arrived)),
-        out_specs=[VMEM_BLOCK] * (5 + levels),
+        out_specs=[VMEM_BLOCK] * (4 + levels),
         out_shape=[
             prob,
             prob,
@@ -313,7 +328,7 @@
             jax.ShapeDtypeStruct((2, (levels - 2) * rows, width), BF16),
             jax.ShapeDtypeStruct((1, width), F32),
         ]
-        + [jax.ShapeDtypeStruct((2 * rows, width), BF16)] * levels,
+        + [jax.ShapeDtypeStruct((2 * rows, width), BF16)] * (levels - 1),
         compiler_params=params(),
         cost_estimate=pl.CostEstimate(
             flops=8 * tokens * levels * rows * width, bytes_accessed=16 * tokens * width, transcendentals=0
@@ -324,10 +339,11 @@
 
 def local_kernel(
     q_ref, k_ref, v_ref, ga_ref, far4_ref, far1_ref, far_ref, grown_ref, gp_ref, use_ref, w_ref, u_ref,
-    attn_ref, gq_ref, gk_ref, gv_ref,
+    attn_ref, gq_ref, gk_ref, gv_ref, g4_ref,
 ):
     tokens = q_ref.shape[0]
     rows = tokens // STEP
+    near = tokens + rows
     for h in range(q_ref.shape[1] // DH):
         cols = slice(h * DH, (h + 1) * DH)
         k = jnp.concatenate(
@@ -336,15 +352,19 @@
         v = jnp.concatenate(
             [v_ref[:, cols], far4_ref[rows:, cols], far1_ref[rows:, cols], far_ref[1, :, cols]], 0
         )
-        prob = grown_ref[h, :tokens] * use_ref[h, 0:1]
+        prob = grown_ref[h, :near] * use_ref[h, 0:1]
         near_weights = prob.astype(BF16)
-        near_scores = (prob * (gp_ref[h, :tokens] - use_ref[h, 1:2])).astype(BF16)
+        near_scores = (prob * (gp_ref[h, :near] - use_ref[h, 1:2])).astype(BF16)
         weights = jnp.concatenate([near_weights, w_ref[h]], 0)
         grad_scores = jnp.concatenate([near_scores, u_ref[h]], 0)
         attn_ref[:, cols] = tn(weights, v).astype(BF16)
         gq_ref[:, cols] = (tn(grad_scores, k) * SCALE).astype(BF16)
-        gk_ref[:, cols] = nn(near_scores, q_ref[:, cols]) * SCALE
-        gv_ref[:, cols] = nn(near_weights, ga_ref[:, cols])
+        gk = nn(near_scores, q_ref[:, cols]) * SCALE
+        gv = nn(near_weights, ga_ref[:, cols])
+        gk_ref[:, cols] = gk[:tokens]
+        gv_ref[:, cols] = gv[:tokens]
+        g4_ref[:rows, cols] = gk[tokens:].astype(BF16)
+        g4_ref[rows:, cols] = gv[tokens:].astype(BF16)
 
 
 def attention_local(q, *operands):
@@ -354,8 +374,8 @@
     return pl.pallas_call(
         local_kernel,
         in_specs=[VMEM_BLOCK] * (1 + len(operands)),
-        out_specs=[VMEM_BLOCK] * 4,
-        out_shape=[bf, bf, f32, f32],
+        out_specs=[VMEM_BLOCK] * 5,
+        out_shape=[bf, bf, f32, f32, jax.ShapeDtypeStruct((2 * tokens // STEP, width), BF16)],
         compiler_params=params(),
         cost_estimate=pl.CostEstimate(
             flops=12 * tokens * tokens * width, bytes_accessed=16 * tokens * width, transcendentals=0
@@ -417,7 +437,7 @@
     return out if count > 1 else out[0]
 
 
-def settle_kernel(me_ref, core_ref, gk_ref, gv_ref, last_ref, one_ref, two_ref, three_ref, *out_refs):
+def settle_kernel(me_ref, core_ref, gk_ref, gv_ref, last_ref, one_ref, two_ref, three_ref, *rest):
     tokens = gk_ref.shape[0]
     rows = tokens // STEP
     back = [last_ref[...]]
@@ -427,9 +447,19 @@
     at = lax.broadcasted_iota(jnp.int32, (tokens, rows), 0)
     spot = (at == lax.broadcasted_iota(jnp.int32, (tokens, rows), 1) * STEP).astype(BF16)
     spot = jnp.concatenate([spot] * len(back), 1)
-    for i, (near_ref, out_ref) in enumerate(zip((gk_ref, gv_ref), out_refs)):
-        extra = nn(spot, jnp.concatenate([b[i * rows : (i + 1) * rows] for b in back], 0))
-        out_ref[...] = (near_ref[...] + extra).astype(BF16)
+    out_hbms, (ready, sems) = rest[:2], rest[2:]
+    half = gk_ref.shape[1] // 2
+    sent = []
+    for i, (near_ref, out_hbm) in enumerate(zip((gk_ref, gv_ref), out_hbms)):
+        for c in (0, 1):
+            cols = slice(c * half, (c + 1) * half)
+            extra = nn(spot, jnp.concatenate([b[i * rows : (i + 1) * rows, cols] for b in back], 0))
+            ready[i, :, cols] = (near_ref[:, cols] + extra).astype(BF16)
+            copy = pltpu.make_async_copy(ready.at[i, :, cols], out_hbm.at[:, cols], sems.at[2 * i + c])
+            copy.start()
+            sent.append(copy)
+    for copy in sent:
+        copy.wait()
 
 
 def settle(me, core, gk, gv, last, one, two, three):
@@ -437,8 +467,9 @@
     return pl.pallas_call(
         settle_kernel,
         in_specs=[SMEM_BLOCK] * 2 + [VMEM_BLOCK] * 6,
-        out_specs=[VMEM_BLOCK] * 2,
+        out_specs=[HBM_BLOCK] * 2,
         out_shape=[out, out],
+        scratch_shapes=[pltpu.VMEM((2,) + gk.shape, BF16), pltpu.SemaphoreType.DMA((4,))],
         compiler_params=params(),
         name="settle",
     )(me, core, gk, gv, last, one, two, three)
@@ -477,7 +508,7 @@
     grown, grad_prob, stats, bias = attention_near(
         me, bounds, queries, keys, values, ga, far4, far1, levels
     )
-    weights, grad_scores, use, far, passes, g4, two, three, four, *more = attention_far(
+    weights, grad_scores, use, far, passes, two, three, four, *more = attention_far(
         me, core, queries, ga, grown, grad_prob, stats, bias, arrived
     )
     for i in reversed(range(len(more))):
@@ -491,7 +522,7 @@
     one = mixed(two, (twos, nexts))
     two = mixed(three, (ones, hops))
     three = mixed((four.astype(F32) + one.astype(F32) * passes).astype(BF16), (hops, twos))
-    attn, gq, gk, gv = attention_local(
+    attn, gq, gk, gv, g4 = attention_local(
         queries, keys, values, ga, far4, far1, far, grown, grad_prob, use, weights, grad_scores
     )
     back = (one, two, three)

time: 59.8 us -> 59.9 us (level)
  transfers between devices with their start and end apart: 10 -> 10, of which waited for: 4 -> 4; matrix products, arithmetic and copies ran while one was open for 0% -> 0% of each run, Pallas kernels for 27% -> 28%
where the time goes in v12:
time: 59.9 us; the launch traced here: 59.5 us
  starting transfers between devices  22.8 us (38%)
  Pallas kernels  20.4 us (34%)
  waiting for transfers between devices  14.3 us (24%)
  local copies, waits for them, and re-layouts  1.06 us (2%)
  between operations  0.84 us (1%)
    ppermute x5, starting transfers between devices, mixed(): return lax.ppermute(block, ('ctx', 'head'), route)  13.1 us
    ppermute x5, waiting for transfers between devices, mixed(): return lax.ppermute(block, ('ctx', 'head'), route)  9.62 us
    pallas_call x1, Pallas kernels, grad_attn(): pl.pallas_call(grad_attn_kernel, in_specs=[SMEM_BLOCK, VMEM_BLOCK, HBM_BL...  5.23 us
    ppermute x1, waiting for transfers between devices, per_device(): last = lax.ppermute(g4, 'ctx', hop(-4, n))  4.71 us
    ppermute x1, starting transfers between devices, per_device(): far4 = lax.ppermute(picked, 'ctx', hop(4, n))  4.51 us
    pallas_call x1, Pallas kernels, project(): pl.pallas_call(project_kernel, in_specs=[SMEM_BLOCK, VMEM_BLOCK, VMEM_BLO...  3.73 us
    ppermute x1, starting transfers between devices, per_device(): far1 = lax.ppermute(picked, 'ctx', hop(1, n))  3.42 us
    pallas_call x1, Pallas kernels, attention_local(): pl.pallas_call(local_kernel, in_specs=[VMEM_BLOCK] * (1 + len(operands)),...  2.77 us
  transfers between devices with their start and end apart: 10, of which 4 were waited for; matrix products, arithmetic and copies ran while one was open for 0% of the time, Pallas kernels for 28%

profile of v12, /device:TPU:0, one launch (start us, length us, event | category | flops | bytes accessed | tf_op | source)
XLA Modules:
  0.0 59.5 jit_solution(8451999088651714063)
XLA Ops:
  0.6 0.5 collective-permute-start
  1.1 2.3 %pick.1.picked_ref = bf16[128,1024]{1,0:T(8,128)(2,1)} custom-call(bf16[256,1024]{1,0:T(8,128)(2,1)} %k_ref.3, bf16[256,1024]{1,0:T(8,128)(2,1)} %v_ref.3), custom_call_target="tpu_custom_call" | custom-call | tf_op jit(solution)/shard_map/pick/pallas_call | solution.py:90
  3.5 4.5 %collective-permute-start.1 = (bf16[128,1024]{1,0:T(8,128)(2,1)}, bf16[128,1024]{1,0:T(8,128)(2,1)S(1)}, u32[]{:S(2)}, u32[]{:S(2)}) collective-permute-start(bf16[128,1024]{1,0:T(8,128)(2,1)} %pick.1.picked_ref), channel_id=1, source_target_pairs={{0,8},{2,10},{4,12},{6,14},{8,16},{10,18},{12,20},{14,22},{16,24},... | collective-permute-start | bytes 786440 | tf_op jit(solution)/shard_map/ppermute | solution.py:493
  8.0 3.4 %collective-permute-start.2 = (bf16[128,1024]{1,0:T(8,128)(2,1)}, bf16[128,1024]{1,0:T(8,128)(2,1)S(1)}, u32[]{:S(2)}, u32[]{:S(2)}) collective-permute-start(bf16[128,1024]{1,0:T(8,128)(2,1)} %pick.1.picked_ref), channel_id=1, source_target_pairs={{0,2},{2,4},{4,6},{6,8},{8,10},{10,12},{12,14},{14,16},{16,18},{18... | collective-permute-start | bytes 786440 | tf_op jit(solution)/shard_map/ppermute | solution.py:494
  11.4 1.0 %copy-done.4 = bf16[256,1024]{1,0:T(8,128)(2,1)S(1)} copy-done((bf16[256,1024]{1,0:T(8,128)(2,1)S(1)}, bf16[256,1024]{1,0:T(8,128)(2,1)}, u32[]{:S(2)}) %copy-start.4) | copy-done | bytes 524312
  12.5 5.2 %grad_attn.1 = (bf16[256,1024]{1,0:T(8,128)(2,1)S(1)}, f32[8,128]{1,0:T(8,128)S(1)}) custom-call(s32[1]{0:T(128)} %bitcast.core_ref.refs_1_, bf16[256,1024]{1,0:T(8,128)(2,1)S(1)} %copy-done.4, bf16[256,1024]{1,0:T(8,128)(2,1)} %collective-permute-done.other_hbm, bf16[2048,2048]{1,0:T(8,128)(2,1)} %w_hbm.3), custom_call_target="tpu_custom_call" | custom-call | flops 1073741824 | bytes 6291456 | tf_op jit(solution)/shard_map/grad_attn/pallas_call | solution.py:128
  17.8 0.1 choose.1
  17.8 3.5 %collective-permute-start.3 = (bf16[128,1024]{1,0:T(8,128)(2,1)S(1)}, bf16[128,1024]{1,0:T(8,128)(2,1)S(1)}, u32[]{:S(2)}, u32[]{:S(2)}) collective-permute-start(bf16[128,1024]{1,0:T(8,128)(2,1)S(1)} %get-tuple-element.33), channel_id=1, source_target_pairs={{0,8},{2,10},{4,12},{6,14},{8,16},{10,18},{12,20},{14,22},{16,24},... | collective-permute-start | bytes 786440 | tf_op jit(solution)/shard_map/ppermute | solution.py:43
  21.3 3.4 %collective-permute-start.4 = (bf16[128,1024]{1,0:T(8,128)(2,1)S(1)}, bf16[128,1024]{1,0:T(8,128)(2,1)S(1)}, u32[]{:S(2)}, u32[]{:S(2)}) collective-permute-start(bf16[128,1024]{1,0:T(8,128)(2,1)S(1)} %get-tuple-element.34), channel_id=1, source_target_pairs={{0,4},{2,6},{4,0},{6,2},{8,12},{10,14},{12,8},{14,10},{16,20},{18,... | collective-permute-start | bytes 786440 | tf_op jit(solution)/shard_map/ppermute | solution.py:43
  24.8 2.1 %attention_near.1 = (f32[8,384,256]{2,1,0:T(8,128)S(1)}, f32[8,384,256]{2,1,0:T(8,128)S(1)}, f32[8,8,256]{2,1,0:T(8,128)S(1)}, f32[512,256]{1,0:T(8,128)S(1)}) custom-call(s32[1]{0:T(128)} %bitcast.1.me_ref.refs_0_, s32[4]{0:T(128)S(1)} %copy-done.5, bf16[256,1024]{1,0:T(8,128)(2,1)S(1)} %copy-done, bf16[256,1024]{1,0:T(8,128)(2,1)S(1)} %copy-done.1, ...), custom_call_target="tpu_custom_call" | custom-call | flops 402653184 | bytes 4194304 | tf_op jit(solution)/shard_map/attention_near/pallas_call | solution.py:249
  26.9 2.6 %collective-permute-done.4.refs_9_ = bf16[128,1024]{1,0:T(8,128)(2,1)S(1)} collective-permute-done((bf16[128,1024]{1,0:T(8,128)(2,1)S(1)}, bf16[128,1024]{1,0:T(8,128)(2,1)S(1)}, u32[]{:S(2)}, u32[]{:S(2)}) %collective-permute-start.4) | collective-permute-done | bytes 262176 | tf_op jit(solution)/shard_map/ppermute | solution.py:43
  29.6 2.7 %attention_far.1 = (bf16[8,192,256]{2,1,0:T(8,128)(2,1)S(1)}, bf16[8,192,256]{2,1,0:T(8,128)(2,1)S(1)}, f32[8,8,256]{2,1,0:T(8,128)S(1)}, bf16[2,128,1024]{2,1,0...) custom-call(s32[1]{0:T(128)} %bitcast.1.me_ref.refs_0_, ...), custom_call_target="tpu_custom_call" | custom-call | flops 536870912 | bytes 4194304 | tf_op jit(solution)/shard_map/attention_far/pallas_call | solution.py:320
  32.3 1.6 %collective-permute-start.6 = (bf16[128,1024]{1,0:T(8,128)(2,1)S(1)}, bf16[128,1024]{1,0:T(8,128)(2,1)S(1)}, u32[]{:S(2)}, u32[]{:S(2)}) collective-permute-start(bf16[128,1024]{1,0:T(8,128)(2,1)S(1)} %get-tuple-element.44), channel_id=1, source_target_pairs={{4,0},{6,2},{0,4},{2,6},{12,8},{14,10},{8,12},{10,14},{20,16},{22,... | collective-permute-start | bytes 786440 | tf_op jit(solution)/shard_map/ppermute | solution.py:43
  33.9 3.3 %collective-permute-start.7 = (bf16[128,1024]{1,0:T(8,128)(2,1)S(1)}, bf16[128,1024]{1,0:T(8,128)(2,1)S(1)}, u32[]{:S(2)}, u32[]{:S(2)}) collective-permute-start(bf16[128,1024]{1,0:T(8,128)(2,1)S(1)} %get-tuple-element.45), channel_id=1, source_target_pairs={{2,0},{4,2},{6,4},{0,6},{10,8},{12,10},{14,12},{8,14},{18,16},{20,... | collective-permute-start | bytes 786440 | tf_op jit(solution)/shard_map/ppermute | solution.py:43
  37.2 2.8 %attention_local.1 = (bf16[256,1024]{1,0:T(8,128)(2,1)S(1)}, bf16[256,1024]{1,0:T(8,128)(2,1)}, f32[256,1024]{1,0:T(8,128)S(1)}, f32[256,1024]{1,0:T(8,128)S(1)}, bf16[128,1024]{1,0:T(8,128)(2,1)S(1)}) custom-call(bf16[256,1024]{1,0:T(8,128)(2,1)S(1)} %copy-done, bf16[256,1024]{1,0:T(8,128)(2,1)S(1)} %copy-done.1, bf16[256,1024]{1,0:T(8,128)(2,1)S(1)} %copy-done.2, ...), custom_call_target="tpu_custom_call" | custom-call | flops 805306368 | bytes 4194304 | tf_op jit(solution)/shard_map/attention_local/pallas_call | solution.py:374
  40.0 0.1 add_convert_fusion
  40.0 1.3 %collective-permute-start.8 = (bf16[128,1024]{1,0:T(8,128)(2,1)S(1)}, bf16[128,1024]{1,0:T(8,128)(2,1)S(1)}, u32[]{:S(2)}, u32[]{:S(2)}) collective-permute-start(bf16[128,1024]{1,0:T(8,128)(2,1)S(1)} %add_convert_fusion), channel_id=1, source_target_pairs={{8,0},{10,2},{12,4},{14,6},{16,8},{18,10},{20,12},{22,14},{24,16},... | collective-permute-start | bytes 786440 | tf_op jit(solution)/shard_map/ppermute | solution.py:43
  41.3 0.8 %collective-permute-done.7.two_ref = bf16[128,1024]{1,0:T(8,128)(2,1)S(1)} collective-permute-done((bf16[128,1024]{1,0:T(8,128)(2,1)S(1)}, bf16[128,1024]{1,0:T(8,128)(2,1)S(1)}, u32[]{:S(2)}, u32[]{:S(2)}) %collective-permute-start.7) | collective-permute-done | bytes 262176 | tf_op jit(solution)/shard_map/ppermute | solution.py:43
  42.1 6.2 %collective-permute-done.8.three_ref = bf16[128,1024]{1,0:T(8,128)(2,1)S(1)} collective-permute-done((bf16[128,1024]{1,0:T(8,128)(2,1)S(1)}, bf16[128,1024]{1,0:T(8,128)(2,1)S(1)}, u32[]{:S(2)}, u32[]{:S(2)}) %collective-permute-start.8) | collective-permute-done | bytes 262176 | tf_op jit(solution)/shard_map/ppermute | solution.py:43
  48.3 0.2 collect.1
  48.5 1.3 %collective-permute-start.9 = (bf16[128,1024]{1,0:T(8,128)(2,1)S(1)}, bf16[128,1024]{1,0:T(8,128)(2,1)S(1)}, u32[]{:S(2)}, u32[]{:S(2)}) collective-permute-start(bf16[128,1024]{1,0:T(8,128)(2,1)S(1)} %collect.1), channel_id=1, source_target_pairs={{8,0},{10,2},{12,4},{14,6},{16,8},{18,10},{20,12},{22,14},{24,16},... | collective-permute-start | bytes 786440 | tf_op jit(solution)/shard_map/ppermute | solution.py:530
  49.8 3.7 %project.1 = bf16[256,1024]{1,0:T(8,128)(2,1)} custom-call(s32[1]{0:T(128)} %bitcast.core_ref.refs_1_, bf16[256,1024]{1,0:T(8,128)(2,1)S(1)} %get-tuple-element.39.own_ref, bf16[256,1024]{1,0:T(8,128)(2,1)S(1)} %collective-permute-done.5.other_ref, bf16[2048,2048]{1,0:T(8,128)(2,1)} %w_hbm.3), custom_call_target="tpu_custom_call" | custom-call | flops 1073741824 | bytes 6291456 | tf_op jit(solution)/shard_map/project/pallas_call | solution.py:172
  53.6 4.7 %collective-permute-done.9.last_ref = bf16[128,1024]{1,0:T(8,128)(2,1)S(1)} collective-permute-done((bf16[128,1024]{1,0:T(8,128)(2,1)S(1)}, bf16[128,1024]{1,0:T(8,128)(2,1)S(1)}, u32[]{:S(2)}, u32[]{:S(2)}) %collective-permute-start.9) | collective-permute-done | bytes 262176 | tf_op jit(solution)/shard_map/ppermute | solution.py:530
  58.3 1.3 %settle.1 = (bf16[256,1024]{1,0:T(8,128)(2,1)}, bf16[256,1024]{1,0:T(8,128)(2,1)}) custom-call(s32[1]{0:T(128)} %bitcast.1.me_ref.refs_0_, s32[1]{0:T(128)} %bitcast.core_ref.refs_1_, f32[256,1024]{1,0:T(8,128)S(1)} %get-tuple-element.41.gk_ref, f32[256,1024]{1,0:T(8,128)S(1)} %get-tuple-element.42.gv_ref, ...), custom_call_target="tpu_custom_call" | custom-call | tf_op jit(solution)/shard_map/settle/pallas_call | solution.py:467
  (18 shorter events, 0.0 us)
Async XLA Ops:
  0.6 10.8 %collective-permute-start = (bf16[256,1024]{1,0:T(8,128)(2,1)}, bf16[256,1024]{1,0:T(8,128)(2,1)}, u32[]{:S(2)}, u32[]{:S(2)}) collective-permute-start(bf16[256,1024]{1,0:T(8,128)(2,1)} %own_ref.1), channel_id=1, source_target_pairs={{0,1},{1,0},{2,3},{3,2},{4,5},{5,4},{6,7},{7,6},{8,9},{9,8},{10,11... | collective-permute-start | bytes 1572872 | tf_op jit(solution)/shard_map/ppermute | solution.py:47
  3.5 14.3 %collective-permute-start.1 = (bf16[128,1024]{1,0:T(8,128)(2,1)}, bf16[128,1024]{1,0:T(8,128)(2,1)S(1)}, u32[]{:S(2)}, u32[]{:S(2)}) collective-permute-start(bf16[128,1024]{1,0:T(8,128)(2,1)} %pick.1.picked_ref), channel_id=1, source_target_pairs={{0,8},{2,10},{4,12},{6,14},{8,16},{10,18},{12,20},{14,22},{16,24},... | collective-permute-start | bytes 786440 | tf_op jit(solution)/shard_map/ppermute | solution.py:493
  8.0 16.8 %collective-permute-start.2 = (bf16[128,1024]{1,0:T(8,128)(2,1)}, bf16[128,1024]{1,0:T(8,128)(2,1)S(1)}, u32[]{:S(2)}, u32[]{:S(2)}) collective-permute-start(bf16[128,1024]{1,0:T(8,128)(2,1)} %pick.1.picked_ref), channel_id=1, source_target_pairs={{0,2},{2,4},{4,6},{6,8},{8,10},{10,12},{12,14},{14,16},{16,18},{18... | collective-permute-start | bytes 786440 | tf_op jit(solution)/shard_map/ppermute | solution.py:494
  11.4 1.0 %copy-start.4 = (bf16[256,1024]{1,0:T(8,128)(2,1)S(1)}, bf16[256,1024]{1,0:T(8,128)(2,1)}, u32[]{:S(2)}) copy-start(bf16[256,1024]{1,0:T(8,128)(2,1)} %own_ref.1) | copy-start | bytes 1572868
  12.5 5.3 %copy-start.3 = (bf16[128,1024]{1,0:T(8,128)(2,1)S(1)}, bf16[128,1024]{1,0:T(8,128)(2,1)}, u32[]{:S(2)}) copy-start(bf16[128,1024]{1,0:T(8,128)(2,1)} %pick.1.picked_ref) | copy-start | bytes 786436
  12.5 12.3 %copy-start = (bf16[256,1024]{1,0:T(8,128)(2,1)S(1)}, bf16[256,1024]{1,0:T(8,128)(2,1)}, u32[]{:S(2)}) copy-start(bf16[256,1024]{1,0:T(8,128)(2,1)} %q_ref.3) | copy-start | bytes 1572868
  12.5 12.3 %copy-start.1 = (bf16[256,1024]{1,0:T(8,128)(2,1)S(1)}, bf16[256,1024]{1,0:T(8,128)(2,1)}, u32[]{:S(2)}) copy-start(bf16[256,1024]{1,0:T(8,128)(2,1)} %k_ref.3) | copy-start | bytes 1572868
  12.5 12.3 %copy-start.2 = (bf16[256,1024]{1,0:T(8,128)(2,1)S(1)}, bf16[256,1024]{1,0:T(8,128)(2,1)}, u32[]{:S(2)}) copy-start(bf16[256,1024]{1,0:T(8,128)(2,1)} %v_ref.3) | copy-start | bytes 1572868
  12.5 12.3 %copy-start.5 = (s32[4]{0:T(128)S(1)}, s32[4]{0:T(128)}, u32[]{:S(2)}) copy-start(s32[4]{0:T(128)} %bounds_ref.1) | copy-start | bytes 52
  17.8 9.1 %collective-permute-start.3 = (bf16[128,1024]{1,0:T(8,128)(2,1)S(1)}, bf16[128,1024]{1,0:T(8,128)(2,1)S(1)}, u32[]{:S(2)}, u32[]{:S(2)}) collective-permute-start(bf16[128,1024]{1,0:T(8,128)(2,1)S(1)} %get-tuple-element.33), channel_id=1, source_target_pairs={{0,8},{2,10},{4,12},{6,14},{8,16},{10,18},{12,20},{14,22},{16,24},... | collective-permute-start | bytes 786440 | tf_op jit(solution)/shard_map/ppermute | solution.py:43
  21.3 8.3 %collective-permute-start.4 = (bf16[128,1024]{1,0:T(8,128)(2,1)S(1)}, bf16[128,1024]{1,0:T(8,128)(2,1)S(1)}, u32[]{:S(2)}, u32[]{:S(2)}) collective-permute-start(bf16[128,1024]{1,0:T(8,128)(2,1)S(1)} %get-tuple-element.34), channel_id=1, source_target_pairs={{0,4},{2,6},{4,0},{6,2},{8,12},{10,14},{12,8},{14,10},{16,20},{18,... | collective-permute-start | bytes 786440 | tf_op jit(solution)/shard_map/ppermute | solution.py:43
  32.3 7.7 %collective-permute-start.6 = (bf16[128,1024]{1,0:T(8,128)(2,1)S(1)}, bf16[128,1024]{1,0:T(8,128)(2,1)S(1)}, u32[]{:S(2)}, u32[]{:S(2)}) collective-permute-start(bf16[128,1024]{1,0:T(8,128)(2,1)S(1)} %get-tuple-element.44), channel_id=1, source_target_pairs={{4,0},{6,2},{0,4},{2,6},{12,8},{14,10},{8,12},{10,14},{20,16},{22,... | collective-permute-start | bytes 786440 | tf_op jit(solution)/shard_map/ppermute | solution.py:43
  33.9 8.3 %collective-permute-start.7 = (bf16[128,1024]{1,0:T(8,128)(2,1)S(1)}, bf16[128,1024]{1,0:T(8,128)(2,1)S(1)}, u32[]{:S(2)}, u32[]{:S(2)}) collective-permute-start(bf16[128,1024]{1,0:T(8,128)(2,1)S(1)} %get-tuple-element.45), channel_id=1, source_target_pairs={{2,0},{4,2},{6,4},{0,6},{10,8},{12,10},{14,12},{8,14},{18,16},{20,... | collective-permute-start | bytes 786440 | tf_op jit(solution)/shard_map/ppermute | solution.py:43
  39.9 9.9 %collective-permute-start.5 = (bf16[256,1024]{1,0:T(8,128)(2,1)S(1)}, bf16[256,1024]{1,0:T(8,128)(2,1)S(1)}, u32[]{:S(2)}, u32[]{:S(2)}) collective-permute-start(bf16[256,1024]{1,0:T(8,128)(2,1)S(1)} %get-tuple-element.39.own_ref), channel_id=1, source_target_pairs={{0,1},{1,0},{2,3},{3,2},{4,5},{5,4},{6,7},{7,6},{8,9},{9,8},{10,11... | collective-permute-start | bytes 1572872 | tf_op jit(solution)/shard_map/ppermute | solution.py:47
  40.0 8.3 %collective-permute-start.8 = (bf16[128,1024]{1,0:T(8,128)(2,1)S(1)}, bf16[128,1024]{1,0:T(8,128)(2,1)S(1)}, u32[]{:S(2)}, u32[]{:S(2)}) collective-permute-start(bf16[128,1024]{1,0:T(8,128)(2,1)S(1)} %add_convert_fusion), channel_id=1, source_target_pairs={{8,0},{10,2},{12,4},{14,6},{16,8},{18,10},{20,12},{22,14},{24,16},... | collective-permute-start | bytes 786440 | tf_op jit(solution)/shard_map/ppermute | solution.py:43
  48.5 9.8 %collective-permute-start.9 = (bf16[128,1024]{1,0:T(8,128)(2,1)S(1)}, bf16[128,1024]{1,0:T(8,128)(2,1)S(1)}, u32[]{:S(2)}, u32[]{:S(2)}) collective-permute-start(bf16[128,1024]{1,0:T(8,128)(2,1)S(1)} %collect.1), channel_id=1, source_target_pairs={{8,0},{10,2},{12,4},{14,6},{16,8},{18,10},{20,12},{22,14},{24,16},... | collective-permute-start | bytes 786440 | tf_op jit(solution)/shard_map/ppermute | solution.py:530

commit v13 on v12

--- a/solution.py
+++ b/solution.py
@@ -63,54 +63,39 @@
     return pltpu.CompilerParams(vmem_limit_bytes=int(mib * 1024 * 1024))
 
 
-def pick_kernel(k_hbm, v_hbm, out_hbm, held, ready, in_sems, out_sems):
-    tokens, width = k_hbm.shape
-    rows, half = tokens // STEP, width // 2
-    parts = [(i, x, slice(c * half, (c + 1) * half)) for i, x in enumerate((k_hbm, v_hbm)) for c in (0, 1)]
-    copies = []
-    for n, (i, x, cols) in enumerate(parts):
-        copies.append(pltpu.make_async_copy(x.at[:, cols], held.at[i, :, cols], in_sems.at[n]))
-        copies[n].start()
+def pick_kernel(k_hbm, v_hbm, out_ref, held, sems):
+    tokens = k_hbm.shape[0]
+    rows = tokens // STEP
+    copies = [pltpu.make_async_copy(x, held.at[i], sems.at[i]) for i, x in enumerate((k_hbm, v_hbm))]
+    for copy in copies:
+        copy.start()
     at = lax.broadcasted_iota(jnp.int32, (rows, tokens), 0) * STEP
     choose = (at == lax.broadcasted_iota(jnp.int32, (rows, tokens), 1)).astype(BF16)
-    sent = []
-    for n, (i, x, cols) in enumerate(parts):
-        copies[n].wait()
-        ready[i * rows : (i + 1) * rows, cols] = nn(choose, held[i, :, cols]).astype(BF16)
-        block = pl.ds(i * rows, rows), cols
-        sent.append(pltpu.make_async_copy(ready.at[block], out_hbm.at[block], out_sems.at[n]))
-        sent[n].start()
-    for copy in sent:
+    for i, copy in enumerate(copies):
         copy.wait()
+        out_ref[i * rows : (i + 1) * rows] = nn(choose, held[i]).astype(BF16)
 
 
 def pick(keys, values):
     tokens, width = keys.shape
-    shape = (2 * tokens // STEP, width)
     return pl.pallas_call(
         pick_kernel,
         in_specs=[HBM_BLOCK, HBM_BLOCK],
-        out_specs=HBM_BLOCK,
-        out_shape=jax.ShapeDtypeStruct(shape, BF16),
-        scratch_shapes=[
-            pltpu.VMEM((2, tokens, width), BF16),
-            pltpu.VMEM(shape, BF16),
-            pltpu.SemaphoreType.DMA((4,)),
-            pltpu.SemaphoreType.DMA((4,)),
-        ],
+        out_shape=jax.ShapeDtypeStruct((2 * tokens // STEP, width), BF16),
+        scratch_shapes=[pltpu.VMEM((2, tokens, width), BF16), pltpu.SemaphoreType.DMA((2,))],
         compiler_params=params(63.5),
         name="pick",
     )(keys, values)
 
 
-def grad_attn_kernel(core_ref, own_ref, other_hbm, w_hbm, out_ref, done_ref, got, held, got_sem, sems):
+def grad_attn_kernel(part, core_ref, own_ref, other_hbm, w_hbm, after, out_ref, done_ref, got, held, got_sem, sems):
     pieces, tile, _ = held.shape
     core = core_ref[0]
     fetch = pltpu.make_async_copy(other_hbm, got, got_sem)
     fetch.start()
     copies = []
     for i in range(pieces):
-        rows = w_hbm.at[pl.ds((core * pieces + i) * tile, tile), :]
+        rows = w_hbm.at[pl.ds(((core * 2 + part) * pieces + i) * tile, tile), :]
         copies.append(pltpu.make_async_copy(rows, held.at[i], sems.at[i]))
         copies[i].start()
     done_ref[...] = jnp.zeros_like(done_ref)
@@ -122,29 +107,34 @@
         out_ref[:, i * tile : (i + 1) * tile] = nt(cot, held[i]).astype(BF16)
 
 
-def grad_attn(core, own, other, weight):
+def grad_attn(part, core, own, other, weight, after):
     tokens, width = own.shape
-    pieces = 4
-    return pl.pallas_call(
-        grad_attn_kernel,
-        in_specs=[SMEM_BLOCK, VMEM_BLOCK, HBM_BLOCK, HBM_BLOCK],
+    pieces = 2
+    return pl.pallas_call(
+        functools.partial(grad_attn_kernel, part),
+        in_specs=[SMEM_BLOCK, VMEM_BLOCK, HBM_BLOCK, HBM_BLOCK, pl.BlockSpec(memory_space=pl.ANY)],
         out_specs=[VMEM_BLOCK] * 2,
         out_shape=[
-            jax.ShapeDtypeStruct((tokens, width), BF16),
+            jax.ShapeDtypeStruct((tokens, width // 2), BF16),
             jax.ShapeDtypeStruct((8, DH), F32),
         ],
         scratch_shapes=[
             pltpu.VMEM((tokens, width), BF16),
-            pltpu.VMEM((pieces, width // pieces, weight.shape[1]), BF16),
+            pltpu.VMEM((pieces, width // (2 * pieces), weight.shape[1]), BF16),
             pltpu.SemaphoreType.DMA,
             pltpu.SemaphoreType.DMA((pieces,)),
         ],
         compiler_params=params(52),
         cost_estimate=pl.CostEstimate(
-            flops=4 * tokens * width * width, bytes_accessed=6 * width * width, transcendentals=0
+            flops=2 * tokens * width * width, bytes_accessed=3 * width * width, transcendentals=0
         ),
-        name="grad_attn",
-    )(core, own, other, weight)
+        name=f"grad_attn{part}",
+    )(core, own, other, weight, after)
+
+
+def of_head(halves, h):
+    count = halves[0].shape[1] // DH
+    return halves[h // count][:, (h % count) * DH : (h % count + 1) * DH]
 
 
 def project_kernel(core_ref, own_ref, other_ref, w_hbm, out_ref, held, sems):
@@ -219,7 +209,7 @@
 
 
 def near_kernel(
-    levels, me_ref, bounds_ref, q_ref, k_ref, v_ref, ga_ref, far4_ref, far1_ref,
+    levels, me_ref, bounds_ref, q_ref, k_ref, v_ref, low_ga_ref, high_ga_ref, far4_ref, far1_ref,
     grown_ref, gp_ref, stat_ref, bias_ref,
 ):
     tokens = q_ref.shape[0]
@@ -233,7 +223,7 @@
         scores = nt(k, q_ref[:, cols]) + bias_ref[:near]
         top = jnp.max(scores, axis=0, keepdims=True)
         grown = jnp.exp2((scores - top) * POWER)
-        grad_prob = nt(v, ga_ref[:, cols])
+        grad_prob = nt(v, of_head((low_ga_ref, high_ga_ref), h))
         grown_ref[h] = grown
         gp_ref[h] = grad_prob
         stat_ref[h, 0:1] = top
@@ -248,7 +238,7 @@
     early = jax.ShapeDtypeStruct((heads, near, tokens), F32)
     return pl.pallas_call(
         functools.partial(near_kernel, levels),
-        in_specs=[SMEM_BLOCK, SMEM_BLOCK] + [VMEM_BLOCK] * 6,
+        in_specs=[SMEM_BLOCK, SMEM_BLOCK] + [VMEM_BLOCK] * 7,
         out_specs=[VMEM_BLOCK] * 4,
         out_shape=[
             early,
@@ -261,11 +251,12 @@
             flops=4 * tokens * near * width, bytes_accessed=16 * tokens * width, transcendentals=0
         ),
         name="attention_near",
-    )(me, bounds, q, k, v, ga, far4, far1)
+    )(me, bounds, q, k, v, *ga, far4, far1)
 
 
 def far_kernel(levels, *refs):
-    me_ref, core_ref, q_ref, ga_ref, grown_ref, gp_ref, stat_ref, bias_ref = refs[:8]
+    me_ref, core_ref, q_ref, low_ga_ref, high_ga_ref, grown_ref, gp_ref, stat_ref, bias_ref = refs[:9]
+    refs = refs[1:]
     arrived_refs = refs[8 : 6 + levels]
     w_ref, u_ref, use_ref, far_ref, pass_ref = refs[6 + levels : 11 + levels]
     gfar_refs = refs[11 + levels :]
@@ -277,7 +268,7 @@
     pass_ref[...] = jnp.full(pass_ref.shape, passes, F32)
     for h in range(q_ref.shape[1] // DH):
         cols = slice(h * DH, (h + 1) * DH)
-        q, ga = q_ref[:, cols], ga_ref[:, cols]
+        q, ga = q_ref[:, cols], of_head((low_ga_ref, high_ga_ref), h)
         far = sort_arrived(first, *[r[:, cols] for r in arrived_refs])
         k = jnp.concatenate([f[:rows] for f in far], 0)
         v = jnp.concatenate([f[rows:] for f in far], 0)
@@ -319,7 +310,7 @@
     prob = jax.ShapeDtypeStruct((heads, (levels - 1) * rows, tokens), BF16)
     return pl.pallas_call(
         functools.partial(far_kernel, levels),
-        in_specs=[SMEM_BLOCK] * 2 + [VMEM_BLOCK] * (6 + len(arrived)),
+        in_specs=[SMEM_BLOCK] * 2 + [VMEM_BLOCK] * (7 + len(arrived)),
         out_specs=[VMEM_BLOCK] * (4 + levels),
         out_shape=[
             prob,
@@ -334,11 +325,11 @@
             flops=8 * tokens * levels * rows * width, bytes_accessed=16 * tokens * width, transcendentals=0
         ),
         name="attention_far",
-    )(me, core, q, ga, grown, grad_prob, stats, bias, *arrived)
+    )(me, core, q, *ga, grown, grad_prob, stats, bias, *arrived)
 
 
 def local_kernel(
-    q_ref, k_ref, v_ref, ga_ref, far4_ref, far1_ref, far_ref, grown_ref, gp_ref, use_ref, w_ref, u_ref,
+    q_ref, k_ref, v_ref, low_ga_ref, high_ga_ref, far4_ref, far1_ref, far_ref, grown_ref, gp_ref, use_ref, w_ref, u_ref,
     attn_ref, gq_ref, gk_ref, gv_ref, g4_ref,
 ):
     tokens = q_ref.shape[0]
@@ -360,7 +351,7 @@
         attn_ref[:, cols] = tn(weights, v).astype(BF16)
         gq_ref[:, cols] = (tn(grad_scores, k) * SCALE).astype(BF16)
         gk = nn(near_scores, q_ref[:, cols]) * SCALE
-        gv = nn(near_weights, ga_ref[:, cols])
+        gv = nn(near_weights, of_head((low_ga_ref, high_ga_ref), h))
         gk_ref[:, cols] = gk[:tokens]
         gv_ref[:, cols] = gv[:tokens]
         g4_ref[:rows, cols] = gk[tokens:].astype(BF16)
@@ -492,10 +483,11 @@
     picked = pick(keys, values)
     far4 = lax.ppermute(picked, "ctx", hop(4, n))
     far1 = lax.ppermute(picked, "ctx", hop(1, n))
-    ga, done = grad_attn(core, cotangent, other_cot, out_weight)
+    low_ga, done = grad_attn(0, core, cotangent, other_cot, out_weight, me)
 
     hops, twos = hop(4, n), pairs(n)
     two, three = small(choose_kernel, "choose", 2, me, core, picked, far4, done)
+    ga = low_ga, grad_attn(1, core, cotangent, other_cot, out_weight, two)[0]
     two = mixed(two, (hops, twos))
     three = mixed(three, (twos, hops))
     arrived = [two, three]
@@ -523,7 +515,7 @@
     two = mixed(three, (ones, hops))
     three = mixed((four.astype(F32) + one.astype(F32) * passes).astype(BF16), (hops, twos))
     attn, gq, gk, gv, g4 = attention_local(
-        queries, keys, values, ga, far4, far1, far, grown, grad_prob, use, weights, grad_scores
+        queries, keys, values, *ga, far4, far1, far, grown, grad_prob, use, weights, grad_scores
     )
     back = (one, two, three)
     g4 = small(collect_kernel, "collect", 1, me, core, g4, *back)

time: 59.9 us -> 58.2 us (0.972)
  waiting for transfers between devices: 14.3 us -> 11.7 us
    ppermute x5, waiting for transfers between devices: 9.62 us -> 6.97 us  [mixed(): return lax.ppermute(block, ('ctx', 'head'), route)]
    pallas_call x2 -> x3, Pallas kernels: 7.55 us -> 8.22 us  [the longest x2 6.04 us: grad_attn(): pl.pallas_call(functools.partial(grad_attn_kernel, part), in_specs=[SMEM_...]
  transfers between devices with their start and end apart: 10 -> 10, of which waited for: 4 -> 3; matrix products, arithmetic and copies ran while one was open for 0% -> 0% of each run, Pallas kernels for 28% -> 30%
where the time goes in v13:
time: 58.2 us; the launch traced here: 57.8 us
  starting transfers between devices  23.1 us (40%)
  Pallas kernels  20.9 us (36%)
  waiting for transfers between devices  11.7 us (20%)
  local copies, waits for them, and re-layouts  1.07 us (2%)
  between operations  0.88 us (2%)
    ppermute x5, starting transfers between devices, mixed(): return lax.ppermute(block, ('ctx', 'head'), route)  13.4 us
    ppermute x5, waiting for transfers between devices, mixed(): return lax.ppermute(block, ('ctx', 'head'), route)  6.97 us
    pallas_call x2, Pallas kernels, grad_attn(): pl.pallas_call(functools.partial(grad_attn_kernel, part), in_specs=[SMEM_...  6.04 us
    ppermute x1, waiting for transfers between devices, per_device(): last = lax.ppermute(g4, 'ctx', hop(-4, n))  4.71 us
    ppermute x1, starting transfers between devices, per_device(): far4 = lax.ppermute(picked, 'ctx', hop(4, n))  4.51 us
    pallas_call x1, Pallas kernels, project(): pl.pallas_call(project_kernel, in_specs=[SMEM_BLOCK, VMEM_BLOCK, VMEM_BLO...  3.73 us
    ppermute x1, starting transfers between devices, per_device(): far1 = lax.ppermute(picked, 'ctx', hop(1, n))  3.41 us
    pallas_call x1, Pallas kernels, attention_local(): pl.pallas_call(local_kernel, in_specs=[VMEM_BLOCK] * (1 + len(operands)),...  2.78 us
  transfers between devices with their start and end apart: 10, of which 3 were waited for; matrix products, arithmetic and copies ran while one was open for 0% of the time, Pallas kernels for 30%

profile of v13, /device:TPU:0, one launch (start us, length us, event | category | flops | bytes accessed | tf_op | source)
XLA Modules:
  0.0 57.8 jit_solution(12737345512071323499)
XLA Ops:
  0.6 0.5 collective-permute-start
  1.1 2.2 %pick.1.picked_ref = bf16[128,1024]{1,0:T(8,128)(2,1)} custom-call(bf16[256,1024]{1,0:T(8,128)(2,1)} %k_ref.3, bf16[256,1024]{1,0:T(8,128)(2,1)} %v_ref.3), custom_call_target="tpu_custom_call" | custom-call | tf_op jit(solution)/shard_map/pick/pallas_call | solution.py:81
  3.3 4.5 %collective-permute-start.1 = (bf16[128,1024]{1,0:T(8,128)(2,1)}, bf16[128,1024]{1,0:T(8,128)(2,1)S(1)}, u32[]{:S(2)}, u32[]{:S(2)}) collective-permute-start(bf16[128,1024]{1,0:T(8,128)(2,1)} %pick.1.picked_ref), channel_id=1, source_target_pairs={{0,8},{2,10},{4,12},{6,14},{8,16},{10,18},{12,20},{14,22},{16,24},... | collective-permute-start | bytes 786440 | tf_op jit(solution)/shard_map/ppermute | solution.py:484
  7.9 3.4 %collective-permute-start.2 = (bf16[128,1024]{1,0:T(8,128)(2,1)}, bf16[128,1024]{1,0:T(8,128)(2,1)S(1)}, u32[]{:S(2)}, u32[]{:S(2)}) collective-permute-start(bf16[128,1024]{1,0:T(8,128)(2,1)} %pick.1.picked_ref), channel_id=1, source_target_pairs={{0,2},{2,4},{4,6},{6,8},{8,10},{10,12},{12,14},{14,16},{16,18},{18... | collective-permute-start | bytes 786440 | tf_op jit(solution)/shard_map/ppermute | solution.py:485
  11.3 1.0 %copy-done.3 = bf16[256,1024]{1,0:T(8,128)(2,1)S(1)} copy-done((bf16[256,1024]{1,0:T(8,128)(2,1)S(1)}, bf16[256,1024]{1,0:T(8,128)(2,1)}, u32[]{:S(2)}) %copy-start.3) | copy-done | bytes 524312
  12.3 3.0 %grad_attn0.1 = (bf16[256,512]{1,0:T(8,128)(2,1)S(1)}, f32[8,128]{1,0:T(8,128)S(1)}) custom-call(s32[1]{0:T(128)} %bitcast.core_ref.refs_1_, bf16[256,1024]{1,0:T(8,128)(2,1)S(1)} %copy-done.3, bf16[256,1024]{1,0:T(8,128)(2,1)} %collective-permute-done.other_hbm, bf16[2048,2048]{1,0:T(8,128)(2,1)} %w_hbm.5, s32[1]{0:T(128)} %bitcast.1.after.me_ref.refs_0_), custom_call_target="tpu_custom_call" | custom-call | flops 536870912 | bytes 3145728 | tf_op jit(solution)/shard_map/grad_attn0/pallas_call | solution.py:113
  15.4 0.1 choose.1
  15.5 3.5 %collective-permute-start.3 = (bf16[128,1024]{1,0:T(8,128)(2,1)S(1)}, bf16[128,1024]{1,0:T(8,128)(2,1)S(1)}, u32[]{:S(2)}, u32[]{:S(2)}) collective-permute-start(bf16[128,1024]{1,0:T(8,128)(2,1)S(1)} %get-tuple-element.30.after), channel_id=1, source_target_pairs={{0,8},{2,10},{4,12},{6,14},{8,16},{10,18},{12,20},{14,22},{16,24},... | collective-permute-start | bytes 786440 | tf_op jit(solution)/shard_map/ppermute | solution.py:43
  19.0 3.6 %collective-permute-start.4 = (bf16[128,1024]{1,0:T(8,128)(2,1)S(1)}, bf16[128,1024]{1,0:T(8,128)(2,1)S(1)}, u32[]{:S(2)}, u32[]{:S(2)}) collective-permute-start(bf16[128,1024]{1,0:T(8,128)(2,1)S(1)} %get-tuple-element.36), channel_id=1, source_target_pairs={{0,4},{2,6},{4,0},{6,2},{8,12},{10,14},{12,8},{14,10},{16,20},{18,... | collective-permute-start | bytes 786440 | tf_op jit(solution)/shard_map/ppermute | solution.py:43
  22.6 3.0 %grad_attn1.1 = (bf16[256,512]{1,0:T(8,128)(2,1)S(1)}, f32[8,128]{1,0:T(8,128)}) custom-call(s32[1]{0:T(128)} %bitcast.core_ref.refs_1_, bf16[256,1024]{1,0:T(8,128)(2,1)S(1)} %copy-done.3, bf16[256,1024]{1,0:T(8,128)(2,1)} %collective-permute-done.other_hbm, bf16[2048,2048]{1,0:T(8,128)(2,1)} %w_hbm.5, bf16[128,1024]{1,0:T(8,128)(2,1)S(1)} %get-tuple-element.30.after), custom_call_target="tpu_custom_call" | custom-call | flops 536870912 | bytes 3145728 | tf_op jit(solution)/shard_map/grad_attn1/pallas_call | solution.py:113
  25.6 2.1 %attention_near.1 = (f32[8,384,256]{2,1,0:T(8,128)S(1)}, f32[8,384,256]{2,1,0:T(8,128)S(1)}, f32[8,8,256]{2,1,0:T(8,128)S(1)}, f32[512,256]{1,0:T(8,128)S(1)}) custom-call(s32[1]{0:T(128)} %bitcast.1.after.me_ref.refs_0_, s32[4]{0:T(128)S(1)} %copy-done.5, bf16[256,1024]{1,0:T(8,128)(2,1)S(1)} %copy-done, bf16[256,1024]{1,0:T(8,128)(2,1)S(1)} %copy-done.1, ...), custom_call_target="tpu_custom_call" | custom-call | flops 402653184 | bytes 4194304 | tf_op jit(solution)/shard_map/attention_near/pallas_call | solution.py:239
  27.8 2.6 %attention_far.1 = (bf16[8,192,256]{2,1,0:T(8,128)(2,1)S(1)}, bf16[8,192,256]{2,1,0:T(8,128)(2,1)S(1)}, f32[8,8,256]{2,1,0:T(8,128)S(1)}, bf16[2,128,1024]{2,1,0...) custom-call(s32[1]{0:T(128)} %bitcast.1.after.me_ref.refs_0_, ...), custom_call_target="tpu_custom_call" | custom-call | flops 536870912 | bytes 4194304 | tf_op jit(solution)/shard_map/attention_far/pallas_call | solution.py:311
  30.4 1.2 %collective-permute-start.6 = (bf16[128,1024]{1,0:T(8,128)(2,1)S(1)}, bf16[128,1024]{1,0:T(8,128)(2,1)S(1)}, u32[]{:S(2)}, u32[]{:S(2)}) collective-permute-start(bf16[128,1024]{1,0:T(8,128)(2,1)S(1)} %get-tuple-element.46), channel_id=1, source_target_pairs={{4,0},{6,2},{0,4},{2,6},{12,8},{14,10},{8,12},{10,14},{20,16},{22,... | collective-permute-start | bytes 786440 | tf_op jit(solution)/shard_map/ppermute | solution.py:43
  31.6 3.9 %collective-permute-start.7 = (bf16[128,1024]{1,0:T(8,128)(2,1)S(1)}, bf16[128,1024]{1,0:T(8,128)(2,1)S(1)}, u32[]{:S(2)}, u32[]{:S(2)}) collective-permute-start(bf16[128,1024]{1,0:T(8,128)(2,1)S(1)} %get-tuple-element.47), channel_id=1, source_target_pairs={{2,0},{4,2},{6,4},{0,6},{10,8},{12,10},{14,12},{8,14},{18,16},{20,... | collective-permute-start | bytes 786440 | tf_op jit(solution)/shard_map/ppermute | solution.py:43
  35.4 2.8 %attention_local.1 = (bf16[256,1024]{1,0:T(8,128)(2,1)S(1)}, bf16[256,1024]{1,0:T(8,128)(2,1)}, f32[256,1024]{1,0:T(8,128)S(1)}, f32[256,1024]{1,0:T(8,128)S(1)}, bf16[128,1024]{1,0:T(8,128)(2,1)S(1)}) custom-call(bf16[256,1024]{1,0:T(8,128)(2,1)S(1)} %copy-done, bf16[256,1024]{1,0:T(8,128)(2,1)S(1)} %copy-done.1, bf16[256,1024]{1,0:T(8,128)(2,1)S(1)} %copy-done.2, ...), custom_call_target="tpu_custom_call" | custom-call | flops 805306368 | bytes 4194304 | tf_op jit(solution)/shard_map/attention_local/pallas_call | solution.py:365
  38.2 0.1 add_convert_fusion
  38.3 1.3 %collective-permute-start.8 = (bf16[128,1024]{1,0:T(8,128)(2,1)S(1)}, bf16[128,1024]{1,0:T(8,128)(2,1)S(1)}, u32[]{:S(2)}, u32[]{:S(2)}) collective-permute-start(bf16[128,1024]{1,0:T(8,128)(2,1)S(1)} %add_convert_fusion), channel_id=1, source_target_pairs={{8,0},{10,2},{12,4},{14,6},{16,8},{18,10},{20,12},{22,14},{24,16},... | collective-permute-start | bytes 786440 | tf_op jit(solution)/shard_map/ppermute | solution.py:43
  39.6 0.2 collective-permute-done.7.two_ref
  39.8 6.8 %collective-permute-done.8.three_ref = bf16[128,1024]{1,0:T(8,128)(2,1)S(1)} collective-permute-done((bf16[128,1024]{1,0:T(8,128)(2,1)S(1)}, bf16[128,1024]{1,0:T(8,128)(2,1)S(1)}, u32[]{:S(2)}, u32[]{:S(2)}) %collective-permute-start.8) | collective-permute-done | bytes 262176 | tf_op jit(solution)/shard_map/ppermute | solution.py:43
  46.6 0.2 collect.1
  46.8 1.3 %collective-permute-start.9 = (bf16[128,1024]{1,0:T(8,128)(2,1)S(1)}, bf16[128,1024]{1,0:T(8,128)(2,1)S(1)}, u32[]{:S(2)}, u32[]{:S(2)}) collective-permute-start(bf16[128,1024]{1,0:T(8,128)(2,1)S(1)} %collect.1), channel_id=1, source_target_pairs={{8,0},{10,2},{12,4},{14,6},{16,8},{18,10},{20,12},{22,14},{24,16},... | collective-permute-start | bytes 786440 | tf_op jit(solution)/shard_map/ppermute | solution.py:522
  48.1 3.7 %project.1 = bf16[256,1024]{1,0:T(8,128)(2,1)} custom-call(s32[1]{0:T(128)} %bitcast.core_ref.refs_1_, bf16[256,1024]{1,0:T(8,128)(2,1)S(1)} %get-tuple-element.41.own_ref, bf16[256,1024]{1,0:T(8,128)(2,1)S(1)} %collective-permute-done.5.other_ref, bf16[2048,2048]{1,0:T(8,128)(2,1)} %w_hbm.5), custom_call_target="tpu_custom_call" | custom-call | flops 1073741824 | bytes 6291456 | tf_op jit(solution)/shard_map/project/pallas_call | solution.py:162
  51.8 4.7 %collective-permute-done.9.last_ref = bf16[128,1024]{1,0:T(8,128)(2,1)S(1)} collective-permute-done((bf16[128,1024]{1,0:T(8,128)(2,1)S(1)}, bf16[128,1024]{1,0:T(8,128)(2,1)S(1)}, u32[]{:S(2)}, u32[]{:S(2)}) %collective-permute-start.9) | collective-permute-done | bytes 262176 | tf_op jit(solution)/shard_map/ppermute | solution.py:522
  56.5 1.3 %settle.1 = (bf16[256,1024]{1,0:T(8,128)(2,1)}, bf16[256,1024]{1,0:T(8,128)(2,1)}) custom-call(s32[1]{0:T(128)} %bitcast.1.after.me_ref.refs_0_, s32[1]{0:T(128)} %bitcast.core_ref.refs_1_, f32[256,1024]{1,0:T(8,128)S(1)} %get-tuple-element.43.gk_ref, f32[256,1024]{1,0:T(8,128)S(1)} %get-tuple-element.44.gv_ref, ...), custom_call_target="tpu_custom_call" | custom-call | tf_op jit(solution)/shard_map/settle/pallas_call | solution.py:458
  (19 shorter events, 0.1 us)
Async XLA Ops:
  0.6 10.7 %collective-permute-start = (bf16[256,1024]{1,0:T(8,128)(2,1)}, bf16[256,1024]{1,0:T(8,128)(2,1)}, u32[]{:S(2)}, u32[]{:S(2)}) collective-permute-start(bf16[256,1024]{1,0:T(8,128)(2,1)} %own_ref.3), channel_id=1, source_target_pairs={{0,1},{1,0},{2,3},{3,2},{4,5},{5,4},{6,7},{7,6},{8,9},{9,8},{10,11... | collective-permute-start | bytes 1572872 | tf_op jit(solution)/shard_map/ppermute | solution.py:47
  3.3 12.0 %collective-permute-start.1 = (bf16[128,1024]{1,0:T(8,128)(2,1)}, bf16[128,1024]{1,0:T(8,128)(2,1)S(1)}, u32[]{:S(2)}, u32[]{:S(2)}) collective-permute-start(bf16[128,1024]{1,0:T(8,128)(2,1)} %pick.1.picked_ref), channel_id=1, source_target_pairs={{0,8},{2,10},{4,12},{6,14},{8,16},{10,18},{12,20},{14,22},{16,24},... | collective-permute-start | bytes 786440 | tf_op jit(solution)/shard_map/ppermute | solution.py:484
  7.9 17.7 %collective-permute-start.2 = (bf16[128,1024]{1,0:T(8,128)(2,1)}, bf16[128,1024]{1,0:T(8,128)(2,1)S(1)}, u32[]{:S(2)}, u32[]{:S(2)}) collective-permute-start(bf16[128,1024]{1,0:T(8,128)(2,1)} %pick.1.picked_ref), channel_id=1, source_target_pairs={{0,2},{2,4},{4,6},{6,8},{8,10},{10,12},{12,14},{14,16},{16,18},{18... | collective-permute-start | bytes 786440 | tf_op jit(solution)/shard_map/ppermute | solution.py:485
  11.3 1.0 %copy-start.3 = (bf16[256,1024]{1,0:T(8,128)(2,1)S(1)}, bf16[256,1024]{1,0:T(8,128)(2,1)}, u32[]{:S(2)}) copy-start(bf16[256,1024]{1,0:T(8,128)(2,1)} %own_ref.3) | copy-start | bytes 1572868
  12.3 3.1 %copy-start.4 = (bf16[128,1024]{1,0:T(8,128)(2,1)S(1)}, bf16[128,1024]{1,0:T(8,128)(2,1)}, u32[]{:S(2)}) copy-start(bf16[128,1024]{1,0:T(8,128)(2,1)} %pick.1.picked_ref) | copy-start | bytes 786436
  15.5 12.3 %collective-permute-start.3 = (bf16[128,1024]{1,0:T(8,128)(2,1)S(1)}, bf16[128,1024]{1,0:T(8,128)(2,1)S(1)}, u32[]{:S(2)}, u32[]{:S(2)}) collective-permute-start(bf16[128,1024]{1,0:T(8,128)(2,1)S(1)} %get-tuple-element.30.after), channel_id=1, source_target_pairs={{0,8},{2,10},{4,12},{6,14},{8,16},{10,18},{12,20},{14,22},{16,24},... | collective-permute-start | bytes 786440 | tf_op jit(solution)/shard_map/ppermute | solution.py:43
  19.0 6.6 %copy-start = (bf16[256,1024]{1,0:T(8,128)(2,1)S(1)}, bf16[256,1024]{1,0:T(8,128)(2,1)}, u32[]{:S(2)}) copy-start(bf16[256,1024]{1,0:T(8,128)(2,1)} %q_ref.3) | copy-start | bytes 1572868
  19.0 6.6 %copy-start.1 = (bf16[256,1024]{1,0:T(8,128)(2,1)S(1)}, bf16[256,1024]{1,0:T(8,128)(2,1)}, u32[]{:S(2)}) copy-start(bf16[256,1024]{1,0:T(8,128)(2,1)} %k_ref.3) | copy-start | bytes 1572868
  19.0 6.6 %copy-start.2 = (bf16[256,1024]{1,0:T(8,128)(2,1)S(1)}, bf16[256,1024]{1,0:T(8,128)(2,1)}, u32[]{:S(2)}) copy-start(bf16[256,1024]{1,0:T(8,128)(2,1)} %v_ref.3) | copy-start | bytes 1572868
  19.0 6.6 %copy-start.5 = (s32[4]{0:T(128)S(1)}, s32[4]{0:T(128)}, u32[]{:S(2)}) copy-start(s32[4]{0:T(128)} %bounds_ref.1) | copy-start | bytes 52
  19.0 8.7 %collective-permute-start.4 = (bf16[128,1024]{1,0:T(8,128)(2,1)S(1)}, bf16[128,1024]{1,0:T(8,128)(2,1)S(1)}, u32[]{:S(2)}, u32[]{:S(2)}) collective-permute-start(bf16[128,1024]{1,0:T(8,128)(2,1)S(1)} %get-tuple-element.36), channel_id=1, source_target_pairs={{0,4},{2,6},{4,0},{6,2},{8,12},{10,14},{12,8},{14,10},{16,20},{18,... | collective-permute-start | bytes 786440 | tf_op jit(solution)/shard_map/ppermute | solution.py:43
  30.4 7.9 %collective-permute-start.6 = (bf16[128,1024]{1,0:T(8,128)(2,1)S(1)}, bf16[128,1024]{1,0:T(8,128)(2,1)S(1)}, u32[]{:S(2)}, u32[]{:S(2)}) collective-permute-start(bf16[128,1024]{1,0:T(8,128)(2,1)S(1)} %get-tuple-element.46), channel_id=1, source_target_pairs={{4,0},{6,2},{0,4},{2,6},{12,8},{14,10},{8,12},{10,14},{20,16},{22,... | collective-permute-start | bytes 786440 | tf_op jit(solution)/shard_map/ppermute | solution.py:43
  31.6 8.3 %collective-permute-start.7 = (bf16[128,1024]{1,0:T(8,128)(2,1)S(1)}, bf16[128,1024]{1,0:T(8,128)(2,1)S(1)}, u32[]{:S(2)}, u32[]{:S(2)}) collective-permute-start(bf16[128,1024]{1,0:T(8,128)(2,1)S(1)} %get-tuple-element.47), channel_id=1, source_target_pairs={{2,0},{4,2},{6,4},{0,6},{10,8},{12,10},{14,12},{8,14},{18,16},{20,... | collective-permute-start | bytes 786440 | tf_op jit(solution)/shard_map/ppermute | solution.py:43
  38.2 9.9 %collective-permute-start.5 = (bf16[256,1024]{1,0:T(8,128)(2,1)S(1)}, bf16[256,1024]{1,0:T(8,128)(2,1)S(1)}, u32[]{:S(2)}, u32[]{:S(2)}) collective-permute-start(bf16[256,1024]{1,0:T(8,128)(2,1)S(1)} %get-tuple-element.41.own_ref), channel_id=1, source_target_pairs={{0,1},{1,0},{2,3},{3,2},{4,5},{5,4},{6,7},{7,6},{8,9},{9,8},{10,11... | collective-permute-start | bytes 1572872 | tf_op jit(solution)/shard_map/ppermute | solution.py:47
  38.3 8.3 %collective-permute-start.8 = (bf16[128,1024]{1,0:T(8,128)(2,1)S(1)}, bf16[128,1024]{1,0:T(8,128)(2,1)S(1)}, u32[]{:S(2)}, u32[]{:S(2)}) collective-permute-start(bf16[128,1024]{1,0:T(8,128)(2,1)S(1)} %add_convert_fusion), channel_id=1, source_target_pairs={{8,0},{10,2},{12,4},{14,6},{16,8},{18,10},{20,12},{22,14},{24,16},... | collective-permute-start | bytes 786440 | tf_op jit(solution)/shard_map/ppermute | solution.py:43
  46.8 9.8 %collective-permute-start.9 = (bf16[128,1024]{1,0:T(8,128)(2,1)S(1)}, bf16[128,1024]{1,0:T(8,128)(2,1)S(1)}, u32[]{:S(2)}, u32[]{:S(2)}) collective-permute-start(bf16[128,1024]{1,0:T(8,128)(2,1)S(1)} %collect.1), channel_id=1, source_target_pairs={{8,0},{10,2},{12,4},{14,6},{16,8},{18,10},{20,12},{22,14},{24,16},... | collective-permute-start | bytes 786440 | tf_op jit(solution)/shard_map/ppermute | solution.py:522

commit v14 on v13

--- a/solution.py
+++ b/solution.py
@@ -109,7 +109,7 @@
 
 def grad_attn(part, core, own, other, weight, after):
     tokens, width = own.shape
-    pieces = 2
+    pieces = 4
     return pl.pallas_call(
         functools.partial(grad_attn_kernel, part),
         in_specs=[SMEM_BLOCK, VMEM_BLOCK, HBM_BLOCK, HBM_BLOCK, pl.BlockSpec(memory_space=pl.ANY)],

time: 58.2 us -> 61 us (1.048)
  Pallas kernels: 20.9 us -> 23.9 us
    pallas_call x2, Pallas kernels: 6.04 us -> 9.02 us  [grad_attn(): pl.pallas_call(functools.partial(grad_attn_kernel, part), in_specs=[SMEM_...]
  transfers between devices with their start and end apart: 10 -> 10, of which waited for: 3 -> 2; matrix products, arithmetic and copies ran while one was open for 0% -> 0% of each run, Pallas kernels for 30% -> 33%
where the time goes in v14:
time: 61 us; the launch traced here: 60.6 us
  Pallas kernels  23.9 us (39%)
  starting transfers between devices  23 us (38%)
  waiting for transfers between devices  11.7 us (19%)
  local copies, waits for them, and re-layouts  1.07 us (2%)
  between operations  0.88 us (1%)
    ppermute x5, starting transfers between devices, mixed(): return lax.ppermute(block, ('ctx', 'head'), route)  13.2 us
    pallas_call x2, Pallas kernels, grad_attn(): pl.pallas_call(functools.partial(grad_attn_kernel, part), in_specs=[SMEM_...  9.02 us
    ppermute x5, waiting for transfers between devices, mixed(): return lax.ppermute(block, ('ctx', 'head'), route)  6.97 us
    ppermute x1, waiting for transfers between devices, per_device(): last = lax.ppermute(g4, 'ctx', hop(-4, n))  4.71 us
    ppermute x1, starting transfers between devices, per_device(): far4 = lax.ppermute(picked, 'ctx', hop(4, n))  4.51 us
    pallas_call x1, Pallas kernels, project(): pl.pallas_call(project_kernel, in_specs=[SMEM_BLOCK, VMEM_BLOCK, VMEM_BLO...  3.73 us
    ppermute x1, starting transfers between devices, per_device(): far1 = lax.ppermute(picked, 'ctx', hop(1, n))  3.41 us
    pallas_call x1, Pallas kernels, attention_local(): pl.pallas_call(local_kernel, in_specs=[VMEM_BLOCK] * (1 + len(operands)),...  2.78 us
  transfers between devices with their start and end apart: 10, of which 2 were waited for; matrix products, arithmetic and copies ran while one was open for 0% of the time, Pallas kernels for 33%

profile of v14, /device:TPU:0, one launch (start us, length us, event | category | flops | bytes accessed | tf_op | source)
XLA Modules:
  0.0 60.6 jit_solution(15643955274171814099)
XLA Ops:
  0.6 0.5 collective-permute-start
  1.1 2.2 %pick.1.picked_ref = bf16[128,1024]{1,0:T(8,128)(2,1)} custom-call(bf16[256,1024]{1,0:T(8,128)(2,1)} %k_ref.3, bf16[256,1024]{1,0:T(8,128)(2,1)} %v_ref.3), custom_call_target="tpu_custom_call" | custom-call | tf_op jit(solution)/shard_map/pick/pallas_call | solution.py:81
  3.3 4.5 %collective-permute-start.1 = (bf16[128,1024]{1,0:T(8,128)(2,1)}, bf16[128,1024]{1,0:T(8,128)(2,1)S(1)}, u32[]{:S(2)}, u32[]{:S(2)}) collective-permute-start(bf16[128,1024]{1,0:T(8,128)(2,1)} %pick.1.picked_ref), channel_id=1, source_target_pairs={{0,8},{2,10},{4,12},{6,14},{8,16},{10,18},{12,20},{14,22},{16,24},... | collective-permute-start | bytes 786440 | tf_op jit(solution)/shard_map/ppermute | solution.py:484
  7.9 3.4 %collective-permute-start.2 = (bf16[128,1024]{1,0:T(8,128)(2,1)}, bf16[128,1024]{1,0:T(8,128)(2,1)S(1)}, u32[]{:S(2)}, u32[]{:S(2)}) collective-permute-start(bf16[128,1024]{1,0:T(8,128)(2,1)} %pick.1.picked_ref), channel_id=1, source_target_pairs={{0,2},{2,4},{4,6},{6,8},{8,10},{10,12},{12,14},{14,16},{16,18},{18... | collective-permute-start | bytes 786440 | tf_op jit(solution)/shard_map/ppermute | solution.py:485
  11.3 0.0 copy-start.3
  11.3 1.0 %copy-done.3 = bf16[256,1024]{1,0:T(8,128)(2,1)S(1)} copy-done((bf16[256,1024]{1,0:T(8,128)(2,1)S(1)}, bf16[256,1024]{1,0:T(8,128)(2,1)}, u32[]{:S(2)}) %copy-start.3) | copy-done | bytes 524312
  12.3 4.5 %grad_attn0.1 = (bf16[256,512]{1,0:T(8,128)(2,1)S(1)}, f32[8,128]{1,0:T(8,128)S(1)}) custom-call(s32[1]{0:T(128)} %bitcast.core_ref.refs_1_, bf16[256,1024]{1,0:T(8,128)(2,1)S(1)} %copy-done.3, bf16[256,1024]{1,0:T(8,128)(2,1)} %collective-permute-done.other_hbm, bf16[2048,2048]{1,0:T(8,128)(2,1)} %w_hbm.5, s32[1]{0:T(128)} %bitcast.1.after.me_ref.refs_0_), custom_call_target="tpu_custom_call" | custom-call | flops 536870912 | bytes 3145728 | tf_op jit(solution)/shard_map/grad_attn0/pallas_call | solution.py:113
  16.9 0.1 choose.1
  17.0 3.5 %collective-permute-start.3 = (bf16[128,1024]{1,0:T(8,128)(2,1)S(1)}, bf16[128,1024]{1,0:T(8,128)(2,1)S(1)}, u32[]{:S(2)}, u32[]{:S(2)}) collective-permute-start(bf16[128,1024]{1,0:T(8,128)(2,1)S(1)} %get-tuple-element.30.after), channel_id=1, source_target_pairs={{0,8},{2,10},{4,12},{6,14},{8,16},{10,18},{12,20},{14,22},{16,24},... | collective-permute-start | bytes 786440 | tf_op jit(solution)/shard_map/ppermute | solution.py:43
  20.5 3.6 %collective-permute-start.4 = (bf16[128,1024]{1,0:T(8,128)(2,1)S(1)}, bf16[128,1024]{1,0:T(8,128)(2,1)S(1)}, u32[]{:S(2)}, u32[]{:S(2)}) collective-permute-start(bf16[128,1024]{1,0:T(8,128)(2,1)S(1)} %get-tuple-element.36), channel_id=1, source_target_pairs={{0,4},{2,6},{4,0},{6,2},{8,12},{10,14},{12,8},{14,10},{16,20},{18,... | collective-permute-start | bytes 786440 | tf_op jit(solution)/shard_map/ppermute | solution.py:43
  24.1 4.5 %grad_attn1.1 = (bf16[256,512]{1,0:T(8,128)(2,1)S(1)}, f32[8,128]{1,0:T(8,128)}) custom-call(s32[1]{0:T(128)} %bitcast.core_ref.refs_1_, bf16[256,1024]{1,0:T(8,128)(2,1)S(1)} %copy-done.3, bf16[256,1024]{1,0:T(8,128)(2,1)} %collective-permute-done.other_hbm, bf16[2048,2048]{1,0:T(8,128)(2,1)} %w_hbm.5, bf16[128,1024]{1,0:T(8,128)(2,1)S(1)} %get-tuple-element.30.after), custom_call_target="tpu_custom_call" | custom-call | flops 536870912 | bytes 3145728 | tf_op jit(solution)/shard_map/grad_attn1/pallas_call | solution.py:113
  28.6 2.1 %attention_near.1 = (f32[8,384,256]{2,1,0:T(8,128)S(1)}, f32[8,384,256]{2,1,0:T(8,128)S(1)}, f32[8,8,256]{2,1,0:T(8,128)S(1)}, f32[512,256]{1,0:T(8,128)S(1)}) custom-call(s32[1]{0:T(128)} %bitcast.1.after.me_ref.refs_0_, s32[4]{0:T(128)S(1)} %copy-done.5, bf16[256,1024]{1,0:T(8,128)(2,1)S(1)} %copy-done, bf16[256,1024]{1,0:T(8,128)(2,1)S(1)} %copy-done.1, ...), custom_call_target="tpu_custom_call" | custom-call | flops 402653184 | bytes 4194304 | tf_op jit(solution)/shard_map/attention_near/pallas_call | solution.py:239
  30.7 2.6 %attention_far.1 = (bf16[8,192,256]{2,1,0:T(8,128)(2,1)S(1)}, bf16[8,192,256]{2,1,0:T(8,128)(2,1)S(1)}, f32[8,8,256]{2,1,0:T(8,128)S(1)}, bf16[2,128,1024]{2,1,0...) custom-call(s32[1]{0:T(128)} %bitcast.1.after.me_ref.refs_0_, ...), custom_call_target="tpu_custom_call" | custom-call | flops 536870912 | bytes 4194304 | tf_op jit(solution)/shard_map/attention_far/pallas_call | solution.py:311
  33.3 0.6 collective-permute-start.6
  33.9 4.3 %collective-permute-start.7 = (bf16[128,1024]{1,0:T(8,128)(2,1)S(1)}, bf16[128,1024]{1,0:T(8,128)(2,1)S(1)}, u32[]{:S(2)}, u32[]{:S(2)}) collective-permute-start(bf16[128,1024]{1,0:T(8,128)(2,1)S(1)} %get-tuple-element.47), channel_id=1, source_target_pairs={{2,0},{4,2},{6,4},{0,6},{10,8},{12,10},{14,12},{8,14},{18,16},{20,... | collective-permute-start | bytes 786440 | tf_op jit(solution)/shard_map/ppermute | solution.py:43
  38.3 2.8 %attention_local.1 = (bf16[256,1024]{1,0:T(8,128)(2,1)S(1)}, bf16[256,1024]{1,0:T(8,128)(2,1)}, f32[256,1024]{1,0:T(8,128)S(1)}, f32[256,1024]{1,0:T(8,128)S(1)}, bf16[128,1024]{1,0:T(8,128)(2,1)S(1)}) custom-call(bf16[256,1024]{1,0:T(8,128)(2,1)S(1)} %copy-done, bf16[256,1024]{1,0:T(8,128)(2,1)S(1)} %copy-done.1, bf16[256,1024]{1,0:T(8,128)(2,1)S(1)} %copy-done.2, ...), custom_call_target="tpu_custom_call" | custom-call | flops 805306368 | bytes 4194304 | tf_op jit(solution)/shard_map/attention_local/pallas_call | solution.py:365
  41.0 0.1 add_convert_fusion
  41.1 1.3 %collective-permute-start.8 = (bf16[128,1024]{1,0:T(8,128)(2,1)S(1)}, bf16[128,1024]{1,0:T(8,128)(2,1)S(1)}, u32[]{:S(2)}, u32[]{:S(2)}) collective-permute-start(bf16[128,1024]{1,0:T(8,128)(2,1)S(1)} %add_convert_fusion), channel_id=1, source_target_pairs={{8,0},{10,2},{12,4},{14,6},{16,8},{18,10},{20,12},{22,14},{24,16},... | collective-permute-start | bytes 786440 | tf_op jit(solution)/shard_map/ppermute | solution.py:43
  42.4 7.0 %collective-permute-done.8.three_ref = bf16[128,1024]{1,0:T(8,128)(2,1)S(1)} collective-permute-done((bf16[128,1024]{1,0:T(8,128)(2,1)S(1)}, bf16[128,1024]{1,0:T(8,128)(2,1)S(1)}, u32[]{:S(2)}, u32[]{:S(2)}) %collective-permute-start.8) | collective-permute-done | bytes 262176 | tf_op jit(solution)/shard_map/ppermute | solution.py:43
  49.4 0.2 collect.1
  49.6 1.3 %collective-permute-start.9 = (bf16[128,1024]{1,0:T(8,128)(2,1)S(1)}, bf16[128,1024]{1,0:T(8,128)(2,1)S(1)}, u32[]{:S(2)}, u32[]{:S(2)}) collective-permute-start(bf16[128,1024]{1,0:T(8,128)(2,1)S(1)} %collect.1), channel_id=1, source_target_pairs={{8,0},{10,2},{12,4},{14,6},{16,8},{18,10},{20,12},{22,14},{24,16},... | collective-permute-start | bytes 786440 | tf_op jit(solution)/shard_map/ppermute | solution.py:522
  50.9 3.7 %project.1 = bf16[256,1024]{1,0:T(8,128)(2,1)} custom-call(s32[1]{0:T(128)} %bitcast.core_ref.refs_1_, bf16[256,1024]{1,0:T(8,128)(2,1)S(1)} %get-tuple-element.41.own_ref, bf16[256,1024]{1,0:T(8,128)(2,1)S(1)} %collective-permute-done.5.other_ref, bf16[2048,2048]{1,0:T(8,128)(2,1)} %w_hbm.5), custom_call_target="tpu_custom_call" | custom-call | flops 1073741824 | bytes 6291456 | tf_op jit(solution)/shard_map/project/pallas_call | solution.py:162
  54.6 4.7 %collective-permute-done.9.last_ref = bf16[128,1024]{1,0:T(8,128)(2,1)S(1)} collective-permute-done((bf16[128,1024]{1,0:T(8,128)(2,1)S(1)}, bf16[128,1024]{1,0:T(8,128)(2,1)S(1)}, u32[]{:S(2)}, u32[]{:S(2)}) %collective-permute-start.9) | collective-permute-done | bytes 262176 | tf_op jit(solution)/shard_map/ppermute | solution.py:522
  59.3 1.3 %settle.1 = (bf16[256,1024]{1,0:T(8,128)(2,1)}, bf16[256,1024]{1,0:T(8,128)(2,1)}) custom-call(s32[1]{0:T(128)} %bitcast.1.after.me_ref.refs_0_, s32[1]{0:T(128)} %bitcast.core_ref.refs_1_, f32[256,1024]{1,0:T(8,128)S(1)} %get-tuple-element.43.gk_ref, f32[256,1024]{1,0:T(8,128)S(1)} %get-tuple-element.44.gv_ref, ...), custom_call_target="tpu_custom_call" | custom-call | tf_op jit(solution)/shard_map/settle/pallas_call | solution.py:458
  (19 shorter events, 0.1 us)
Async XLA Ops:
  0.6 10.7 %collective-permute-start = (bf16[256,1024]{1,0:T(8,128)(2,1)}, bf16[256,1024]{1,0:T(8,128)(2,1)}, u32[]{:S(2)}, u32[]{:S(2)}) collective-permute-start(bf16[256,1024]{1,0:T(8,128)(2,1)} %own_ref.3), channel_id=1, source_target_pairs={{0,1},{1,0},{2,3},{3,2},{4,5},{5,4},{6,7},{7,6},{8,9},{9,8},{10,11... | collective-permute-start | bytes 1572872 | tf_op jit(solution)/shard_map/ppermute | solution.py:47
  3.3 13.5 %collective-permute-start.1 = (bf16[128,1024]{1,0:T(8,128)(2,1)}, bf16[128,1024]{1,0:T(8,128)(2,1)S(1)}, u32[]{:S(2)}, u32[]{:S(2)}) collective-permute-start(bf16[128,1024]{1,0:T(8,128)(2,1)} %pick.1.picked_ref), channel_id=1, source_target_pairs={{0,8},{2,10},{4,12},{6,14},{8,16},{10,18},{12,20},{14,22},{16,24},... | collective-permute-start | bytes 786440 | tf_op jit(solution)/shard_map/ppermute | solution.py:484
  7.9 20.7 %collective-permute-start.2 = (bf16[128,1024]{1,0:T(8,128)(2,1)}, bf16[128,1024]{1,0:T(8,128)(2,1)S(1)}, u32[]{:S(2)}, u32[]{:S(2)}) collective-permute-start(bf16[128,1024]{1,0:T(8,128)(2,1)} %pick.1.picked_ref), channel_id=1, source_target_pairs={{0,2},{2,4},{4,6},{6,8},{8,10},{10,12},{12,14},{14,16},{16,18},{18... | collective-permute-start | bytes 786440 | tf_op jit(solution)/shard_map/ppermute | solution.py:485
  11.3 1.0 %copy-start.3 = (bf16[256,1024]{1,0:T(8,128)(2,1)S(1)}, bf16[256,1024]{1,0:T(8,128)(2,1)}, u32[]{:S(2)}) copy-start(bf16[256,1024]{1,0:T(8,128)(2,1)} %own_ref.3) | copy-start | bytes 1572868
  12.3 4.5 %copy-start.4 = (bf16[128,1024]{1,0:T(8,128)(2,1)S(1)}, bf16[128,1024]{1,0:T(8,128)(2,1)}, u32[]{:S(2)}) copy-start(bf16[128,1024]{1,0:T(8,128)(2,1)} %pick.1.picked_ref) | copy-start | bytes 786436
  17.0 13.7 %collective-permute-start.3 = (bf16[128,1024]{1,0:T(8,128)(2,1)S(1)}, bf16[128,1024]{1,0:T(8,128)(2,1)S(1)}, u32[]{:S(2)}, u32[]{:S(2)}) collective-permute-start(bf16[128,1024]{1,0:T(8,128)(2,1)S(1)} %get-tuple-element.30.after), channel_id=1, source_target_pairs={{0,8},{2,10},{4,12},{6,14},{8,16},{10,18},{12,20},{14,22},{16,24},... | collective-permute-start | bytes 786440 | tf_op jit(solution)/shard_map/ppermute | solution.py:43
  20.4 8.1 %copy-start = (bf16[256,1024]{1,0:T(8,128)(2,1)S(1)}, bf16[256,1024]{1,0:T(8,128)(2,1)}, u32[]{:S(2)}) copy-start(bf16[256,1024]{1,0:T(8,128)(2,1)} %q_ref.3) | copy-start | bytes 1572868
  20.5 8.1 %copy-start.1 = (bf16[256,1024]{1,0:T(8,128)(2,1)S(1)}, bf16[256,1024]{1,0:T(8,128)(2,1)}, u32[]{:S(2)}) copy-start(bf16[256,1024]{1,0:T(8,128)(2,1)} %k_ref.3) | copy-start | bytes 1572868
  20.5 8.1 %copy-start.2 = (bf16[256,1024]{1,0:T(8,128)(2,1)S(1)}, bf16[256,1024]{1,0:T(8,128)(2,1)}, u32[]{:S(2)}) copy-start(bf16[256,1024]{1,0:T(8,128)(2,1)} %v_ref.3) | copy-start | bytes 1572868
  20.5 8.1 %copy-start.5 = (s32[4]{0:T(128)S(1)}, s32[4]{0:T(128)}, u32[]{:S(2)}) copy-start(s32[4]{0:T(128)} %bounds_ref.1) | copy-start | bytes 52
  20.5 10.2 %collective-permute-start.4 = (bf16[128,1024]{1,0:T(8,128)(2,1)S(1)}, bf16[128,1024]{1,0:T(8,128)(2,1)S(1)}, u32[]{:S(2)}, u32[]{:S(2)}) collective-permute-start(bf16[128,1024]{1,0:T(8,128)(2,1)S(1)} %get-tuple-element.36), channel_id=1, source_target_pairs={{0,4},{2,6},{4,0},{6,2},{8,12},{10,14},{12,8},{14,10},{16,20},{18,... | collective-permute-start | bytes 786440 | tf_op jit(solution)/shard_map/ppermute | solution.py:43
  33.3 7.7 %collective-permute-start.6 = (bf16[128,1024]{1,0:T(8,128)(2,1)S(1)}, bf16[128,1024]{1,0:T(8,128)(2,1)S(1)}, u32[]{:S(2)}, u32[]{:S(2)}) collective-permute-start(bf16[128,1024]{1,0:T(8,128)(2,1)S(1)} %get-tuple-element.46), channel_id=1, source_target_pairs={{4,0},{6,2},{0,4},{2,6},{12,8},{14,10},{8,12},{10,14},{20,16},{22,... | collective-permute-start | bytes 786440 | tf_op jit(solution)/shard_map/ppermute | solution.py:43
  33.9 8.5 %collective-permute-start.7 = (bf16[128,1024]{1,0:T(8,128)(2,1)S(1)}, bf16[128,1024]{1,0:T(8,128)(2,1)S(1)}, u32[]{:S(2)}, u32[]{:S(2)}) collective-permute-start(bf16[128,1024]{1,0:T(8,128)(2,1)S(1)} %get-tuple-element.47), channel_id=1, source_target_pairs={{2,0},{4,2},{6,4},{0,6},{10,8},{12,10},{14,12},{8,14},{18,16},{20,... | collective-permute-start | bytes 786440 | tf_op jit(solution)/shard_map/ppermute | solution.py:43
  41.0 9.9 %collective-permute-start.5 = (bf16[256,1024]{1,0:T(8,128)(2,1)S(1)}, bf16[256,1024]{1,0:T(8,128)(2,1)S(1)}, u32[]{:S(2)}, u32[]{:S(2)}) collective-permute-start(bf16[256,1024]{1,0:T(8,128)(2,1)S(1)} %get-tuple-element.41.own_ref), channel_id=1, source_target_pairs={{0,1},{1,0},{2,3},{3,2},{4,5},{5,4},{6,7},{7,6},{8,9},{9,8},{10,11... | collective-permute-start | bytes 1572872 | tf_op jit(solution)/shard_map/ppermute | solution.py:47
  41.1 8.3 %collective-permute-start.8 = (bf16[128,1024]{1,0:T(8,128)(2,1)S(1)}, bf16[128,1024]{1,0:T(8,128)(2,1)S(1)}, u32[]{:S(2)}, u32[]{:S(2)}) collective-permute-start(bf16[128,1024]{1,0:T(8,128)(2,1)S(1)} %add_convert_fusion), channel_id=1, source_target_pairs={{8,0},{10,2},{12,4},{14,6},{16,8},{18,10},{20,12},{22,14},{24,16},... | collective-permute-start | bytes 786440 | tf_op jit(solution)/shard_map/ppermute | solution.py:43
  49.6 9.8 %collective-permute-start.9 = (bf16[128,1024]{1,0:T(8,128)(2,1)S(1)}, bf16[128,1024]{1,0:T(8,128)(2,1)S(1)}, u32[]{:S(2)}, u32[]{:S(2)}) collective-permute-start(bf16[128,1024]{1,0:T(8,128)(2,1)S(1)} %collect.1), channel_id=1, source_target_pairs={{8,0},{10,2},{12,4},{14,6},{16,8},{18,10},{20,12},{22,14},{24,16},... | collective-permute-start | bytes 786440 | tf_op jit(solution)/shard_map/ppermute | solution.py:522
